TPU v7x, 32 devices: a whole 2x2x4 slice. The times are simulated.
32 devices in a mesh: sub: 16 (over z, y, x), crow: 2 (over core), ccol: 1.
Axes of the slice: x: 2, y: 2, z: 4, core: 2. Of those that a mesh axis runs over, the one named last changes fastest.
Arguments:
- loads: bfloat16 [32, 1024, 128], P('sub'), may hold values from -6 to 6
- stiffness: bfloat16 [32, 1024, 1024], P('sub', ('crow', 'ccol'))
- local_inverse: bfloat16 [32, 1024, 1024], P('sub', ('crow', 'ccol'))
- coarse_basis: bfloat16 [32, 1024, 48], P('sub', ('crow', 'ccol')), may hold values from -0.1875 to 0.1875
- coarse_inverse: bfloat16 [1536, 1536], P('sub', ('crow', 'ccol'))
- coarse_index: int32 [32, 48], P('sub'), may hold values from 0 to 1535, as said below
- left_rows: int32 [32, 128], P('sub'), may hold values from 0 to 1023, as said below
- right_rows: int32 [32, 128], P('sub'), may hold values from 0 to 1023, as said below
Outputs:
- second_pass: float32 [32, 1024, 128], P('sub', ('crow', 'ccol'))
- final_residual: float32 [32, 1024, 128], P('sub', ('crow', 'ccol'))
Inputs may be any that keep to these rules, and one draw needn't show every extreme that they name: `coarse_index`: every value 0 to 1535 appears exactly once in the whole array. Of the 96 values in the rows of one index of sub, at most 96 lie in one block of 768 consecutive coarse rows starting at a multiple of 768, and that most is reached. In each subdomain the 128 entries of left_rows and the 128 entries of right_rows are 256 distinct rows. `right_rows`: see left_rows.
All inputs are finite; a program needn't handle non-finite values.
Results may differ from a plain program's by a relative error of at most 0.0067.
Values may be sent and summed in bfloat16 or wider, within the bound.
No kernel may reach another device: no remote copies, remote signals or barrier semaphores. Data moves between devices by JAX's collectives and lax.ppermute only.
A program may use at most 64 MiB of HBM per device.

v0:
```python
import jax
import jax.numpy as jnp
from jax import lax
from jax.sharding import PartitionSpec as P


def padded(block, sides, width):
    for axis, dim in sides:
        count = lax.axis_size(axis)
        forward = [(i, i + 1) for i in range(count - 1)]
        forward.append((count - 1, 0))
        backward = [(target, source) for source, target in forward]
        low = lax.ppermute(
            lax.slice_in_dim(block, block.shape[dim] - width, None, axis=dim), axis, forward
        )
        high = lax.ppermute(lax.slice_in_dim(block, 0, width, axis=dim), axis, backward)
        block = jnp.concatenate([low, block, high], axis=dim)
    return block


def fold_product(matrix, gathered_piece):
    return jnp.einsum("sij,sjc->sic", matrix, gathered_piece, preferred_element_type=jnp.float32)


def apply_stiffness(iterate, stiffness, left_rows, right_rows, pick_left, pick_right):
    sub_count, row_count, case_count = iterate.shape
    rounded = iterate.astype(jnp.bfloat16)
    product = fold_product(stiffness, lax.all_gather(rounded, ("crow", "ccol"), axis=1, tiled=True))
    product_b = product.astype(jnp.bfloat16)
    whole_rows = lax.all_gather(product_b, ("crow", "ccol"), axis=1, tiled=True)
    sub_rows = jnp.arange(sub_count, dtype=jnp.int32)[:, None]
    boundary = jnp.stack(
        [whole_rows[sub_rows, left_rows], whole_rows[sub_rows, right_rows]], axis=1
    )
    extended = padded(boundary, (("sub", 0),), 1)
    from_before = extended[:sub_count, 1]
    from_after = extended[2:, 0]
    added_left = jnp.einsum(
        "sfi,sfc->sic", pick_left, from_before, preferred_element_type=jnp.float32
    )
    added_right = jnp.einsum(
        "sfi,sfc->sic", pick_right, from_after, preferred_element_type=jnp.float32
    )
    return product_b.astype(jnp.float32) + added_left + added_right


def coarse_step(restricted, coarse_inverse, coarse_index):
    sub_count, mode_count, case_count = restricted.shape
    flat_rows = restricted.reshape(sub_count * mode_count, case_count)
    flat_index = coarse_index.reshape(-1)
    owned_rows, block_width = coarse_inverse.shape
    block_index = lax.axis_index(("crow", "ccol"))
    arrived, arrived_index = (
        lax.all_gather(flat_rows, "sub", axis=0, tiled=True),
        lax.all_gather(flat_index, "sub", axis=0, tiled=True),
    )
    shifted_place = arrived_index - block_index * block_width
    inside = (shifted_place >= 0) & (shifted_place < block_width)
    arrived_place = jnp.where(inside, shifted_place, block_width)
    ordered = (
        jnp.zeros((block_width + 1, case_count), jnp.bfloat16)
        .at[arrived_place]
        .set(arrived)[:block_width]
    )
    partial_coarse = jnp.dot(coarse_inverse, ordered, preferred_element_type=jnp.float32)
    coarse = lax.psum(partial_coarse, ("crow", "ccol")).astype(jnp.bfloat16)
    everything = lax.all_gather(coarse, "sub", axis=0, tiled=True)
    picked = everything[flat_index]
    return picked.reshape(sub_count, mode_count, case_count)


def precondition(local_part, residual_rows, coarse_basis, coarse_inverse, coarse_index):
    partial_modes = jnp.einsum(
        "sik,sic->skc", coarse_basis, residual_rows, preferred_element_type=jnp.float32
    )
    restricted = lax.psum(partial_modes, ("crow", "ccol")).astype(jnp.bfloat16)
    picked = coarse_step(restricted, coarse_inverse, coarse_index)
    return local_part + jnp.einsum(
        "sik,skc->sic", coarse_basis, picked, preferred_element_type=jnp.float32
    )


def body(
    loads,
    stiffness,
    local_inverse,
    coarse_basis,
    coarse_inverse,
    coarse_index,
    left_rows,
    right_rows,
):
    sub_count, row_count, iface_count = stiffness.shape
    group_index = lax.axis_index(("crow", "ccol"))
    first_row = group_index * row_count
    loads_rows = lax.dynamic_slice_in_dim(loads, first_row, row_count, 1)
    local_rows = first_row + jnp.arange(row_count, dtype=jnp.int32)
    pick_left = (left_rows[:, :, None] == local_rows[None, None, :]).astype(jnp.bfloat16)
    pick_right = (right_rows[:, :, None] == local_rows[None, None, :]).astype(jnp.bfloat16)
    first_local = jnp.einsum(
        "sij,sjc->sic", local_inverse, loads, preferred_element_type=jnp.float32
    )
    first_pass = precondition(first_local, loads_rows, coarse_basis, coarse_inverse, coarse_index)
    image_first = apply_stiffness(
        first_pass, stiffness, left_rows, right_rows, pick_left, pick_right
    )
    residual_b = (loads_rows.astype(jnp.float32) - image_first).astype(jnp.bfloat16)
    second_local = fold_product(
        local_inverse, lax.all_gather(residual_b, ("crow", "ccol"), axis=1, tiled=True)
    )
    second_pass = first_pass + precondition(
        second_local, residual_b, coarse_basis, coarse_inverse, coarse_index
    )
    image_second = apply_stiffness(
        second_pass, stiffness, left_rows, right_rows, pick_left, pick_right
    )
    final_residual = loads_rows.astype(jnp.float32) - image_second
    return (second_pass, final_residual)


def solution(mesh):
    return jax.shard_map(
        body,
        mesh=mesh,
        in_specs=(
            P("sub", None, None),
            P("sub", ("crow", "ccol"), None),
            P("sub", ("crow", "ccol"), None),
            P("sub", ("crow", "ccol"), None),
            P("sub", ("crow", "ccol")),
            P("sub", None),
            P("sub", None),
            P("sub", None),
        ),
        out_specs=(P("sub", ("crow", "ccol"), None), P("sub", ("crow", "ccol"), None)),
        check_vma=False,
    )
```

profile of v0, /device:TPU:0, one launch (start us, length us, event | category | flops | bytes accessed | tf_op | source)
XLA Modules:
  0.0 261.2 jit_solution(998459613266780102)
XLA Ops:
  2.3 1.2 convolution_bitcast_fusion.4
  3.5 3.8 %psum.28 = bf16[2,48,128]{2,1,0:T(8,128)(2,1)S(1)} all-reduce(f32[2,48,128]{2,1,0:T(8,128)S(1)} %convolution_bitcast_fusion.4), channel_id=1, replica_groups=mesh['sub'=16,'crow'=2,'ccol'=1] {'crow','ccol'}, use_global_device_ids=true, to_apply=%region_0.0 | all-reduce | flops 12288 | bytes 73728 | tf_op jit(solution)/shard_map/psum | solution.py:76
  7.3 44.4 %all_gather.32 = bf16[1536,128]{1,0:T(8,128)(2,1)S(1)} all-gather(bf16[96,128]{1,0:T(8,128)(2,1)S(1)} %bitcast.89), channel_id=1, replica_groups=mesh['sub'=16,'crow'=2,'ccol'=1] {'sub'}, dimensions={0}, use_global_device_ids=true | all-gather | bytes 417792 | tf_op jit(solution)/shard_map/all_gather | solution.py:54
  51.7 1.2 dynamic-slice
  53.9 8.6 %all-reduce = s32[1536]{0:T(1024)S(1)} all-reduce(s32[1536]{0:T(1024)S(1)} %dynamic-update-slice), channel_id=1, replica_groups=mesh['sub'=16,'crow'=2,'ccol'=1] {'sub'}, use_global_device_ids=true, to_apply=%add | all-reduce | flops 1536 | bytes 12288
  62.6 4.5 %scatter_custom_fusion = bf16[769,128]{1,0:T(8,128)(2,1)S(1)} fusion(s32[1536]{0:T(1024)S(1)} %compare_select_fusion, bf16[1536,128]{1,0:T(8,128)(2,1)S(1)} %all_gather.32, bf16[]{:T(256)} %constant.8.clone.1), kind=kCustom, calls=%fused_computation.51 | custom fusion | bytes 196866 | tf_op jit(solution)/shard_map/scatter | solution.py:63
  67.0 1.1 convolution_bitcast_fusion.3
  68.2 3.5 %psum.29 = bf16[96,128]{1,0:T(8,128)(2,1)S(1)} all-reduce(f32[96,128]{1,0:T(8,128)S(1)} %convolution_bitcast_fusion.3), channel_id=1, replica_groups=mesh['sub'=16,'crow'=2,'ccol'=1] {'crow','ccol'}, use_global_device_ids=true, to_apply=%region_2.3 | all-reduce | flops 12288 | bytes 73728 | tf_op jit(solution)/shard_map/psum | solution.py:66
  71.7 46.1 %all_gather.33 = bf16[1536,128]{1,0:T(8,128)(2,1)} all-gather(bf16[96,128]{1,0:T(8,128)(2,1)S(1)} %psum.29), channel_id=1, replica_groups=mesh['sub'=16,'crow'=2,'ccol'=1] {'sub'}, dimensions={0}, use_global_device_ids=true | all-gather | bytes 417792 | tf_op jit(solution)/shard_map/all_gather | solution.py:67
  118.6 1.7 gather_fusion
  121.3 2.2 all_gather.34
  124.2 2.2 all_gather.35
  126.4 2.3 gather_fusion.1
  128.7 2.3 gather_fusion.2
  131.9 2.0 collective-permute-start
  133.9 2.8 %collective-permute-done.1 = bf16[1,2,128,128]{3,2,0,1:T(8,128)(2,1)S(1)} collective-permute-done((bf16[1,2,128,128]{3,2,0,1:T(8,128)(2,1)S(1)}, bf16[1,2,128,128]{3,2,0,1:T(8,128)(2,1)S(1)}, u32[]{:S(2)}, u32[]{:S(2)}) %collective-permute-start.1) | collective-permute-done | bytes 65568 | tf_op jit(solution)/shard_map/ppermute | solution.py:16
  137.7 2.1 collective-permute-done
  141.0 2.2 all_gather.36
  143.2 3.5 %psum.30 = bf16[2,48,128]{2,1,0:T(8,128)(2,1)S(1)} all-reduce(f32[2,48,128]{2,1,0:T(8,128)S(1)} %convolution_bitcast_fusion.2), channel_id=1, replica_groups=mesh['sub'=16,'crow'=2,'ccol'=1] {'crow','ccol'}, use_global_device_ids=true, to_apply=%region_3.4 | all-reduce | flops 12288 | bytes 73728 | tf_op jit(solution)/shard_map/psum | solution.py:76
  146.7 41.0 %all_gather.37 = bf16[1536,128]{1,0:T(8,128)(2,1)} all-gather(bf16[96,128]{1,0:T(8,128)(2,1)S(1)} %bitcast.90), channel_id=1, replica_groups=mesh['sub'=16,'crow'=2,'ccol'=1] {'sub'}, dimensions={0}, use_global_device_ids=true | all-gather | bytes 417792 | tf_op jit(solution)/shard_map/all_gather | solution.py:54
  187.7 4.8 %scatter_custom_fusion.1 = bf16[769,128]{1,0:T(8,128)(2,1)S(1)} fusion(s32[1536]{0:T(1024)S(1)} %compare_select_fusion, bf16[1536,128]{1,0:T(8,128)(2,1)} %all_gather.37, bf16[]{:T(256)} %constant.8.clone.1), kind=kCustom, calls=%fused_computation.49 | custom fusion | bytes 197376 | tf_op jit(solution)/shard_map/scatter | solution.py:63
  193.6 3.5 %psum.31 = bf16[96,128]{1,0:T(8,128)(2,1)S(1)} all-reduce(f32[96,128]{1,0:T(8,128)S(1)} %convolution_bitcast_fusion.1), channel_id=1, replica_groups=mesh['sub'=16,'crow'=2,'ccol'=1] {'crow','ccol'}, use_global_device_ids=true, to_apply=%region_5.6 | all-reduce | flops 12288 | bytes 73728 | tf_op jit(solution)/shard_map/psum | solution.py:66
  197.2 40.9 %all_gather.38 = bf16[1536,128]{1,0:T(8,128)(2,1)} all-gather(bf16[96,128]{1,0:T(8,128)(2,1)S(1)} %psum.31), channel_id=1, replica_groups=mesh['sub'=16,'crow'=2,'ccol'=1] {'sub'}, dimensions={0}, use_global_device_ids=true | all-gather | bytes 417792 | tf_op jit(solution)/shard_map/all_gather | solution.py:67
  238.0 1.7 gather_fusion.3
  241.8 2.2 all_gather.39
  244.7 2.4 all_gather.40
  247.1 1.7 gather_fusion.5
  248.7 1.7 gather_fusion.4
  250.4 1.2 collective-permute-start.3
  252.5 2.2 collective-permute-done.3
  255.0 4.5 %collective-permute-done.2 = bf16[1,2,128,128]{3,2,0,1:T(8,128)(2,1)S(1)} collective-permute-done((bf16[1,2,128,128]{3,2,0,1:T(8,128)(2,1)S(1)}, bf16[1,2,128,128]{3,2,0,1:T(8,128)(2,1)S(1)}, u32[]{:S(2)}, u32[]{:S(2)}) %collective-permute-start.2) | collective-permute-done | bytes 65568 | tf_op jit(solution)/shard_map/ppermute | solution.py:13
  259.5 1.8 fusion.6
  (41 shorter events, 12.7 us)
Async XLA Ops:
  0.6 117.2 %copy-start = (bf16[2,512,1024]{2,1,0:T(8,128)(2,1)S(1)}, bf16[2,512,1024]{2,1,0:T(8,128)(2,1)}, u32[]{:S(2)}) copy-start(bf16[2,512,1024]{2,1,0:T(8,128)(2,1)} %param.10) | copy-start | bytes 6291460
  0.6 117.2 %copy-start.1 = (bf16[2,1024,128]{2,1,0:T(8,128)(2,1)S(1)}, bf16[2,1024,128]{2,1,0:T(8,128)(2,1)}, u32[]{:S(2)}) copy-start(bf16[2,1024,128]{2,1,0:T(8,128)(2,1)} %param.8) | copy-start | bytes 1572868
  67.0 53.2 %copy-start.3 = (bf16[2,512,48]{1,2,0:T(8,128)(2,1)S(1)}, bf16[2,512,48]{1,2,0:T(8,128)(2,1)}, u32[]{:S(2)}) copy-start(bf16[2,512,48]{1,2,0:T(8,128)(2,1)} %param.11) | copy-start | bytes 294916
  120.3 3.3 %copy-start.6 = (bf16[2,512,1024]{2,1,0:T(8,128)(2,1)S(1)}, bf16[2,512,1024]{2,1,0:T(8,128)(2,1)}, u32[]{:S(2)}) copy-start(bf16[2,512,1024]{2,1,0:T(8,128)(2,1)} %param.9) | copy-start | bytes 6291460
  123.5 2.9 %copy-start.5 = (s32[2,128]{1,0:T(2,128)S(1)}, s32[2,128]{1,0:T(2,128)}, u32[]{:S(2)}) copy-start(s32[2,128]{1,0:T(2,128)} %param.14) | copy-start | bytes 3076
  123.5 2.9 %copy-start.4 = (s32[2,128]{1,0:T(2,128)S(1)}, s32[2,128]{1,0:T(2,128)}, u32[]{:S(2)}) copy-start(s32[2,128]{1,0:T(2,128)} %param.15) | copy-start | bytes 3076
  131.8 4.9 %collective-permute-start.1 = (bf16[1,2,128,128]{3,2,0,1:T(8,128)(2,1)S(1)}, bf16[1,2,128,128]{3,2,0,1:T(8,128)(2,1)S(1)}, u32[]{:S(2)}, u32[]{:S(2)}) collective-permute-start(bf16[1,2,128,128]{3,2,0,1:T(8,128)(2,1)S(1)} %get-tuple-element.5), channel_id=1, source_target_pairs={{2,0},{4,2},{6,4},{8,6},{10,8},{12,10},{14,12},{16,14},{18,16},{20... | collective-permute-start | bytes 196616 | tf_op jit(solution)/shard_map/ppermute | solution.py:16
  131.9 7.9 %collective-permute-start = (bf16[1,2,128,128]{3,2,0,1:T(8,128)(2,1)S(1)}, bf16[1,2,128,128]{3,2,0,1:T(8,128)(2,1)S(1)}, u32[]{:S(2)}, u32[]{:S(2)}) collective-permute-start(bf16[1,2,128,128]{3,2,0,1:T(8,128)(2,1)S(1)} %get-tuple-element.4), channel_id=1, source_target_pairs={{0,2},{2,4},{4,6},{6,8},{8,10},{10,12},{12,14},{14,16},{16,18},{18... | collective-permute-start | bytes 196616 | tf_op jit(solution)/shard_map/ppermute | solution.py:13
  239.7 1.0 copy-start.2
  240.4 3.6 %copy-start.7 = (bf16[2,512,1024]{2,1,0:T(8,128)(2,1)S(1)}, bf16[2,512,1024]{2,1,0:T(8,128)(2,1)}, u32[]{:S(2)}) copy-start(bf16[2,512,1024]{2,1,0:T(8,128)(2,1)} %param.9) | copy-start | bytes 6291460
  250.4 4.3 %collective-permute-start.3 = (bf16[1,2,128,128]{3,2,0,1:T(8,128)(2,1)S(1)}, bf16[1,2,128,128]{3,2,0,1:T(8,128)(2,1)S(1)}, u32[]{:S(2)}, u32[]{:S(2)}) collective-permute-start(bf16[1,2,128,128]{3,2,0,1:T(8,128)(2,1)S(1)} %get-tuple-element.3), channel_id=1, source_target_pairs={{2,0},{4,2},{6,4},{8,6},{10,8},{12,10},{14,12},{16,14},{18,16},{20... | collective-permute-start | bytes 196616 | tf_op jit(solution)/shard_map/ppermute | solution.py:16
  251.6 7.9 %collective-permute-start.2 = (bf16[1,2,128,128]{3,2,0,1:T(8,128)(2,1)S(1)}, bf16[1,2,128,128]{3,2,0,1:T(8,128)(2,1)S(1)}, u32[]{:S(2)}, u32[]{:S(2)}) collective-permute-start(bf16[1,2,128,128]{3,2,0,1:T(8,128)(2,1)S(1)} %get-tuple-element.2), channel_id=1, source_target_pairs={{0,2},{2,4},{4,6},{6,8},{8,10},{10,12},{12,14},{14,16},{16,18},{18... | collective-permute-start | bytes 196616 | tf_op jit(solution)/shard_map/ppermute | solution.py:13
where the time goes:
time: 262 us; the launch traced here: 261 us
  blocking collectives  206 us (79%)
  local copies, waits for them, and re-layouts  24 us (9%)
  matrix products  12.7 us (5%)
  waiting for transfers between devices  11.6 us (4%)
  starting transfers between devices  4.15 us (2%)
    all_gather x2, blocking collectives, coarse_step(): everything = lax.all_gather(coarse, 'sub', axis=0, tiled=True)  87 us
    all_gather x2, blocking collectives, coarse_step(): lax.all_gather(flat_rows, 'sub', axis=0, tiled=True)  85.4 us
    scatter x2, local copies, waits for them, and re-layouts, coarse_step(): ordered = jnp.zeros((block_width + 1, case_count), jnp.bfloat16).at[arriv...  9.28 us
    unnamed x1, blocking collectives  8.64 us
    psum x2, blocking collectives, precondition(): restricted = lax.psum(partial_modes, ('crow', 'ccol')).astype(jnp.bfloat16)  7.28 us
    psum x2, blocking collectives, coarse_step(): coarse = lax.psum(partial_coarse, ('crow', 'ccol')).astype(jnp.bfloat16)  7.01 us
    ppermute x2, waiting for transfers between devices, padded(): lax.ppermute(lax.slice_in_dim(block, block.shape[dim] - width, None, axis...  6.52 us
  transfers between devices with their start and end apart: 4, of which 4 were waited for; matrix products, arithmetic and copies ran while one was open for 1% of the time, Pallas kernels for 0%

commit v1 on v0

--- a/solution.py
+++ b/solution.py
@@ -16,6 +16,37 @@
         high = lax.ppermute(lax.slice_in_dim(block, 0, width, axis=dim), axis, backward)
         block = jnp.concatenate([low, block, high], axis=dim)
     return block
+
+
+def stages(count):
+    widths = []
+    stride = 1
+    while count > 1:
+        factor = 2 if count % 2 == 0 else count
+        widths.append((stride, factor))
+        stride *= factor
+        count //= factor
+    return widths
+
+
+def gather_staged(block, axis):
+    count = lax.axis_size(axis)
+    out = block[None]
+    for stride, factor in stages(count):
+        groups = [
+            [base + stride * k for k in range(factor)]
+            for base in range(count)
+            if (base // stride) % factor == 0
+        ]
+        out = lax.all_gather(out, axis, axis=0, tiled=True, axis_index_groups=groups)
+    return out.reshape((count * block.shape[0],) + block.shape[1:])
+
+
+def gather_direct(block, axis):
+    count = lax.axis_size(axis)
+    copies = jnp.broadcast_to(block[None], (count,) + block.shape)
+    out = lax.all_to_all(copies, axis, 0, 0)
+    return out.reshape((count * block.shape[0],) + block.shape[1:])
 
 
 def fold_product(matrix, gathered_piece):
@@ -44,14 +75,14 @@
     return product_b.astype(jnp.float32) + added_left + added_right
 
 
-def coarse_step(restricted, coarse_inverse, coarse_index):
+def coarse_step(restricted, coarse_inverse, coarse_index, spread):
     sub_count, mode_count, case_count = restricted.shape
     flat_rows = restricted.reshape(sub_count * mode_count, case_count)
     flat_index = coarse_index.reshape(-1)
     owned_rows, block_width = coarse_inverse.shape
     block_index = lax.axis_index(("crow", "ccol"))
     arrived, arrived_index = (
-        lax.all_gather(flat_rows, "sub", axis=0, tiled=True),
+        spread(flat_rows, "sub"),
         lax.all_gather(flat_index, "sub", axis=0, tiled=True),
     )
     shifted_place = arrived_index - block_index * block_width
@@ -64,17 +95,17 @@
     )
     partial_coarse = jnp.dot(coarse_inverse, ordered, preferred_element_type=jnp.float32)
     coarse = lax.psum(partial_coarse, ("crow", "ccol")).astype(jnp.bfloat16)
-    everything = lax.all_gather(coarse, "sub", axis=0, tiled=True)
+    everything = spread(coarse, "sub")
     picked = everything[flat_index]
     return picked.reshape(sub_count, mode_count, case_count)
 
 
-def precondition(local_part, residual_rows, coarse_basis, coarse_inverse, coarse_index):
+def precondition(local_part, residual_rows, coarse_basis, coarse_inverse, coarse_index, spread):
     partial_modes = jnp.einsum(
         "sik,sic->skc", coarse_basis, residual_rows, preferred_element_type=jnp.float32
     )
     restricted = lax.psum(partial_modes, ("crow", "ccol")).astype(jnp.bfloat16)
-    picked = coarse_step(restricted, coarse_inverse, coarse_index)
+    picked = coarse_step(restricted, coarse_inverse, coarse_index, spread)
     return local_part + jnp.einsum(
         "sik,skc->sic", coarse_basis, picked, preferred_element_type=jnp.float32
     )
@@ -100,7 +131,9 @@
     first_local = jnp.einsum(
         "sij,sjc->sic", local_inverse, loads, preferred_element_type=jnp.float32
     )
-    first_pass = precondition(first_local, loads_rows, coarse_basis, coarse_inverse, coarse_index)
+    first_pass = precondition(
+        first_local, loads_rows, coarse_basis, coarse_inverse, coarse_index, gather_staged
+    )
     image_first = apply_stiffness(
         first_pass, stiffness, left_rows, right_rows, pick_left, pick_right
     )
@@ -109,7 +142,7 @@
         local_inverse, lax.all_gather(residual_b, ("crow", "ccol"), axis=1, tiled=True)
     )
     second_pass = first_pass + precondition(
-        second_local, residual_b, coarse_basis, coarse_inverse, coarse_index
+        second_local, residual_b, coarse_basis, coarse_inverse, coarse_index, gather_direct
     )
     image_second = apply_stiffness(
         second_pass, stiffness, left_rows, right_rows, pick_left, pick_right

time: 262 us -> 180 us (0.69)
  blocking collectives: 206 us -> 106 us
  waiting for transfers between devices: 11.6 us -> 23.4 us
  starting transfers between devices: 4.15 us -> 8.76 us
    all_gather x4 -> x8, blocking collectives: 172 us -> 49.1 us  [gather_staged(): lax.all_gather(out, axis, axis=0, tiled=True, axis_index_groups=groups)]
    all_to_all x0 -> x1, blocking collectives: none -> 16.4 us  [gather_direct(): out = lax.all_to_all(copies, axis, 0, 0)]
    all_to_all x0 -> x1, waiting for transfers between devices: none -> 9.47 us  [gather_direct(): out = lax.all_to_all(copies, axis, 0, 0)]
    unnamed x1, blocking collectives: 8.64 us -> 14.9 us
    all_to_all x0 -> x1, starting transfers between devices: none -> 4.2 us  [gather_direct(): out = lax.all_to_all(copies, axis, 0, 0)]
    ppermute x2, waiting for transfers between devices: 6.52 us -> 9.5 us  [padded(): lax.ppermute(lax.slice_in_dim(block, block.shape[dim] - width, None, axis...]
    ppermute x2, starting transfers between devices: 1.25 us -> 4.08 us  [padded(): lax.ppermute(lax.slice_in_dim(block, 0, width, axis=dim), axis, backward)]
  transfers between devices with their start and end apart: 4 -> 5, of which waited for: 4 -> 5; matrix products, arithmetic and copies ran while one was open for 1% -> 2% of each run, Pallas kernels for 0% -> 0%
where the time goes in v1:
time: 180 us; the launch traced here: 179 us
  blocking collectives  106 us (59%)
  local copies, waits for them, and re-layouts  24.6 us (14%)
  waiting for transfers between devices  23.4 us (13%)
  matrix products  14.6 us (8%)
  starting transfers between devices  8.76 us (5%)
    all_gather x8, blocking collectives, gather_staged(): lax.all_gather(out, axis, axis=0, tiled=True, axis_index_groups=groups)  49.1 us
    all_to_all x1, blocking collectives, gather_direct(): out = lax.all_to_all(copies, axis, 0, 0)  16.4 us
    unnamed x1, blocking collectives  14.9 us
    ppermute x2, waiting for transfers between devices, padded(): lax.ppermute(lax.slice_in_dim(block, block.shape[dim] - width, None, axis...  9.5 us
    all_to_all x1, waiting for transfers between devices, gather_direct(): out = lax.all_to_all(copies, axis, 0, 0)  9.47 us
    scatter x2, local copies, waits for them, and re-layouts, coarse_step(): ordered = jnp.zeros((block_width + 1, case_count), jnp.bfloat16).at[arriv...  9.28 us
    psum x2, blocking collectives, precondition(): restricted = lax.psum(partial_modes, ('crow', 'ccol')).astype(jnp.bfloat16)  7.3 us
    psum x2, blocking collectives, coarse_step(): coarse = lax.psum(partial_coarse, ('crow', 'ccol')).astype(jnp.bfloat16)  7.01 us
  transfers between devices with their start and end apart: 5, of which 5 were waited for; matrix products, arithmetic and copies ran while one was open for 2% of the time, Pallas kernels for 0%

profile of v1, /device:TPU:0, one launch (start us, length us, event | category | flops | bytes accessed | tf_op | source)
XLA Modules:
  0.0 179.4 jit_solution(16672707694038929224)
XLA Ops:
  3.5 3.8 %psum.28 = bf16[2,48,128]{2,1,0:T(8,128)(2,1)S(1)} all-reduce(f32[2,48,128]{2,1,0:T(8,128)S(1)} %convolution_bitcast_fusion.4), channel_id=1, replica_groups=mesh['sub'=16,'crow'=2,'ccol'=1] {'crow','ccol'}, use_global_device_ids=true, to_apply=%region_0.0 | all-reduce | flops 12288 | bytes 73728 | tf_op jit(solution)/shard_map/psum | solution.py:107
  7.3 5.1 %all_gather.44 = bf16[2,96,128]{2,1,0:T(8,128)(2,1)S(1)} all-gather(bf16[1,96,128]{2,1,0:T(8,128)(2,1)S(1)} %bitcast.99), channel_id=1, replica_groups={{0,2},{4,6},{8,10},{12,14},{16,18},{20,22},{24,26},{28,30},{1,3},{5,7},..., dimensions={0}, use_global_device_ids=true | all-gather | bytes 73728 | tf_op jit(solution)/shard_map/all_gather | solution.py:41
  12.4 4.8 %all_gather.45 = bf16[4,96,128]{2,1,0:T(8,128)(2,1)S(1)} all-gather(bf16[2,96,128]{2,1,0:T(8,128)(2,1)S(1)} %all_gather.44), channel_id=1, replica_groups={{0,4},{2,6},{8,12},{10,14},{16,20},{18,22},{24,28},{26,30},{1,5},{3,7},..., dimensions={0}, use_global_device_ids=true | all-gather | bytes 147456 | tf_op jit(solution)/shard_map/all_gather | solution.py:41
  17.2 5.3 %all_gather.46 = bf16[8,96,128]{2,1,0:T(8,128)(2,1)S(1)} all-gather(bf16[4,96,128]{2,1,0:T(8,128)(2,1)S(1)} %all_gather.45), channel_id=1, replica_groups={{0,8},{2,10},{4,12},{6,14},{16,24},{18,26},{20,28},{22,30},{1,9},{3,11}..., dimensions={0}, use_global_device_ids=true | all-gather | bytes 294912 | tf_op jit(solution)/shard_map/all_gather | solution.py:41
  22.5 9.9 %all_gather.47 = bf16[16,96,128]{2,1,0:T(8,128)(2,1)S(1)} all-gather(bf16[8,96,128]{2,1,0:T(8,128)(2,1)S(1)} %all_gather.46), channel_id=1, replica_groups={{0,16},{2,18},{4,20},{6,22},{8,24},{10,26},{12,28},{14,30},{1,17},{3,19..., dimensions={0}, use_global_device_ids=true | all-gather | bytes 589824 | tf_op jit(solution)/shard_map/all_gather | solution.py:41
  34.6 14.9 %all-reduce = s32[1536]{0:T(1024)S(1)} all-reduce(s32[1536]{0:T(1024)S(1)} %dynamic-update-slice), channel_id=1, replica_groups=mesh['sub'=16,'crow'=2,'ccol'=1] {'sub'}, use_global_device_ids=true, to_apply=%add | all-reduce | flops 1536 | bytes 12288
  49.5 4.5 %scatter_custom_fusion = bf16[769,128]{1,0:T(8,128)(2,1)S(1)} fusion(s32[1536]{0:T(1024)S(1)} %compare_select_fusion, bf16[1536,128]{1,0:T(8,128)(2,1)S(1)} %bitcast.94, bf16[]{:T(256)} %constant.8.clone.1), kind=kCustom, calls=%fused_computation.51 | custom fusion | bytes 196866 | tf_op jit(solution)/shard_map/scatter | solution.py:94
  55.1 3.5 %psum.29 = bf16[96,128]{1,0:T(8,128)(2,1)S(1)} all-reduce(f32[96,128]{1,0:T(8,128)S(1)} %convolution_bitcast_fusion.3), channel_id=1, replica_groups=mesh['sub'=16,'crow'=2,'ccol'=1] {'crow','ccol'}, use_global_device_ids=true, to_apply=%region_2.3 | all-reduce | flops 12288 | bytes 73728 | tf_op jit(solution)/shard_map/psum | solution.py:97
  58.6 4.5 %all-gather = bf16[192,128]{1,0:T(8,128)(2,1)S(1)} all-gather(bf16[96,128]{1,0:T(8,128)(2,1)S(1)} %psum.29), channel_id=2, replica_groups={{0,2},{4,6},{8,10},{12,14},{16,18},{20,22},{24,26},{28,30},{1,3},{5,7},..., dimensions={0}, use_global_device_ids=true | all-gather | bytes 73728 | tf_op jit(solution)/shard_map/all_gather | solution.py:41
  63.1 4.8 %all_gather.49 = bf16[4,96,128]{2,1,0:T(8,128)(2,1)S(1)} all-gather(bf16[2,96,128]{2,1,0:T(8,128)(2,1)S(1)} %bitcast.96), channel_id=1, replica_groups={{0,4},{2,6},{8,12},{10,14},{16,20},{18,22},{24,28},{26,30},{1,5},{3,7},..., dimensions={0}, use_global_device_ids=true | all-gather | bytes 147456 | tf_op jit(solution)/shard_map/all_gather | solution.py:41
  67.8 5.4 %all_gather.50 = bf16[8,96,128]{2,1,0:T(8,128)(2,1)S(1)} all-gather(bf16[4,96,128]{2,1,0:T(8,128)(2,1)S(1)} %all_gather.49), channel_id=1, replica_groups={{0,8},{2,10},{4,12},{6,14},{16,24},{18,26},{20,28},{22,30},{1,9},{3,11}..., dimensions={0}, use_global_device_ids=true | all-gather | bytes 294912 | tf_op jit(solution)/shard_map/all_gather | solution.py:41
  73.2 9.3 %all_gather.51 = bf16[16,96,128]{2,1,0:T(8,128)(2,1)} all-gather(bf16[8,96,128]{2,1,0:T(8,128)(2,1)S(1)} %all_gather.50), channel_id=1, replica_groups={{0,16},{2,18},{4,20},{6,22},{8,24},{10,26},{12,28},{14,30},{1,17},{3,19..., dimensions={0}, use_global_device_ids=true | all-gather | bytes 589824 | tf_op jit(solution)/shard_map/all_gather | solution.py:41
  86.0 2.2 %all_gather.52 = bf16[2,1024,128]{2,1,0:T(8,128)(2,1)S(1)} all-gather(bf16[2,512,128]{2,1,0:T(8,128)(2,1)S(1)} %get-tuple-element.6), channel_id=1, replica_groups=mesh['sub'=16,'crow'=2,'ccol'=1] {'crow','ccol'}, dimensions={1}, use_global_device_ids=true | all-gather | bytes 786432 | tf_op jit(solution)/shard_map/all_gather | solution.py:59
  88.9 2.2 %all_gather.53 = bf16[2,1024,128]{2,1,0:T(8,128)(2,1)S(1)} all-gather(bf16[2,512,128]{2,1,0:T(8,128)(2,1)S(1)} %fusion.8), channel_id=1, replica_groups=mesh['sub'=16,'crow'=2,'ccol'=1] {'crow','ccol'}, dimensions={1}, use_global_device_ids=true | all-gather | bytes 786432 | tf_op jit(solution)/shard_map/all_gather | solution.py:61
  91.1 2.3 %gather_fusion.1 = bf16[256,128]{1,0:T(8,128)(2,1)} fusion(bf16[2,1024,128]{2,1,0:T(8,128)(2,1)S(1)} %all_gather.53, s32[256]{0:T(256)S(1)} %fusion.54), kind=kCustom, calls=%fused_computation.1 | custom fusion | bytes 133120 | tf_op jit(solution)/shard_map/gather | solution.py:64
  93.4 2.3 %gather_fusion.2 = bf16[256,128]{1,0:T(8,128)(2,1)} fusion(bf16[2,1024,128]{2,1,0:T(8,128)(2,1)S(1)} %all_gather.53, s32[256]{0:T(256)S(1)} %fusion.53), kind=kCustom, calls=%fused_computation.2 | custom fusion | bytes 133120 | tf_op jit(solution)/shard_map/gather | solution.py:64
  98.6 2.2 %collective-permute-done.1 = bf16[1,2,128,128]{3,2,0,1:T(8,128)(2,1)S(1)} collective-permute-done((bf16[1,2,128,128]{3,2,0,1:T(8,128)(2,1)S(1)}, bf16[1,2,128,128]{3,2,0,1:T(8,128)(2,1)S(1)}, u32[]{:S(2)}, u32[]{:S(2)}) %collective-permute-start.1) | collective-permute-done | bytes 65568 | tf_op jit(solution)/shard_map/ppermute | solution.py:16
  101.8 4.1 %collective-permute-done = bf16[1,2,128,128]{3,2,0,1:T(8,128)(2,1)S(1)} collective-permute-done((bf16[1,2,128,128]{3,2,0,1:T(8,128)(2,1)S(1)}, bf16[1,2,128,128]{3,2,0,1:T(8,128)(2,1)S(1)}, u32[]{:S(2)}, u32[]{:S(2)}) %collective-permute-start) | collective-permute-done | bytes 65568 | tf_op jit(solution)/shard_map/ppermute | solution.py:13
  107.2 3.5 %psum.30 = bf16[2,48,128]{2,1,0:T(8,128)(2,1)S(1)} all-reduce(f32[2,48,128]{2,1,0:T(8,128)S(1)} %convolution_bitcast_fusion.2), channel_id=1, replica_groups=mesh['sub'=16,'crow'=2,'ccol'=1] {'crow','ccol'}, use_global_device_ids=true, to_apply=%region_3.4 | all-reduce | flops 12288 | bytes 73728 | tf_op jit(solution)/shard_map/psum | solution.py:107
  110.8 16.4 %all_to_all.10 = bf16[16,96,128]{2,1,0:T(8,128)(2,1)} all-to-all(bf16[16,96,128]{2,1,0:T(8,128)(2,1)S(1)} %broadcast_in_dim.28), channel_id=1, replica_groups=mesh['sub'=16,'crow'=2,'ccol'=1] {'sub'}, dimensions={0} | all-to-all | bytes 786432 | tf_op jit(solution)/shard_map/all_to_all | solution.py:48
  127.2 4.8 %scatter_custom_fusion.1 = bf16[769,128]{1,0:T(8,128)(2,1)S(1)} fusion(s32[1536]{0:T(1024)S(1)} %compare_select_fusion, bf16[1536,128]{1,0:T(8,128)(2,1)} %bitcast.95, bf16[]{:T(256)} %constant.8.clone.1), kind=kCustom, calls=%fused_computation.49 | custom fusion | bytes 197376 | tf_op jit(solution)/shard_map/scatter | solution.py:94
  133.1 3.5 %psum.31 = bf16[96,128]{1,0:T(8,128)(2,1)S(1)} all-reduce(f32[96,128]{1,0:T(8,128)S(1)} %convolution_bitcast_fusion.1), channel_id=1, replica_groups=mesh['sub'=16,'crow'=2,'ccol'=1] {'crow','ccol'}, use_global_device_ids=true, to_apply=%region_5.6 | all-reduce | flops 12288 | bytes 73728 | tf_op jit(solution)/shard_map/psum | solution.py:97
  137.4 4.2 %all-to-all-start.1 = ((bf16[16,96,128]{2,1,0:T(8,128)(2,1)}), bf16[16,96,128]{2,1,0:T(8,128)(2,1)}, u32[]{:S(2)}, u32[]{:S(2)}) async-start(bf16[16,96,128]{2,1,0:T(8,128)(2,1)} %broadcast_in_dim.29), calls=%async_computation.1 | async-start | bytes 786432 | tf_op jit(solution)/shard_map/all_to_all | solution.py:48
  141.6 2.2 %all_gather.54 = bf16[2,1024,128]{2,1,0:T(8,128)(2,1)S(1)} all-gather(bf16[2,512,128]{2,1,0:T(8,128)(2,1)S(1)} %fusion.7), channel_id=1, replica_groups=mesh['sub'=16,'crow'=2,'ccol'=1] {'crow','ccol'}, dimensions={1}, use_global_device_ids=true | all-gather | bytes 786432 | tf_op jit(solution)/shard_map/all_gather | solution.py:142
  145.3 9.5 %all-to-all-done.1 = bf16[16,96,128]{2,1,0:T(8,128)(2,1)} async-done(((bf16[16,96,128]{2,1,0:T(8,128)(2,1)}), bf16[16,96,128]{2,1,0:T(8,128)(2,1)}, u32[]{:S(2)}, u32[]{:S(2)}) %all-to-all-start.1) | async-done | bytes 393248 | tf_op jit(solution)/shard_map/all_to_all | solution.py:48
  156.5 2.3 %fusion.62 = (bf16[2,512,128]{2,1,0:T(8,128)(2,1)S(1)}, f32[2,512,128]{2,1,0:T(8,128)}) fusion(f32[2,512,128]{2,1,0:T(8,128)S(1)} %copy-done.2, f32[2,128,512]{1,2,0:T(8,128)} %fusion.64, bf16[2,48,128]{2,1,0:T(8,128)(2,1)S(1)} %bitcast.97, bf16[2,512,48]{1,2,0:T(8,128)(2,1)S(1)} %copy-done.3), kind=kOutput, calls=%fused_computation.97 | convolution fusion | flops 12976128 | bytes 1957888 | tf_op jit(solution)/shard_map/sik,skc->sic/dot_general | solution.py:109
  158.7 2.3 %all_gather.55 = bf16[2,1024,128]{2,1,0:T(8,128)(2,1)S(1)} all-gather(bf16[2,512,128]{2,1,0:T(8,128)(2,1)S(1)} %get-tuple-element.8), channel_id=1, replica_groups=mesh['sub'=16,'crow'=2,'ccol'=1] {'crow','ccol'}, dimensions={1}, use_global_device_ids=true | all-gather | bytes 786432 | tf_op jit(solution)/shard_map/all_gather | solution.py:59
  161.8 2.2 %all_gather.56 = bf16[2,1024,128]{2,1,0:T(8,128)(2,1)S(1)} all-gather(bf16[2,512,128]{2,1,0:T(8,128)(2,1)S(1)} %fusion.9), channel_id=1, replica_groups=mesh['sub'=16,'crow'=2,'ccol'=1] {'crow','ccol'}, dimensions={1}, use_global_device_ids=true | all-gather | bytes 786432 | tf_op jit(solution)/shard_map/all_gather | solution.py:61
  167.3 2.5 %collective-permute-start.3 = (bf16[1,2,128,128]{3,2,0,1:T(8,128)(2,1)S(1)}, bf16[1,2,128,128]{3,2,0,1:T(8,128)(2,1)S(1)}, u32[]{:S(2)}, u32[]{:S(2)}) collective-permute-start(bf16[1,2,128,128]{3,2,0,1:T(8,128)(2,1)S(1)} %get-tuple-element.3), channel_id=1, source_target_pairs={{2,0},{4,2},{6,4},{8,6},{10,8},{12,10},{14,12},{16,14},{18,16},{20... | collective-permute-start | bytes 196616 | tf_op jit(solution)/shard_map/ppermute | solution.py:16
  169.8 2.2 %collective-permute-done.3 = bf16[1,2,128,128]{3,2,0,1:T(8,128)(2,1)S(1)} collective-permute-done((bf16[1,2,128,128]{3,2,0,1:T(8,128)(2,1)S(1)}, bf16[1,2,128,128]{3,2,0,1:T(8,128)(2,1)S(1)}, u32[]{:S(2)}, u32[]{:S(2)}) %collective-permute-start.3) | collective-permute-done | bytes 65568 | tf_op jit(solution)/shard_map/ppermute | solution.py:16
  172.3 5.4 %collective-permute-done.2 = bf16[1,2,128,128]{3,2,0,1:T(8,128)(2,1)S(1)} collective-permute-done((bf16[1,2,128,128]{3,2,0,1:T(8,128)(2,1)S(1)}, bf16[1,2,128,128]{3,2,0,1:T(8,128)(2,1)S(1)}, u32[]{:S(2)}, u32[]{:S(2)}) %collective-permute-start.2) | collective-permute-done | bytes 65568 | tf_op jit(solution)/shard_map/ppermute | solution.py:13
  177.7 1.8 fusion.6
  (50 shorter events, 24.3 us)
Async XLA Ops:
  0.6 81.9 %copy-start = (bf16[2,512,1024]{2,1,0:T(8,128)(2,1)S(1)}, bf16[2,512,1024]{2,1,0:T(8,128)(2,1)}, u32[]{:S(2)}) copy-start(bf16[2,512,1024]{2,1,0:T(8,128)(2,1)} %param.10) | copy-start | bytes 6291460
  0.6 81.9 %copy-start.1 = (bf16[2,1024,128]{2,1,0:T(8,128)(2,1)S(1)}, bf16[2,1024,128]{2,1,0:T(8,128)(2,1)}, u32[]{:S(2)}) copy-start(bf16[2,1024,128]{2,1,0:T(8,128)(2,1)} %param.8) | copy-start | bytes 1572868
  67.8 17.1 %copy-start.3 = (bf16[2,512,48]{1,2,0:T(8,128)(2,1)S(1)}, bf16[2,512,48]{1,2,0:T(8,128)(2,1)}, u32[]{:S(2)}) copy-start(bf16[2,512,48]{1,2,0:T(8,128)(2,1)} %param.11) | copy-start | bytes 294916
  84.9 3.3 %copy-start.6 = (bf16[2,512,1024]{2,1,0:T(8,128)(2,1)S(1)}, bf16[2,512,1024]{2,1,0:T(8,128)(2,1)}, u32[]{:S(2)}) copy-start(bf16[2,512,1024]{2,1,0:T(8,128)(2,1)} %param.9) | copy-start | bytes 6291460
  88.2 2.9 %copy-start.5 = (s32[2,128]{1,0:T(2,128)S(1)}, s32[2,128]{1,0:T(2,128)}, u32[]{:S(2)}) copy-start(s32[2,128]{1,0:T(2,128)} %param.14) | copy-start | bytes 3076
  88.2 2.9 %copy-start.4 = (s32[2,128]{1,0:T(2,128)S(1)}, s32[2,128]{1,0:T(2,128)}, u32[]{:S(2)}) copy-start(s32[2,128]{1,0:T(2,128)} %param.15) | copy-start | bytes 3076
  96.5 4.3 %collective-permute-start.1 = (bf16[1,2,128,128]{3,2,0,1:T(8,128)(2,1)S(1)}, bf16[1,2,128,128]{3,2,0,1:T(8,128)(2,1)S(1)}, u32[]{:S(2)}, u32[]{:S(2)}) collective-permute-start(bf16[1,2,128,128]{3,2,0,1:T(8,128)(2,1)S(1)} %get-tuple-element.5), channel_id=1, source_target_pairs={{2,0},{4,2},{6,4},{8,6},{10,8},{12,10},{14,12},{16,14},{18,16},{20... | collective-permute-start | bytes 196616 | tf_op jit(solution)/shard_map/ppermute | solution.py:16
  98.1 7.9 %collective-permute-start = (bf16[1,2,128,128]{3,2,0,1:T(8,128)(2,1)S(1)}, bf16[1,2,128,128]{3,2,0,1:T(8,128)(2,1)S(1)}, u32[]{:S(2)}, u32[]{:S(2)}) collective-permute-start(bf16[1,2,128,128]{3,2,0,1:T(8,128)(2,1)S(1)} %get-tuple-element.4), channel_id=1, source_target_pairs={{0,2},{2,4},{4,6},{6,8},{8,10},{10,12},{12,14},{14,16},{16,18},{18... | collective-permute-start | bytes 196616 | tf_op jit(solution)/shard_map/ppermute | solution.py:13
  137.4 17.4 %all-to-all-start.1 = ((bf16[16,96,128]{2,1,0:T(8,128)(2,1)}), bf16[16,96,128]{2,1,0:T(8,128)(2,1)}, u32[]{:S(2)}, u32[]{:S(2)}) async-start(bf16[16,96,128]{2,1,0:T(8,128)(2,1)} %broadcast_in_dim.29), calls=%async_computation.1 | async-start | bytes 786432 | tf_op jit(solution)/shard_map/all_to_all | solution.py:48
  143.8 12.6 %copy-start.2 = (f32[2,512,128]{2,1,0:T(8,128)S(1)}, f32[2,512,128]{2,1,0:T(8,128)}, u32[]{:S(2)}) copy-start(f32[2,512,128]{2,1,0:T(8,128)} %get-tuple-element.7) | copy-start | bytes 1572868
  156.5 4.6 %copy-start.7 = (bf16[2,512,1024]{2,1,0:T(8,128)(2,1)S(1)}, bf16[2,512,1024]{2,1,0:T(8,128)(2,1)}, u32[]{:S(2)}) copy-start(bf16[2,512,1024]{2,1,0:T(8,128)(2,1)} %param.9) | copy-start | bytes 6291460
  167.3 4.7 %collective-permute-start.3 = (bf16[1,2,128,128]{3,2,0,1:T(8,128)(2,1)S(1)}, bf16[1,2,128,128]{3,2,0,1:T(8,128)(2,1)S(1)}, u32[]{:S(2)}, u32[]{:S(2)}) collective-permute-start(bf16[1,2,128,128]{3,2,0,1:T(8,128)(2,1)S(1)} %get-tuple-element.3), channel_id=1, source_target_pairs={{2,0},{4,2},{6,4},{8,6},{10,8},{12,10},{14,12},{16,14},{18,16},{20... | collective-permute-start | bytes 196616 | tf_op jit(solution)/shard_map/ppermute | solution.py:16
  169.8 7.9 %collective-permute-start.2 = (bf16[1,2,128,128]{3,2,0,1:T(8,128)(2,1)S(1)}, bf16[1,2,128,128]{3,2,0,1:T(8,128)(2,1)S(1)}, u32[]{:S(2)}, u32[]{:S(2)}) collective-permute-start(bf16[1,2,128,128]{3,2,0,1:T(8,128)(2,1)S(1)} %get-tuple-element.2), channel_id=1, source_target_pairs={{0,2},{2,4},{4,6},{6,8},{8,10},{10,12},{12,14},{14,16},{16,18},{18... | collective-permute-start | bytes 196616 | tf_op jit(solution)/shard_map/ppermute | solution.py:13

commit v2 on v0

v2 whole, which is shorter than its diff:
```python
import functools

import jax
import jax.numpy as jnp
import numpy as np
from jax import lax
from jax.experimental import pallas as pl
from jax.experimental.pallas import tpu as pltpu
from jax.sharding import PartitionSpec as P

GROUP = ("crow", "ccol")
F32 = jnp.float32
BF16 = jnp.bfloat16
VMEM_BYTES = 48 * 1024 * 1024
DIGIT_ROWS = 16
DIGIT = 256


def dot(a, b):
    return lax.dot_general(a, b, (((1,), (0,)), ((), ())), preferred_element_type=F32)


def dot_tn(a, b):
    return lax.dot_general(a, b, (((0,), (0,)), ((), ())), preferred_element_type=F32)


def dot_nt(a, b):
    return lax.dot_general(a, b, (((1,), (1,)), ((), ())), preferred_element_type=F32)


class Sizes:
    def __init__(self, loads, stiffness, coarse_basis, coarse_inverse, left_rows):
        self.n = lax.axis_size("sub")
        self.group = lax.axis_size(GROUP)
        self.subs, self.rows, self.cases = loads.shape
        self.own = stiffness.shape[1]
        self.modes = coarse_basis.shape[2]
        self.owned, self.block = coarse_inverse.shape
        self.total = self.block * self.group
        self.face = left_rows.shape[1]
        self.width = self.cases // self.group
        self.lanes = max(self.cases, -(-self.subs * self.width // 128) * 128)
        self.columns = self.n * self.modes


def lane_mask(z, block, shape):
    lane = lax.broadcasted_iota(jnp.int32, shape, len(shape) - 1)
    return (lane >= block * z.width) & (lane < (block + 1) * z.width)


def select(z, parts):
    out = jnp.zeros_like(parts[0])
    for s, part in enumerate(parts):
        out = jnp.where(lane_mask(z, s, part.shape), part, out)
    return out


def fold(z, packed):
    if z.lanes == z.subs * z.width:
        out = packed
        for k in range(1, z.subs):
            out = out + pltpu.roll(packed, k * z.width, 1)
        return out
    out = packed
    for k in range(1, z.subs):
        out = out + pltpu.roll(packed, k * z.width, 1)
        out = out + pltpu.roll(packed, z.lanes - k * z.width, 1)
    return out


def shift_matrix(z, source, target):
    row = lax.broadcasted_iota(jnp.int32, (z.lanes, z.lanes), 0)
    lane = lax.broadcasted_iota(jnp.int32, (z.lanes, z.lanes), 1)
    hit = (row - source * z.width == lane - target * z.width) & lane_mask(z, target, (z.lanes, z.lanes))
    return jnp.where(hit, 1.0, 0.0).astype(BF16)


def place_matrix(z, block):
    row = lax.broadcasted_iota(jnp.int32, (z.modes, 3 * z.modes), 0)
    lane = lax.broadcasted_iota(jnp.int32, (z.modes, 3 * z.modes), 1)
    return jnp.where(row + block * z.modes == lane, 1.0, 0.0).astype(BF16)


def piece_start(z, k, size):
    place = lax.rem(lax.axis_index(GROUP) + k, z.group)
    return pl.multiple_of(place * size, size)


def scatter_matrix(z, rows_of):
    row = lax.broadcasted_iota(jnp.int32, (z.rows, z.face), 0)
    return jnp.where(row == rows_of, 1.0, 0.0).astype(BF16)


def open_kernel(z, *refs):
    pieces = refs[: z.group]
    loads, digits, load_rows, basis_t, message = refs[z.group :]
    group = lax.axis_index(GROUP)
    for k, piece in enumerate(pieces):
        basis_t[:, :, pl.ds(piece_start(z, k, z.own), z.own)] = piece[...]
    row = lax.broadcasted_iota(jnp.int32, (z.cases, z.lanes), 0)
    lane = lax.broadcasted_iota(jnp.int32, (z.cases, z.lanes), 1)
    packed = jnp.zeros((z.rows, z.lanes), F32)
    for s in range(z.subs):
        hit = (row - group * z.width == lane - s * z.width) & lane_mask(z, s, row.shape)
        packed = packed + dot(loads[s], jnp.where(hit, 1.0, 0.0).astype(BF16))
    packed = packed.astype(BF16)
    load_rows[...] = packed
    modes = select(z, [dot(basis_t[s], packed) for s in range(z.subs)]).astype(BF16)
    for k in range(z.n):
        message[k, : z.modes, :] = modes
        message[k, z.modes :, :] = digits[...]


def multiply(z, pieces, vector, store):
    for k, piece in enumerate(pieces):
        parts = [dot(piece[s], vector) for s in range(z.subs)]
        store(piece_start(z, k, z.own), select(z, parts))


def face_picks(z, image, rows_ref, s):
    return dot_tn(scatter_matrix(z, rows_ref[s : s + 1, :]), image).astype(BF16)


def image_kernel(z, first, *refs):
    inverse, stiffness = refs[: z.group], refs[z.group : 2 * z.group]
    rest = refs[2 * z.group :]
    if first:
        vector, basis_t, left_rows, right_rows = rest[:4]
        solved, image, to_before, to_after, basis, image_basis = rest[4:10]
        rounded = rest[10]
    else:
        vector, base, left_rows, right_rows = rest[:4]
        solved, image, to_before, to_after = rest[4:8]
        rounded = rest[8]
    operand = vector[...]

    def store_solved(start, value):
        if not first:
            value = value + base[pl.ds(start, z.own), :]
        solved[pl.ds(start, z.own), :] = value
        rounded[pl.ds(start, z.own), :] = value.astype(BF16)

    multiply(z, inverse, operand, store_solved)

    def store_image(start, value):
        image[pl.ds(start, z.own), :] = value

    multiply(z, stiffness, rounded[...], store_image)
    if first:
        for s in range(z.subs):
            basis[s] = jnp.transpose(basis_t[s].astype(F32)).astype(BF16)
            for k, piece in enumerate(stiffness):
                start = piece_start(z, k, z.own)
                image_basis[s, pl.ds(start, z.own), :] = dot(piece[s], basis[s]).astype(BF16)
    image_b = image[...].astype(BF16)
    for s in range(z.subs):
        for rows_ref, out, target in (
            (left_rows, to_before, (s - 1) % z.subs),
            (right_rows, to_after, (s + 1) % z.subs),
        ):
            picked = face_picks(z, image_b, rows_ref, s)
            out[s, :, : z.lanes] = dot(picked, shift_matrix(z, s, target)).astype(BF16)
            if first:
                out[s, :, z.lanes : z.lanes + z.modes] = face_picks(z, image_basis[s], rows_ref, s)


def join_kernel(z, first, *refs):
    load_rows, image, to_before, to_after, from_before, from_after, left_rows, right_rows = refs[:8]
    if first:
        image_basis, residual, joined = refs[8:]
    else:
        (residual,) = refs[8:]
    added = []
    for s in range(z.subs):
        before = from_before[...] if s == 0 else to_after[s - 1]
        after = from_after[...] if s == z.subs - 1 else to_before[s + 1]
        left = scatter_matrix(z, left_rows[s : s + 1, :])
        right = scatter_matrix(z, right_rows[s : s + 1, :])
        added.append(dot(left, before[:, : z.lanes]) + dot(right, after[:, : z.lanes]))
        if first:
            cut = slice(z.lanes, z.lanes + z.modes)
            total = dot(left, dot(before[:, cut], place_matrix(z, 0)).astype(BF16))
            total = total + dot(image_basis[s], place_matrix(z, 1))
            total = total + dot(right, dot(after[:, cut], place_matrix(z, 2)).astype(BF16))
            joined[s] = total.astype(BF16)
    residual[...] = load_rows[...].astype(F32) - image[...] - select(z, added)


def coarse_rows(z, ordered_inverse, arrived):
    parts = [dot(ordered_inverse[s], arrived) for s in range(z.subs)]
    rows = fold(z, select(z, parts))
    return select(z, [rows[s * z.modes : (s + 1) * z.modes, :] for s in range(z.subs)]).astype(BF16)


def order_kernel(z, *refs):
    pieces = refs[: z.group]
    arrived, repeat, own_row, ordered_inverse, index, message, whole = refs[z.group :]
    for k, piece in enumerate(pieces):
        whole[:, pl.ds(piece_start(z, k, z.block), z.block)] = piece[...]
    digits = arrived[:, z.modes :, :].astype(F32)
    for s in range(z.subs):
        high = jnp.sum(jnp.where(digit_row(digits.shape, 2 * s), digits, 0.0), axis=1)
        low = jnp.sum(jnp.where(digit_row(digits.shape, 2 * s + 1), digits, 0.0), axis=1)
        index[s] = high * DIGIT + low
        spread = dot(high.astype(BF16), repeat[...]) * DIGIT + dot(low.astype(BF16), repeat[...])
        places = jnp.sum(spread * own_row[...], axis=0, keepdims=True).astype(jnp.int32)
        for at in range(0, z.columns, 768):
            wide = min(768, z.columns - at)
            total = jnp.zeros((z.owned, wide), F32)
            for first in range(0, z.total, 256):
                deep = min(256, z.total - first)
                row = lax.broadcasted_iota(jnp.int32, (deep, wide), 0) + first
                hot = jnp.where(row == places[:, at : at + wide], 1.0, 0.0).astype(BF16)
                total = total + dot(whole[:, first : first + deep], hot)
            ordered_inverse[s, :, at : at + wide] = total.astype(BF16)
    rows = arrived[:, : z.modes, :].reshape(z.columns, z.lanes)
    packed = coarse_rows(z, ordered_inverse, rows)
    for k in range(z.n):
        message[k] = packed


def digit_row(shape, row):
    return lax.broadcasted_iota(jnp.int32, shape, 1) == row


def pick_kernel(z, index, place, picks):
    here = lax.axis_index("sub")
    device = lax.broadcasted_iota(jnp.int32, (z.n, z.lanes), 0)
    for t in range(z.subs + 2):
        if t == 0:
            s, owner = z.subs - 1, lax.rem(here + z.n - 1, z.n)
        elif t == z.subs + 1:
            s, owner = 0, lax.rem(here + 1, z.n)
        else:
            s, owner = t - 1, here
        row = jnp.sum(jnp.where(device == owner, index[s], 0.0), axis=0, keepdims=True)
        column = jnp.transpose(jnp.broadcast_to(row, (z.lanes, z.lanes)))[: z.modes, 0:1]
        column = column.astype(jnp.int32)
        for h in range(z.subs):
            hit = column == place[h : h + 1, :]
            picks[h, t * z.modes : (t + 1) * z.modes, :] = jnp.where(hit, 1.0, 0.0).astype(BF16)


def picked_rows(z, arrived, picks):
    flat = arrived[...].reshape(z.columns, z.lanes)
    return fold(z, select(z, [dot(picks[h], flat) for h in range(z.subs)])).astype(BF16)


def update_kernel(z, arrived, picks, solved, residual, basis, joined, basis_t, first_pass, rounded, message):
    chosen = picked_rows(z, arrived, picks)
    m = z.modes
    first_pass[...] = solved[...] + select(
        z, [dot(basis[s], chosen[(s + 1) * m : (s + 2) * m]) for s in range(z.subs)]
    )
    left = residual[...] - select(z, [dot(joined[s], chosen[s * m : (s + 3) * m]) for s in range(z.subs)])
    left = left.astype(BF16)
    rounded[...] = left
    modes = select(z, [dot(basis_t[s], left) for s in range(z.subs)]).astype(BF16)
    for k in range(z.n):
        message[k] = modes


def coarse_kernel(z, arrived, ordered_inverse, message):
    packed = coarse_rows(z, ordered_inverse, arrived[...].reshape(z.columns, z.lanes))
    for k in range(z.n):
        message[k] = packed


def last_kernel(z, arrived, picks, solved, residual, basis, joined, out):
    chosen = picked_rows(z, arrived, picks)
    m = z.modes
    second = solved[...] + select(
        z, [dot(basis[s], chosen[(s + 1) * m : (s + 2) * m]) for s in range(z.subs)]
    )
    left = residual[...] - select(z, [dot(joined[s], chosen[s * m : (s + 3) * m]) for s in range(z.subs)])
    for k in range(z.group):
        out[k, 0] = second[k * z.own : (k + 1) * z.own, :]
        out[k, 1] = left[k * z.own : (k + 1) * z.own, :]


def unpack_kernel(z, arrived, second_pass, final_residual):
    for at, out in enumerate((second_pass, final_residual)):
        for s in range(z.subs):
            total = jnp.zeros((z.own, z.lanes), F32)
            for k in range(z.group):
                turned = arrived[k, at]
                turn = ((k - s) * z.width) % z.lanes
                if turn:
                    turned = pltpu.roll(turned, turn, 1)
                total = jnp.where(lane_mask(z, k, turned.shape), turned, total)
            out[s] = total[:, : z.cases]


def call(kernel, outs, operands, flops, scratch=(), name=None):
    vmem = pl.BlockSpec(memory_space=pltpu.VMEM)
    moved = sum(int(np.prod(x.shape)) * x.dtype.itemsize for x in (*operands, *outs))
    return pl.pallas_call(
        kernel,
        out_shape=[jax.ShapeDtypeStruct(o.shape, o.dtype) for o in outs],
        in_specs=[vmem] * len(operands),
        out_specs=[vmem] * len(outs),
        scratch_shapes=list(scratch),
        compiler_params=pltpu.CompilerParams(vmem_limit_bytes=VMEM_BYTES),
        cost_estimate=pl.CostEstimate(flops=flops, bytes_accessed=moved, transcendentals=0),
        name=name,
    )(*operands)


def shape(dims, dtype):
    return jax.ShapeDtypeStruct(dims, dtype)


def pieces_of(block, group):
    out = [block]
    for k in range(1, group):
        out.append(lax.ppermute(block, GROUP, [((g + k) % group, g) for g in range(group)]))
    return out


def body(loads, stiffness, local_inverse, coarse_basis, coarse_inverse, coarse_index, left_rows, right_rows):
    z = Sizes(loads, stiffness, coarse_basis, coarse_inverse, left_rows)
    n, group, subs, rows, lanes, modes = z.n, z.group, z.subs, z.rows, z.lanes, z.modes
    own_t = jnp.swapaxes(coarse_basis, 1, 2)
    basis_pieces = pieces_of(own_t, group)
    high, low = coarse_index // DIGIT, coarse_index % DIGIT
    digits = jnp.stack([high, low], axis=1).reshape(2 * subs, modes).astype(BF16)
    digits = jnp.pad(digits, ((0, DIGIT_ROWS - 2 * subs), (0, lanes - modes)))
    column = np.arange(z.columns)
    repeat = jnp.asarray(np.arange(lanes)[:, None] == column[None, :] % modes, BF16)
    own_row = jnp.asarray(np.arange(n)[:, None] == column[None, :] // modes, F32)
    place = jnp.asarray(
        (column // modes * z.owned + column % modes)[None, :] + np.arange(subs)[:, None] * modes, jnp.int32
    )
    packed_f = shape((rows, lanes), F32)
    packed_b = shape((rows, lanes), BF16)
    copies = shape((n, modes, lanes), BF16)
    spread = functools.partial(lax.all_to_all, axis_name="sub", split_axis=0, concat_axis=0)

    load_rows, basis_t, message = call(
        functools.partial(open_kernel, z),
        [packed_b, shape((subs, modes, rows), BF16), shape((n, modes + DIGIT_ROWS, lanes), BF16)],
        [*basis_pieces, loads, digits],
        4 * rows * lanes * lanes,
        name="open",
    )
    restricted = spread(message)

    inverse_pieces = pieces_of(local_inverse, group)
    stiffness_pieces = pieces_of(stiffness, group)
    inverse_columns = pieces_of(coarse_inverse, group)
    work = 4 * subs * rows * rows * lanes
    faces = shape((subs, z.face, 2 * lanes), BF16)
    solved, image, to_before, to_after, basis, image_basis = call(
        functools.partial(image_kernel, z, True),
        [packed_f, packed_f, faces, faces, shape((subs, rows, modes), BF16), shape((subs, rows, modes), BF16)],
        [*inverse_pieces, *stiffness_pieces, load_rows, basis_t, left_rows, right_rows],
        work,
        [pltpu.VMEM((rows, lanes), BF16)],
        name="first_image",
    )
    forward = [(i, (i + 1) % n) for i in range(n)]
    backward = [(target, source) for source, target in forward]
    from_before = lax.ppermute(to_after[subs - 1], "sub", forward)
    from_after = lax.ppermute(to_before[0], "sub", backward)
    residual, joined = call(
        functools.partial(join_kernel, z, True),
        [packed_f, shape((subs, rows, 3 * modes), BF16)],
        [load_rows, image, to_before, to_after, from_before, from_after, left_rows, right_rows, image_basis],
        work // 8,
        name="first_join",
    )

    ordered_inverse, index, message = call(
        functools.partial(order_kernel, z),
        [shape((subs, z.owned, z.columns), BF16), shape((subs, n, lanes), F32), copies],
        [*inverse_columns, restricted, repeat, own_row],
        2 * z.owned * z.total * z.total,
        [pltpu.VMEM((z.owned, z.total), BF16)],
        name="order",
    )
    coarse = spread(message)
    (picks,) = call(
        functools.partial(pick_kernel, z),
        [shape((subs, (subs + 2) * modes, z.columns), BF16)],
        [index, place],
        work // 64,
        name="picks",
    )
    first_pass, rounded, message = call(
        functools.partial(update_kernel, z),
        [packed_f, packed_b, copies],
        [coarse, picks, solved, residual, basis, joined, basis_t],
        work // 8,
        name="update",
    )
    restricted = spread(message)

    faces = shape((subs, z.face, lanes), BF16)
    solved, image, to_before, to_after = call(
        functools.partial(image_kernel, z, False),
        [packed_f, packed_f, faces, faces],
        [*inverse_pieces, *stiffness_pieces, rounded, first_pass, left_rows, right_rows],
        work,
        [pltpu.VMEM((rows, lanes), BF16)],
        name="second_image",
    )
    from_before = lax.ppermute(to_after[subs - 1], "sub", forward)
    from_after = lax.ppermute(to_before[0], "sub", backward)
    (residual,) = call(
        functools.partial(join_kernel, z, False),
        [packed_f],
        [load_rows, image, to_before, to_after, from_before, from_after, left_rows, right_rows],
        work // 8,
        name="second_join",
    )
    (message,) = call(
        functools.partial(coarse_kernel, z), [copies], [restricted, ordered_inverse], work // 64, name="coarse"
    )
    coarse = spread(message)
    (parts,) = call(
        functools.partial(last_kernel, z),
        [shape((group, 2, z.own, lanes), F32)],
        [coarse, picks, solved, residual, basis, joined],
        work // 8,
        name="last",
    )
    parts = lax.all_to_all(parts, GROUP, 0, 0)
    out = shape((subs, z.own, z.cases), F32)
    return tuple(call(functools.partial(unpack_kernel, z), [out, out], [parts], work // 64, name="unpack"))


def solution(mesh):
    return jax.shard_map(
        body,
        mesh=mesh,
        in_specs=(
            P("sub", None, None),
            P("sub", GROUP, None),
            P("sub", GROUP, None),
            P("sub", GROUP, None),
            P("sub", GROUP),
            P("sub", None),
            P("sub", None),
            P("sub", None),
        ),
        out_specs=(P("sub", GROUP, None), P("sub", GROUP, None)),
        check_vma=False,
    )
```

time: 262 us -> 112 us (0.43)
  blocking collectives: 206 us -> 4.58 us
  starting transfers between devices: 4.15 us -> 38.7 us
  Pallas kernels: 0 us -> 25.2 us
  matrix products: 12.7 us -> 0 us
  waiting for transfers between devices: 11.6 us -> 17.9 us
    all_gather x9 -> x0, blocking collectives: 184 us -> none  [the longest x2 87 us: coarse_step(): everything = lax.all_gather(coarse, 'sub', axis=0, tiled=True)]
    all_to_all x0 -> x4, starting transfers between devices: none -> 26.3 us  [the longest x2 15.3 us: body(): restricted = spread(message)]
    pallas_call x0 -> x11, Pallas kernels: none -> 25.2 us  [call(): pl.pallas_call(kernel, out_shape=[jax.ShapeDtypeStruct(o.shape, o.dtype)...]
    unnamed x19 -> x62, local copies, waits for them, and re-layouts: 1.87 us -> 21.6 us
    psum x4 -> x0, blocking collectives: 14.3 us -> none  [the longest x2 7.28 us: precondition(): restricted = lax.psum(partial_modes, ('crow', 'ccol')).astype(jnp.bfloat16)]
    dot_general x14 -> x0, matrix products: 12.7 us -> none  [the longest x2 2.83 us: apply_stiffness(): jnp.einsum('sfi,sfc->sic', pick_left, from_before, preferred_element_type...]
    gather x6 -> x0, local copies, waits for them, and re-layouts: 11.2 us -> none  [the longest x2 3.93 us: apply_stiffness(): whole_rows[sub_rows, left_rows]]
    scatter x2 -> x0, local copies, waits for them, and re-layouts: 9.28 us -> none  [coarse_step(): ordered = jnp.zeros((block_width + 1, case_count), jnp.bfloat16).at[arriv...]
  transfers between devices with their start and end apart: 4 -> 12, of which waited for: 4 -> 5; matrix products, arithmetic and copies ran while one was open for 1% -> 1% of each run, Pallas kernels for 0% -> 17%
where the time goes in v2:
time: 112 us; the launch traced here: 110 us
  starting transfers between devices  38.7 us (35%)
  Pallas kernels  25.2 us (22%)
  local copies, waits for them, and re-layouts  22.4 us (20%)
  waiting for transfers between devices  17.9 us (16%)
  blocking collectives  4.58 us (4%)
    pallas_call x11, Pallas kernels, call(): pl.pallas_call(kernel, out_shape=[jax.ShapeDtypeStruct(o.shape, o.dtype)...  25.2 us
    unnamed x62, local copies, waits for them, and re-layouts  21.6 us
    all_to_all x2, starting transfers between devices, body(): restricted = spread(message)  15.3 us
    all_to_all x2, starting transfers between devices, body(): coarse = spread(message)  11 us
    all_to_all x2, waiting for transfers between devices, body(): restricted = spread(message)  8.53 us
    ppermute x2, starting transfers between devices, body(): from_after = lax.ppermute(to_before[0], 'sub', backward)  7.57 us
    ppermute x2, waiting for transfers between devices, body(): from_before = lax.ppermute(to_after[subs - 1], 'sub', forward)  4.78 us
    ppermute x4, waiting for transfers between devices, pieces_of(): lax.ppermute(block, GROUP, [((g + k) % group, g) for g in range(group)])  4.61 us
  transfers between devices with their start and end apart: 12, of which 5 were waited for; matrix products, arithmetic and copies ran while one was open for 1% of the time, Pallas kernels for 17%

profile of v2, /device:TPU:0, one launch (start us, length us, event | category | flops | bytes accessed | tf_op | source)
XLA Modules:
  0.0 110.5 jit_solution(1339679839885371441)
XLA Ops:
  2.4 3.0 %collective-permute-done.1.refs_1_ = bf16[2,48,512]{2,1,0:T(8,128)(2,1)S(1)} collective-permute-done((bf16[2,48,512]{2,1,0:T(8,128)(2,1)}, bf16[2,48,512]{2,1,0:T(8,128)(2,1)S(1)}, u32[]{:S(2)}, u32[]{:S(2)}) %collective-permute-start.1) | collective-permute-done | bytes 98336 | tf_op jit(solution)/shard_map/ppermute | solution.py:316
  5.4 1.0 copy-done.14
  7.4 1.3 %open.1 = (bf16[1024,128]{1,0:T(8,128)(2,1)S(1)}, bf16[2,48,1024]{2,1,0:T(8,128)(2,1)S(1)}, bf16[16,64,128]{2,1,0:T(8,128)(2,1)}) custom-call(bf16[2,48,512]{2,1,0:T(8,128)(2,1)S(1)} %bitcast.15, bf16[2,48,512]{2,1,0:T(8,128)(2,1)S(1)} %collective-permute-done.1.refs_1_, bf16[2,1024,128]{2,1,0:T(8,128)(2,1)S(1)} %copy-done.14, bf16[16,128]{1,0:T(8,128)(2,1)S(1)} %pad.4.refs_3_), custom_call_target="tpu_custom_call" | custom-call | flops 67108864 | bytes 1445888 | tf_op jit(solution)/shard_map/open/pallas_call | solution.py:297
  8.6 8.2 %all-to-all-start = ((bf16[16,64,128]{2,1,0:T(8,128)(2,1)}), bf16[16,64,128]{2,1,0:T(8,128)(2,1)S(1)}, u32[]{:S(2)}, u32[]{:S(2)}) async-start(bf16[16,64,128]{2,1,0:T(8,128)(2,1)} %get-tuple-element.23), calls=%async_computation | async-start | bytes 524288 | tf_op jit(solution)/shard_map/all_to_all | solution.py:346
  17.0 1.6 %collective-permute-done.refs_1_ = bf16[96,768]{1,0:T(8,128)(2,1)S(1)} collective-permute-done((bf16[96,768]{1,0:T(8,128)(2,1)}, bf16[96,768]{1,0:T(8,128)(2,1)S(1)}, u32[]{:S(2)}, u32[]{:S(2)}) %collective-permute-start) | collective-permute-done | bytes 147488 | tf_op jit(solution)/shard_map/ppermute | solution.py:316
  18.5 8.5 %all-to-all-done.refs_2_ = bf16[16,64,128]{2,1,0:T(8,128)(2,1)S(1)} async-done(((bf16[16,64,128]{2,1,0:T(8,128)(2,1)}), bf16[16,64,128]{2,1,0:T(8,128)(2,1)S(1)}, u32[]{:S(2)}, u32[]{:S(2)}) %all-to-all-start) | async-done | bytes 262176 | tf_op jit(solution)/shard_map/all_to_all | solution.py:346
  29.7 2.1 %order.1 = (bf16[2,96,768]{2,1,0:T(8,128)(2,1)S(1)}, f32[2,16,128]{2,1,0:T(8,128)S(1)}, bf16[16,48,128]{2,1,0:T(8,128)(2,1)}) custom-call(bf16[96,768]{1,0:T(8,128)(2,1)S(1)} %copy-done.28, bf16[96,768]{1,0:T(8,128)(2,1)S(1)} %collective-permute-done.refs_1_, bf16[16,64,128]{2,1,0:T(8,128)(2,1)S(1)} %all-to-all-done.refs_2_, ...), custom_call_target="tpu_custom_call" | custom-call | flops 452984832 | bytes 1310720 | tf_op jit(solution)/shard_map/order/pallas_call | solution.py:297
  32.5 4.2 %all-to-all-start.1 = ((bf16[16,48,128]{2,1,0:T(8,128)(2,1)}), bf16[16,48,128]{2,1,0:T(8,128)(2,1)}, u32[]{:S(2)}, u32[]{:S(2)}) async-start(bf16[16,48,128]{2,1,0:T(8,128)(2,1)} %get-tuple-element.24), calls=%async_computation.1 | async-start | bytes 393216 | tf_op jit(solution)/shard_map/all_to_all | solution.py:381
  36.8 7.6 %first_image.1 = (f32[1024,128]{1,0:T(8,128)S(1)}, f32[1024,128]{1,0:T(8,128)S(1)}, bf16[2,128,256]{2,1,0:T(8,128)(2,1)S(1)}, bf16[2,128,256]{2,1,0:T(8,128)(2,1...) custom-call(bf16[2,512,1024]{2,1,0:T(8,128)(2,1)S(1)} %copy-done, ...), custom_call_target="tpu_custom_call" | custom-call | flops 1073741824 | bytes 10553344 | tf_op jit(solution)/shard_map/first_image/pallas_call | solution.py:297
  44.4 1.8 %collective-permute-start.4 = (bf16[128,256]{1,0:T(8,128)(2,1)S(1)}, bf16[128,256]{1,0:T(8,128)(2,1)S(1)}, u32[]{:S(2)}, u32[]{:S(2)}) collective-permute-start(bf16[128,256]{1,0:T(8,128)(2,1)S(1)} %slice_bitcast_fusion.1), channel_id=1, source_target_pairs={{0,2},{2,4},{4,6},{6,8},{8,10},{10,12},{12,14},{14,16},{16,18},{18... | collective-permute-start | bytes 196616 | tf_op jit(solution)/shard_map/ppermute | solution.py:363
  46.2 3.9 %collective-permute-start.5 = (bf16[128,256]{1,0:T(8,128)(2,1)S(1)}, bf16[128,256]{1,0:T(8,128)(2,1)S(1)}, u32[]{:S(2)}, u32[]{:S(2)}) collective-permute-start(bf16[128,256]{1,0:T(8,128)(2,1)S(1)} %slice_bitcast_fusion), channel_id=1, source_target_pairs={{2,0},{4,2},{6,4},{8,6},{10,8},{12,10},{14,12},{16,14},{18,16},{20... | collective-permute-start | bytes 196616 | tf_op jit(solution)/shard_map/ppermute | solution.py:364
  50.3 2.0 %collective-permute-done.4.refs_4_ = bf16[128,256]{1,0:T(8,128)(2,1)S(1)} collective-permute-done((bf16[128,256]{1,0:T(8,128)(2,1)S(1)}, bf16[128,256]{1,0:T(8,128)(2,1)S(1)}, u32[]{:S(2)}, u32[]{:S(2)}) %collective-permute-start.4) | collective-permute-done | bytes 65568 | tf_op jit(solution)/shard_map/ppermute | solution.py:363
  52.3 1.4 %first_join.1 = (f32[1024,128]{1,0:T(8,128)S(1)}, bf16[2,1024,144]{2,1,0:T(8,128)(2,1)S(1)}) custom-call(bf16[1024,128]{1,0:T(8,128)(2,1)S(1)} %get-tuple-element.26.refs_4_.refs_0_, f32[1024,128]{1,0:T(8,128)S(1)} %get-tuple-element.29.refs_1_, bf16[2,128,256]{2,1,0:T(8,128)(2,1)S(1)} %get-tuple-element.30.refs_2_, ...), custom_call_target="tpu_custom_call" | custom-call | flops 134217728 | bytes 2492416 | tf_op jit(solution)/shard_map/first_join/pallas_call | solution.py:297
  53.7 1.0 copy-done.1
  55.5 1.2 %copy-done.2 = bf16[2,1024,144]{2,1,0:T(8,128)(2,1)S(1)} copy-done((bf16[2,1024,144]{2,1,0:T(8,128)(2,1)S(1)}, bf16[2,1024,144]{2,1,0:T(8,128)(2,1)}, u32[]{:S(2)}) %copy-start.2) | copy-done | bytes 589848
  57.6 1.0 copy-done.9
  58.7 1.0 copy-done.11
  59.7 2.0 %update.1 = (f32[1024,128]{1,0:T(8,128)S(1)}, bf16[1024,128]{1,0:T(8,128)(2,1)S(1)}, bf16[16,48,128]{2,1,0:T(8,128)(2,1)S(1)}) custom-call(bf16[16,48,128]{2,1,0:T(8,128)(2,1)} %all-to-all-done.1.arrived, bf16[2,192,768]{2,1,0:T(8,128)(2,1)S(1)} %picks.1, f32[1024,128]{1,0:T(8,128)S(1)} %copy-done.9, f32[1024,128]{1,0:T(8,128)S(1)} %copy-done.11, ...), custom_call_target="tpu_custom_call" | custom-call | flops 134217728 | bytes 3801088 | tf_op jit(solution)/shard_map/update/pallas_call | solution.py:297
  63.9 7.0 %all-to-all-start.2 = ((bf16[16,48,128]{2,1,0:T(8,128)(2,1)}), bf16[16,48,128]{2,1,0:T(8,128)(2,1)}, u32[]{:S(2)}, u32[]{:S(2)}) async-start(bf16[16,48,128]{2,1,0:T(8,128)(2,1)} %copy-done.21), calls=%async_computation.2 | async-start | bytes 393216 | tf_op jit(solution)/shard_map/all_to_all | solution.py:396
  71.0 1.0 copy-done.13
  72.0 0.9 copy-done.20
  72.9 6.2 %second_image.1 = (f32[1024,128]{1,0:T(8,128)S(1)}, f32[1024,128]{1,0:T(8,128)S(1)}, bf16[2,128,128]{2,1,0:T(8,128)(2,1)S(1)}, bf16[2,128,128]{2,1,0:T(8,128)(2,1)S(1)}) custom-call(bf16[2,512,1024]{2,1,0:T(8,128)(2,1)S(1)} %copy-done, bf16[2,512,1024]{2,1,0:T(8,128)(2,1)} %collective-permute-done.2.refs_1_, bf16[2,512,1024]{2,1,0:T(8,128)(2,1)} %refs_2_.5, ...), custom_call_target="tpu_custom_call" | custom-call | flops 1073741824 | bytes 10356736 | tf_op jit(solution)/shard_map/second_image/pallas_call | solution.py:297
  81.4 1.0 copy-done.18
  82.4 1.9 %coarse.1 = bf16[16,48,128]{2,1,0:T(8,128)(2,1)} custom-call(bf16[16,48,128]{2,1,0:T(8,128)(2,1)} %all-to-all-done.2.arrived, bf16[2,96,768]{2,1,0:T(8,128)(2,1)S(1)} %copy-done.18), custom_call_target="tpu_custom_call" | custom-call | flops 16777216 | bytes 688128 | tf_op jit(solution)/shard_map/coarse/pallas_call | solution.py:297
  84.3 6.9 %all-to-all-start.3 = ((bf16[16,48,128]{2,1,0:T(8,128)(2,1)}), bf16[16,48,128]{2,1,0:T(8,128)(2,1)S(1)}, u32[]{:S(2)}, u32[]{:S(2)}) async-start(bf16[16,48,128]{2,1,0:T(8,128)(2,1)} %coarse.1), calls=%async_computation.3 | async-start | bytes 393216 | tf_op jit(solution)/shard_map/all_to_all | solution.py:419
  92.0 1.9 %collective-permute-start.6 = (bf16[128,128]{1,0:T(8,128)(2,1)S(1)}, bf16[128,128]{1,0:T(8,128)(2,1)S(1)}, u32[]{:S(2)}, u32[]{:S(2)}) collective-permute-start(bf16[128,128]{1,0:T(8,128)(2,1)S(1)} %slice_bitcast_fusion.3), channel_id=1, source_target_pairs={{0,2},{2,4},{4,6},{6,8},{8,10},{10,12},{12,14},{14,16},{16,18},{18... | collective-permute-start | bytes 98312 | tf_op jit(solution)/shard_map/ppermute | solution.py:407
  93.9 3.7 %collective-permute-start.7 = (bf16[128,128]{1,0:T(8,128)(2,1)S(1)}, bf16[128,128]{1,0:T(8,128)(2,1)S(1)}, u32[]{:S(2)}, u32[]{:S(2)}) collective-permute-start(bf16[128,128]{1,0:T(8,128)(2,1)S(1)} %slice_bitcast_fusion.2), channel_id=1, source_target_pairs={{2,0},{4,2},{6,4},{8,6},{10,8},{12,10},{14,12},{16,14},{18,16},{20... | collective-permute-start | bytes 98312 | tf_op jit(solution)/shard_map/ppermute | solution.py:408
  97.6 2.8 %collective-permute-done.6.refs_4_ = bf16[128,128]{1,0:T(8,128)(2,1)S(1)} collective-permute-done((bf16[128,128]{1,0:T(8,128)(2,1)S(1)}, bf16[128,128]{1,0:T(8,128)(2,1)S(1)}, u32[]{:S(2)}, u32[]{:S(2)}) %collective-permute-start.6) | collective-permute-done | bytes 32800 | tf_op jit(solution)/shard_map/ppermute | solution.py:407
  100.4 1.0 copy-done.16
  102.7 1.0 copy-done.7
  104.7 4.6 %all_to_all.25.arrived = f32[2,2,512,128]{3,2,1,0:T(8,128)S(1)} all-to-all(f32[2,2,512,128]{3,2,1,0:T(8,128)S(1)} %last.1), channel_id=1, replica_groups=mesh['sub'=16,'crow'=2,'ccol'=1] {'crow','ccol'}, dimensions={0} | all-to-all | bytes 2097152 | tf_op jit(solution)/shard_map/all_to_all | solution.py:427
  109.2 1.2 %unpack.1 = (f32[2,512,128]{2,1,0:T(8,128)}, f32[2,512,128]{2,1,0:T(8,128)}) custom-call(f32[2,2,512,128]{3,2,1,0:T(8,128)S(1)} %all_to_all.25.arrived), custom_call_target="tpu_custom_call" | custom-call | flops 16777216 | bytes 2097152 | tf_op jit(solution)/shard_map/unpack/pallas_call | solution.py:297
  (74 shorter events, 15.4 us)
Async XLA Ops:
  0.6 36.1 %copy-start = (bf16[2,512,1024]{2,1,0:T(8,128)(2,1)S(1)}, bf16[2,512,1024]{2,1,0:T(8,128)(2,1)}, u32[]{:S(2)}) copy-start(bf16[2,512,1024]{2,1,0:T(8,128)(2,1)} %refs_0_.5) | copy-start | bytes 6291460
  0.6 36.1 %collective-permute-start.2 = (bf16[2,512,1024]{2,1,0:T(8,128)(2,1)}, bf16[2,512,1024]{2,1,0:T(8,128)(2,1)}, u32[]{:S(2)}, u32[]{:S(2)}) collective-permute-start(bf16[2,512,1024]{2,1,0:T(8,128)(2,1)} %refs_0_.5), channel_id=1, source_target_pairs={{1,0},{0,1},{3,2},{2,3},{5,4},{4,5},{7,6},{6,7},{9,8},{8,9},{11,10... | collective-permute-start | bytes 6291464 | tf_op jit(solution)/shard_map/ppermute | solution.py:316
  1.2 35.6 %collective-permute-start.3 = (bf16[2,512,1024]{2,1,0:T(8,128)(2,1)}, bf16[2,512,1024]{2,1,0:T(8,128)(2,1)}, u32[]{:S(2)}, u32[]{:S(2)}) collective-permute-start(bf16[2,512,1024]{2,1,0:T(8,128)(2,1)} %refs_2_.5), channel_id=1, source_target_pairs={{1,0},{0,1},{3,2},{2,3},{5,4},{4,5},{7,6},{6,7},{9,8},{8,9},{11,10... | collective-permute-start | bytes 6291464 | tf_op jit(solution)/shard_map/ppermute | solution.py:316
  1.2 4.2 %collective-permute-start.1 = (bf16[2,48,512]{2,1,0:T(8,128)(2,1)}, bf16[2,48,512]{2,1,0:T(8,128)(2,1)S(1)}, u32[]{:S(2)}, u32[]{:S(2)}) collective-permute-start(bf16[2,48,512]{2,1,0:T(8,128)(2,1)} %bitcast.14), channel_id=1, source_target_pairs={{1,0},{0,1},{3,2},{2,3},{5,4},{4,5},{7,6},{6,7},{9,8},{8,9},{11,10... | collective-permute-start | bytes 294920 | tf_op jit(solution)/shard_map/ppermute | solution.py:316
  5.4 1.0 copy-start.14
  7.4 29.4 %copy-start.25 = (s32[2,128]{1,0:T(2,128)S(1)}, s32[2,128]{1,0:T(2,128)}, u32[]{:S(2)}) copy-start(s32[2,128]{1,0:T(2,128)} %refs_6_.7) | copy-start | bytes 3076
  7.4 29.4 %copy-start.26 = (s32[2,128]{1,0:T(2,128)S(1)}, s32[2,128]{1,0:T(2,128)}, u32[]{:S(2)}) copy-start(s32[2,128]{1,0:T(2,128)} %refs_7_.7) | copy-start | bytes 3076
  8.6 35.7 %copy-start.4 = (bf16[2,48,1024]{2,1,0:T(8,128)(2,1)}, bf16[2,48,1024]{2,1,0:T(8,128)(2,1)S(1)}, u32[]{:S(2)}) copy-start(bf16[2,48,1024]{2,1,0:T(8,128)(2,1)S(1)} %get-tuple-element.27.refs_5_.basis_t) | copy-start | bytes 589828
  8.6 18.4 %all-to-all-start = ((bf16[16,64,128]{2,1,0:T(8,128)(2,1)}), bf16[16,64,128]{2,1,0:T(8,128)(2,1)S(1)}, u32[]{:S(2)}, u32[]{:S(2)}) async-start(bf16[16,64,128]{2,1,0:T(8,128)(2,1)} %get-tuple-element.23), calls=%async_computation | async-start | bytes 524288 | tf_op jit(solution)/shard_map/all_to_all | solution.py:346
  16.9 1.6 %collective-permute-start = (bf16[96,768]{1,0:T(8,128)(2,1)}, bf16[96,768]{1,0:T(8,128)(2,1)S(1)}, u32[]{:S(2)}, u32[]{:S(2)}) collective-permute-start(bf16[96,768]{1,0:T(8,128)(2,1)} %refs_0_.3), channel_id=1, source_target_pairs={{1,0},{0,1},{3,2},{2,3},{5,4},{4,5},{7,6},{6,7},{9,8},{8,9},{11,10... | collective-permute-start | bytes 442376 | tf_op jit(solution)/shard_map/ppermute | solution.py:316
  27.0 0.9 copy-start.28
  28.0 0.9 copy-start.29
  32.5 23.0 %all-to-all-start.1 = ((bf16[16,48,128]{2,1,0:T(8,128)(2,1)}), bf16[16,48,128]{2,1,0:T(8,128)(2,1)}, u32[]{:S(2)}, u32[]{:S(2)}) async-start(bf16[16,48,128]{2,1,0:T(8,128)(2,1)} %get-tuple-element.24), calls=%async_computation.1 | async-start | bytes 393216 | tf_op jit(solution)/shard_map/all_to_all | solution.py:381
  36.8 13.3 %copy-start.27 = (s32[2,768]{1,0:T(2,128)S(1)}, s32[2,768]{1,0:T(2,128)}, u32[]{:S(2)}) copy-start(s32[2,768]{1,0:T(2,128)} %constant.39.clone.place) | copy-start | bytes 18436
  44.3 7.9 %copy-start.8 = (f32[1024,128]{1,0:T(8,128)}, f32[1024,128]{1,0:T(8,128)S(1)}, u32[]{:S(2)}) copy-start(f32[1024,128]{1,0:T(8,128)S(1)} %get-tuple-element.28.solved) | copy-start | bytes 1572868
  44.4 7.9 %collective-permute-start.4 = (bf16[128,256]{1,0:T(8,128)(2,1)S(1)}, bf16[128,256]{1,0:T(8,128)(2,1)S(1)}, u32[]{:S(2)}, u32[]{:S(2)}) collective-permute-start(bf16[128,256]{1,0:T(8,128)(2,1)S(1)} %slice_bitcast_fusion.1), channel_id=1, source_target_pairs={{0,2},{2,4},{4,6},{6,8},{8,10},{10,12},{12,14},{14,16},{16,18},{18... | collective-permute-start | bytes 196616 | tf_op jit(solution)/shard_map/ppermute | solution.py:363
  46.2 6.1 %collective-permute-start.5 = (bf16[128,256]{1,0:T(8,128)(2,1)S(1)}, bf16[128,256]{1,0:T(8,128)(2,1)S(1)}, u32[]{:S(2)}, u32[]{:S(2)}) collective-permute-start(bf16[128,256]{1,0:T(8,128)(2,1)S(1)} %slice_bitcast_fusion), channel_id=1, source_target_pairs={{2,0},{4,2},{6,4},{8,6},{10,8},{12,10},{14,12},{16,14},{18,16},{20... | collective-permute-start | bytes 196616 | tf_op jit(solution)/shard_map/ppermute | solution.py:364
  53.7 1.0 copy-start.1
  55.5 1.2 %copy-start.2 = (bf16[2,1024,144]{2,1,0:T(8,128)(2,1)S(1)}, bf16[2,1024,144]{2,1,0:T(8,128)(2,1)}, u32[]{:S(2)}) copy-start(bf16[2,1024,144]{2,1,0:T(8,128)(2,1)} %copy-done.1) | copy-start | bytes 1769476
  56.7 0.9 copy-start.5
  57.6 1.0 copy-start.9
  58.7 1.0 copy-start.11
  63.9 17.5 %all-to-all-start.2 = ((bf16[16,48,128]{2,1,0:T(8,128)(2,1)}), bf16[16,48,128]{2,1,0:T(8,128)(2,1)}, u32[]{:S(2)}, u32[]{:S(2)}) async-start(bf16[16,48,128]{2,1,0:T(8,128)(2,1)} %copy-done.21), calls=%async_computation.2 | async-start | bytes 393216 | tf_op jit(solution)/shard_map/all_to_all | solution.py:396
  71.0 1.0 copy-start.13
  72.0 0.9 copy-start.20
  81.4 21.4 %copy-start.3 = (bf16[2,1024,144]{2,1,0:T(8,128)(2,1)S(1)}, bf16[2,1024,144]{2,1,0:T(8,128)(2,1)}, u32[]{:S(2)}) copy-start(bf16[2,1024,144]{2,1,0:T(8,128)(2,1)} %copy-done.1) | copy-start | bytes 1769476
  81.4 1.1 copy-start.18
  84.3 18.4 %all-to-all-start.3 = ((bf16[16,48,128]{2,1,0:T(8,128)(2,1)}), bf16[16,48,128]{2,1,0:T(8,128)(2,1)S(1)}, u32[]{:S(2)}, u32[]{:S(2)}) async-start(bf16[16,48,128]{2,1,0:T(8,128)(2,1)} %coarse.1), calls=%async_computation.3 | async-start | bytes 393216 | tf_op jit(solution)/shard_map/all_to_all | solution.py:419
  92.0 8.4 %collective-permute-start.6 = (bf16[128,128]{1,0:T(8,128)(2,1)S(1)}, bf16[128,128]{1,0:T(8,128)(2,1)S(1)}, u32[]{:S(2)}, u32[]{:S(2)}) collective-permute-start(bf16[128,128]{1,0:T(8,128)(2,1)S(1)} %slice_bitcast_fusion.3), channel_id=1, source_target_pairs={{0,2},{2,4},{4,6},{6,8},{8,10},{10,12},{12,14},{14,16},{16,18},{18... | collective-permute-start | bytes 98312 | tf_op jit(solution)/shard_map/ppermute | solution.py:407
  93.9 6.5 %collective-permute-start.7 = (bf16[128,128]{1,0:T(8,128)(2,1)S(1)}, bf16[128,128]{1,0:T(8,128)(2,1)S(1)}, u32[]{:S(2)}, u32[]{:S(2)}) collective-permute-start(bf16[128,128]{1,0:T(8,128)(2,1)S(1)} %slice_bitcast_fusion.2), channel_id=1, source_target_pairs={{2,0},{4,2},{6,4},{8,6},{10,8},{12,10},{14,12},{16,14},{18,16},{20... | collective-permute-start | bytes 98312 | tf_op jit(solution)/shard_map/ppermute | solution.py:408
  100.4 1.0 copy-start.16
  102.7 1.0 copy-start.7
  (11 other events, 8.4 us)

commit v3 on v2

--- a/solution.py
+++ b/solution.py
@@ -11,7 +11,7 @@
 GROUP = ("crow", "ccol")
 F32 = jnp.float32
 BF16 = jnp.bfloat16
-VMEM_BYTES = 48 * 1024 * 1024
+VMEM_BYTES = 16 * 1024 * 1024
 DIGIT_ROWS = 16
 DIGIT = 256
 
@@ -41,6 +41,10 @@
         self.width = self.cases // self.group
         self.lanes = max(self.cases, -(-self.subs * self.width // 128) * 128)
         self.columns = self.n * self.modes
+        self.near = 1
+        while self.near * self.near < self.n and self.n % (2 * self.near) == 0:
+            self.near *= 2
+        self.far = self.n // self.near
 
 
 def lane_mask(z, block, shape):
@@ -242,7 +246,7 @@
 
 
 def picked_rows(z, arrived, picks):
-    flat = arrived[...].reshape(z.columns, z.lanes)
+    flat = in_order(z, arrived)
     return fold(z, select(z, [dot(picks[h], flat) for h in range(z.subs)])).astype(BF16)
 
 
@@ -256,13 +260,19 @@
     left = left.astype(BF16)
     rounded[...] = left
     modes = select(z, [dot(basis_t[s], left) for s in range(z.subs)]).astype(BF16)
-    for k in range(z.n):
+    for k in range(message.shape[0]):
         message[k] = modes
 
 
+def in_order(z, arrived):
+    if len(arrived.shape) == 3:
+        return arrived[...].reshape(z.columns, z.lanes)
+    return jnp.concatenate([arrived[a, b] for b in range(z.far) for a in range(z.near)], axis=0)
+
+
 def coarse_kernel(z, arrived, ordered_inverse, message):
-    packed = coarse_rows(z, ordered_inverse, arrived[...].reshape(z.columns, z.lanes))
-    for k in range(z.n):
+    packed = coarse_rows(z, ordered_inverse, in_order(z, arrived))
+    for k in range(message.shape[0]):
         message[k] = packed
 
 
@@ -334,7 +344,15 @@
     packed_f = shape((rows, lanes), F32)
     packed_b = shape((rows, lanes), BF16)
     copies = shape((n, modes, lanes), BF16)
+    few = shape((z.far, modes, lanes), BF16)
     spread = functools.partial(lax.all_to_all, axis_name="sub", split_axis=0, concat_axis=0)
+    far_groups = [[a + z.near * b for b in range(z.far)] for a in range(z.near)]
+    near_groups = [[a + z.near * b for a in range(z.near)] for b in range(z.far)]
+
+    def spread_staged(message):
+        part = spread(message, axis_index_groups=far_groups)
+        return spread(jnp.broadcast_to(part[None], (z.near, *part.shape)), axis_index_groups=near_groups)
+
 
     load_rows, basis_t, message = call(
         functools.partial(open_kernel, z),
@@ -388,12 +406,12 @@
     )
     first_pass, rounded, message = call(
         functools.partial(update_kernel, z),
-        [packed_f, packed_b, copies],
+        [packed_f, packed_b, few],
         [coarse, picks, solved, residual, basis, joined, basis_t],
         work // 8,
         name="update",
     )
-    restricted = spread(message)
+    restricted = spread_staged(message)
 
     faces = shape((subs, z.face, lanes), BF16)
     solved, image, to_before, to_after = call(
@@ -414,9 +432,9 @@
         name="second_join",
     )
     (message,) = call(
-        functools.partial(coarse_kernel, z), [copies], [restricted, ordered_inverse], work // 64, name="coarse"
-    )
-    coarse = spread(message)
+        functools.partial(coarse_kernel, z), [few], [restricted, ordered_inverse], work // 64, name="coarse"
+    )
+    coarse = spread_staged(message)
     (parts,) = call(
         functools.partial(last_kernel, z),
         [shape((group, 2, z.own, lanes), F32)],

time: 112 us -> 124 us (1.11)
  blocking collectives: 4.58 us -> 13.2 us
  local copies, waits for them, and re-layouts: 22.4 us -> 26.4 us
  waiting for transfers between devices: 17.9 us -> 20.1 us
  starting transfers between devices: 38.7 us -> 37.3 us
    all_to_all x0 -> x3, starting transfers between devices: none -> 13.1 us  [the longest x2 9.82 us: spread_staged(): spread(jnp.broadcast_to(part[None], (z.near, *part.shape)), axis_index_gr...]
    all_to_all x0 -> x1, blocking collectives: none -> 8.59 us  [spread_staged(): part = spread(message, axis_index_groups=far_groups)]
    all_to_all x2 -> x1, starting transfers between devices: 15.3 us -> 8.24 us  [body(): restricted = spread(message)]
    all_to_all x2 -> x1, starting transfers between devices: 11 us -> 4.17 us  [body(): coarse = spread(message)]
    all_to_all x0 -> x3, waiting for transfers between devices: none -> 2.88 us  [the longest x1 2.88 us: spread_staged(): part = spread(message, axis_index_groups=far_groups)]
    ppermute x2, waiting for transfers between devices: 4.78 us -> 1.97 us  [body(): from_before = lax.ppermute(to_after[subs - 1], 'sub', forward)]
    unnamed x62 -> x64, local copies, waits for them, and re-layouts: 21.6 us -> 24.1 us
    ppermute x2, waiting for transfers between devices: 0.01 us -> 2.12 us  [body(): from_after = lax.ppermute(to_before[0], 'sub', backward)]
  transfers between devices with their start and end apart: 12 -> 13, of which waited for: 5 -> 6; matrix products, arithmetic and copies ran while one was open for 1% -> 2% of each run, Pallas kernels for 17% -> 15%
where the time goes in v3:
time: 124 us; the launch traced here: 123 us
  starting transfers between devices  37.3 us (30%)
  local copies, waits for them, and re-layouts  26.4 us (21%)
  Pallas kernels  24 us (19%)
  waiting for transfers between devices  20.1 us (16%)
  blocking collectives  13.2 us (11%)
    unnamed x64, local copies, waits for them, and re-layouts  24.1 us
    pallas_call x11, Pallas kernels, call(): pl.pallas_call(kernel, out_shape=[jax.ShapeDtypeStruct(o.shape, o.dtype)...  24 us
    all_to_all x2, starting transfers between devices, spread_staged(): spread(jnp.broadcast_to(part[None], (z.near, *part.shape)), axis_index_gr...  9.82 us
    all_to_all x1, blocking collectives, spread_staged(): part = spread(message, axis_index_groups=far_groups)  8.59 us
    all_to_all x1, waiting for transfers between devices, body(): restricted = spread(message)  8.52 us
    all_to_all x1, starting transfers between devices, body(): restricted = spread(message)  8.24 us
    ppermute x2, starting transfers between devices, body(): from_after = lax.ppermute(to_before[0], 'sub', backward)  6.93 us
    ppermute x4, waiting for transfers between devices, pieces_of(): lax.ppermute(block, GROUP, [((g + k) % group, g) for g in range(group)])  4.61 us
  transfers between devices with their start and end apart: 13, of which 6 were waited for; matrix products, arithmetic and copies ran while one was open for 2% of the time, Pallas kernels for 15%

profile of v3, /device:TPU:0, one launch (start us, length us, event | category | flops | bytes accessed | tf_op | source)
XLA Modules:
  0.0 122.5 jit_solution(18255416839248086656)
XLA Ops:
  2.4 3.0 %collective-permute-done.1.refs_1_ = bf16[2,48,512]{2,1,0:T(8,128)(2,1)S(1)} collective-permute-done((bf16[2,48,512]{2,1,0:T(8,128)(2,1)}, bf16[2,48,512]{2,1,0:T(8,128)(2,1)S(1)}, u32[]{:S(2)}, u32[]{:S(2)}) %collective-permute-start.1) | collective-permute-done | bytes 98336 | tf_op jit(solution)/shard_map/ppermute | solution.py:326
  5.4 1.0 copy-done.16
  7.4 1.3 %open.1 = (bf16[1024,128]{1,0:T(8,128)(2,1)S(1)}, bf16[2,48,1024]{2,1,0:T(8,128)(2,1)S(1)}, bf16[16,64,128]{2,1,0:T(8,128)(2,1)}) custom-call(bf16[2,48,512]{2,1,0:T(8,128)(2,1)S(1)} %bitcast.15, bf16[2,48,512]{2,1,0:T(8,128)(2,1)S(1)} %collective-permute-done.1.refs_1_, bf16[2,1024,128]{2,1,0:T(8,128)(2,1)S(1)} %copy-done.16, bf16[16,128]{1,0:T(8,128)(2,1)S(1)} %pad.4.refs_3_), custom_call_target="tpu_custom_call" | custom-call | flops 67108864 | bytes 1445888 | tf_op jit(solution)/shard_map/open/pallas_call | solution.py:307
  8.6 8.2 %all-to-all-start = ((bf16[16,64,128]{2,1,0:T(8,128)(2,1)}), bf16[16,64,128]{2,1,0:T(8,128)(2,1)S(1)}, u32[]{:S(2)}, u32[]{:S(2)}) async-start(bf16[16,64,128]{2,1,0:T(8,128)(2,1)} %get-tuple-element.23), calls=%async_computation | async-start | bytes 524288 | tf_op jit(solution)/shard_map/all_to_all | solution.py:364
  17.0 1.6 %collective-permute-done.refs_1_ = bf16[96,768]{1,0:T(8,128)(2,1)S(1)} collective-permute-done((bf16[96,768]{1,0:T(8,128)(2,1)}, bf16[96,768]{1,0:T(8,128)(2,1)S(1)}, u32[]{:S(2)}, u32[]{:S(2)}) %collective-permute-start) | collective-permute-done | bytes 147488 | tf_op jit(solution)/shard_map/ppermute | solution.py:326
  18.5 8.5 %all-to-all-done.refs_2_ = bf16[16,64,128]{2,1,0:T(8,128)(2,1)S(1)} async-done(((bf16[16,64,128]{2,1,0:T(8,128)(2,1)}), bf16[16,64,128]{2,1,0:T(8,128)(2,1)S(1)}, u32[]{:S(2)}, u32[]{:S(2)}) %all-to-all-start) | async-done | bytes 262176 | tf_op jit(solution)/shard_map/all_to_all | solution.py:364
  29.7 2.2 %order.1 = (bf16[2,96,768]{2,1,0:T(8,128)(2,1)S(1)}, f32[2,16,128]{2,1,0:T(8,128)S(1)}, bf16[16,48,128]{2,1,0:T(8,128)(2,1)}) custom-call(bf16[96,768]{1,0:T(8,128)(2,1)S(1)} %copy-done.29, bf16[96,768]{1,0:T(8,128)(2,1)S(1)} %collective-permute-done.refs_1_, bf16[16,64,128]{2,1,0:T(8,128)(2,1)S(1)} %all-to-all-done.refs_2_, ...), custom_call_target="tpu_custom_call" | custom-call | flops 452984832 | bytes 1310720 | tf_op jit(solution)/shard_map/order/pallas_call | solution.py:307
  32.6 4.2 %all-to-all-start.1 = ((bf16[16,48,128]{2,1,0:T(8,128)(2,1)}), bf16[16,48,128]{2,1,0:T(8,128)(2,1)}, u32[]{:S(2)}, u32[]{:S(2)}) async-start(bf16[16,48,128]{2,1,0:T(8,128)(2,1)} %get-tuple-element.24), calls=%async_computation.1 | async-start | bytes 393216 | tf_op jit(solution)/shard_map/all_to_all | solution.py:399
  36.8 1.6 %copy-done.1 = bf16[2,512,1024]{2,1,0:T(8,128)(2,1)S(1)} copy-done((bf16[2,512,1024]{2,1,0:T(8,128)(2,1)S(1)}, bf16[2,512,1024]{2,1,0:T(8,128)(2,1)}, u32[]{:S(2)}) %copy-start.1) | copy-done | bytes 2097176
  38.4 6.9 %first_image.1 = (f32[1024,128]{1,0:T(8,128)S(1)}, f32[1024,128]{1,0:T(8,128)S(1)}, bf16[2,128,256]{2,1,0:T(8,128)(2,1)S(1)}, bf16[2,128,256]{2,1,0:T(8,128)(2,1...) custom-call(bf16[2,512,1024]{2,1,0:T(8,128)(2,1)S(1)} %copy-done, ...), custom_call_target="tpu_custom_call" | custom-call | flops 1073741824 | bytes 10553344 | tf_op jit(solution)/shard_map/first_image/pallas_call | solution.py:307
  45.4 1.8 %collective-permute-start.4 = (bf16[128,256]{1,0:T(8,128)(2,1)S(1)}, bf16[128,256]{1,0:T(8,128)(2,1)S(1)}, u32[]{:S(2)}, u32[]{:S(2)}) collective-permute-start(bf16[128,256]{1,0:T(8,128)(2,1)S(1)} %slice_bitcast_fusion.1), channel_id=1, source_target_pairs={{0,2},{2,4},{4,6},{6,8},{8,10},{10,12},{12,14},{14,16},{16,18},{18... | collective-permute-start | bytes 196616 | tf_op jit(solution)/shard_map/ppermute | solution.py:381
  47.2 3.9 %collective-permute-start.5 = (bf16[128,256]{1,0:T(8,128)(2,1)S(1)}, bf16[128,256]{1,0:T(8,128)(2,1)S(1)}, u32[]{:S(2)}, u32[]{:S(2)}) collective-permute-start(bf16[128,256]{1,0:T(8,128)(2,1)S(1)} %slice_bitcast_fusion), channel_id=1, source_target_pairs={{2,0},{4,2},{6,4},{8,6},{10,8},{12,10},{14,12},{16,14},{18,16},{20... | collective-permute-start | bytes 196616 | tf_op jit(solution)/shard_map/ppermute | solution.py:382
  51.3 2.0 %collective-permute-done.4.refs_4_ = bf16[128,256]{1,0:T(8,128)(2,1)S(1)} collective-permute-done((bf16[128,256]{1,0:T(8,128)(2,1)S(1)}, bf16[128,256]{1,0:T(8,128)(2,1)S(1)}, u32[]{:S(2)}, u32[]{:S(2)}) %collective-permute-start.4) | collective-permute-done | bytes 65568 | tf_op jit(solution)/shard_map/ppermute | solution.py:381
  53.3 1.4 %first_join.1 = (f32[1024,128]{1,0:T(8,128)S(1)}, bf16[2,1024,144]{2,1,0:T(8,128)(2,1)S(1)}) custom-call(bf16[1024,128]{1,0:T(8,128)(2,1)S(1)} %get-tuple-element.26.refs_4_.refs_0_, f32[1024,128]{1,0:T(8,128)S(1)} %get-tuple-element.29.refs_1_, bf16[2,128,256]{2,1,0:T(8,128)(2,1)S(1)} %get-tuple-element.30.refs_2_, ...), custom_call_target="tpu_custom_call" | custom-call | flops 134217728 | bytes 2492416 | tf_op jit(solution)/shard_map/first_join/pallas_call | solution.py:307
  56.5 1.2 copy-done.4
  58.6 1.0 copy-done.11
  60.7 2.0 %update.1 = (f32[1024,128]{1,0:T(8,128)S(1)}, bf16[1024,128]{1,0:T(8,128)(2,1)S(1)}, bf16[4,48,128]{2,1,0:T(8,128)(2,1)S(1)}) custom-call(bf16[16,48,128]{2,1,0:T(8,128)(2,1)} %all-to-all-done.1.arrived, bf16[2,192,768]{2,1,0:T(8,128)(2,1)S(1)} %picks.1, f32[1024,128]{1,0:T(8,128)S(1)} %copy-done.11, f32[1024,128]{1,0:T(8,128)S(1)} %copy-done.15, ...), custom_call_target="tpu_custom_call" | custom-call | flops 134217728 | bytes 3653632 | tf_op jit(solution)/shard_map/update/pallas_call | solution.py:307
  64.2 8.6 %all_to_all.35 = bf16[4,48,128]{2,1,0:T(8,128)(2,1)S(1)} all-to-all(bf16[4,48,128]{2,1,0:T(8,128)(2,1)S(1)} %get-tuple-element.36), channel_id=1, replica_groups={{0,8,16,24},{2,10,18,26},{4,12,20,28},{6,14,22,30},{1,9,17,25},{3,11,19..., dimensions={0} | all-to-all | bytes 98304 | tf_op jit(solution)/shard_map/all_to_all | solution.py:353
  73.5 5.6 %all-to-all-start.3 = ((bf16[4,4,48,128]{3,2,1,0:T(8,128)(2,1)}), bf16[4,4,48,128]{3,2,1,0:T(8,128)(2,1)}, u32[]{:S(2)}, u32[]{:S(2)}) async-start(bf16[4,4,48,128]{3,2,1,0:T(8,128)(2,1)} %broadcast_in_dim.4), calls=%async_computation.3 | async-start | bytes 393216 | tf_op jit(solution)/shard_map/all_to_all | solution.py:354
  79.1 1.6 %copy-done.2 = bf16[2,512,1024]{2,1,0:T(8,128)(2,1)S(1)} copy-done((bf16[2,512,1024]{2,1,0:T(8,128)(2,1)S(1)}, bf16[2,512,1024]{2,1,0:T(8,128)(2,1)}, u32[]{:S(2)}) %copy-start.2) | copy-done | bytes 2097176
  82.7 5.6 %second_image.1 = (f32[1024,128]{1,0:T(8,128)S(1)}, f32[1024,128]{1,0:T(8,128)S(1)}, bf16[2,128,128]{2,1,0:T(8,128)(2,1)S(1)}, bf16[2,128,128]{2,1,0:T(8,128)(2,1)S(1)}) custom-call(bf16[2,512,1024]{2,1,0:T(8,128)(2,1)S(1)} %copy-done, bf16[2,512,1024]{2,1,0:T(8,128)(2,1)} %collective-permute-done.2.refs_1_, bf16[2,512,1024]{2,1,0:T(8,128)(2,1)S(1)} %copy-done.2, ...), custom_call_target="tpu_custom_call" | custom-call | flops 1073741824 | bytes 10356736 | tf_op jit(solution)/shard_map/second_image/pallas_call | solution.py:307
  90.5 1.0 copy-done.20
  91.6 1.8 %coarse.1 = bf16[4,48,128]{2,1,0:T(8,128)(2,1)} custom-call(bf16[4,4,48,128]{3,2,1,0:T(8,128)(2,1)} %all-to-all-done.3.arrived, bf16[2,96,768]{2,1,0:T(8,128)(2,1)S(1)} %copy-done.20), custom_call_target="tpu_custom_call" | custom-call | flops 16777216 | bytes 540672 | tf_op jit(solution)/shard_map/coarse/pallas_call | solution.py:307
  93.4 3.3 %all-to-all-start.4 = ((bf16[4,48,128]{2,1,0:T(8,128)(2,1)}), bf16[4,48,128]{2,1,0:T(8,128)(2,1)S(1)}, u32[]{:S(2)}, u32[]{:S(2)}) async-start(bf16[4,48,128]{2,1,0:T(8,128)(2,1)} %coarse.1), calls=%async_computation.4 | async-start | bytes 98304 | tf_op jit(solution)/shard_map/all_to_all | solution.py:353
  97.4 2.0 %collective-permute-start.6 = (bf16[128,128]{1,0:T(8,128)(2,1)S(1)}, bf16[128,128]{1,0:T(8,128)(2,1)S(1)}, u32[]{:S(2)}, u32[]{:S(2)}) collective-permute-start(bf16[128,128]{1,0:T(8,128)(2,1)S(1)} %slice_bitcast_fusion.3), channel_id=1, source_target_pairs={{0,2},{2,4},{4,6},{6,8},{8,10},{10,12},{12,14},{14,16},{16,18},{18... | collective-permute-start | bytes 98312 | tf_op jit(solution)/shard_map/ppermute | solution.py:425
  99.5 2.9 %all-to-all-done.4 = bf16[4,48,128]{2,1,0:T(8,128)(2,1)S(1)} async-done(((bf16[4,48,128]{2,1,0:T(8,128)(2,1)}), bf16[4,48,128]{2,1,0:T(8,128)(2,1)S(1)}, u32[]{:S(2)}, u32[]{:S(2)}) %all-to-all-start.4) | async-done | bytes 49184 | tf_op jit(solution)/shard_map/all_to_all | solution.py:353
  103.1 4.2 %all-to-all-start.5 = ((bf16[4,4,48,128]{3,2,1,0:T(8,128)(2,1)}), bf16[4,4,48,128]{3,2,1,0:T(8,128)(2,1)S(1)}, u32[]{:S(2)}, u32[]{:S(2)}) async-start(bf16[4,4,48,128]{3,2,1,0:T(8,128)(2,1)} %broadcast_in_dim.5), calls=%async_computation.5 | async-start | bytes 393216 | tf_op jit(solution)/shard_map/all_to_all | solution.py:354
  107.3 3.1 %collective-permute-start.7 = (bf16[128,128]{1,0:T(8,128)(2,1)S(1)}, bf16[128,128]{1,0:T(8,128)(2,1)S(1)}, u32[]{:S(2)}, u32[]{:S(2)}) collective-permute-start(bf16[128,128]{1,0:T(8,128)(2,1)S(1)} %slice_bitcast_fusion.2), channel_id=1, source_target_pairs={{2,0},{4,2},{6,4},{8,6},{10,8},{12,10},{14,12},{16,14},{18,16},{20... | collective-permute-start | bytes 98312 | tf_op jit(solution)/shard_map/ppermute | solution.py:426
  110.3 2.1 %collective-permute-done.7.refs_5_ = bf16[128,128]{1,0:T(8,128)(2,1)S(1)} collective-permute-done((bf16[128,128]{1,0:T(8,128)(2,1)S(1)}, bf16[128,128]{1,0:T(8,128)(2,1)S(1)}, u32[]{:S(2)}, u32[]{:S(2)}) %collective-permute-start.7) | collective-permute-done | bytes 32800 | tf_op jit(solution)/shard_map/ppermute | solution.py:426
  112.4 1.0 copy-done.18
  116.7 4.6 %all_to_all.36.arrived = f32[2,2,512,128]{3,2,1,0:T(8,128)S(1)} all-to-all(f32[2,2,512,128]{3,2,1,0:T(8,128)S(1)} %last.1), channel_id=1, replica_groups=mesh['sub'=16,'crow'=2,'ccol'=1] {'crow','ccol'}, dimensions={0} | all-to-all | bytes 2097152 | tf_op jit(solution)/shard_map/all_to_all | solution.py:445
  121.3 1.2 %unpack.1 = (f32[2,512,128]{2,1,0:T(8,128)}, f32[2,512,128]{2,1,0:T(8,128)}) custom-call(f32[2,2,512,128]{3,2,1,0:T(8,128)S(1)} %all_to_all.36.arrived), custom_call_target="tpu_custom_call" | custom-call | flops 16777216 | bytes 2097152 | tf_op jit(solution)/shard_map/unpack/pallas_call | solution.py:307
  (81 shorter events, 21.2 us)
Async XLA Ops:
  0.6 36.1 %copy-start = (bf16[2,512,1024]{2,1,0:T(8,128)(2,1)S(1)}, bf16[2,512,1024]{2,1,0:T(8,128)(2,1)}, u32[]{:S(2)}) copy-start(bf16[2,512,1024]{2,1,0:T(8,128)(2,1)} %refs_0_.5) | copy-start | bytes 6291460
  0.6 36.1 %collective-permute-start.2 = (bf16[2,512,1024]{2,1,0:T(8,128)(2,1)}, bf16[2,512,1024]{2,1,0:T(8,128)(2,1)}, u32[]{:S(2)}, u32[]{:S(2)}) collective-permute-start(bf16[2,512,1024]{2,1,0:T(8,128)(2,1)} %refs_0_.5), channel_id=1, source_target_pairs={{1,0},{0,1},{3,2},{2,3},{5,4},{4,5},{7,6},{6,7},{9,8},{8,9},{11,10... | collective-permute-start | bytes 6291464 | tf_op jit(solution)/shard_map/ppermute | solution.py:326
  1.2 35.6 %collective-permute-start.3 = (bf16[2,512,1024]{2,1,0:T(8,128)(2,1)}, bf16[2,512,1024]{2,1,0:T(8,128)(2,1)}, u32[]{:S(2)}, u32[]{:S(2)}) collective-permute-start(bf16[2,512,1024]{2,1,0:T(8,128)(2,1)} %refs_2_.5), channel_id=1, source_target_pairs={{1,0},{0,1},{3,2},{2,3},{5,4},{4,5},{7,6},{6,7},{9,8},{8,9},{11,10... | collective-permute-start | bytes 6291464 | tf_op jit(solution)/shard_map/ppermute | solution.py:326
  1.2 4.2 %collective-permute-start.1 = (bf16[2,48,512]{2,1,0:T(8,128)(2,1)}, bf16[2,48,512]{2,1,0:T(8,128)(2,1)S(1)}, u32[]{:S(2)}, u32[]{:S(2)}) collective-permute-start(bf16[2,48,512]{2,1,0:T(8,128)(2,1)} %bitcast.14), channel_id=1, source_target_pairs={{1,0},{0,1},{3,2},{2,3},{5,4},{4,5},{7,6},{6,7},{9,8},{8,9},{11,10... | collective-permute-start | bytes 294920 | tf_op jit(solution)/shard_map/ppermute | solution.py:326
  5.4 1.0 copy-start.16
  7.4 29.4 %copy-start.26 = (s32[2,128]{1,0:T(2,128)S(1)}, s32[2,128]{1,0:T(2,128)}, u32[]{:S(2)}) copy-start(s32[2,128]{1,0:T(2,128)} %refs_6_.7) | copy-start | bytes 3076
  7.4 29.4 %copy-start.27 = (s32[2,128]{1,0:T(2,128)S(1)}, s32[2,128]{1,0:T(2,128)}, u32[]{:S(2)}) copy-start(s32[2,128]{1,0:T(2,128)} %refs_7_.7) | copy-start | bytes 3076
  8.6 36.7 %copy-start.6 = (bf16[2,48,1024]{2,1,0:T(8,128)(2,1)}, bf16[2,48,1024]{2,1,0:T(8,128)(2,1)S(1)}, u32[]{:S(2)}) copy-start(bf16[2,48,1024]{2,1,0:T(8,128)(2,1)S(1)} %get-tuple-element.27.refs_5_.basis_t) | copy-start | bytes 589828
  8.6 18.4 %all-to-all-start = ((bf16[16,64,128]{2,1,0:T(8,128)(2,1)}), bf16[16,64,128]{2,1,0:T(8,128)(2,1)S(1)}, u32[]{:S(2)}, u32[]{:S(2)}) async-start(bf16[16,64,128]{2,1,0:T(8,128)(2,1)} %get-tuple-element.23), calls=%async_computation | async-start | bytes 524288 | tf_op jit(solution)/shard_map/all_to_all | solution.py:364
  16.9 1.6 %collective-permute-start = (bf16[96,768]{1,0:T(8,128)(2,1)}, bf16[96,768]{1,0:T(8,128)(2,1)S(1)}, u32[]{:S(2)}, u32[]{:S(2)}) collective-permute-start(bf16[96,768]{1,0:T(8,128)(2,1)} %refs_0_.3), channel_id=1, source_target_pairs={{1,0},{0,1},{3,2},{2,3},{5,4},{4,5},{7,6},{6,7},{9,8},{8,9},{11,10... | collective-permute-start | bytes 442376 | tf_op jit(solution)/shard_map/ppermute | solution.py:326
  32.6 23.9 %all-to-all-start.1 = ((bf16[16,48,128]{2,1,0:T(8,128)(2,1)}), bf16[16,48,128]{2,1,0:T(8,128)(2,1)}, u32[]{:S(2)}, u32[]{:S(2)}) async-start(bf16[16,48,128]{2,1,0:T(8,128)(2,1)} %get-tuple-element.24), calls=%async_computation.1 | async-start | bytes 393216 | tf_op jit(solution)/shard_map/all_to_all | solution.py:399
  36.8 1.6 %copy-start.1 = (bf16[2,512,1024]{2,1,0:T(8,128)(2,1)S(1)}, bf16[2,512,1024]{2,1,0:T(8,128)(2,1)}, u32[]{:S(2)}) copy-start(bf16[2,512,1024]{2,1,0:T(8,128)(2,1)} %refs_2_.5) | copy-start | bytes 6291460
  38.4 12.7 %copy-start.28 = (s32[2,768]{1,0:T(2,128)S(1)}, s32[2,768]{1,0:T(2,128)}, u32[]{:S(2)}) copy-start(s32[2,768]{1,0:T(2,128)} %constant.39.clone.place) | copy-start | bytes 18436
  45.3 7.9 %copy-start.10 = (f32[1024,128]{1,0:T(8,128)}, f32[1024,128]{1,0:T(8,128)S(1)}, u32[]{:S(2)}) copy-start(f32[1024,128]{1,0:T(8,128)S(1)} %get-tuple-element.28.solved) | copy-start | bytes 1572868
  45.4 7.9 %collective-permute-start.4 = (bf16[128,256]{1,0:T(8,128)(2,1)S(1)}, bf16[128,256]{1,0:T(8,128)(2,1)S(1)}, u32[]{:S(2)}, u32[]{:S(2)}) collective-permute-start(bf16[128,256]{1,0:T(8,128)(2,1)S(1)} %slice_bitcast_fusion.1), channel_id=1, source_target_pairs={{0,2},{2,4},{4,6},{6,8},{8,10},{10,12},{12,14},{14,16},{16,18},{18... | collective-permute-start | bytes 196616 | tf_op jit(solution)/shard_map/ppermute | solution.py:381
  47.2 6.1 %collective-permute-start.5 = (bf16[128,256]{1,0:T(8,128)(2,1)S(1)}, bf16[128,256]{1,0:T(8,128)(2,1)S(1)}, u32[]{:S(2)}, u32[]{:S(2)}) collective-permute-start(bf16[128,256]{1,0:T(8,128)(2,1)S(1)} %slice_bitcast_fusion), channel_id=1, source_target_pairs={{2,0},{4,2},{6,4},{8,6},{10,8},{12,10},{14,12},{16,14},{18,16},{20... | collective-permute-start | bytes 196616 | tf_op jit(solution)/shard_map/ppermute | solution.py:382
  54.7 1.0 copy-start.3
  56.5 1.2 %copy-start.4 = (bf16[2,1024,144]{2,1,0:T(8,128)(2,1)S(1)}, bf16[2,1024,144]{2,1,0:T(8,128)(2,1)}, u32[]{:S(2)}) copy-start(bf16[2,1024,144]{2,1,0:T(8,128)(2,1)} %copy-done.3) | copy-start | bytes 1769476
  58.6 1.0 copy-start.11
  59.7 1.0 copy-start.15
  73.5 17.0 %all-to-all-start.3 = ((bf16[4,4,48,128]{3,2,1,0:T(8,128)(2,1)}), bf16[4,4,48,128]{3,2,1,0:T(8,128)(2,1)}, u32[]{:S(2)}, u32[]{:S(2)}) async-start(bf16[4,4,48,128]{3,2,1,0:T(8,128)(2,1)} %broadcast_in_dim.4), calls=%async_computation.3 | async-start | bytes 393216 | tf_op jit(solution)/shard_map/all_to_all | solution.py:354
  79.1 1.6 %copy-start.2 = (bf16[2,512,1024]{2,1,0:T(8,128)(2,1)S(1)}, bf16[2,512,1024]{2,1,0:T(8,128)(2,1)}, u32[]{:S(2)}) copy-start(bf16[2,512,1024]{2,1,0:T(8,128)(2,1)} %refs_2_.5) | copy-start | bytes 6291460
  80.7 1.0 copy-start.13
  81.8 0.9 copy-start.22
  90.5 24.3 %copy-start.5 = (bf16[2,1024,144]{2,1,0:T(8,128)(2,1)S(1)}, bf16[2,1024,144]{2,1,0:T(8,128)(2,1)}, u32[]{:S(2)}) copy-start(bf16[2,1024,144]{2,1,0:T(8,128)(2,1)} %copy-done.3) | copy-start | bytes 1769476
  90.5 1.1 copy-start.20
  93.4 8.9 %all-to-all-start.4 = ((bf16[4,48,128]{2,1,0:T(8,128)(2,1)}), bf16[4,48,128]{2,1,0:T(8,128)(2,1)S(1)}, u32[]{:S(2)}, u32[]{:S(2)}) async-start(bf16[4,48,128]{2,1,0:T(8,128)(2,1)} %coarse.1), calls=%async_computation.4 | async-start | bytes 98304 | tf_op jit(solution)/shard_map/all_to_all | solution.py:353
  97.4 12.9 %collective-permute-start.6 = (bf16[128,128]{1,0:T(8,128)(2,1)S(1)}, bf16[128,128]{1,0:T(8,128)(2,1)S(1)}, u32[]{:S(2)}, u32[]{:S(2)}) collective-permute-start(bf16[128,128]{1,0:T(8,128)(2,1)S(1)} %slice_bitcast_fusion.3), channel_id=1, source_target_pairs={{0,2},{2,4},{4,6},{6,8},{8,10},{10,12},{12,14},{14,16},{16,18},{18... | collective-permute-start | bytes 98312 | tf_op jit(solution)/shard_map/ppermute | solution.py:425
  103.1 11.7 %all-to-all-start.5 = ((bf16[4,4,48,128]{3,2,1,0:T(8,128)(2,1)}), bf16[4,4,48,128]{3,2,1,0:T(8,128)(2,1)S(1)}, u32[]{:S(2)}, u32[]{:S(2)}) async-start(bf16[4,4,48,128]{3,2,1,0:T(8,128)(2,1)} %broadcast_in_dim.5), calls=%async_computation.5 | async-start | bytes 393216 | tf_op jit(solution)/shard_map/all_to_all | solution.py:354
  107.3 5.2 %collective-permute-start.7 = (bf16[128,128]{1,0:T(8,128)(2,1)S(1)}, bf16[128,128]{1,0:T(8,128)(2,1)S(1)}, u32[]{:S(2)}, u32[]{:S(2)}) collective-permute-start(bf16[128,128]{1,0:T(8,128)(2,1)S(1)} %slice_bitcast_fusion.2), channel_id=1, source_target_pairs={{2,0},{4,2},{6,4},{8,6},{10,8},{12,10},{14,12},{16,14},{18,16},{20... | collective-permute-start | bytes 98312 | tf_op jit(solution)/shard_map/ppermute | solution.py:426
  112.4 1.0 copy-start.18
  114.8 1.0 copy-start.9
  (13 other events, 10.5 us)

commit v4 on v2

--- a/solution.py
+++ b/solution.py
@@ -11,7 +11,7 @@
 GROUP = ("crow", "ccol")
 F32 = jnp.float32
 BF16 = jnp.bfloat16
-VMEM_BYTES = 48 * 1024 * 1024
+VMEM_BYTES = 40 * 1024 * 1024
 DIGIT_ROWS = 16
 DIGIT = 256
 
@@ -121,7 +121,7 @@
     return dot_tn(scatter_matrix(z, rows_ref[s : s + 1, :]), image).astype(BF16)
 
 
-def image_kernel(z, first, *refs):
+def image_kernel(z, first, wait, *refs):
     inverse, stiffness = refs[: z.group], refs[z.group : 2 * z.group]
     rest = refs[2 * z.group :]
     if first:
@@ -145,6 +145,8 @@
     def store_image(start, value):
         image[pl.ds(start, z.own), :] = value
 
+    for k in range(z.group):
+        wait(z.group + k)
     multiply(z, stiffness, rounded[...], store_image)
     if first:
         for s in range(z.subs):
@@ -186,46 +188,17 @@
     residual[...] = load_rows[...].astype(F32) - image[...] - select(z, added)
 
 
-def coarse_rows(z, ordered_inverse, arrived):
-    parts = [dot(ordered_inverse[s], arrived) for s in range(z.subs)]
-    rows = fold(z, select(z, parts))
-    return select(z, [rows[s * z.modes : (s + 1) * z.modes, :] for s in range(z.subs)]).astype(BF16)
-
-
-def order_kernel(z, *refs):
-    pieces = refs[: z.group]
-    arrived, repeat, own_row, ordered_inverse, index, message, whole = refs[z.group :]
-    for k, piece in enumerate(pieces):
-        whole[:, pl.ds(piece_start(z, k, z.block), z.block)] = piece[...]
-    digits = arrived[:, z.modes :, :].astype(F32)
-    for s in range(z.subs):
-        high = jnp.sum(jnp.where(digit_row(digits.shape, 2 * s), digits, 0.0), axis=1)
-        low = jnp.sum(jnp.where(digit_row(digits.shape, 2 * s + 1), digits, 0.0), axis=1)
-        index[s] = high * DIGIT + low
-        spread = dot(high.astype(BF16), repeat[...]) * DIGIT + dot(low.astype(BF16), repeat[...])
-        places = jnp.sum(spread * own_row[...], axis=0, keepdims=True).astype(jnp.int32)
-        for at in range(0, z.columns, 768):
-            wide = min(768, z.columns - at)
-            total = jnp.zeros((z.owned, wide), F32)
-            for first in range(0, z.total, 256):
-                deep = min(256, z.total - first)
-                row = lax.broadcasted_iota(jnp.int32, (deep, wide), 0) + first
-                hot = jnp.where(row == places[:, at : at + wide], 1.0, 0.0).astype(BF16)
-                total = total + dot(whole[:, first : first + deep], hot)
-            ordered_inverse[s, :, at : at + wide] = total.astype(BF16)
-    rows = arrived[:, : z.modes, :].reshape(z.columns, z.lanes)
-    packed = coarse_rows(z, ordered_inverse, rows)
-    for k in range(z.n):
-        message[k] = packed
-
-
 def digit_row(shape, row):
     return lax.broadcasted_iota(jnp.int32, shape, 1) == row
 
 
-def pick_kernel(z, index, place, picks):
+def choose_kernel(z, block, arrived, repeat, own_row, chosen, rows):
+    digits = arrived[:, z.modes :, :].astype(F32)
+    high = [jnp.sum(jnp.where(digit_row(digits.shape, 2 * s), digits, 0.0), axis=1) for s in range(z.subs)]
+    low = [jnp.sum(jnp.where(digit_row(digits.shape, 2 * s + 1), digits, 0.0), axis=1) for s in range(z.subs)]
     here = lax.axis_index("sub")
     device = lax.broadcasted_iota(jnp.int32, (z.n, z.lanes), 0)
+    row_of = lax.broadcasted_iota(jnp.int32, (z.modes, z.total), 1)
     for t in range(z.subs + 2):
         if t == 0:
             s, owner = z.subs - 1, lax.rem(here + z.n - 1, z.n)
@@ -233,26 +206,45 @@
             s, owner = 0, lax.rem(here + 1, z.n)
         else:
             s, owner = t - 1, here
-        row = jnp.sum(jnp.where(device == owner, index[s], 0.0), axis=0, keepdims=True)
-        column = jnp.transpose(jnp.broadcast_to(row, (z.lanes, z.lanes)))[: z.modes, 0:1]
-        column = column.astype(jnp.int32)
-        for h in range(z.subs):
-            hit = column == place[h : h + 1, :]
-            picks[h, t * z.modes : (t + 1) * z.modes, :] = jnp.where(hit, 1.0, 0.0).astype(BF16)
-
-
-def picked_rows(z, arrived, picks):
-    flat = arrived[...].reshape(z.columns, z.lanes)
-    return fold(z, select(z, [dot(picks[h], flat) for h in range(z.subs)])).astype(BF16)
-
-
-def update_kernel(z, arrived, picks, solved, residual, basis, joined, basis_t, first_pass, rounded, message):
-    chosen = picked_rows(z, arrived, picks)
+        places = high[s] * DIGIT + low[s]
+        row = jnp.sum(jnp.where(device == owner, places, 0.0), axis=0, keepdims=True)
+        column = jnp.transpose(jnp.broadcast_to(row, (z.lanes, z.lanes)))[: z.modes, 0:1].astype(jnp.int32)
+        hot = jnp.where(row_of == column, 1.0, 0.0).astype(BF16)
+        rows[t * z.modes : (t + 1) * z.modes, :] = dot(hot, block[...]).astype(BF16)
+    first = lax.axis_index(GROUP) * z.block
+    for s in range(z.subs):
+        spread = dot(high[s].astype(BF16), repeat[...]) * DIGIT + dot(low[s].astype(BF16), repeat[...])
+        places = jnp.sum(spread * own_row[...], axis=0, keepdims=True).astype(jnp.int32) - first
+        for at in range(0, z.columns, 768):
+            wide = min(768, z.columns - at)
+            total = jnp.zeros((rows.shape[0], wide), F32)
+            for start in range(0, z.block, 256):
+                deep = min(256, z.block - start)
+                row = lax.broadcasted_iota(jnp.int32, (deep, wide), 0) + start
+                hot = jnp.where(row == places[:, at : at + wide], 1.0, 0.0).astype(BF16)
+                total = total + dot(rows[:, start : start + deep], hot)
+            chosen[s, :, at : at + wide] = total.astype(BF16)
+
+
+def coarse_rows(z, chosen, arrived):
+    flat = arrived[:, : z.modes, :].reshape(z.columns, z.lanes)
+    return fold(z, select(z, [dot(chosen[s], flat) for s in range(z.subs)])).astype(BF16)
+
+
+def update_kernel(z, *refs):
+    pieces = refs[: z.group]
+    arrived, solved, residual, basis, joined, basis_t, first_pass, rounded, message, chosen = refs[z.group :]
+    for s in range(z.subs):
+        total = pieces[0][s].astype(F32)
+        for piece in pieces[1:]:
+            total = total + piece[s].astype(F32)
+        chosen[s] = total.astype(BF16)
+    coarse = coarse_rows(z, chosen, arrived)
     m = z.modes
     first_pass[...] = solved[...] + select(
-        z, [dot(basis[s], chosen[(s + 1) * m : (s + 2) * m]) for s in range(z.subs)]
-    )
-    left = residual[...] - select(z, [dot(joined[s], chosen[s * m : (s + 3) * m]) for s in range(z.subs)])
+        z, [dot(basis[s], coarse[(s + 1) * m : (s + 2) * m]) for s in range(z.subs)]
+    )
+    left = residual[...] - select(z, [dot(joined[s], coarse[s * m : (s + 3) * m]) for s in range(z.subs)])
     left = left.astype(BF16)
     rounded[...] = left
     modes = select(z, [dot(basis_t[s], left) for s in range(z.subs)]).astype(BF16)
@@ -260,46 +252,67 @@
         message[k] = modes
 
 
-def coarse_kernel(z, arrived, ordered_inverse, message):
-    packed = coarse_rows(z, ordered_inverse, arrived[...].reshape(z.columns, z.lanes))
-    for k in range(z.n):
-        message[k] = packed
-
-
-def last_kernel(z, arrived, picks, solved, residual, basis, joined, out):
-    chosen = picked_rows(z, arrived, picks)
+def last_kernel(z, arrived, chosen, solved, residual, basis, joined, *outs):
+    coarse = coarse_rows(z, chosen, arrived)
     m = z.modes
     second = solved[...] + select(
-        z, [dot(basis[s], chosen[(s + 1) * m : (s + 2) * m]) for s in range(z.subs)]
-    )
-    left = residual[...] - select(z, [dot(joined[s], chosen[s * m : (s + 3) * m]) for s in range(z.subs)])
-    for k in range(z.group):
-        out[k, 0] = second[k * z.own : (k + 1) * z.own, :]
-        out[k, 1] = left[k * z.own : (k + 1) * z.own, :]
-
-
-def unpack_kernel(z, arrived, second_pass, final_residual):
-    for at, out in enumerate((second_pass, final_residual)):
+        z, [dot(basis[s], coarse[(s + 1) * m : (s + 2) * m]) for s in range(z.subs)]
+    )
+    left = residual[...] - select(z, [dot(joined[s], coarse[s * m : (s + 3) * m]) for s in range(z.subs)])
+    *outs, whole = outs
+    whole[0] = second
+    whole[1] = left
+    for k, out in enumerate(outs):
+        out[...] = whole[:, pl.ds(piece_start(z, k, z.own), z.own), :]
+
+
+def unpack_kernel(z, *refs):
+    pieces, outs = refs[: z.group], refs[z.group :]
+    for at, out in enumerate(outs):
         for s in range(z.subs):
             total = jnp.zeros((z.own, z.lanes), F32)
-            for k in range(z.group):
-                turned = arrived[k, at]
-                turn = ((k - s) * z.width) % z.lanes
-                if turn:
-                    turned = pltpu.roll(turned, turn, 1)
-                total = jnp.where(lane_mask(z, k, turned.shape), turned, total)
+            for k, piece in enumerate(pieces):
+                place = lax.rem(lax.axis_index(GROUP) + k, z.group)
+                turn = lax.rem((place - s + z.subs * z.group) * z.width, z.lanes)
+                turned = pltpu.roll(piece[at], turn, 1)
+                total = jnp.where(lane_mask(z, place, turned.shape), turned, total)
             out[s] = total[:, : z.cases]
 
 
-def call(kernel, outs, operands, flops, scratch=(), name=None):
-    vmem = pl.BlockSpec(memory_space=pltpu.VMEM)
+def call(kernel, outs, operands, flops, scratch=(), late=(), name=None):
     moved = sum(int(np.prod(x.shape)) * x.dtype.itemsize for x in (*operands, *outs))
+    n_in, n_out = len(operands), len(outs)
+
+    def whole(*refs):
+        hbm, refs = refs[: n_in + n_out], refs[n_in + n_out :]
+        vmem, refs = refs[: n_in + n_out], refs[n_in + n_out :]
+        in_sems, out_sems, *rest = refs
+        arriving = [pltpu.make_async_copy(hbm[i], vmem[i], in_sems.at[i]) for i in range(n_in)]
+        for copy in arriving:
+            copy.start()
+        for i, copy in enumerate(arriving):
+            if i not in late:
+                copy.wait()
+        extra = [lambda i: arriving[i].wait()] if late else []
+        kernel(*extra, *vmem, *rest)
+        leaving = [pltpu.make_async_copy(vmem[n_in + i], hbm[n_in + i], out_sems.at[i]) for i in range(n_out)]
+        for copy in leaving:
+            copy.start()
+        for copy in leaving:
+            copy.wait()
+
+    anywhere = pl.BlockSpec(memory_space=pl.ANY)
     return pl.pallas_call(
-        kernel,
+        whole,
         out_shape=[jax.ShapeDtypeStruct(o.shape, o.dtype) for o in outs],
-        in_specs=[vmem] * len(operands),
-        out_specs=[vmem] * len(outs),
-        scratch_shapes=list(scratch),
+        in_specs=[anywhere] * n_in,
+        out_specs=[anywhere] * n_out,
+        scratch_shapes=[
+            *[pltpu.VMEM(x.shape, x.dtype) for x in (*operands, *outs)],
+            pltpu.SemaphoreType.DMA((n_in,)),
+            pltpu.SemaphoreType.DMA((n_out,)),
+            *scratch,
+        ],
         compiler_params=pltpu.CompilerParams(vmem_limit_bytes=VMEM_BYTES),
         cost_estimate=pl.CostEstimate(flops=flops, bytes_accessed=moved, transcendentals=0),
         name=name,
@@ -321,6 +334,7 @@
     z = Sizes(loads, stiffness, coarse_basis, coarse_inverse, left_rows)
     n, group, subs, rows, lanes, modes = z.n, z.group, z.subs, z.rows, z.lanes, z.modes
     own_t = jnp.swapaxes(coarse_basis, 1, 2)
+    gathered = lax.all_gather(coarse_inverse, "sub", axis=0, tiled=True)
     basis_pieces = pieces_of(own_t, group)
     high, low = coarse_index // DIGIT, coarse_index % DIGIT
     digits = jnp.stack([high, low], axis=1).reshape(2 * subs, modes).astype(BF16)
@@ -328,9 +342,6 @@
     column = np.arange(z.columns)
     repeat = jnp.asarray(np.arange(lanes)[:, None] == column[None, :] % modes, BF16)
     own_row = jnp.asarray(np.arange(n)[:, None] == column[None, :] // modes, F32)
-    place = jnp.asarray(
-        (column // modes * z.owned + column % modes)[None, :] + np.arange(subs)[:, None] * modes, jnp.int32
-    )
     packed_f = shape((rows, lanes), F32)
     packed_b = shape((rows, lanes), BF16)
     copies = shape((n, modes, lanes), BF16)
@@ -347,7 +358,6 @@
 
     inverse_pieces = pieces_of(local_inverse, group)
     stiffness_pieces = pieces_of(stiffness, group)
-    inverse_columns = pieces_of(coarse_inverse, group)
     work = 4 * subs * rows * rows * lanes
     faces = shape((subs, z.face, 2 * lanes), BF16)
     solved, image, to_before, to_after, basis, image_basis = call(
@@ -356,6 +366,7 @@
         [*inverse_pieces, *stiffness_pieces, load_rows, basis_t, left_rows, right_rows],
         work,
         [pltpu.VMEM((rows, lanes), BF16)],
+        range(group, 2 * group),
         name="first_image",
     )
     forward = [(i, (i + 1) % n) for i in range(n)]
@@ -370,26 +381,20 @@
         name="first_join",
     )
 
-    ordered_inverse, index, message = call(
-        functools.partial(order_kernel, z),
-        [shape((subs, z.owned, z.columns), BF16), shape((subs, n, lanes), F32), copies],
-        [*inverse_columns, restricted, repeat, own_row],
-        2 * z.owned * z.total * z.total,
-        [pltpu.VMEM((z.owned, z.total), BF16)],
-        name="order",
-    )
-    coarse = spread(message)
-    (picks,) = call(
-        functools.partial(pick_kernel, z),
-        [shape((subs, (subs + 2) * modes, z.columns), BF16)],
-        [index, place],
-        work // 64,
-        name="picks",
-    )
-    first_pass, rounded, message = call(
+    near = (subs + 2) * modes
+    columns = shape((subs, near, z.columns), BF16)
+    (chosen,) = call(
+        functools.partial(choose_kernel, z),
+        [columns],
+        [gathered, restricted, repeat, own_row],
+        2 * near * z.total * z.total,
+        [pltpu.VMEM((near, z.block), BF16)],
+        name="choose",
+    )
+    first_pass, rounded, message, chosen = call(
         functools.partial(update_kernel, z),
-        [packed_f, packed_b, copies],
-        [coarse, picks, solved, residual, basis, joined, basis_t],
+        [packed_f, packed_b, copies, columns],
+        [*pieces_of(chosen, group), restricted, solved, residual, basis, joined, basis_t],
         work // 8,
         name="update",
     )
@@ -402,6 +407,7 @@
         [*inverse_pieces, *stiffness_pieces, rounded, first_pass, left_rows, right_rows],
         work,
         [pltpu.VMEM((rows, lanes), BF16)],
+        range(group, 2 * group),
         name="second_image",
     )
     from_before = lax.ppermute(to_after[subs - 1], "sub", forward)
@@ -413,20 +419,21 @@
         work // 8,
         name="second_join",
     )
-    (message,) = call(
-        functools.partial(coarse_kernel, z), [copies], [restricted, ordered_inverse], work // 64, name="coarse"
-    )
-    coarse = spread(message)
-    (parts,) = call(
+    parts = shape((2, z.own, lanes), F32)
+    parts = call(
         functools.partial(last_kernel, z),
-        [shape((group, 2, z.own, lanes), F32)],
-        [coarse, picks, solved, residual, basis, joined],
+        [parts] * group,
+        [restricted, chosen, solved, residual, basis, joined],
         work // 8,
+        [pltpu.VMEM((2, rows, lanes), F32)],
         name="last",
     )
-    parts = lax.all_to_all(parts, GROUP, 0, 0)
+    swapped = [parts[0]]
+    for k in range(1, group):
+        swapped.append(lax.ppermute(parts[k], GROUP, [(g, (g + k) % group) for g in range(group)]))
+    swapped = [swapped[(group - k) % group] for k in range(group)]
     out = shape((subs, z.own, z.cases), F32)
-    return tuple(call(functools.partial(unpack_kernel, z), [out, out], [parts], work // 64, name="unpack"))
+    return tuple(call(functools.partial(unpack_kernel, z), [out, out], swapped, work // 64, name="unpack"))
 
 
 def solution(mesh):

time: 112 us -> 149 us (1.33)
  waiting for transfers between devices: 17.9 us -> 49.8 us
  starting transfers between devices: 38.7 us -> 19.3 us
  blocking collectives: 4.58 us -> 20.7 us
  between operations: 0.9 us -> 14.4 us
  local copies, waits for them, and re-layouts: 22.4 us -> 17.5 us
    all_gather x0 -> x1, waiting for transfers between devices: none -> 39.8 us  [body(): gathered = lax.all_gather(coarse_inverse, 'sub', axis=0, tiled=True)]
    all_to_all x1, blocking collectives: 4.58 us -> 20.7 us  [body(): restricted = spread(message)]
    all_to_all x2 -> x0, starting transfers between devices: 11 us -> none  [body(): coarse = spread(message)]
    all_to_all x2 -> x1, waiting for transfers between devices: 8.53 us -> 0.01 us  [body(): restricted = spread(message)]
    all_to_all x2 -> x1, starting transfers between devices: 15.3 us -> 6.81 us  [body(): restricted = spread(message)]
    unnamed x62 -> x50, local copies, waits for them, and re-layouts: 21.6 us -> 17.4 us
    ppermute x0 -> x1, waiting for transfers between devices: none -> 1.9 us  [body(): lax.ppermute(parts[k], GROUP, [(g, (g + k) % group) for g in range(group)])]
    ppermute x4, waiting for transfers between devices: 4.61 us -> 3.05 us  [pieces_of(): lax.ppermute(block, GROUP, [((g + k) % group, g) for g in range(group)])]
  transfers between devices with their start and end apart: 12 -> 11, of which waited for: 5 -> 5; matrix products, arithmetic and copies ran while one was open for 1% -> 0% of each run, Pallas kernels for 17% -> 14%
where the time goes in v4:
time: 149 us
  waiting for transfers between devices  49.8 us (33%)
  Pallas kernels  26.2 us (18%)
  blocking collectives  20.7 us (14%)
  starting transfers between devices  19.3 us (13%)
  local copies, waits for them, and re-layouts  17.5 us (12%)
  between operations  14.4 us (10%)
    all_gather x1, waiting for transfers between devices, body(): gathered = lax.all_gather(coarse_inverse, 'sub', axis=0, tiled=True)  39.8 us
    pallas_call x9, Pallas kernels, call(): pl.pallas_call(whole, out_shape=[jax.ShapeDtypeStruct(o.shape, o.dtype) f...  26.2 us
    all_to_all x1, blocking collectives, body(): restricted = spread(message)  20.7 us
    unnamed x50, local copies, waits for them, and re-layouts  17.4 us
    ppermute x2, starting transfers between devices, body(): from_after = lax.ppermute(to_before[0], 'sub', backward)  7.94 us
    all_to_all x1, starting transfers between devices, body(): restricted = spread(message)  6.81 us
    ppermute x2, waiting for transfers between devices, body(): from_before = lax.ppermute(to_after[subs - 1], 'sub', forward)  4.37 us
    ppermute x2, starting transfers between devices, body(): from_before = lax.ppermute(to_after[subs - 1], 'sub', forward)  3.36 us
  transfers between devices with their start and end apart: 11, of which 5 were waited for; matrix products, arithmetic and copies ran while one was open for 0% of the time, Pallas kernels for 14%

profile of v4, /device:TPU:0, one launch (start us, length us, event | category | flops | bytes accessed | tf_op | source)
XLA Modules:
  0.0 148.6 jit_solution(1414395194130069)
XLA Ops:
  9.7 3.0 %collective-permute-done.refs_1_ = bf16[2,48,512]{2,1,0:T(8,128)(2,1)S(1)} collective-permute-done((bf16[2,48,512]{2,1,0:T(8,128)(2,1)}, bf16[2,48,512]{2,1,0:T(8,128)(2,1)S(1)}, u32[]{:S(2)}, u32[]{:S(2)}) %collective-permute-start) | collective-permute-done | bytes 98336 | tf_op jit(solution)/shard_map/ppermute | solution.py:329
  12.7 1.0 copy-done.14
  13.7 0.9 copy-done.21
  14.6 1.2 open.1
  15.9 20.7 %all_to_all.10.refs_1_.refs_2_ = bf16[16,64,128]{2,1,0:T(8,128)(2,1)S(1)} all-to-all(bf16[16,64,128]{2,1,0:T(8,128)(2,1)S(1)} %get-tuple-element.23), channel_id=1, replica_groups=mesh['sub'=16,'crow'=2,'ccol'=1] {'sub'}, dimensions={0} | all-to-all | bytes 524288 | tf_op jit(solution)/shard_map/all_to_all | solution.py:357
  36.6 39.8 %all-gather.2.cloned.1.call-done.refs_0_ = bf16[1536,768]{1,0:T(8,128)(2,1)} async-done(((bf16[96,768]{1,0:T(8,128)(2,1)}), bf16[1536,768]{1,0:T(8,128)(2,1)}) %all-gather.2.cloned.1.call-update) | async-done | bytes 2359312 | tf_op jit(solution)/shard_map/all_gather | solution.py:337
  76.4 1.7 %copy-done.3 = bf16[1536,768]{1,0:T(8,128)(2,1)S(1)} copy-done((bf16[1536,768]{1,0:T(8,128)(2,1)S(1)}, bf16[1536,768]{1,0:T(8,128)(2,1)}, u32[]{:S(2)}) %copy-start.3) | copy-done | bytes 2359320
  78.1 0.9 copy-done.20
  79.8 3.4 %choose.1.refs_0_ = bf16[2,192,768]{2,1,0:T(8,128)(2,1)S(1)} custom-call(bf16[1536,768]{1,0:T(8,128)(2,1)S(1)} %copy-done.3, bf16[16,64,128]{2,1,0:T(8,128)(2,1)S(1)} %all_to_all.10.refs_1_.refs_2_, bf16[128,768]{1,0:T(8,128)(2,1)S(1)} %copy-done.20, f32[16,768]{1,0:T(8,128)S(1)} %copy-done.22), custom_call_target="tpu_custom_call" | custom-call | flops 905969664 | bytes 3457024 | tf_op jit(solution)/shard_map/choose/pallas_call | solution.py:305
  83.4 1.6 %copy-done.1 = bf16[2,512,1024]{2,1,0:T(8,128)(2,1)S(1)} copy-done((bf16[2,512,1024]{2,1,0:T(8,128)(2,1)S(1)}, bf16[2,512,1024]{2,1,0:T(8,128)(2,1)}, u32[]{:S(2)}) %copy-start.1) | copy-done | bytes 2097176
  85.0 7.0 %first_image.1 = (f32[1024,128]{1,0:T(8,128)S(1)}, f32[1024,128]{1,0:T(8,128)S(1)}, bf16[2,128,256]{2,1,0:T(8,128)(2,1)S(1)}, bf16[2,128,256]{2,1,0:T(8,128)(2,1...) custom-call(bf16[2,512,1024]{2,1,0:T(8,128)(2,1)S(1)} %copy-done, ...), custom_call_target="tpu_custom_call" | custom-call | flops 1073741824 | bytes 10553344 | tf_op jit(solution)/shard_map/first_image/pallas_call | solution.py:305
  92.1 1.5 %collective-permute-start.4 = (bf16[128,256]{1,0:T(8,128)(2,1)S(1)}, bf16[128,256]{1,0:T(8,128)(2,1)S(1)}, u32[]{:S(2)}, u32[]{:S(2)}) collective-permute-start(bf16[128,256]{1,0:T(8,128)(2,1)S(1)} %slice_bitcast_fusion.1), channel_id=1, source_target_pairs={{0,2},{2,4},{4,6},{6,8},{8,10},{10,12},{12,14},{14,16},{16,18},{18... | collective-permute-start | bytes 196616 | tf_op jit(solution)/shard_map/ppermute | solution.py:374
  93.6 4.2 %collective-permute-start.5 = (bf16[128,256]{1,0:T(8,128)(2,1)S(1)}, bf16[128,256]{1,0:T(8,128)(2,1)S(1)}, u32[]{:S(2)}, u32[]{:S(2)}) collective-permute-start(bf16[128,256]{1,0:T(8,128)(2,1)S(1)} %slice_bitcast_fusion), channel_id=1, source_target_pairs={{2,0},{4,2},{6,4},{8,6},{10,8},{12,10},{14,12},{16,14},{18,16},{20... | collective-permute-start | bytes 196616 | tf_op jit(solution)/shard_map/ppermute | solution.py:375
  97.8 2.5 %collective-permute-done.4.refs_4_ = bf16[128,256]{1,0:T(8,128)(2,1)S(1)} collective-permute-done((bf16[128,256]{1,0:T(8,128)(2,1)S(1)}, bf16[128,256]{1,0:T(8,128)(2,1)S(1)}, u32[]{:S(2)}, u32[]{:S(2)}) %collective-permute-start.4) | collective-permute-done | bytes 65568 | tf_op jit(solution)/shard_map/ppermute | solution.py:374
  100.2 2.2 %first_join.1 = (f32[1024,128]{1,0:T(8,128)S(1)}, bf16[2,1024,144]{2,1,0:T(8,128)(2,1)S(1)}) custom-call(bf16[1024,128]{1,0:T(8,128)(2,1)S(1)} %get-tuple-element.24.refs_4_.refs_0_, f32[1024,128]{1,0:T(8,128)S(1)} %get-tuple-element.27.refs_1_, bf16[2,128,256]{2,1,0:T(8,128)(2,1)S(1)} %get-tuple-element.28.refs_2_, ...), custom_call_target="tpu_custom_call" | custom-call | flops 134217728 | bytes 2492416 | tf_op jit(solution)/shard_map/first_join/pallas_call | solution.py:305
  102.5 2.3 %update.1 = (f32[1024,128]{1,0:T(8,128)S(1)}, bf16[1024,128]{1,0:T(8,128)(2,1)S(1)}, bf16[16,48,128]{2,1,0:T(8,128)(2,1)S(1)}, bf16[2,192,768]{2,1,0:T(8,128)(2,1)S(1)}) custom-call(bf16[2,192,768]{2,1,0:T(8,128)(2,1)S(1)} %choose.1.refs_0_, bf16[2,192,768]{2,1,0:T(8,128)(2,1)S(1)} %collective-permute-done.1.refs_1_, bf16[16,64,128]{2,1,0:T(8,128)(2,1)S(1)} %copy-done.5, ...), custom_call_target="tpu_custom_call" | custom-call | flops 134217728 | bytes 5046272 | tf_op jit(solution)/shard_map/update/pallas_call | solution.py:305
  104.8 0.8 copy-done.10
  107.8 6.8 %all-to-all-start.1 = ((bf16[16,48,128]{2,1,0:T(8,128)(2,1)}), bf16[16,48,128]{2,1,0:T(8,128)(2,1)}, u32[]{:S(2)}, u32[]{:S(2)}) async-start(bf16[16,48,128]{2,1,0:T(8,128)(2,1)} %copy-done.19), calls=%async_computation.1 | async-start | bytes 393216 | tf_op jit(solution)/shard_map/all_to_all | solution.py:401
  114.7 1.6 %copy-done.2 = bf16[2,512,1024]{2,1,0:T(8,128)(2,1)S(1)} copy-done((bf16[2,512,1024]{2,1,0:T(8,128)(2,1)S(1)}, bf16[2,512,1024]{2,1,0:T(8,128)(2,1)}, u32[]{:S(2)}) %copy-start.2) | copy-done | bytes 2097176
  116.3 1.0 copy-done.13
  117.3 0.9 copy-done.18
  118.3 5.5 %second_image.1 = (f32[1024,128]{1,0:T(8,128)S(1)}, f32[1024,128]{1,0:T(8,128)S(1)}, bf16[2,128,128]{2,1,0:T(8,128)(2,1)S(1)}, bf16[2,128,128]{2,1,0:T(8,128)(2,1)S(1)}) custom-call(bf16[2,512,1024]{2,1,0:T(8,128)(2,1)S(1)} %copy-done, bf16[2,512,1024]{2,1,0:T(8,128)(2,1)} %collective-permute-done.2.refs_1_, bf16[2,512,1024]{2,1,0:T(8,128)(2,1)S(1)} %copy-done.2, ...), custom_call_target="tpu_custom_call" | custom-call | flops 1073741824 | bytes 10356736 | tf_op jit(solution)/shard_map/second_image/pallas_call | solution.py:305
  124.6 1.9 %collective-permute-start.6 = (bf16[128,128]{1,0:T(8,128)(2,1)S(1)}, bf16[128,128]{1,0:T(8,128)(2,1)S(1)}, u32[]{:S(2)}, u32[]{:S(2)}) collective-permute-start(bf16[128,128]{1,0:T(8,128)(2,1)S(1)} %slice_bitcast_fusion.3), channel_id=1, source_target_pairs={{0,2},{2,4},{4,6},{6,8},{8,10},{10,12},{12,14},{14,16},{16,18},{18... | collective-permute-start | bytes 98312 | tf_op jit(solution)/shard_map/ppermute | solution.py:413
  126.5 3.8 %collective-permute-start.7 = (bf16[128,128]{1,0:T(8,128)(2,1)S(1)}, bf16[128,128]{1,0:T(8,128)(2,1)S(1)}, u32[]{:S(2)}, u32[]{:S(2)}) collective-permute-start(bf16[128,128]{1,0:T(8,128)(2,1)S(1)} %slice_bitcast_fusion.2), channel_id=1, source_target_pairs={{2,0},{4,2},{6,4},{8,6},{10,8},{12,10},{14,12},{16,14},{18,16},{20... | collective-permute-start | bytes 98312 | tf_op jit(solution)/shard_map/ppermute | solution.py:414
  130.2 1.9 %collective-permute-done.6.refs_4_ = bf16[128,128]{1,0:T(8,128)(2,1)S(1)} collective-permute-done((bf16[128,128]{1,0:T(8,128)(2,1)S(1)}, bf16[128,128]{1,0:T(8,128)(2,1)S(1)}, u32[]{:S(2)}, u32[]{:S(2)}) %collective-permute-start.6) | collective-permute-done | bytes 32800 | tf_op jit(solution)/shard_map/ppermute | solution.py:413
  132.1 0.9 second_join.1.refs_3_
  133.0 1.0 copy-done.7
  134.0 1.1 copy-done.11
  135.1 1.0 copy-done.16
  136.1 2.1 %last.1 = (f32[2,512,128]{2,1,0:T(8,128)S(1)}, f32[2,512,128]{2,1,0:T(8,128)S(1)}) custom-call(bf16[16,48,128]{2,1,0:T(8,128)(2,1)} %all-to-all-done.1.refs_0_, bf16[2,192,768]{2,1,0:T(8,128)(2,1)S(1)} %copy-done.11, f32[1024,128]{1,0:T(8,128)S(1)} %copy-done.16, f32[1024,128]{1,0:T(8,128)S(1)} %second_join.1.refs_3_, bf16[2,1024,48]{2,1,0:T(8,128)(2,1)S(1)} %copy-done.7, ...), custom_call_target="tpu_custom_call" | custom-call | flops 134217728 | bytes 3670016 | tf_op jit(solution)/shard_map/last/pallas_call | solution.py:305
  138.3 1.9 %collective-permute-done.8.refs_1_ = f32[2,512,128]{2,1,0:T(8,128)S(1)} collective-permute-done((f32[2,512,128]{2,1,0:T(8,128)S(1)}, f32[2,512,128]{2,1,0:T(8,128)S(1)}, u32[]{:S(2)}, u32[]{:S(2)}) %collective-permute-start.8) | collective-permute-done | bytes 524320 | tf_op jit(solution)/shard_map/ppermute | solution.py:433
  140.2 1.5 %unpack.1 = (f32[2,512,128]{2,1,0:T(8,128)}, f32[2,512,128]{2,1,0:T(8,128)}) custom-call(f32[2,512,128]{2,1,0:T(8,128)S(1)} %get-tuple-element.42.refs_0_, f32[2,512,128]{2,1,0:T(8,128)S(1)} %collective-permute-done.8.refs_1_), custom_call_target="tpu_custom_call" | custom-call | flops 16777216 | bytes 2097152 | tf_op jit(solution)/shard_map/unpack/pallas_call | solution.py:305
  (59 shorter events, 6.5 us)
Async XLA Ops:
  7.2 69.2 %all-gather.2.cloned.1.call-start = ((), (), s32[]{:S(2)}) async-start(), calls=%async_computation.2 | async-start | bytes 2506752 | tf_op jit(solution)/shard_map/all_gather | solution.py:337
  7.9 75.4 %collective-permute-start.3 = (bf16[2,512,1024]{2,1,0:T(8,128)(2,1)}, bf16[2,512,1024]{2,1,0:T(8,128)(2,1)}, u32[]{:S(2)}, u32[]{:S(2)}) collective-permute-start(bf16[2,512,1024]{2,1,0:T(8,128)(2,1)} %refs_2_.6), channel_id=1, source_target_pairs={{1,0},{0,1},{3,2},{2,3},{5,4},{4,5},{7,6},{6,7},{9,8},{8,9},{11,10... | collective-permute-start | bytes 6291464 | tf_op jit(solution)/shard_map/ppermute | solution.py:329
  8.4 74.9 %collective-permute-start.2 = (bf16[2,512,1024]{2,1,0:T(8,128)(2,1)}, bf16[2,512,1024]{2,1,0:T(8,128)(2,1)}, u32[]{:S(2)}, u32[]{:S(2)}) collective-permute-start(bf16[2,512,1024]{2,1,0:T(8,128)(2,1)} %refs_0_.3), channel_id=1, source_target_pairs={{1,0},{0,1},{3,2},{2,3},{5,4},{4,5},{7,6},{6,7},{9,8},{8,9},{11,10... | collective-permute-start | bytes 6291464 | tf_op jit(solution)/shard_map/ppermute | solution.py:329
  8.5 4.2 %collective-permute-start = (bf16[2,48,512]{2,1,0:T(8,128)(2,1)}, bf16[2,48,512]{2,1,0:T(8,128)(2,1)S(1)}, u32[]{:S(2)}, u32[]{:S(2)}) collective-permute-start(bf16[2,48,512]{2,1,0:T(8,128)(2,1)} %bitcast.14), channel_id=1, source_target_pairs={{1,0},{0,1},{3,2},{2,3},{5,4},{4,5},{7,6},{6,7},{9,8},{8,9},{11,10... | collective-permute-start | bytes 294920 | tf_op jit(solution)/shard_map/ppermute | solution.py:329
  12.7 1.0 copy-start.14
  13.7 0.9 copy-start.21
  14.6 68.7 %copy-start.23 = (s32[2,128]{1,0:T(2,128)S(1)}, s32[2,128]{1,0:T(2,128)}, u32[]{:S(2)}) copy-start(s32[2,128]{1,0:T(2,128)} %refs_6_.7) | copy-start | bytes 3076
  14.6 68.7 %copy-start.24 = (s32[2,128]{1,0:T(2,128)S(1)}, s32[2,128]{1,0:T(2,128)}, u32[]{:S(2)}) copy-start(s32[2,128]{1,0:T(2,128)} %refs_7_.7) | copy-start | bytes 3076
  15.8 76.2 %copy-start.8 = (bf16[2,48,1024]{2,1,0:T(8,128)(2,1)}, bf16[2,48,1024]{2,1,0:T(8,128)(2,1)S(1)}, u32[]{:S(2)}) copy-start(bf16[2,48,1024]{2,1,0:T(8,128)(2,1)S(1)} %get-tuple-element.25.refs_5_.refs_7_) | copy-start | bytes 589828
  15.8 67.5 %copy-start = (bf16[2,512,1024]{2,1,0:T(8,128)(2,1)S(1)}, bf16[2,512,1024]{2,1,0:T(8,128)(2,1)}, u32[]{:S(2)}) copy-start(bf16[2,512,1024]{2,1,0:T(8,128)(2,1)} %refs_0_.3) | copy-start | bytes 6291460
  36.6 55.4 %copy-start.4 = (bf16[16,64,128]{2,1,0:T(8,128)(2,1)}, bf16[16,64,128]{2,1,0:T(8,128)(2,1)S(1)}, u32[]{:S(2)}) copy-start(bf16[16,64,128]{2,1,0:T(8,128)(2,1)S(1)} %all_to_all.10.refs_1_.refs_2_) | copy-start | bytes 786436
  76.4 1.7 %copy-start.3 = (bf16[1536,768]{1,0:T(8,128)(2,1)S(1)}, bf16[1536,768]{1,0:T(8,128)(2,1)}, u32[]{:S(2)}) copy-start(bf16[1536,768]{1,0:T(8,128)(2,1)} %all-gather.2.cloned.1.call-done.refs_0_) | copy-start | bytes 7077892
  78.1 0.9 copy-start.20
  79.0 0.8 copy-start.22
  83.2 19.2 %collective-permute-start.1 = (bf16[2,192,768]{2,1,0:T(8,128)(2,1)S(1)}, bf16[2,192,768]{2,1,0:T(8,128)(2,1)S(1)}, u32[]{:S(2)}, u32[]{:S(2)}) collective-permute-start(bf16[2,192,768]{2,1,0:T(8,128)(2,1)S(1)} %choose.1.refs_0_), channel_id=1, source_target_pairs={{1,0},{0,1},{3,2},{2,3},{5,4},{4,5},{7,6},{6,7},{9,8},{8,9},{11,10... | collective-permute-start | bytes 1769480 | tf_op jit(solution)/shard_map/ppermute | solution.py:329
  83.4 1.6 %copy-start.1 = (bf16[2,512,1024]{2,1,0:T(8,128)(2,1)S(1)}, bf16[2,512,1024]{2,1,0:T(8,128)(2,1)}, u32[]{:S(2)}) copy-start(bf16[2,512,1024]{2,1,0:T(8,128)(2,1)} %refs_2_.6) | copy-start | bytes 6291460
  92.0 12.8 %copy-start.6 = (bf16[2,1024,48]{2,1,0:T(8,128)(2,1)}, bf16[2,1024,48]{2,1,0:T(8,128)(2,1)S(1)}, u32[]{:S(2)}) copy-start(bf16[2,1024,48]{2,1,0:T(8,128)(2,1)S(1)} %get-tuple-element.32.refs_5_.refs_4_) | copy-start | bytes 589828
  92.0 10.5 %copy-start.5 = (bf16[16,64,128]{2,1,0:T(8,128)(2,1)S(1)}, bf16[16,64,128]{2,1,0:T(8,128)(2,1)}, u32[]{:S(2)}) copy-start(bf16[16,64,128]{2,1,0:T(8,128)(2,1)} %copy-done.4) | copy-start | bytes 786436
  92.0 10.5 %copy-start.9 = (bf16[2,48,1024]{2,1,0:T(8,128)(2,1)S(1)}, bf16[2,48,1024]{2,1,0:T(8,128)(2,1)}, u32[]{:S(2)}) copy-start(bf16[2,48,1024]{2,1,0:T(8,128)(2,1)} %copy-done.8) | copy-start | bytes 589828
  92.1 8.2 %collective-permute-start.4 = (bf16[128,256]{1,0:T(8,128)(2,1)S(1)}, bf16[128,256]{1,0:T(8,128)(2,1)S(1)}, u32[]{:S(2)}, u32[]{:S(2)}) collective-permute-start(bf16[128,256]{1,0:T(8,128)(2,1)S(1)} %slice_bitcast_fusion.1), channel_id=1, source_target_pairs={{0,2},{2,4},{4,6},{6,8},{8,10},{10,12},{12,14},{14,16},{16,18},{18... | collective-permute-start | bytes 196616 | tf_op jit(solution)/shard_map/ppermute | solution.py:374
  93.6 6.7 %collective-permute-start.5 = (bf16[128,256]{1,0:T(8,128)(2,1)S(1)}, bf16[128,256]{1,0:T(8,128)(2,1)S(1)}, u32[]{:S(2)}, u32[]{:S(2)}) collective-permute-start(bf16[128,256]{1,0:T(8,128)(2,1)S(1)} %slice_bitcast_fusion), channel_id=1, source_target_pairs={{2,0},{4,2},{6,4},{8,6},{10,8},{12,10},{14,12},{16,14},{18,16},{20... | collective-permute-start | bytes 196616 | tf_op jit(solution)/shard_map/ppermute | solution.py:375
  104.8 0.8 copy-start.10
  107.8 25.1 %all-to-all-start.1 = ((bf16[16,48,128]{2,1,0:T(8,128)(2,1)}), bf16[16,48,128]{2,1,0:T(8,128)(2,1)}, u32[]{:S(2)}, u32[]{:S(2)}) async-start(bf16[16,48,128]{2,1,0:T(8,128)(2,1)} %copy-done.19), calls=%async_computation.1 | async-start | bytes 393216 | tf_op jit(solution)/shard_map/all_to_all | solution.py:401
  114.7 1.6 %copy-start.2 = (bf16[2,512,1024]{2,1,0:T(8,128)(2,1)S(1)}, bf16[2,512,1024]{2,1,0:T(8,128)(2,1)}, u32[]{:S(2)}) copy-start(bf16[2,512,1024]{2,1,0:T(8,128)(2,1)} %refs_2_.6) | copy-start | bytes 6291460
  116.3 1.0 copy-start.13
  117.3 0.9 copy-start.18
  124.6 7.5 %collective-permute-start.6 = (bf16[128,128]{1,0:T(8,128)(2,1)S(1)}, bf16[128,128]{1,0:T(8,128)(2,1)S(1)}, u32[]{:S(2)}, u32[]{:S(2)}) collective-permute-start(bf16[128,128]{1,0:T(8,128)(2,1)S(1)} %slice_bitcast_fusion.3), channel_id=1, source_target_pairs={{0,2},{2,4},{4,6},{6,8},{8,10},{10,12},{12,14},{14,16},{16,18},{18... | collective-permute-start | bytes 98312 | tf_op jit(solution)/shard_map/ppermute | solution.py:413
  126.5 5.6 %collective-permute-start.7 = (bf16[128,128]{1,0:T(8,128)(2,1)S(1)}, bf16[128,128]{1,0:T(8,128)(2,1)S(1)}, u32[]{:S(2)}, u32[]{:S(2)}) collective-permute-start(bf16[128,128]{1,0:T(8,128)(2,1)S(1)} %slice_bitcast_fusion.2), channel_id=1, source_target_pairs={{2,0},{4,2},{6,4},{8,6},{10,8},{12,10},{14,12},{16,14},{18,16},{20... | collective-permute-start | bytes 98312 | tf_op jit(solution)/shard_map/ppermute | solution.py:414
  133.0 1.0 copy-start.7
  134.0 1.1 copy-start.11
  135.1 1.0 copy-start.16
  138.3 2.0 %collective-permute-start.8 = (f32[2,512,128]{2,1,0:T(8,128)S(1)}, f32[2,512,128]{2,1,0:T(8,128)S(1)}, u32[]{:S(2)}, u32[]{:S(2)}) collective-permute-start(f32[2,512,128]{2,1,0:T(8,128)S(1)} %get-tuple-element.43), channel_id=1, source_target_pairs={{0,1},{1,0},{2,3},{3,2},{4,5},{5,4},{6,7},{7,6},{8,9},{9,8},{10,11... | collective-permute-start | bytes 1572872 | tf_op jit(solution)/shard_map/ppermute | solution.py:433
  (4 other events, 3.0 us)
Sparse Core Ops, SparseCore 0:
  10.8 65.5 all-gather.1

commit v5 on v4

--- a/solution.py
+++ b/solution.py
@@ -11,7 +11,7 @@
 GROUP = ("crow", "ccol")
 F32 = jnp.float32
 BF16 = jnp.bfloat16
-VMEM_BYTES = 40 * 1024 * 1024
+VMEM_BYTES = 48 * 1024 * 1024
 DIGIT_ROWS = 16
 DIGIT = 256
 
@@ -41,6 +41,10 @@
         self.width = self.cases // self.group
         self.lanes = max(self.cases, -(-self.subs * self.width // 128) * 128)
         self.columns = self.n * self.modes
+        self.near = 1
+        while self.near * self.near < self.n and self.n % (2 * self.near) == 0:
+            self.near *= 2
+        self.far = self.n // self.near
 
 
 def lane_mask(z, block, shape):
@@ -192,13 +196,51 @@
     return lax.broadcasted_iota(jnp.int32, shape, 1) == row
 
 
-def choose_kernel(z, block, arrived, repeat, own_row, chosen, rows):
+def coarse_rows(z, ordered_inverse, arrived, message):
+    flat = arrived[:, : z.modes, :].reshape(z.columns, z.lanes)
+    rows = fold(z, select(z, [dot(ordered_inverse[s], flat) for s in range(z.subs)]))
+    for k in range(z.far):
+        place = lax.rem(lax.axis_index("sub") // z.near + k, z.far)
+        start = k * z.owned
+        packed = select(
+            z, [rows[start + s * z.modes : start + (s + 1) * z.modes, :] for s in range(z.subs)]
+        ).astype(BF16)
+        for a in range(z.near):
+            message[a, place] = packed
+
+
+def order_kernel(z, *refs):
+    blocks = refs[: z.group]
+    arrived, repeat, own_row, ordered_inverse, index, message = refs[z.group :]
     digits = arrived[:, z.modes :, :].astype(F32)
-    high = [jnp.sum(jnp.where(digit_row(digits.shape, 2 * s), digits, 0.0), axis=1) for s in range(z.subs)]
-    low = [jnp.sum(jnp.where(digit_row(digits.shape, 2 * s + 1), digits, 0.0), axis=1) for s in range(z.subs)]
+    for s in range(z.subs):
+        high = jnp.sum(jnp.where(digit_row(digits.shape, 2 * s), digits, 0.0), axis=1)
+        low = jnp.sum(jnp.where(digit_row(digits.shape, 2 * s + 1), digits, 0.0), axis=1)
+        index[s] = high * DIGIT + low
+        spread = dot(high.astype(BF16), repeat[...]) * DIGIT + dot(low.astype(BF16), repeat[...])
+        places = jnp.sum(spread * own_row[...], axis=0, keepdims=True).astype(jnp.int32)
+        for at in range(0, z.columns, 768):
+            wide = min(768, z.columns - at)
+            total = jnp.zeros((z.far * z.owned, wide), F32)
+            for k, block in enumerate(blocks):
+                inside = places[:, at : at + wide] - piece_start(z, k, z.block)
+                for first in range(0, z.block, 768):
+                    deep = min(768, z.block - first)
+                    row = lax.broadcasted_iota(jnp.int32, (deep, wide), 0) + first
+                    hot = jnp.where(row == inside, 1.0, 0.0).astype(BF16)
+                    rows = block[:, :, first : first + deep].reshape(z.far * z.owned, deep)
+                    total = total + dot(rows, hot)
+            ordered_inverse[s, :, at : at + wide] = total.astype(BF16)
+    coarse_rows(z, ordered_inverse, arrived, message)
+
+
+def coarse_kernel(z, arrived, ordered_inverse, message):
+    coarse_rows(z, ordered_inverse, arrived, message)
+
+
+def pick_kernel(z, index, place, picks):
     here = lax.axis_index("sub")
     device = lax.broadcasted_iota(jnp.int32, (z.n, z.lanes), 0)
-    row_of = lax.broadcasted_iota(jnp.int32, (z.modes, z.total), 1)
     for t in range(z.subs + 2):
         if t == 0:
             s, owner = z.subs - 1, lax.rem(here + z.n - 1, z.n)
@@ -206,45 +248,26 @@
             s, owner = 0, lax.rem(here + 1, z.n)
         else:
             s, owner = t - 1, here
-        places = high[s] * DIGIT + low[s]
-        row = jnp.sum(jnp.where(device == owner, places, 0.0), axis=0, keepdims=True)
-        column = jnp.transpose(jnp.broadcast_to(row, (z.lanes, z.lanes)))[: z.modes, 0:1].astype(jnp.int32)
-        hot = jnp.where(row_of == column, 1.0, 0.0).astype(BF16)
-        rows[t * z.modes : (t + 1) * z.modes, :] = dot(hot, block[...]).astype(BF16)
-    first = lax.axis_index(GROUP) * z.block
-    for s in range(z.subs):
-        spread = dot(high[s].astype(BF16), repeat[...]) * DIGIT + dot(low[s].astype(BF16), repeat[...])
-        places = jnp.sum(spread * own_row[...], axis=0, keepdims=True).astype(jnp.int32) - first
-        for at in range(0, z.columns, 768):
-            wide = min(768, z.columns - at)
-            total = jnp.zeros((rows.shape[0], wide), F32)
-            for start in range(0, z.block, 256):
-                deep = min(256, z.block - start)
-                row = lax.broadcasted_iota(jnp.int32, (deep, wide), 0) + start
-                hot = jnp.where(row == places[:, at : at + wide], 1.0, 0.0).astype(BF16)
-                total = total + dot(rows[:, start : start + deep], hot)
-            chosen[s, :, at : at + wide] = total.astype(BF16)
-
-
-def coarse_rows(z, chosen, arrived):
-    flat = arrived[:, : z.modes, :].reshape(z.columns, z.lanes)
-    return fold(z, select(z, [dot(chosen[s], flat) for s in range(z.subs)])).astype(BF16)
-
-
-def update_kernel(z, *refs):
-    pieces = refs[: z.group]
-    arrived, solved, residual, basis, joined, basis_t, first_pass, rounded, message, chosen = refs[z.group :]
-    for s in range(z.subs):
-        total = pieces[0][s].astype(F32)
-        for piece in pieces[1:]:
-            total = total + piece[s].astype(F32)
-        chosen[s] = total.astype(BF16)
-    coarse = coarse_rows(z, chosen, arrived)
+        row = jnp.sum(jnp.where(device == owner, index[s], 0.0), axis=0, keepdims=True)
+        column = jnp.transpose(jnp.broadcast_to(row, (z.lanes, z.lanes)))[: z.modes, 0:1]
+        column = column.astype(jnp.int32)
+        for h in range(z.subs):
+            hit = column == place[h : h + 1, :]
+            picks[h, t * z.modes : (t + 1) * z.modes, :] = jnp.where(hit, 1.0, 0.0).astype(BF16)
+
+
+def picked_rows(z, arrived, picks):
+    flat = jnp.concatenate([arrived[a, b] for b in range(z.far) for a in range(z.near)], axis=0)
+    return fold(z, select(z, [dot(picks[h], flat) for h in range(z.subs)])).astype(BF16)
+
+
+def update_kernel(z, arrived, picks, solved, residual, basis, joined, basis_t, first_pass, rounded, message):
+    chosen = picked_rows(z, arrived, picks)
     m = z.modes
     first_pass[...] = solved[...] + select(
-        z, [dot(basis[s], coarse[(s + 1) * m : (s + 2) * m]) for s in range(z.subs)]
-    )
-    left = residual[...] - select(z, [dot(joined[s], coarse[s * m : (s + 3) * m]) for s in range(z.subs)])
+        z, [dot(basis[s], chosen[(s + 1) * m : (s + 2) * m]) for s in range(z.subs)]
+    )
+    left = residual[...] - select(z, [dot(joined[s], chosen[s * m : (s + 3) * m]) for s in range(z.subs)])
     left = left.astype(BF16)
     rounded[...] = left
     modes = select(z, [dot(basis_t[s], left) for s in range(z.subs)]).astype(BF16)
@@ -252,13 +275,13 @@
         message[k] = modes
 
 
-def last_kernel(z, arrived, chosen, solved, residual, basis, joined, *outs):
-    coarse = coarse_rows(z, chosen, arrived)
+def last_kernel(z, arrived, picks, solved, residual, basis, joined, *outs):
+    chosen = picked_rows(z, arrived, picks)
     m = z.modes
     second = solved[...] + select(
-        z, [dot(basis[s], coarse[(s + 1) * m : (s + 2) * m]) for s in range(z.subs)]
-    )
-    left = residual[...] - select(z, [dot(joined[s], coarse[s * m : (s + 3) * m]) for s in range(z.subs)])
+        z, [dot(basis[s], chosen[(s + 1) * m : (s + 2) * m]) for s in range(z.subs)]
+    )
+    left = residual[...] - select(z, [dot(joined[s], chosen[s * m : (s + 3) * m]) for s in range(z.subs)])
     *outs, whole = outs
     whole[0] = second
     whole[1] = left
@@ -279,12 +302,12 @@
             out[s] = total[:, : z.cases]
 
 
-def call(kernel, outs, operands, flops, scratch=(), late=(), name=None):
+def call(kernel, outs, operands, flops, scratch=(), late=(), after=(), loose=(), name=None):
     moved = sum(int(np.prod(x.shape)) * x.dtype.itemsize for x in (*operands, *outs))
     n_in, n_out = len(operands), len(outs)
 
     def whole(*refs):
-        hbm, refs = refs[: n_in + n_out], refs[n_in + n_out :]
+        hbm, refs = (*refs[:n_in], *refs[n_in + len(after) :][:n_out]), refs[n_in + len(after) + n_out :]
         vmem, refs = refs[: n_in + n_out], refs[n_in + n_out :]
         in_sems, out_sems, *rest = refs
         arriving = [pltpu.make_async_copy(hbm[i], vmem[i], in_sems.at[i]) for i in range(n_in)]
@@ -301,12 +324,16 @@
         for copy in leaving:
             copy.wait()
 
-    anywhere = pl.BlockSpec(memory_space=pl.ANY)
+    hbm_spec = pl.BlockSpec(memory_space=pltpu.HBM)
+    any_spec = pl.BlockSpec(memory_space=pl.ANY)
+    placed = [
+        x if i in loose else pltpu.with_memory_space_constraint(x, pltpu.HBM) for i, x in enumerate(operands)
+    ]
     return pl.pallas_call(
         whole,
-        out_shape=[jax.ShapeDtypeStruct(o.shape, o.dtype) for o in outs],
-        in_specs=[anywhere] * n_in,
-        out_specs=[anywhere] * n_out,
+        out_shape=[pltpu.HBM(o.shape, o.dtype) for o in outs],
+        in_specs=[*[any_spec if i in loose else hbm_spec for i in range(n_in)], *[any_spec] * len(after)],
+        out_specs=[hbm_spec] * n_out,
         scratch_shapes=[
             *[pltpu.VMEM(x.shape, x.dtype) for x in (*operands, *outs)],
             pltpu.SemaphoreType.DMA((n_in,)),
@@ -316,7 +343,7 @@
         compiler_params=pltpu.CompilerParams(vmem_limit_bytes=VMEM_BYTES),
         cost_estimate=pl.CostEstimate(flops=flops, bytes_accessed=moved, transcendentals=0),
         name=name,
-    )(*operands)
+    )(*placed, *after)
 
 
 def shape(dims, dtype):
@@ -334,7 +361,6 @@
     z = Sizes(loads, stiffness, coarse_basis, coarse_inverse, left_rows)
     n, group, subs, rows, lanes, modes = z.n, z.group, z.subs, z.rows, z.lanes, z.modes
     own_t = jnp.swapaxes(coarse_basis, 1, 2)
-    gathered = lax.all_gather(coarse_inverse, "sub", axis=0, tiled=True)
     basis_pieces = pieces_of(own_t, group)
     high, low = coarse_index // DIGIT, coarse_index % DIGIT
     digits = jnp.stack([high, low], axis=1).reshape(2 * subs, modes).astype(BF16)
@@ -342,16 +368,27 @@
     column = np.arange(z.columns)
     repeat = jnp.asarray(np.arange(lanes)[:, None] == column[None, :] % modes, BF16)
     own_row = jnp.asarray(np.arange(n)[:, None] == column[None, :] // modes, F32)
+    place = jnp.asarray(
+        (column // modes * z.owned + column % modes)[None, :] + np.arange(subs)[:, None] * modes, jnp.int32
+    )
     packed_f = shape((rows, lanes), F32)
     packed_b = shape((rows, lanes), BF16)
     copies = shape((n, modes, lanes), BF16)
+    few = shape((z.near, z.far, modes, lanes), BF16)
     spread = functools.partial(lax.all_to_all, axis_name="sub", split_axis=0, concat_axis=0)
+    groups = [[a + z.near * b for a in range(z.near)] for b in range(z.far)]
+    spread_near = functools.partial(spread, axis_index_groups=groups)
+    shared = [coarse_inverse]
+    for k in range(1, z.far):
+        shared.append(lax.ppermute(coarse_inverse, "sub", [((i + k * z.near) % n, i) for i in range(n)]))
+    shared = jnp.stack(shared)
 
     load_rows, basis_t, message = call(
         functools.partial(open_kernel, z),
         [packed_b, shape((subs, modes, rows), BF16), shape((n, modes + DIGIT_ROWS, lanes), BF16)],
         [*basis_pieces, loads, digits],
         4 * rows * lanes * lanes,
+        loose=range(1, group),
         name="open",
     )
     restricted = spread(message)
@@ -367,6 +404,7 @@
         work,
         [pltpu.VMEM((rows, lanes), BF16)],
         range(group, 2 * group),
+        loose=[*range(1, group), *range(group + 1, 2 * group)],
         name="first_image",
     )
     forward = [(i, (i + 1) % n) for i in range(n)]
@@ -378,23 +416,31 @@
         [packed_f, shape((subs, rows, 3 * modes), BF16)],
         [load_rows, image, to_before, to_after, from_before, from_after, left_rows, right_rows, image_basis],
         work // 8,
+        loose=[4, 5],
         name="first_join",
     )
 
-    near = (subs + 2) * modes
-    columns = shape((subs, near, z.columns), BF16)
-    (chosen,) = call(
-        functools.partial(choose_kernel, z),
-        [columns],
-        [gathered, restricted, repeat, own_row],
-        2 * near * z.total * z.total,
-        [pltpu.VMEM((near, z.block), BF16)],
-        name="choose",
-    )
-    first_pass, rounded, message, chosen = call(
+    ordered_inverse, index, message = call(
+        functools.partial(order_kernel, z),
+        [shape((subs, z.far * z.owned, z.columns), BF16), shape((subs, n, lanes), F32), few],
+        [*pieces_of(shared, group), restricted, repeat, own_row],
+        2 * z.far * z.owned * z.total * z.total,
+        after=[to_before],
+        loose=range(1, group),
+        name="order",
+    )
+    coarse = spread_near(message)
+    (picks,) = call(
+        functools.partial(pick_kernel, z),
+        [shape((subs, (subs + 2) * modes, z.columns), BF16)],
+        [index, place],
+        work // 64,
+        name="picks",
+    )
+    first_pass, rounded, message = call(
         functools.partial(update_kernel, z),
-        [packed_f, packed_b, copies, columns],
-        [*pieces_of(chosen, group), restricted, solved, residual, basis, joined, basis_t],
+        [packed_f, packed_b, copies],
+        [coarse, picks, solved, residual, basis, joined, basis_t],
         work // 8,
         name="update",
     )
@@ -408,6 +454,7 @@
         work,
         [pltpu.VMEM((rows, lanes), BF16)],
         range(group, 2 * group),
+        loose=[*range(1, group), *range(group + 1, 2 * group)],
         name="second_image",
     )
     from_before = lax.ppermute(to_after[subs - 1], "sub", forward)
@@ -417,13 +464,23 @@
         [packed_f],
         [load_rows, image, to_before, to_after, from_before, from_after, left_rows, right_rows],
         work // 8,
+        loose=[4, 5],
         name="second_join",
     )
+    (message,) = call(
+        functools.partial(coarse_kernel, z),
+        [few],
+        [restricted, ordered_inverse],
+        work // 64,
+        after=[to_before],
+        name="coarse",
+    )
+    coarse = spread_near(message)
     parts = shape((2, z.own, lanes), F32)
     parts = call(
         functools.partial(last_kernel, z),
         [parts] * group,
-        [restricted, chosen, solved, residual, basis, joined],
+        [coarse, picks, solved, residual, basis, joined],
         work // 8,
         [pltpu.VMEM((2, rows, lanes), F32)],
         name="last",
@@ -433,7 +490,7 @@
         swapped.append(lax.ppermute(parts[k], GROUP, [(g, (g + k) % group) for g in range(group)]))
     swapped = [swapped[(group - k) % group] for k in range(group)]
     out = shape((subs, z.own, z.cases), F32)
-    return tuple(call(functools.partial(unpack_kernel, z), [out, out], swapped, work // 64, name="unpack"))
+    return tuple(call(functools.partial(unpack_kernel, z), [out, out], swapped, work // 64, loose=range(1, group), name="unpack"))
 
 
 def solution(mesh):

time: 149 us -> 117 us (0.79)
  waiting for transfers between devices: 49.8 us -> 27.8 us
  blocking collectives: 20.7 us -> 0 us
  Pallas kernels: 26.2 us -> 44.4 us
  starting transfers between devices: 19.3 us -> 34.8 us
  between operations: 14.4 us -> 1.04 us
  local copies, waits for them, and re-layouts: 17.5 us -> 6.14 us
    all_gather x1 -> x0, waiting for transfers between devices: 39.8 us -> none  [body(): gathered = lax.all_gather(coarse_inverse, 'sub', axis=0, tiled=True)]
    all_to_all x1 -> x0, blocking collectives: 20.7 us -> none  [body(): restricted = spread(message)]
    pallas_call x9 -> x11, Pallas kernels: 26.2 us -> 44.4 us  [call(): pl.pallas_call(whole, out_shape=[pltpu.HBM(o.shape, o.dtype) for o in out...]
    unnamed x50 -> x16, local copies, waits for them, and re-layouts: 17.4 us -> 3.79 us
    ppermute x0 -> x3, waiting for transfers between devices: none -> 11.3 us  [body(): lax.ppermute(coarse_inverse, 'sub', [((i + k * z.near) % n, i) for i in r...]
    ppermute x2, waiting for transfers between devices: 4.37 us -> 11.9 us  [body(): from_before = lax.ppermute(to_after[subs - 1], 'sub', forward)]
    all_to_all x0 -> x2, starting transfers between devices: none -> 7.19 us  [body(): coarse = spread_near(message)]
    ppermute x0 -> x3, starting transfers between devices: none -> 6.04 us  [body(): lax.ppermute(coarse_inverse, 'sub', [((i + k * z.near) % n, i) for i in r...]
  transfers between devices with their start and end apart: 11 -> 16, of which waited for: 5 -> 9; matrix products, arithmetic and copies ran while one was open for 0% -> 3% of each run, Pallas kernels for 14% -> 23%
where the time goes in v5:
time: 117 us; the launch traced here: 116 us
  Pallas kernels  44.4 us (38%)
  starting transfers between devices  34.8 us (30%)
  waiting for transfers between devices  27.8 us (24%)
  local copies, waits for them, and re-layouts  6.14 us (5%)
  other arithmetic  1.68 us (1%)
    pallas_call x11, Pallas kernels, call(): pl.pallas_call(whole, out_shape=[pltpu.HBM(o.shape, o.dtype) for o in out...  44.4 us
    ppermute x2, waiting for transfers between devices, body(): from_before = lax.ppermute(to_after[subs - 1], 'sub', forward)  11.9 us
    ppermute x3, waiting for transfers between devices, body(): lax.ppermute(coarse_inverse, 'sub', [((i + k * z.near) % n, i) for i in r...  11.3 us
    ppermute x2, starting transfers between devices, body(): from_after = lax.ppermute(to_before[0], 'sub', backward)  11.2 us
    all_to_all x2, starting transfers between devices, body(): restricted = spread(message)  9.63 us
    all_to_all x2, starting transfers between devices, body(): coarse = spread_near(message)  7.19 us
    ppermute x3, starting transfers between devices, body(): lax.ppermute(coarse_inverse, 'sub', [((i + k * z.near) % n, i) for i in r...  6.04 us
    unnamed x16, local copies, waits for them, and re-layouts  3.79 us
  transfers between devices with their start and end apart: 16, of which 9 were waited for; matrix products, arithmetic and copies ran while one was open for 3% of the time, Pallas kernels for 23%

profile of v5, /device:TPU:0, one launch (start us, length us, event | category | flops | bytes accessed | tf_op | source)
XLA Modules:
  0.0 115.8 jit_solution(3354261014268348)
XLA Ops:
  1.2 5.0 %collective-permute-start = (bf16[96,768]{1,0:T(8,128)(2,1)}, bf16[96,768]{1,0:T(8,128)(2,1)S(1)}, u32[]{:S(2)}, u32[]{:S(2)}) collective-permute-start(bf16[96,768]{1,0:T(8,128)(2,1)} %param.15), channel_id=1, source_target_pairs={{8,0},{10,2},{12,4},{14,6},{16,8},{18,10},{20,12},{22,14},{24,16},... | collective-permute-start | bytes 442376 | tf_op jit(solution)/shard_map/ppermute | solution.py:383
  6.3 1.0 collective-permute-start.1
  8.0 2.9 %collective-permute-done = bf16[96,768]{1,0:T(8,128)(2,1)S(1)} collective-permute-done((bf16[96,768]{1,0:T(8,128)(2,1)}, bf16[96,768]{1,0:T(8,128)(2,1)S(1)}, u32[]{:S(2)}, u32[]{:S(2)}) %collective-permute-start) | collective-permute-done | bytes 147488 | tf_op jit(solution)/shard_map/ppermute | solution.py:383
  10.8 4.2 %collective-permute-done.2 = bf16[96,768]{1,0:T(8,128)(2,1)S(1)} collective-permute-done((bf16[96,768]{1,0:T(8,128)(2,1)}, bf16[96,768]{1,0:T(8,128)(2,1)S(1)}, u32[]{:S(2)}, u32[]{:S(2)}) %collective-permute-start.2) | collective-permute-done | bytes 147488 | tf_op jit(solution)/shard_map/ppermute | solution.py:383
  15.1 4.2 %collective-permute-done.1 = bf16[96,768]{1,0:T(8,128)(2,1)S(1)} collective-permute-done((bf16[96,768]{1,0:T(8,128)(2,1)}, bf16[96,768]{1,0:T(8,128)(2,1)S(1)}, u32[]{:S(2)}, u32[]{:S(2)}) %collective-permute-start.1) | collective-permute-done | bytes 147488 | tf_op jit(solution)/shard_map/ppermute | solution.py:383
  19.2 1.0 pad_maximum_fusion.refs_0_
  21.0 2.5 %open.1 = (bf16[1024,128]{1,0:T(8,128)(2,1)}, bf16[2,48,1024]{2,1,0:T(8,128)(2,1)}, bf16[16,64,128]{2,1,0:T(8,128)(2,1)}) custom-call(bf16[2,48,512]{2,1,0:T(8,128)(2,1)} %bitcast.23, bf16[2,48,512]{2,1,0:T(8,128)(2,1)S(1)} %collective-permute-done.4.refs_1_, bf16[2,1024,128]{2,1,0:T(8,128)(2,1)} %refs_2_.3, bf16[16,128]{1,0:T(8,128)(2,1)} %pad.4.refs_3_), custom_call_target="tpu_custom_call" | custom-call | flops 67108864 | bytes 1445888 | tf_op jit(solution)/shard_map/open/pallas_call | solution.py:332
  23.5 5.9 %all-to-all-start = ((bf16[16,64,128]{2,1,0:T(8,128)(2,1)}), bf16[16,64,128]{2,1,0:T(8,128)(2,1)}, u32[]{:S(2)}, u32[]{:S(2)}) async-start(bf16[16,64,128]{2,1,0:T(8,128)(2,1)} %get-tuple-element.25), calls=%async_computation | async-start | bytes 524288 | tf_op jit(solution)/shard_map/all_to_all | solution.py:394
  29.5 8.7 %first_image.1 = (f32[1024,128]{1,0:T(8,128)}, f32[1024,128]{1,0:T(8,128)}, bf16[2,128,256]{2,1,0:T(8,128)(2,1)}, bf16[2,128,256]{2,1,0:T(8,128)(2,1)}, bf16[2,1...) custom-call(bf16[2,512,1024]{2,1,0:T(8,128)(2,1)} %refs_0_.3, bf16[2,512,1024]{2,1,0:T(8,128)(2,1)} %collective-permute-done.5.refs_1_, ...), custom_call_target="tpu_custom_call" | custom-call | flops 1073741824 | bytes 10553344 | tf_op jit(solution)/shard_map/first_image/pallas_call | solution.py:332
  38.2 0.9 slice_bitcast_fusion
  39.1 0.9 all-to-all-done.refs_2_
  40.0 0.9 copy-done.1
  40.9 4.8 %order.1 = (bf16[2,384,768]{2,1,0:T(8,128)(2,1)}, f32[2,16,128]{2,1,0:T(8,128)}, bf16[4,4,48,128]{3,2,1,0:T(8,128)(2,1)}) custom-call(bf16[4,96,768]{2,1,0:T(8,128)(2,1)} %copy-done.5, bf16[4,96,768]{2,1,0:T(8,128)(2,1)S(1)} %collective-permute-done.3.refs_1_, bf16[16,64,128]{2,1,0:T(8,128)(2,1)} %all-to-all-done.refs_2_, ...), custom_call_target="tpu_custom_call" | custom-call | flops 1811939328 | bytes 3080192 | tf_op jit(solution)/shard_map/order/pallas_call | solution.py:332
  45.7 3.4 %all-to-all-start.1 = ((bf16[4,4,48,128]{3,2,1,0:T(8,128)(2,1)}), bf16[4,4,48,128]{3,2,1,0:T(8,128)(2,1)S(1)}, u32[]{:S(2)}, u32[]{:S(2)}) async-start(bf16[4,4,48,128]{3,2,1,0:T(8,128)(2,1)} %get-tuple-element.29), calls=%async_computation.1 | async-start | bytes 393216 | tf_op jit(solution)/shard_map/all_to_all | solution.py:432
  49.1 5.5 %collective-permute-start.8 = (bf16[128,256]{1,0:T(8,128)(2,1)S(1)}, bf16[128,256]{1,0:T(8,128)(2,1)S(1)}, u32[]{:S(2)}, u32[]{:S(2)}) collective-permute-start(bf16[128,256]{1,0:T(8,128)(2,1)S(1)} %slice_bitcast_fusion), channel_id=1, source_target_pairs={{2,0},{4,2},{6,4},{8,6},{10,8},{12,10},{14,12},{16,14},{18,16},{20... | collective-permute-start | bytes 196616 | tf_op jit(solution)/shard_map/ppermute | solution.py:413
  54.5 1.8 %picks.1.refs_1_ = bf16[2,192,768]{2,1,0:T(8,128)(2,1)} custom-call(f32[2,16,128]{2,1,0:T(8,128)} %get-tuple-element.30.refs_0_, s32[2,768]{1,0:T(2,128)} %constant.39.clone.refs_1_), custom_call_target="tpu_custom_call" | custom-call | flops 16777216 | bytes 612352 | tf_op jit(solution)/shard_map/picks/pallas_call | solution.py:332
  56.4 6.0 %collective-permute-done.7.refs_4_ = bf16[128,256]{1,0:T(8,128)(2,1)S(1)} collective-permute-done((bf16[128,256]{1,0:T(8,128)(2,1)S(1)}, bf16[128,256]{1,0:T(8,128)(2,1)S(1)}, u32[]{:S(2)}, u32[]{:S(2)}) %collective-permute-start.7) | collective-permute-done | bytes 65568 | tf_op jit(solution)/shard_map/ppermute | solution.py:412
  62.4 3.9 %first_join.1 = (f32[1024,128]{1,0:T(8,128)}, bf16[2,1024,144]{2,1,0:T(8,128)(2,1)}) custom-call(bf16[1024,128]{1,0:T(8,128)(2,1)} %get-tuple-element.26.refs_4_.refs_0_, f32[1024,128]{1,0:T(8,128)} %get-tuple-element.32.refs_1_, bf16[2,128,256]{2,1,0:T(8,128)(2,1)} %get-tuple-element.28.refs_5_.refs_2_, bf16[2,128,256]{2,1,0:T(8,128)(2,1)} %get-tuple-element.33.refs_3_, ...), custom_call_target="tpu_custom_call" | custom-call | flops 134217728 | bytes 2492416 | tf_op jit(solution)/shard_map/first_join/pallas_call | solution.py:332
  67.0 3.8 %update.1 = (f32[1024,128]{1,0:T(8,128)}, bf16[1024,128]{1,0:T(8,128)(2,1)}, bf16[16,48,128]{2,1,0:T(8,128)(2,1)}) custom-call(bf16[4,4,48,128]{3,2,1,0:T(8,128)(2,1)} %copy-done.2, bf16[2,192,768]{2,1,0:T(8,128)(2,1)} %picks.1.refs_1_, f32[1024,128]{1,0:T(8,128)} %get-tuple-element.31.refs_2_, f32[1024,128]{1,0:T(8,128)} %get-tuple-element.35.refs_3_, ...), custom_call_target="tpu_custom_call" | custom-call | flops 134217728 | bytes 3801088 | tf_op jit(solution)/shard_map/update/pallas_call | solution.py:332
  70.8 3.7 %all-to-all-start.2 = ((bf16[16,48,128]{2,1,0:T(8,128)(2,1)}), bf16[16,48,128]{2,1,0:T(8,128)(2,1)S(1)}, u32[]{:S(2)}, u32[]{:S(2)}) async-start(bf16[16,48,128]{2,1,0:T(8,128)(2,1)} %get-tuple-element.38), calls=%async_computation.2 | async-start | bytes 393216 | tf_op jit(solution)/shard_map/all_to_all | solution.py:447
  74.6 7.2 %second_image.1 = (f32[1024,128]{1,0:T(8,128)}, f32[1024,128]{1,0:T(8,128)}, bf16[2,128,128]{2,1,0:T(8,128)(2,1)}, bf16[2,128,128]{2,1,0:T(8,128)(2,1)}) custom-call(bf16[2,512,1024]{2,1,0:T(8,128)(2,1)} %refs_0_.3, bf16[2,512,1024]{2,1,0:T(8,128)(2,1)} %collective-permute-done.5.refs_1_, bf16[2,512,1024]{2,1,0:T(8,128)(2,1)} %refs_2_.5, ...), custom_call_target="tpu_custom_call" | custom-call | flops 1073741824 | bytes 10356736 | tf_op jit(solution)/shard_map/second_image/pallas_call | solution.py:332
  81.8 0.8 slice_bitcast_fusion.2
  83.2 0.8 copy-done
  84.1 2.6 %coarse.1 = bf16[4,4,48,128]{3,2,1,0:T(8,128)(2,1)} custom-call(bf16[16,48,128]{2,1,0:T(8,128)(2,1)} %copy-done.3, bf16[2,384,768]{2,1,0:T(8,128)(2,1)} %get-tuple-element.39.refs_1_, bf16[2,128,128]{2,1,0:T(8,128)(2,1)S(1)} %copy-done), custom_call_target="tpu_custom_call" | custom-call | flops 16777216 | bytes 1572864 | tf_op jit(solution)/shard_map/coarse/pallas_call | solution.py:332
  86.7 3.8 %all-to-all-start.3 = ((bf16[4,4,48,128]{3,2,1,0:T(8,128)(2,1)}), bf16[4,4,48,128]{3,2,1,0:T(8,128)(2,1)S(1)}, u32[]{:S(2)}, u32[]{:S(2)}) async-start(bf16[4,4,48,128]{3,2,1,0:T(8,128)(2,1)} %coarse.1), calls=%async_computation.3 | async-start | bytes 393216 | tf_op jit(solution)/shard_map/all_to_all | solution.py:478
  90.5 5.7 %collective-permute-start.10 = (bf16[128,128]{1,0:T(8,128)(2,1)S(1)}, bf16[128,128]{1,0:T(8,128)(2,1)S(1)}, u32[]{:S(2)}, u32[]{:S(2)}) collective-permute-start(bf16[128,128]{1,0:T(8,128)(2,1)S(1)} %slice_bitcast_fusion.2), channel_id=1, source_target_pairs={{2,0},{4,2},{6,4},{8,6},{10,8},{12,10},{14,12},{16,14},{18,16},{20... | collective-permute-start | bytes 98312 | tf_op jit(solution)/shard_map/ppermute | solution.py:461
  96.2 1.6 %collective-permute-done.10.refs_5_ = bf16[128,128]{1,0:T(8,128)(2,1)S(1)} collective-permute-done((bf16[128,128]{1,0:T(8,128)(2,1)S(1)}, bf16[128,128]{1,0:T(8,128)(2,1)S(1)}, u32[]{:S(2)}, u32[]{:S(2)}) %collective-permute-start.10) | collective-permute-done | bytes 32800 | tf_op jit(solution)/shard_map/ppermute | solution.py:461
  97.8 5.9 %collective-permute-done.9.refs_4_ = bf16[128,128]{1,0:T(8,128)(2,1)S(1)} collective-permute-done((bf16[128,128]{1,0:T(8,128)(2,1)S(1)}, bf16[128,128]{1,0:T(8,128)(2,1)S(1)}, u32[]{:S(2)}, u32[]{:S(2)}) %collective-permute-start.9) | collective-permute-done | bytes 32800 | tf_op jit(solution)/shard_map/ppermute | solution.py:460
  103.7 2.4 %second_join.1.refs_3_ = f32[1024,128]{1,0:T(8,128)} custom-call(bf16[1024,128]{1,0:T(8,128)(2,1)} %get-tuple-element.26.refs_4_.refs_0_, f32[1024,128]{1,0:T(8,128)} %get-tuple-element.44.refs_1_, bf16[2,128,128]{2,1,0:T(8,128)(2,1)} %get-tuple-element.42.refs_2_, bf16[2,128,128]{2,1,0:T(8,128)(2,1)} %get-tuple-element.45.refs_3_, ...), custom_call_target="tpu_custom_call" | custom-call | flops 134217728 | bytes 1509376 | tf_op jit(solution)/shard_map/second_join/pallas_call | solution.py:332
  106.9 4.1 %last.1 = (f32[2,512,128]{2,1,0:T(8,128)}, f32[2,512,128]{2,1,0:T(8,128)}) custom-call(bf16[4,4,48,128]{3,2,1,0:T(8,128)(2,1)} %copy-done.4, bf16[2,192,768]{2,1,0:T(8,128)(2,1)} %picks.1.refs_1_, f32[1024,128]{1,0:T(8,128)} %get-tuple-element.43.refs_2_, f32[1024,128]{1,0:T(8,128)} %second_join.1.refs_3_, bf16[2,1024,48]{2,1,0:T(8,128)(2,1)} %get-tuple-element.36.refs_4_, ...), custom_call_target="tpu_custom_call" | custom-call | flops 134217728 | bytes 3670016 | tf_op jit(solution)/shard_map/last/pallas_call | solution.py:332
  111.1 2.1 %collective-permute-done.11.refs_1_ = f32[2,512,128]{2,1,0:T(8,128)S(1)} collective-permute-done((f32[2,512,128]{2,1,0:T(8,128)}, f32[2,512,128]{2,1,0:T(8,128)S(1)}, u32[]{:S(2)}, u32[]{:S(2)}) %collective-permute-start.11) | collective-permute-done | bytes 524320 | tf_op jit(solution)/shard_map/ppermute | solution.py:490
  113.2 2.5 %unpack.1 = (f32[2,512,128]{2,1,0:T(8,128)}, f32[2,512,128]{2,1,0:T(8,128)}) custom-call(f32[2,512,128]{2,1,0:T(8,128)} %get-tuple-element.46.refs_0_, f32[2,512,128]{2,1,0:T(8,128)S(1)} %collective-permute-done.11.refs_1_), custom_call_target="tpu_custom_call" | custom-call | flops 16777216 | bytes 2097152 | tf_op jit(solution)/shard_map/unpack/pallas_call | solution.py:332
  (36 shorter events, 4.3 us)
Async XLA Ops:
  0.6 28.8 %collective-permute-start.6 = (bf16[2,512,1024]{2,1,0:T(8,128)(2,1)}, bf16[2,512,1024]{2,1,0:T(8,128)(2,1)S(1)}, u32[]{:S(2)}, u32[]{:S(2)}) collective-permute-start(bf16[2,512,1024]{2,1,0:T(8,128)(2,1)} %refs_2_.5), channel_id=1, source_target_pairs={{1,0},{0,1},{3,2},{2,3},{5,4},{4,5},{7,6},{6,7},{9,8},{8,9},{11,10... | collective-permute-start | bytes 6291464 | tf_op jit(solution)/shard_map/ppermute | solution.py:356
  1.1 28.3 %collective-permute-start.5 = (bf16[2,512,1024]{2,1,0:T(8,128)(2,1)}, bf16[2,512,1024]{2,1,0:T(8,128)(2,1)}, u32[]{:S(2)}, u32[]{:S(2)}) collective-permute-start(bf16[2,512,1024]{2,1,0:T(8,128)(2,1)} %refs_0_.3), channel_id=1, source_target_pairs={{1,0},{0,1},{3,2},{2,3},{5,4},{4,5},{7,6},{6,7},{9,8},{8,9},{11,10... | collective-permute-start | bytes 6291464 | tf_op jit(solution)/shard_map/ppermute | solution.py:356
  1.2 9.6 %collective-permute-start = (bf16[96,768]{1,0:T(8,128)(2,1)}, bf16[96,768]{1,0:T(8,128)(2,1)S(1)}, u32[]{:S(2)}, u32[]{:S(2)}) collective-permute-start(bf16[96,768]{1,0:T(8,128)(2,1)} %param.15), channel_id=1, source_target_pairs={{8,0},{10,2},{12,4},{14,6},{16,8},{18,10},{20,12},{22,14},{24,16},... | collective-permute-start | bytes 442376 | tf_op jit(solution)/shard_map/ppermute | solution.py:383
  6.3 8.8 %collective-permute-start.2 = (bf16[96,768]{1,0:T(8,128)(2,1)}, bf16[96,768]{1,0:T(8,128)(2,1)S(1)}, u32[]{:S(2)}, u32[]{:S(2)}) collective-permute-start(bf16[96,768]{1,0:T(8,128)(2,1)} %param.15), channel_id=1, source_target_pairs={{24,0},{26,2},{28,4},{30,6},{0,8},{2,10},{4,12},{6,14},{8,16},{10,... | collective-permute-start | bytes 442376 | tf_op jit(solution)/shard_map/ppermute | solution.py:383
  6.3 13.0 %collective-permute-start.1 = (bf16[96,768]{1,0:T(8,128)(2,1)}, bf16[96,768]{1,0:T(8,128)(2,1)S(1)}, u32[]{:S(2)}, u32[]{:S(2)}) collective-permute-start(bf16[96,768]{1,0:T(8,128)(2,1)} %param.15), channel_id=1, source_target_pairs={{16,0},{18,2},{20,4},{22,6},{24,8},{26,10},{28,12},{30,14},{0,16},... | collective-permute-start | bytes 442376 | tf_op jit(solution)/shard_map/ppermute | solution.py:383
  10.8 10.2 %collective-permute-start.4 = (bf16[2,48,512]{2,1,0:T(8,128)(2,1)}, bf16[2,48,512]{2,1,0:T(8,128)(2,1)S(1)}, u32[]{:S(2)}, u32[]{:S(2)}) collective-permute-start(bf16[2,48,512]{2,1,0:T(8,128)(2,1)} %bitcast.22), channel_id=1, source_target_pairs={{1,0},{0,1},{3,2},{2,3},{5,4},{4,5},{7,6},{6,7},{9,8},{8,9},{11,10... | collective-permute-start | bytes 294920 | tf_op jit(solution)/shard_map/ppermute | solution.py:356
  20.2 18.0 %copy-start.5 = (bf16[4,96,768]{2,1,0:T(8,128)(2,1)}, bf16[4,96,768]{2,1,0:T(8,128)(2,1)S(1)}, u32[]{:S(2)}) copy-start(bf16[4,96,768]{2,1,0:T(8,128)(2,1)S(1)} %pad_maximum_fusion.refs_0_) | copy-start | bytes 1769476
  20.2 19.7 %collective-permute-start.3 = (bf16[4,96,768]{2,1,0:T(8,128)(2,1)S(1)}, bf16[4,96,768]{2,1,0:T(8,128)(2,1)S(1)}, u32[]{:S(2)}, u32[]{:S(2)}) collective-permute-start(bf16[4,96,768]{2,1,0:T(8,128)(2,1)S(1)} %pad_maximum_fusion.refs_0_), channel_id=1, source_target_pairs={{1,0},{0,1},{3,2},{2,3},{5,4},{4,5},{7,6},{6,7},{9,8},{8,9},{11,10... | collective-permute-start | bytes 1769480 | tf_op jit(solution)/shard_map/ppermute | solution.py:356
  23.5 16.4 %all-to-all-start = ((bf16[16,64,128]{2,1,0:T(8,128)(2,1)}), bf16[16,64,128]{2,1,0:T(8,128)(2,1)}, u32[]{:S(2)}, u32[]{:S(2)}) async-start(bf16[16,64,128]{2,1,0:T(8,128)(2,1)} %get-tuple-element.25), calls=%async_computation | async-start | bytes 524288 | tf_op jit(solution)/shard_map/all_to_all | solution.py:394
  38.2 10.8 %copy-start.6 = (bf16[2,128,256]{2,1,0:T(8,128)(2,1)S(1)}, bf16[2,128,256]{2,1,0:T(8,128)(2,1)}, u32[]{:S(2)}) copy-start(bf16[2,128,256]{2,1,0:T(8,128)(2,1)} %get-tuple-element.33.refs_3_) | copy-start | bytes 393220
  40.0 0.9 copy-start.1
  45.7 20.7 %all-to-all-start.1 = ((bf16[4,4,48,128]{3,2,1,0:T(8,128)(2,1)}), bf16[4,4,48,128]{3,2,1,0:T(8,128)(2,1)S(1)}, u32[]{:S(2)}, u32[]{:S(2)}) async-start(bf16[4,4,48,128]{3,2,1,0:T(8,128)(2,1)} %get-tuple-element.29), calls=%async_computation.1 | async-start | bytes 393216 | tf_op jit(solution)/shard_map/all_to_all | solution.py:432
  49.1 7.4 %collective-permute-start.8 = (bf16[128,256]{1,0:T(8,128)(2,1)S(1)}, bf16[128,256]{1,0:T(8,128)(2,1)S(1)}, u32[]{:S(2)}, u32[]{:S(2)}) collective-permute-start(bf16[128,256]{1,0:T(8,128)(2,1)S(1)} %slice_bitcast_fusion), channel_id=1, source_target_pairs={{2,0},{4,2},{6,4},{8,6},{10,8},{12,10},{14,12},{16,14},{18,16},{20... | collective-permute-start | bytes 196616 | tf_op jit(solution)/shard_map/ppermute | solution.py:413
  54.5 7.9 %collective-permute-start.7 = (bf16[128,256]{1,0:T(8,128)(2,1)S(1)}, bf16[128,256]{1,0:T(8,128)(2,1)S(1)}, u32[]{:S(2)}, u32[]{:S(2)}) collective-permute-start(bf16[128,256]{1,0:T(8,128)(2,1)S(1)} %slice_bitcast_fusion.1), channel_id=1, source_target_pairs={{0,2},{2,4},{4,6},{6,8},{8,10},{10,12},{12,14},{14,16},{16,18},{18... | collective-permute-start | bytes 196616 | tf_op jit(solution)/shard_map/ppermute | solution.py:412
  66.3 0.7 copy-start.2
  70.8 11.7 %all-to-all-start.2 = ((bf16[16,48,128]{2,1,0:T(8,128)(2,1)}), bf16[16,48,128]{2,1,0:T(8,128)(2,1)S(1)}, u32[]{:S(2)}, u32[]{:S(2)}) async-start(bf16[16,48,128]{2,1,0:T(8,128)(2,1)} %get-tuple-element.38), calls=%async_computation.2 | async-start | bytes 393216 | tf_op jit(solution)/shard_map/all_to_all | solution.py:447
  81.7 8.8 %copy-start.7 = (bf16[2,128,128]{2,1,0:T(8,128)(2,1)S(1)}, bf16[2,128,128]{2,1,0:T(8,128)(2,1)}, u32[]{:S(2)}) copy-start(bf16[2,128,128]{2,1,0:T(8,128)(2,1)} %get-tuple-element.45.refs_3_) | copy-start | bytes 196612
  82.6 0.7 copy-start.3
  83.2 0.8 copy-start
  86.7 19.5 %all-to-all-start.3 = ((bf16[4,4,48,128]{3,2,1,0:T(8,128)(2,1)}), bf16[4,4,48,128]{3,2,1,0:T(8,128)(2,1)S(1)}, u32[]{:S(2)}, u32[]{:S(2)}) async-start(bf16[4,4,48,128]{3,2,1,0:T(8,128)(2,1)} %coarse.1), calls=%async_computation.3 | async-start | bytes 393216 | tf_op jit(solution)/shard_map/all_to_all | solution.py:478
  90.5 7.3 %collective-permute-start.10 = (bf16[128,128]{1,0:T(8,128)(2,1)S(1)}, bf16[128,128]{1,0:T(8,128)(2,1)S(1)}, u32[]{:S(2)}, u32[]{:S(2)}) collective-permute-start(bf16[128,128]{1,0:T(8,128)(2,1)S(1)} %slice_bitcast_fusion.2), channel_id=1, source_target_pairs={{2,0},{4,2},{6,4},{8,6},{10,8},{12,10},{14,12},{16,14},{18,16},{20... | collective-permute-start | bytes 98312 | tf_op jit(solution)/shard_map/ppermute | solution.py:461
  96.2 7.5 %collective-permute-start.9 = (bf16[128,128]{1,0:T(8,128)(2,1)S(1)}, bf16[128,128]{1,0:T(8,128)(2,1)S(1)}, u32[]{:S(2)}, u32[]{:S(2)}) collective-permute-start(bf16[128,128]{1,0:T(8,128)(2,1)S(1)} %slice_bitcast_fusion.3), channel_id=1, source_target_pairs={{0,2},{2,4},{4,6},{6,8},{8,10},{10,12},{12,14},{14,16},{16,18},{18... | collective-permute-start | bytes 98312 | tf_op jit(solution)/shard_map/ppermute | solution.py:460
  106.2 0.7 copy-start.4
  111.0 2.2 %collective-permute-start.11 = (f32[2,512,128]{2,1,0:T(8,128)}, f32[2,512,128]{2,1,0:T(8,128)S(1)}, u32[]{:S(2)}, u32[]{:S(2)}) collective-permute-start(f32[2,512,128]{2,1,0:T(8,128)} %get-tuple-element.47), channel_id=1, source_target_pairs={{0,1},{1,0},{2,3},{3,2},{4,5},{5,4},{6,7},{7,6},{8,9},{9,8},{10,11... | collective-permute-start | bytes 1572872 | tf_op jit(solution)/shard_map/ppermute | solution.py:490

commit v6 on v5

--- a/solution.py
+++ b/solution.py
@@ -13,7 +13,8 @@
 BF16 = jnp.bfloat16
 VMEM_BYTES = 48 * 1024 * 1024
 DIGIT_ROWS = 16
-DIGIT = 256
+DIGIT_BITS = 8
+DIGIT = 1 << DIGIT_BITS
 
 
 def dot(a, b):
@@ -79,12 +80,6 @@
     return jnp.where(hit, 1.0, 0.0).astype(BF16)
 
 
-def place_matrix(z, block):
-    row = lax.broadcasted_iota(jnp.int32, (z.modes, 3 * z.modes), 0)
-    lane = lax.broadcasted_iota(jnp.int32, (z.modes, 3 * z.modes), 1)
-    return jnp.where(row + block * z.modes == lane, 1.0, 0.0).astype(BF16)
-
-
 def piece_start(z, k, size):
     place = lax.rem(lax.axis_index(GROUP) + k, z.group)
     return pl.multiple_of(place * size, size)
@@ -97,7 +92,7 @@
 
 def open_kernel(z, *refs):
     pieces = refs[: z.group]
-    loads, digits, load_rows, basis_t, message = refs[z.group :]
+    loads, index, load_rows, basis_t, message, digits = refs[z.group :]
     group = lax.axis_index(GROUP)
     for k, piece in enumerate(pieces):
         basis_t[:, :, pl.ds(piece_start(z, k, z.own), z.own)] = piece[...]
@@ -110,9 +105,20 @@
     packed = packed.astype(BF16)
     load_rows[...] = packed
     modes = select(z, [dot(basis_t[s], packed) for s in range(z.subs)]).astype(BF16)
+    digits[...] = jnp.zeros(digits.shape, F32)
+    for s in range(z.subs):
+        places = index[s : s + 1, :]
+        digits[2 * s : 2 * s + 1, : z.modes] = (places >> DIGIT_BITS).astype(F32)
+        digits[2 * s + 1 : 2 * s + 2, : z.modes] = (places & (DIGIT - 1)).astype(F32)
     for k in range(z.n):
         message[k, : z.modes, :] = modes
-        message[k, z.modes :, :] = digits[...]
+        message[k, z.modes :, :] = digits[...].astype(BF16)
+
+
+def stack_kernel(z, *refs):
+    *blocks, out = refs
+    for k, block in enumerate(blocks):
+        out[k] = block[...]
 
 
 def multiply(z, pieces, vector, store):
@@ -121,30 +127,45 @@
         store(piece_start(z, k, z.own), select(z, parts))
 
 
-def face_picks(z, image, rows_ref, s):
-    return dot_tn(scatter_matrix(z, rows_ref[s : s + 1, :]), image).astype(BF16)
-
-
-def image_kernel(z, first, wait, *refs):
+def face_rows(z, image_b, rows_ref, s, target):
+    picked = dot_tn(scatter_matrix(z, rows_ref[s : s + 1, :]), image_b).astype(BF16)
+    return dot(picked, shift_matrix(z, s, target)).astype(BF16)
+
+
+def sides(z, before, after, outer_before, outer_after, s):
+    return (outer_before if s == 0 else after.at[s - 1]), (outer_after if s == z.subs - 1 else before.at[s + 1])
+
+
+def shares(z, s, chosen, values, bases):
+    m = z.modes
+    out = []
+    for value, base, at in ((values[0], bases[0], s), (values[1], bases[1], s + 2)):
+        total = value[:, : z.lanes].astype(F32)
+        total = total + dot(base[:, z.lanes : z.lanes + m], chosen[at * m : (at + 1) * m])
+        out.append(total.astype(BF16))
+    return out
+
+
+def correction(z, s, chosen, image_basis, both, left_rows, right_rows):
+    total = dot(image_basis[s], chosen[(s + 1) * z.modes : (s + 2) * z.modes])
+    total = total + dot(scatter_matrix(z, left_rows[s : s + 1, :]), both[0])
+    return total + dot(scatter_matrix(z, right_rows[s : s + 1, :]), both[1])
+
+
+def first_image_kernel(z, wait, *refs):
     inverse, stiffness = refs[: z.group], refs[z.group : 2 * z.group]
-    rest = refs[2 * z.group :]
-    if first:
-        vector, basis_t, left_rows, right_rows = rest[:4]
-        solved, image, to_before, to_after, basis, image_basis = rest[4:10]
-        rounded = rest[10]
-    else:
-        vector, base, left_rows, right_rows = rest[:4]
-        solved, image, to_before, to_after = rest[4:8]
-        rounded = rest[8]
-    operand = vector[...]
+    load_rows, basis_t, left_rows, right_rows = refs[2 * z.group : 2 * z.group + 4]
+    outs = refs[2 * z.group + 4 :]
+    solved, image, before, after, first_face, last_face, basis, image_basis, left_t, right_t, inner, start_modes = outs[:12]
+    rounded = outs[12]
 
     def store_solved(start, value):
-        if not first:
-            value = value + base[pl.ds(start, z.own), :]
         solved[pl.ds(start, z.own), :] = value
         rounded[pl.ds(start, z.own), :] = value.astype(BF16)
 
-    multiply(z, inverse, operand, store_solved)
+    multiply(z, inverse, load_rows[...], store_solved)
+    for s in range(z.subs):
+        basis[s] = jnp.transpose(basis_t[s].astype(F32)).astype(BF16)
 
     def store_image(start, value):
         image[pl.ds(start, z.own), :] = value
@@ -152,44 +173,65 @@
     for k in range(z.group):
         wait(z.group + k)
     multiply(z, stiffness, rounded[...], store_image)
-    if first:
-        for s in range(z.subs):
-            basis[s] = jnp.transpose(basis_t[s].astype(F32)).astype(BF16)
-            for k, piece in enumerate(stiffness):
-                start = piece_start(z, k, z.own)
-                image_basis[s, pl.ds(start, z.own), :] = dot(piece[s], basis[s]).astype(BF16)
+    for s in range(z.subs):
+        for k, piece in enumerate(stiffness):
+            image_basis[s, pl.ds(piece_start(z, k, z.own), z.own), :] = dot(piece[s], basis[s]).astype(BF16)
     image_b = image[...].astype(BF16)
-    for s in range(z.subs):
-        for rows_ref, out, target in (
-            (left_rows, to_before, (s - 1) % z.subs),
-            (right_rows, to_after, (s + 1) % z.subs),
+    left = (load_rows[...].astype(F32) - image[...]).astype(BF16)
+    start_modes[...] = select(z, [dot(basis_t[s], left) for s in range(z.subs)])
+    for s in range(z.subs):
+        inner[s] = dot(basis_t[s], image_basis[s]).astype(BF16)
+        for rows_ref, out, side_t, target in (
+            (left_rows, before, left_t, (s - 1) % z.subs),
+            (right_rows, after, right_t, (s + 1) % z.subs),
         ):
-            picked = face_picks(z, image_b, rows_ref, s)
-            out[s, :, : z.lanes] = dot(picked, shift_matrix(z, s, target)).astype(BF16)
-            if first:
-                out[s, :, z.lanes : z.lanes + z.modes] = face_picks(z, image_basis[s], rows_ref, s)
-
-
-def join_kernel(z, first, *refs):
-    load_rows, image, to_before, to_after, from_before, from_after, left_rows, right_rows = refs[:8]
-    if first:
-        image_basis, residual, joined = refs[8:]
-    else:
-        (residual,) = refs[8:]
-    added = []
-    for s in range(z.subs):
-        before = from_before[...] if s == 0 else to_after[s - 1]
-        after = from_after[...] if s == z.subs - 1 else to_before[s + 1]
-        left = scatter_matrix(z, left_rows[s : s + 1, :])
-        right = scatter_matrix(z, right_rows[s : s + 1, :])
-        added.append(dot(left, before[:, : z.lanes]) + dot(right, after[:, : z.lanes]))
-        if first:
-            cut = slice(z.lanes, z.lanes + z.modes)
-            total = dot(left, dot(before[:, cut], place_matrix(z, 0)).astype(BF16))
-            total = total + dot(image_basis[s], place_matrix(z, 1))
-            total = total + dot(right, dot(after[:, cut], place_matrix(z, 2)).astype(BF16))
-            joined[s] = total.astype(BF16)
-    residual[...] = load_rows[...].astype(F32) - image[...] - select(z, added)
+            scatter = scatter_matrix(z, rows_ref[s : s + 1, :])
+            side_t[s] = dot(basis_t[s], scatter).astype(BF16)
+            out[s, :, : z.lanes] = face_rows(z, image_b, rows_ref, s, target)
+            out[s, :, z.lanes : z.lanes + z.modes] = dot_tn(scatter, image_basis[s]).astype(BF16)
+            out[s, :, z.lanes + z.modes :] = jnp.zeros((z.face, z.lanes - z.modes), BF16)
+    first_face[...] = before[0]
+    last_face[...] = after[z.subs - 1]
+
+
+def second_image_kernel(z, wait, *refs):
+    inverse, stiffness = refs[: z.group], refs[z.group : 2 * z.group]
+    rest = refs[2 * z.group :]
+    load_rows, old_image, image_basis, old_solved, basis, chosen = rest[:6]
+    before, after, outer_before, outer_after, left_rows, right_rows = rest[6:12]
+    solved, image, new_before, new_after, first_face, last_face, rounded = rest[12:]
+    parts = []
+    for s in range(z.subs):
+        faces = sides(z, before, after, outer_before, outer_after, s)
+        both = shares(z, s, chosen, faces, faces)
+        parts.append(correction(z, s, chosen, image_basis, both, left_rows, right_rows))
+    residual = (load_rows[...].astype(F32) - old_image[...] - select(z, parts)).astype(BF16)
+    m = z.modes
+    solved[...] = old_solved[...] + select(
+        z, [dot(basis[s], chosen[(s + 1) * m : (s + 2) * m]) for s in range(z.subs)]
+    )
+    for k in range(z.group):
+        wait(k)
+
+    def store_solved(start, value):
+        value = value + solved[pl.ds(start, z.own), :]
+        solved[pl.ds(start, z.own), :] = value
+        rounded[pl.ds(start, z.own), :] = value.astype(BF16)
+
+    multiply(z, inverse, residual, store_solved)
+
+    def store_image(start, value):
+        image[pl.ds(start, z.own), :] = value
+
+    for k in range(z.group):
+        wait(z.group + k)
+    multiply(z, stiffness, rounded[...], store_image)
+    image_b = image[...].astype(BF16)
+    for s in range(z.subs):
+        new_before[s] = face_rows(z, image_b, left_rows, s, (s - 1) % z.subs)
+        new_after[s] = face_rows(z, image_b, right_rows, s, (s + 1) % z.subs)
+    first_face[...] = new_before[0]
+    last_face[...] = new_after[z.subs - 1]
 
 
 def digit_row(shape, row):
@@ -234,11 +276,13 @@
     coarse_rows(z, ordered_inverse, arrived, message)
 
 
-def coarse_kernel(z, arrived, ordered_inverse, message):
+def coarse_kernel(z, arrived, ordered_inverse, last_face, message, face):
     coarse_rows(z, ordered_inverse, arrived, message)
-
-
-def pick_kernel(z, index, place, picks):
+    face[...] = last_face[...]
+
+
+def pick_kernel(z, index, place, last_face, picks, face):
+    face[...] = last_face[...]
     here = lax.axis_index("sub")
     device = lax.broadcasted_iota(jnp.int32, (z.n, z.lanes), 0)
     for t in range(z.subs + 2):
@@ -261,30 +305,40 @@
     return fold(z, select(z, [dot(picks[h], flat) for h in range(z.subs)])).astype(BF16)
 
 
-def update_kernel(z, arrived, picks, solved, residual, basis, joined, basis_t, first_pass, rounded, message):
+def update_kernel(z, *refs):
+    arrived, picks, start_modes, inner, left_t, right_t, before, after, outer_before, outer_after = refs[:10]
+    chosen, message = refs[10:]
+    rows = picked_rows(z, arrived, picks)
+    chosen[...] = rows
+    m = z.modes
+    parts = []
+    for s in range(z.subs):
+        faces = sides(z, before, after, outer_before, outer_after, s)
+        both = shares(z, s, rows, faces, faces)
+        total = dot(inner[s], rows[(s + 1) * m : (s + 2) * m])
+        parts.append(total + dot(left_t[s], both[0]) + dot(right_t[s], both[1]))
+    modes = (start_modes[...] - select(z, parts)).astype(BF16)
+    for k in range(z.n):
+        message[k] = modes
+
+
+def last_kernel(z, *refs):
+    arrived, picks, load_rows, image, image_basis, solved, basis = refs[:7]
+    before, after, outer_before, outer_after = refs[7:11]
+    base_before, base_after, base_outer_before, base_outer_after, left_rows, right_rows = refs[11:17]
+    *outs, whole = refs[17:]
     chosen = picked_rows(z, arrived, picks)
     m = z.modes
-    first_pass[...] = solved[...] + select(
+    parts = []
+    for s in range(z.subs):
+        values = sides(z, before, after, outer_before, outer_after, s)
+        bases = sides(z, base_before, base_after, base_outer_before, base_outer_after, s)
+        both = shares(z, s, chosen, values, bases)
+        parts.append(correction(z, s, chosen, image_basis, both, left_rows, right_rows))
+    whole[0] = solved[...] + select(
         z, [dot(basis[s], chosen[(s + 1) * m : (s + 2) * m]) for s in range(z.subs)]
     )
-    left = residual[...] - select(z, [dot(joined[s], chosen[s * m : (s + 3) * m]) for s in range(z.subs)])
-    left = left.astype(BF16)
-    rounded[...] = left
-    modes = select(z, [dot(basis_t[s], left) for s in range(z.subs)]).astype(BF16)
-    for k in range(z.n):
-        message[k] = modes
-
-
-def last_kernel(z, arrived, picks, solved, residual, basis, joined, *outs):
-    chosen = picked_rows(z, arrived, picks)
-    m = z.modes
-    second = solved[...] + select(
-        z, [dot(basis[s], chosen[(s + 1) * m : (s + 2) * m]) for s in range(z.subs)]
-    )
-    left = residual[...] - select(z, [dot(joined[s], chosen[s * m : (s + 3) * m]) for s in range(z.subs)])
-    *outs, whole = outs
-    whole[0] = second
-    whole[1] = left
+    whole[1] = load_rows[...].astype(F32) - image[...] - select(z, parts)
     for k, out in enumerate(outs):
         out[...] = whole[:, pl.ds(piece_start(z, k, z.own), z.own), :]
 
@@ -359,12 +413,8 @@
 
 def body(loads, stiffness, local_inverse, coarse_basis, coarse_inverse, coarse_index, left_rows, right_rows):
     z = Sizes(loads, stiffness, coarse_basis, coarse_inverse, left_rows)
-    n, group, subs, rows, lanes, modes = z.n, z.group, z.subs, z.rows, z.lanes, z.modes
-    own_t = jnp.swapaxes(coarse_basis, 1, 2)
-    basis_pieces = pieces_of(own_t, group)
-    high, low = coarse_index // DIGIT, coarse_index % DIGIT
-    digits = jnp.stack([high, low], axis=1).reshape(2 * subs, modes).astype(BF16)
-    digits = jnp.pad(digits, ((0, DIGIT_ROWS - 2 * subs), (0, lanes - modes)))
+    n, group, subs, rows, lanes, modes, face = z.n, z.group, z.subs, z.rows, z.lanes, z.modes, z.face
+    basis_pieces = pieces_of(jnp.swapaxes(coarse_basis, 1, 2), group)
     column = np.arange(z.columns)
     repeat = jnp.asarray(np.arange(lanes)[:, None] == column[None, :] % modes, BF16)
     own_row = jnp.asarray(np.arange(n)[:, None] == column[None, :] // modes, F32)
@@ -375,114 +425,125 @@
     packed_b = shape((rows, lanes), BF16)
     copies = shape((n, modes, lanes), BF16)
     few = shape((z.near, z.far, modes, lanes), BF16)
+    tall = shape((subs, rows, modes), BF16)
     spread = functools.partial(lax.all_to_all, axis_name="sub", split_axis=0, concat_axis=0)
     groups = [[a + z.near * b for a in range(z.near)] for b in range(z.far)]
     spread_near = functools.partial(spread, axis_index_groups=groups)
+    forward = [(i, (i + 1) % n) for i in range(n)]
+    backward = [(target, source) for source, target in forward]
+    work = 4 * subs * rows * rows * lanes
+
+    load_rows, basis_t, message = call(
+        functools.partial(open_kernel, z),
+        [packed_b, shape((subs, modes, rows), BF16), shape((n, modes + DIGIT_ROWS, lanes), BF16)],
+        [*basis_pieces, loads, coarse_index],
+        4 * rows * lanes * lanes,
+        [pltpu.VMEM((DIGIT_ROWS, lanes), F32)],
+        loose=range(1, group),
+        name="open",
+    )
+    restricted = spread(message)
+
     shared = [coarse_inverse]
     for k in range(1, z.far):
         shared.append(lax.ppermute(coarse_inverse, "sub", [((i + k * z.near) % n, i) for i in range(n)]))
-    shared = jnp.stack(shared)
-
-    load_rows, basis_t, message = call(
-        functools.partial(open_kernel, z),
-        [packed_b, shape((subs, modes, rows), BF16), shape((n, modes + DIGIT_ROWS, lanes), BF16)],
-        [*basis_pieces, loads, digits],
-        4 * rows * lanes * lanes,
-        loose=range(1, group),
-        name="open",
-    )
-    restricted = spread(message)
+    (shared,) = call(
+        functools.partial(stack_kernel, z),
+        [shape((z.far, z.owned, z.block), BF16)],
+        shared,
+        0,
+        after=[message],
+        loose=range(1, z.far),
+        name="stack",
+    )
+    shared = pieces_of(shared, group)
 
     inverse_pieces = pieces_of(local_inverse, group)
     stiffness_pieces = pieces_of(stiffness, group)
-    work = 4 * subs * rows * rows * lanes
-    faces = shape((subs, z.face, 2 * lanes), BF16)
-    solved, image, to_before, to_after, basis, image_basis = call(
-        functools.partial(image_kernel, z, True),
-        [packed_f, packed_f, faces, faces, shape((subs, rows, modes), BF16), shape((subs, rows, modes), BF16)],
+    arrivals = [*range(1, group), *range(group + 1, 2 * group)]
+    faces = shape((subs, face, 2 * lanes), BF16)
+    outer = shape((face, 2 * lanes), BF16)
+    side = shape((subs, modes, face), BF16)
+    (
+        solved, image, before, after, first_face, last_face, basis, image_basis, left_t, right_t, inner, start_modes
+    ) = call(
+        functools.partial(first_image_kernel, z),
+        [
+            packed_f, packed_f, faces, faces, outer, outer, tall, tall, side, side,
+            shape((subs, modes, modes), BF16), shape((modes, lanes), F32),
+        ],
         [*inverse_pieces, *stiffness_pieces, load_rows, basis_t, left_rows, right_rows],
         work,
         [pltpu.VMEM((rows, lanes), BF16)],
-        range(group, 2 * group),
-        loose=[*range(1, group), *range(group + 1, 2 * group)],
+        late=range(group, 2 * group),
+        loose=arrivals,
         name="first_image",
     )
-    forward = [(i, (i + 1) % n) for i in range(n)]
-    backward = [(target, source) for source, target in forward]
-    from_before = lax.ppermute(to_after[subs - 1], "sub", forward)
-    from_after = lax.ppermute(to_before[0], "sub", backward)
-    residual, joined = call(
-        functools.partial(join_kernel, z, True),
-        [packed_f, shape((subs, rows, 3 * modes), BF16)],
-        [load_rows, image, to_before, to_after, from_before, from_after, left_rows, right_rows, image_basis],
-        work // 8,
-        loose=[4, 5],
-        name="first_join",
-    )
-
+    outer_after = lax.ppermute(first_face, "sub", backward)
     ordered_inverse, index, message = call(
         functools.partial(order_kernel, z),
         [shape((subs, z.far * z.owned, z.columns), BF16), shape((subs, n, lanes), F32), few],
-        [*pieces_of(shared, group), restricted, repeat, own_row],
+        [*shared, restricted, repeat, own_row],
         2 * z.far * z.owned * z.total * z.total,
-        after=[to_before],
+        after=[first_face],
         loose=range(1, group),
         name="order",
     )
     coarse = spread_near(message)
-    (picks,) = call(
+    picks, last_face = call(
         functools.partial(pick_kernel, z),
-        [shape((subs, (subs + 2) * modes, z.columns), BF16)],
-        [index, place],
+        [shape((subs, (subs + 2) * modes, z.columns), BF16), outer],
+        [index, place, last_face],
         work // 64,
         name="picks",
     )
-    first_pass, rounded, message = call(
+    outer_before = lax.ppermute(last_face, "sub", forward)
+    chosen, message = call(
         functools.partial(update_kernel, z),
-        [packed_f, packed_b, copies],
-        [coarse, picks, solved, residual, basis, joined, basis_t],
-        work // 8,
+        [shape(((subs + 2) * modes, lanes), BF16), copies],
+        [coarse, picks, start_modes, inner, left_t, right_t, before, after, outer_before, outer_after],
+        work // 64,
+        loose=[8, 9],
         name="update",
     )
     restricted = spread(message)
 
-    faces = shape((subs, z.face, lanes), BF16)
-    solved, image, to_before, to_after = call(
-        functools.partial(image_kernel, z, False),
-        [packed_f, packed_f, faces, faces],
-        [*inverse_pieces, *stiffness_pieces, rounded, first_pass, left_rows, right_rows],
+    bases = [before, after, outer_before, outer_after]
+    faces = shape((subs, face, lanes), BF16)
+    outer = shape((face, lanes), BF16)
+    solved, image, before, after, first_face, last_face = call(
+        functools.partial(second_image_kernel, z),
+        [packed_f, packed_f, faces, faces, outer, outer],
+        [
+            *inverse_pieces, *stiffness_pieces, load_rows, image, image_basis, solved, basis, chosen,
+            *bases, left_rows, right_rows,
+        ],
         work,
         [pltpu.VMEM((rows, lanes), BF16)],
-        range(group, 2 * group),
-        loose=[*range(1, group), *range(group + 1, 2 * group)],
+        late=range(2 * group),
+        loose=[*arrivals, 2 * group + 8, 2 * group + 9],
         name="second_image",
     )
-    from_before = lax.ppermute(to_after[subs - 1], "sub", forward)
-    from_after = lax.ppermute(to_before[0], "sub", backward)
-    (residual,) = call(
-        functools.partial(join_kernel, z, False),
-        [packed_f],
-        [load_rows, image, to_before, to_after, from_before, from_after, left_rows, right_rows],
-        work // 8,
-        loose=[4, 5],
-        name="second_join",
-    )
-    (message,) = call(
+    outer_after = lax.ppermute(first_face, "sub", backward)
+    message, last_face = call(
         functools.partial(coarse_kernel, z),
-        [few],
-        [restricted, ordered_inverse],
+        [few, outer],
+        [restricted, ordered_inverse, last_face],
         work // 64,
-        after=[to_before],
         name="coarse",
     )
     coarse = spread_near(message)
-    parts = shape((2, z.own, lanes), F32)
+    outer_before = lax.ppermute(last_face, "sub", forward)
     parts = call(
         functools.partial(last_kernel, z),
-        [parts] * group,
-        [coarse, picks, solved, residual, basis, joined],
+        [shape((2, z.own, lanes), F32)] * group,
+        [
+            coarse, picks, load_rows, image, image_basis, solved, basis,
+            before, after, outer_before, outer_after, *bases, left_rows, right_rows,
+        ],
         work // 8,
         [pltpu.VMEM((2, rows, lanes), F32)],
+        loose=[9, 10, 13, 14],
         name="last",
     )
     swapped = [parts[0]]
@@ -490,7 +551,11 @@
         swapped.append(lax.ppermute(parts[k], GROUP, [(g, (g + k) % group) for g in range(group)]))
     swapped = [swapped[(group - k) % group] for k in range(group)]
     out = shape((subs, z.own, z.cases), F32)
-    return tuple(call(functools.partial(unpack_kernel, z), [out, out], swapped, work // 64, loose=range(1, group), name="unpack"))
+    return tuple(
+        call(
+            functools.partial(unpack_kernel, z), [out, out], swapped, work // 64, loose=range(1, group), name="unpack"
+        )
+    )
 
 
 def solution(mesh):

time: 117 us -> 110 us (0.940)
  waiting for transfers between devices: 27.8 us -> 21.2 us
  starting transfers between devices: 34.8 us -> 40.4 us
  Pallas kernels: 44.4 us -> 41.6 us
  other arithmetic: 1.68 us -> 0 us
  local copies, waits for them, and re-layouts: 6.14 us -> 4.56 us
    ppermute x3, waiting for transfers between devices: 11.3 us -> 6.6 us  [body(): lax.ppermute(coarse_inverse, 'sub', [((i + k * z.near) % n, i) for i in r...]
    ppermute x4, waiting for transfers between devices: 13.5 us -> 10.2 us  [the longest x2 8.25 us: body(): outer_before = lax.ppermute(last_face, 'sub', forward)]
    all_to_all x2, starting transfers between devices: 9.63 us -> 12.8 us  [body(): restricted = spread(message)]
    pallas_call x11 -> x10, Pallas kernels: 44.4 us -> 41.6 us  [call(): pl.pallas_call(whole, out_shape=[pltpu.HBM(o.shape, o.dtype) for o in out...]
    another operation x3 -> x0, other arithmetic: 1.68 us -> none  [the longest x1 0.98 us: body(): shared = jnp.stack(shared)]
    squeeze x4 -> x0, local copies, waits for them, and re-layouts: 1.68 us -> none  [the longest x2 1.67 us: body(): from_after = lax.ppermute(to_before[0], 'sub', backward)]
    ppermute x3, starting transfers between devices: 6.04 us -> 7.62 us  [body(): lax.ppermute(coarse_inverse, 'sub', [((i + k * z.near) % n, i) for i in r...]
    ppermute x4, waiting for transfers between devices: 0.01 us -> 1.28 us  [pieces_of(): lax.ppermute(block, GROUP, [((g + k) % group, g) for g in range(group)])]
  transfers between devices with their start and end apart: 16 -> 16, of which waited for: 9 -> 7; matrix products, arithmetic and copies ran while one was open for 3% -> 0% of each run, Pallas kernels for 23% -> 22%
where the time goes in v6:
time: 110 us; the launch traced here: 109 us
  Pallas kernels  41.6 us (38%)
  starting transfers between devices  40.4 us (37%)
  waiting for transfers between devices  21.2 us (19%)
  local copies, waits for them, and re-layouts  4.56 us (4%)
    pallas_call x10, Pallas kernels, call(): pl.pallas_call(whole, out_shape=[pltpu.HBM(o.shape, o.dtype) for o in out...  41.6 us
    all_to_all x2, starting transfers between devices, body(): restricted = spread(message)  12.8 us
    ppermute x2, starting transfers between devices, body(): outer_after = lax.ppermute(first_face, 'sub', backward)  9.27 us
    ppermute x2, waiting for transfers between devices, body(): outer_before = lax.ppermute(last_face, 'sub', forward)  8.25 us
    ppermute x3, starting transfers between devices, body(): lax.ppermute(coarse_inverse, 'sub', [((i + k * z.near) % n, i) for i in r...  7.62 us
    all_to_all x2, starting transfers between devices, body(): coarse = spread_near(message)  7.47 us
    ppermute x3, waiting for transfers between devices, body(): lax.ppermute(coarse_inverse, 'sub', [((i + k * z.near) % n, i) for i in r...  6.6 us
    unnamed x14, local copies, waits for them, and re-layouts  4.56 us
  transfers between devices with their start and end apart: 16, of which 7 were waited for; matrix products, arithmetic and copies ran while one was open for 0% of the time, Pallas kernels for 22%

profile of v6, /device:TPU:0, one launch (start us, length us, event | category | flops | bytes accessed | tf_op | source)
XLA Modules:
  0.0 108.8 jit_solution(4653498212746767577)
XLA Ops:
  1.7 4.7 %collective-permute-start = (bf16[96,768]{1,0:T(8,128)(2,1)}, bf16[96,768]{1,0:T(8,128)(2,1)S(1)}, u32[]{:S(2)}, u32[]{:S(2)}) collective-permute-start(bf16[96,768]{1,0:T(8,128)(2,1)} %refs_0_.3), channel_id=1, source_target_pairs={{8,0},{10,2},{12,4},{14,6},{16,8},{18,10},{20,12},{22,14},{24,16},... | collective-permute-start | bytes 442376 | tf_op jit(solution)/shard_map/ppermute | solution.py:449
  6.3 1.3 %collective-permute-done.3.refs_1_ = bf16[2,48,512]{2,1,0:T(8,128)(2,1)S(1)} collective-permute-done((bf16[2,48,512]{2,1,0:T(8,128)(2,1)}, bf16[2,48,512]{2,1,0:T(8,128)(2,1)S(1)}, u32[]{:S(2)}, u32[]{:S(2)}) %collective-permute-start.3) | collective-permute-done | bytes 98336 | tf_op jit(solution)/shard_map/ppermute | solution.py:410
  7.6 2.9 %collective-permute-start.2 = (bf16[96,768]{1,0:T(8,128)(2,1)}, bf16[96,768]{1,0:T(8,128)(2,1)S(1)}, u32[]{:S(2)}, u32[]{:S(2)}) collective-permute-start(bf16[96,768]{1,0:T(8,128)(2,1)} %refs_0_.3), channel_id=1, source_target_pairs={{24,0},{26,2},{28,4},{30,6},{0,8},{2,10},{4,12},{6,14},{8,16},{10,... | collective-permute-start | bytes 442376 | tf_op jit(solution)/shard_map/ppermute | solution.py:449
  10.6 2.5 %open.1 = (bf16[1024,128]{1,0:T(8,128)(2,1)}, bf16[2,48,1024]{2,1,0:T(8,128)(2,1)}, bf16[16,64,128]{2,1,0:T(8,128)(2,1)}) custom-call(bf16[2,48,512]{2,1,0:T(8,128)(2,1)} %bitcast.2, bf16[2,48,512]{2,1,0:T(8,128)(2,1)S(1)} %collective-permute-done.3.refs_1_, bf16[2,1024,128]{2,1,0:T(8,128)(2,1)} %refs_2_.3, s32[2,48]{1,0:T(2,128)} %refs_3_.2), custom_call_target="tpu_custom_call" | custom-call | flops 67108864 | bytes 1442176 | tf_op jit(solution)/shard_map/open/pallas_call | solution.py:386
  13.1 6.6 %collective-permute-done.1.refs_2_ = bf16[96,768]{1,0:T(8,128)(2,1)S(1)} collective-permute-done((bf16[96,768]{1,0:T(8,128)(2,1)}, bf16[96,768]{1,0:T(8,128)(2,1)S(1)}, u32[]{:S(2)}, u32[]{:S(2)}) %collective-permute-start.1) | collective-permute-done | bytes 147488 | tf_op jit(solution)/shard_map/ppermute | solution.py:449
  19.7 0.9 copy-done
  20.6 1.8 %stack.1.refs_0_ = bf16[4,96,768]{2,1,0:T(8,128)(2,1)} custom-call(bf16[96,768]{1,0:T(8,128)(2,1)} %refs_0_.3, bf16[96,768]{1,0:T(8,128)(2,1)S(1)} %collective-permute-done.refs_1_, bf16[96,768]{1,0:T(8,128)(2,1)S(1)} %collective-permute-done.1.refs_2_, bf16[96,768]{1,0:T(8,128)(2,1)S(1)} %collective-permute-done.2.refs_3_, bf16[16,64,128]{2,1,0:T(8,128)(2,1)S(1)} %copy-done), custom_call_target="tpu_custom_call" | custom-call | bytes 1179648 | tf_op jit(solution)/shard_map/stack/pallas_call | solution.py:386
  22.5 6.0 %all-to-all-start = ((bf16[16,64,128]{2,1,0:T(8,128)(2,1)}), bf16[16,64,128]{2,1,0:T(8,128)(2,1)S(1)}, u32[]{:S(2)}, u32[]{:S(2)}) async-start(bf16[16,64,128]{2,1,0:T(8,128)(2,1)} %get-tuple-element.34.refs_4_), calls=%async_computation | async-start | bytes 524288 | tf_op jit(solution)/shard_map/all_to_all | solution.py:445
  28.6 9.4 %first_image.1 = (f32[1024,128]{1,0:T(8,128)}, f32[1024,128]{1,0:T(8,128)}, bf16[2,128,256]{2,1,0:T(8,128)(2,1)}, bf16[2,128,256]{2,1,0:T(8,128)(2,1)}, bf16[128...) custom-call(bf16[2,512,1024]{2,1,0:T(8,128)(2,1)} %refs_0_.5, ...), custom_call_target="tpu_custom_call" | custom-call | flops 1073741824 | bytes 10767360 | tf_op jit(solution)/shard_map/first_image/pallas_call | solution.py:386
  38.0 1.1 all-to-all-done.refs_2_
  39.1 0.7 copy-done.6
  39.8 0.8 copy-done.1
  40.7 4.8 %order.1 = (bf16[2,384,768]{2,1,0:T(8,128)(2,1)}, f32[2,16,128]{2,1,0:T(8,128)}, bf16[4,4,48,128]{3,2,1,0:T(8,128)(2,1)}) custom-call(bf16[4,96,768]{2,1,0:T(8,128)(2,1)} %stack.1.refs_0_, bf16[4,96,768]{2,1,0:T(8,128)(2,1)S(1)} %collective-permute-done.4.refs_1_, bf16[16,64,128]{2,1,0:T(8,128)(2,1)} %copy-done.6, bf16[128,768]{1,0:T(8,128)(2,1)} %constant.6.clone.refs_3_, ...), custom_call_target="tpu_custom_call" | custom-call | flops 1811939328 | bytes 3080192 | tf_op jit(solution)/shard_map/order/pallas_call | solution.py:386
  45.5 3.4 %all-to-all-start.1 = ((bf16[4,4,48,128]{3,2,1,0:T(8,128)(2,1)}), bf16[4,4,48,128]{3,2,1,0:T(8,128)(2,1)S(1)}, u32[]{:S(2)}, u32[]{:S(2)}) async-start(bf16[4,4,48,128]{3,2,1,0:T(8,128)(2,1)} %get-tuple-element.38), calls=%async_computation.1 | async-start | bytes 393216 | tf_op jit(solution)/shard_map/all_to_all | solution.py:492
  48.9 2.0 %picks.1 = (bf16[2,192,768]{2,1,0:T(8,128)(2,1)}, bf16[128,256]{1,0:T(8,128)(2,1)}) custom-call(f32[2,16,128]{2,1,0:T(8,128)} %get-tuple-element.39.refs_0_, s32[2,768]{1,0:T(2,128)} %constant.8.clone.refs_1_, bf16[128,256]{1,0:T(8,128)(2,1)} %get-tuple-element.40.refs_2_), custom_call_target="tpu_custom_call" | custom-call | flops 16777216 | bytes 743424 | tf_op jit(solution)/shard_map/picks/pallas_call | solution.py:386
  50.9 2.0 %collective-permute-start.7 = (bf16[128,256]{1,0:T(8,128)(2,1)}, bf16[128,256]{1,0:T(8,128)(2,1)S(1)}, u32[]{:S(2)}, u32[]{:S(2)}) collective-permute-start(bf16[128,256]{1,0:T(8,128)(2,1)} %get-tuple-element.48), channel_id=1, source_target_pairs={{0,2},{2,4},{4,6},{6,8},{8,10},{10,12},{12,14},{14,16},{16,18},{18... | collective-permute-start | bytes 196616 | tf_op jit(solution)/shard_map/ppermute | solution.py:500
  52.9 3.6 %collective-permute-start.8 = (bf16[128,256]{1,0:T(8,128)(2,1)S(1)}, bf16[128,256]{1,0:T(8,128)(2,1)S(1)}, u32[]{:S(2)}, u32[]{:S(2)}) collective-permute-start(bf16[128,256]{1,0:T(8,128)(2,1)S(1)} %copy-done.2), channel_id=1, source_target_pairs={{2,0},{4,2},{6,4},{8,6},{10,8},{12,10},{14,12},{16,14},{18,16},{20... | collective-permute-start | bytes 196616 | tf_op jit(solution)/shard_map/ppermute | solution.py:482
  56.6 2.4 %collective-permute-done.7.refs_8_.refs_12_.refs_13_ = bf16[128,256]{1,0:T(8,128)(2,1)S(1)} collective-permute-done((bf16[128,256]{1,0:T(8,128)(2,1)}, bf16[128,256]{1,0:T(8,128)(2,1)S(1)}, u32[]{:S(2)}, u32[]{:S(2)}) %collective-permute-start.7) | collective-permute-done | bytes 65568 | tf_op jit(solution)/shard_map/ppermute | solution.py:500
  59.0 0.7 copy-done.4
  59.7 2.8 %update.1 = (bf16[192,128]{1,0:T(8,128)(2,1)}, bf16[16,48,128]{2,1,0:T(8,128)(2,1)}) custom-call(bf16[4,4,48,128]{3,2,1,0:T(8,128)(2,1)} %copy-done.4, bf16[2,192,768]{2,1,0:T(8,128)(2,1)} %get-tuple-element.41.refs_1_, f32[48,128]{1,0:T(8,128)} %get-tuple-element.42.refs_2_, bf16[2,48,48]{2,1,0:T(8,128)(2,1)} %get-tuple-element.43.refs_3_, ...), custom_call_target="tpu_custom_call" | custom-call | flops 16777216 | bytes 1508352 | tf_op jit(solution)/shard_map/update/pallas_call | solution.py:386
  62.5 6.8 %all-to-all-start.2 = ((bf16[16,48,128]{2,1,0:T(8,128)(2,1)}), bf16[16,48,128]{2,1,0:T(8,128)(2,1)S(1)}, u32[]{:S(2)}, u32[]{:S(2)}) async-start(bf16[16,48,128]{2,1,0:T(8,128)(2,1)} %get-tuple-element.49), calls=%async_computation.2 | async-start | bytes 393216 | tf_op jit(solution)/shard_map/all_to_all | solution.py:509
  69.3 8.7 %second_image.1 = (f32[1024,128]{1,0:T(8,128)}, f32[1024,128]{1,0:T(8,128)}, bf16[2,128,128]{2,1,0:T(8,128)(2,1)}, bf16[2,128,128]{2,1,0:T(8,128)(2,1)}, bf16[12...) custom-call(bf16[2,512,1024]{2,1,0:T(8,128)(2,1)} %refs_0_.5, bf16[2,512,1024]{2,1,0:T(8,128)(2,1)S(1)} %collective-permute-done.5.refs_1_, ...), custom_call_target="tpu_custom_call" | custom-call | flops 1073741824 | bytes 11782144 | tf_op jit(solution)/shard_map/second_image/pallas_call | solution.py:386
  78.1 0.7 copy-done.5
  78.7 2.6 %coarse.1 = (bf16[4,4,48,128]{3,2,1,0:T(8,128)(2,1)}, bf16[128,128]{1,0:T(8,128)(2,1)}) custom-call(bf16[16,48,128]{2,1,0:T(8,128)(2,1)} %copy-done.5, bf16[2,384,768]{2,1,0:T(8,128)(2,1)} %get-tuple-element.50.refs_1_, bf16[128,128]{1,0:T(8,128)(2,1)} %get-tuple-element.56.refs_2_), custom_call_target="tpu_custom_call" | custom-call | flops 16777216 | bytes 1638400 | tf_op jit(solution)/shard_map/coarse/pallas_call | solution.py:386
  81.4 4.1 %all-to-all-start.3 = ((bf16[4,4,48,128]{3,2,1,0:T(8,128)(2,1)}), bf16[4,4,48,128]{3,2,1,0:T(8,128)(2,1)S(1)}, u32[]{:S(2)}, u32[]{:S(2)}) async-start(bf16[4,4,48,128]{3,2,1,0:T(8,128)(2,1)} %get-tuple-element.57), calls=%async_computation.3 | async-start | bytes 393216 | tf_op jit(solution)/shard_map/all_to_all | solution.py:535
  85.5 5.6 %collective-permute-start.10 = (bf16[128,128]{1,0:T(8,128)(2,1)}, bf16[128,128]{1,0:T(8,128)(2,1)S(1)}, u32[]{:S(2)}, u32[]{:S(2)}) collective-permute-start(bf16[128,128]{1,0:T(8,128)(2,1)} %get-tuple-element.63), channel_id=1, source_target_pairs={{2,0},{4,2},{6,4},{8,6},{10,8},{12,10},{14,12},{16,14},{18,16},{20... | collective-permute-start | bytes 98312 | tf_op jit(solution)/shard_map/ppermute | solution.py:527
  91.1 1.9 %collective-permute-done.10.refs_10_ = bf16[128,128]{1,0:T(8,128)(2,1)S(1)} collective-permute-done((bf16[128,128]{1,0:T(8,128)(2,1)}, bf16[128,128]{1,0:T(8,128)(2,1)S(1)}, u32[]{:S(2)}, u32[]{:S(2)}) %collective-permute-start.10) | collective-permute-done | bytes 32800 | tf_op jit(solution)/shard_map/ppermute | solution.py:527
  93.0 5.8 %collective-permute-done.9.refs_9_ = bf16[128,128]{1,0:T(8,128)(2,1)S(1)} collective-permute-done((bf16[128,128]{1,0:T(8,128)(2,1)}, bf16[128,128]{1,0:T(8,128)(2,1)S(1)}, u32[]{:S(2)}, u32[]{:S(2)}) %collective-permute-start.9) | collective-permute-done | bytes 32800 | tf_op jit(solution)/shard_map/ppermute | solution.py:536
  98.8 0.7 copy-done.3
  99.5 4.5 %last.1 = (f32[2,512,128]{2,1,0:T(8,128)}, f32[2,512,128]{2,1,0:T(8,128)}) custom-call(bf16[4,4,48,128]{3,2,1,0:T(8,128)(2,1)} %copy-done.3, bf16[2,192,768]{2,1,0:T(8,128)(2,1)} %get-tuple-element.41.refs_1_, bf16[1024,128]{1,0:T(8,128)(2,1)} %get-tuple-element.35.refs_4_.refs_2_, f32[1024,128]{1,0:T(8,128)} %get-tuple-element.58.refs_3_, ...), custom_call_target="tpu_custom_call" | custom-call | flops 134217728 | bytes 4130816 | tf_op jit(solution)/shard_map/last/pallas_call | solution.py:386
  104.0 2.1 %collective-permute-done.11.refs_1_ = f32[2,512,128]{2,1,0:T(8,128)S(1)} collective-permute-done((f32[2,512,128]{2,1,0:T(8,128)}, f32[2,512,128]{2,1,0:T(8,128)S(1)}, u32[]{:S(2)}, u32[]{:S(2)}) %collective-permute-start.11) | collective-permute-done | bytes 524320 | tf_op jit(solution)/shard_map/ppermute | solution.py:551
  106.2 2.5 %unpack.1 = (f32[2,512,128]{2,1,0:T(8,128)}, f32[2,512,128]{2,1,0:T(8,128)}) custom-call(f32[2,512,128]{2,1,0:T(8,128)} %get-tuple-element.64.refs_0_, f32[2,512,128]{2,1,0:T(8,128)S(1)} %collective-permute-done.11.refs_1_), custom_call_target="tpu_custom_call" | custom-call | flops 16777216 | bytes 2097152 | tf_op jit(solution)/shard_map/unpack/pallas_call | solution.py:386
  (24 shorter events, 1.2 us)
Async XLA Ops:
  0.6 27.9 %collective-permute-start.5 = (bf16[2,512,1024]{2,1,0:T(8,128)(2,1)}, bf16[2,512,1024]{2,1,0:T(8,128)(2,1)S(1)}, u32[]{:S(2)}, u32[]{:S(2)}) collective-permute-start(bf16[2,512,1024]{2,1,0:T(8,128)(2,1)} %refs_0_.5), channel_id=1, source_target_pairs={{1,0},{0,1},{3,2},{2,3},{5,4},{4,5},{7,6},{6,7},{9,8},{8,9},{11,10... | collective-permute-start | bytes 6291464 | tf_op jit(solution)/shard_map/ppermute | solution.py:410
  1.1 27.4 %collective-permute-start.6 = (bf16[2,512,1024]{2,1,0:T(8,128)(2,1)}, bf16[2,512,1024]{2,1,0:T(8,128)(2,1)}, u32[]{:S(2)}, u32[]{:S(2)}) collective-permute-start(bf16[2,512,1024]{2,1,0:T(8,128)(2,1)} %refs_2_.5), channel_id=1, source_target_pairs={{1,0},{0,1},{3,2},{2,3},{5,4},{4,5},{7,6},{6,7},{9,8},{8,9},{11,10... | collective-permute-start | bytes 6291464 | tf_op jit(solution)/shard_map/ppermute | solution.py:410
  1.2 6.4 %collective-permute-start.3 = (bf16[2,48,512]{2,1,0:T(8,128)(2,1)}, bf16[2,48,512]{2,1,0:T(8,128)(2,1)S(1)}, u32[]{:S(2)}, u32[]{:S(2)}) collective-permute-start(bf16[2,48,512]{2,1,0:T(8,128)(2,1)} %bitcast.1), channel_id=1, source_target_pairs={{1,0},{0,1},{3,2},{2,3},{5,4},{4,5},{7,6},{6,7},{9,8},{8,9},{11,10... | collective-permute-start | bytes 294920 | tf_op jit(solution)/shard_map/ppermute | solution.py:410
  1.7 11.4 %collective-permute-start = (bf16[96,768]{1,0:T(8,128)(2,1)}, bf16[96,768]{1,0:T(8,128)(2,1)S(1)}, u32[]{:S(2)}, u32[]{:S(2)}) collective-permute-start(bf16[96,768]{1,0:T(8,128)(2,1)} %refs_0_.3), channel_id=1, source_target_pairs={{8,0},{10,2},{12,4},{14,6},{16,8},{18,10},{20,12},{22,14},{24,16},... | collective-permute-start | bytes 442376 | tf_op jit(solution)/shard_map/ppermute | solution.py:449
  6.3 13.3 %collective-permute-start.1 = (bf16[96,768]{1,0:T(8,128)(2,1)}, bf16[96,768]{1,0:T(8,128)(2,1)S(1)}, u32[]{:S(2)}, u32[]{:S(2)}) collective-permute-start(bf16[96,768]{1,0:T(8,128)(2,1)} %refs_0_.3), channel_id=1, source_target_pairs={{16,0},{18,2},{20,4},{22,6},{24,8},{26,10},{28,12},{30,14},{0,16},... | collective-permute-start | bytes 442376 | tf_op jit(solution)/shard_map/ppermute | solution.py:449
  7.6 12.1 %collective-permute-start.2 = (bf16[96,768]{1,0:T(8,128)(2,1)}, bf16[96,768]{1,0:T(8,128)(2,1)S(1)}, u32[]{:S(2)}, u32[]{:S(2)}) collective-permute-start(bf16[96,768]{1,0:T(8,128)(2,1)} %refs_0_.3), channel_id=1, source_target_pairs={{24,0},{26,2},{28,4},{30,6},{0,8},{2,10},{4,12},{6,14},{8,16},{10,... | collective-permute-start | bytes 442376 | tf_op jit(solution)/shard_map/ppermute | solution.py:449
  19.7 1.0 copy-start
  22.5 16.6 %collective-permute-start.4 = (bf16[4,96,768]{2,1,0:T(8,128)(2,1)}, bf16[4,96,768]{2,1,0:T(8,128)(2,1)S(1)}, u32[]{:S(2)}, u32[]{:S(2)}) collective-permute-start(bf16[4,96,768]{2,1,0:T(8,128)(2,1)} %stack.1.refs_0_), channel_id=1, source_target_pairs={{1,0},{0,1},{3,2},{2,3},{5,4},{4,5},{7,6},{6,7},{9,8},{8,9},{11,10... | collective-permute-start | bytes 1769480 | tf_op jit(solution)/shard_map/ppermute | solution.py:410
  22.5 16.6 %all-to-all-start = ((bf16[16,64,128]{2,1,0:T(8,128)(2,1)}), bf16[16,64,128]{2,1,0:T(8,128)(2,1)S(1)}, u32[]{:S(2)}, u32[]{:S(2)}) async-start(bf16[16,64,128]{2,1,0:T(8,128)(2,1)} %get-tuple-element.34.refs_4_), calls=%async_computation | async-start | bytes 524288 | tf_op jit(solution)/shard_map/all_to_all | solution.py:445
  39.1 0.7 copy-start.6
  39.8 0.8 copy-start.1
  40.7 12.3 %copy-start.2 = (bf16[128,256]{1,0:T(8,128)(2,1)S(1)}, bf16[128,256]{1,0:T(8,128)(2,1)}, u32[]{:S(2)}) copy-start(bf16[128,256]{1,0:T(8,128)(2,1)} %get-tuple-element.37.refs_5_) | copy-start | bytes 196612
  45.5 13.6 %all-to-all-start.1 = ((bf16[4,4,48,128]{3,2,1,0:T(8,128)(2,1)}), bf16[4,4,48,128]{3,2,1,0:T(8,128)(2,1)S(1)}, u32[]{:S(2)}, u32[]{:S(2)}) async-start(bf16[4,4,48,128]{3,2,1,0:T(8,128)(2,1)} %get-tuple-element.38), calls=%async_computation.1 | async-start | bytes 393216 | tf_op jit(solution)/shard_map/all_to_all | solution.py:492
  50.9 8.1 %collective-permute-start.7 = (bf16[128,256]{1,0:T(8,128)(2,1)}, bf16[128,256]{1,0:T(8,128)(2,1)S(1)}, u32[]{:S(2)}, u32[]{:S(2)}) collective-permute-start(bf16[128,256]{1,0:T(8,128)(2,1)} %get-tuple-element.48), channel_id=1, source_target_pairs={{0,2},{2,4},{4,6},{6,8},{8,10},{10,12},{12,14},{14,16},{16,18},{18... | collective-permute-start | bytes 196616 | tf_op jit(solution)/shard_map/ppermute | solution.py:500
  52.9 6.1 %collective-permute-start.8 = (bf16[128,256]{1,0:T(8,128)(2,1)S(1)}, bf16[128,256]{1,0:T(8,128)(2,1)S(1)}, u32[]{:S(2)}, u32[]{:S(2)}) collective-permute-start(bf16[128,256]{1,0:T(8,128)(2,1)S(1)} %copy-done.2), channel_id=1, source_target_pairs={{2,0},{4,2},{6,4},{8,6},{10,8},{12,10},{14,12},{16,14},{18,16},{20... | collective-permute-start | bytes 196616 | tf_op jit(solution)/shard_map/ppermute | solution.py:482
  59.0 0.7 copy-start.4
  62.5 15.5 %all-to-all-start.2 = ((bf16[16,48,128]{2,1,0:T(8,128)(2,1)}), bf16[16,48,128]{2,1,0:T(8,128)(2,1)S(1)}, u32[]{:S(2)}, u32[]{:S(2)}) async-start(bf16[16,48,128]{2,1,0:T(8,128)(2,1)} %get-tuple-element.49), calls=%async_computation.2 | async-start | bytes 393216 | tf_op jit(solution)/shard_map/all_to_all | solution.py:509
  78.0 0.7 copy-start.5
  81.4 17.4 %all-to-all-start.3 = ((bf16[4,4,48,128]{3,2,1,0:T(8,128)(2,1)}), bf16[4,4,48,128]{3,2,1,0:T(8,128)(2,1)S(1)}, u32[]{:S(2)}, u32[]{:S(2)}) async-start(bf16[4,4,48,128]{3,2,1,0:T(8,128)(2,1)} %get-tuple-element.57), calls=%async_computation.3 | async-start | bytes 393216 | tf_op jit(solution)/shard_map/all_to_all | solution.py:535
  85.5 7.5 %collective-permute-start.10 = (bf16[128,128]{1,0:T(8,128)(2,1)}, bf16[128,128]{1,0:T(8,128)(2,1)S(1)}, u32[]{:S(2)}, u32[]{:S(2)}) collective-permute-start(bf16[128,128]{1,0:T(8,128)(2,1)} %get-tuple-element.63), channel_id=1, source_target_pairs={{2,0},{4,2},{6,4},{8,6},{10,8},{12,10},{14,12},{16,14},{18,16},{20... | collective-permute-start | bytes 98312 | tf_op jit(solution)/shard_map/ppermute | solution.py:527
  91.1 7.7 %collective-permute-start.9 = (bf16[128,128]{1,0:T(8,128)(2,1)}, bf16[128,128]{1,0:T(8,128)(2,1)S(1)}, u32[]{:S(2)}, u32[]{:S(2)}) collective-permute-start(bf16[128,128]{1,0:T(8,128)(2,1)} %get-tuple-element.62), channel_id=1, source_target_pairs={{0,2},{2,4},{4,6},{6,8},{8,10},{10,12},{12,14},{14,16},{16,18},{18... | collective-permute-start | bytes 98312 | tf_op jit(solution)/shard_map/ppermute | solution.py:536
  98.8 0.7 copy-start.3
  104.0 2.2 %collective-permute-start.11 = (f32[2,512,128]{2,1,0:T(8,128)}, f32[2,512,128]{2,1,0:T(8,128)S(1)}, u32[]{:S(2)}, u32[]{:S(2)}) collective-permute-start(f32[2,512,128]{2,1,0:T(8,128)} %get-tuple-element.65), channel_id=1, source_target_pairs={{0,1},{1,0},{2,3},{3,2},{4,5},{5,4},{6,7},{7,6},{8,9},{9,8},{10,11... | collective-permute-start | bytes 1572872 | tf_op jit(solution)/shard_map/ppermute | solution.py:551

commit v7 on v6

--- a/solution.py
+++ b/solution.py
@@ -42,10 +42,6 @@
         self.width = self.cases // self.group
         self.lanes = max(self.cases, -(-self.subs * self.width // 128) * 128)
         self.columns = self.n * self.modes
-        self.near = 1
-        while self.near * self.near < self.n and self.n % (2 * self.near) == 0:
-            self.near *= 2
-        self.far = self.n // self.near
 
 
 def lane_mask(z, block, shape):
@@ -90,21 +86,26 @@
     return jnp.where(row == rows_of, 1.0, 0.0).astype(BF16)
 
 
+def case_matrix(z, s):
+    row = lax.broadcasted_iota(jnp.int32, (z.cases, z.lanes), 0)
+    lane = lax.broadcasted_iota(jnp.int32, (z.cases, z.lanes), 1)
+    hit = (row - lax.axis_index(GROUP) * z.width == lane - s * z.width) & lane_mask(z, s, row.shape)
+    return jnp.where(hit, 1.0, 0.0).astype(BF16)
+
+
+def join_basis(z, pieces, basis_t):
+    for k, piece in enumerate(pieces):
+        basis_t[:, :, pl.ds(piece_start(z, k, z.own), z.own)] = piece[...]
+
+
 def open_kernel(z, *refs):
     pieces = refs[: z.group]
-    loads, index, load_rows, basis_t, message, digits = refs[z.group :]
-    group = lax.axis_index(GROUP)
-    for k, piece in enumerate(pieces):
-        basis_t[:, :, pl.ds(piece_start(z, k, z.own), z.own)] = piece[...]
-    row = lax.broadcasted_iota(jnp.int32, (z.cases, z.lanes), 0)
-    lane = lax.broadcasted_iota(jnp.int32, (z.cases, z.lanes), 1)
-    packed = jnp.zeros((z.rows, z.lanes), F32)
-    for s in range(z.subs):
-        hit = (row - group * z.width == lane - s * z.width) & lane_mask(z, s, row.shape)
-        packed = packed + dot(loads[s], jnp.where(hit, 1.0, 0.0).astype(BF16))
-    packed = packed.astype(BF16)
-    load_rows[...] = packed
-    modes = select(z, [dot(basis_t[s], packed) for s in range(z.subs)]).astype(BF16)
+    loads, index, message, digits, basis_t = refs[z.group :]
+    join_basis(z, pieces, basis_t)
+    total = jnp.zeros((z.modes, z.lanes), F32)
+    for s in range(z.subs):
+        total = total + dot(dot(basis_t[s], loads[s]).astype(BF16), case_matrix(z, s))
+    modes = total.astype(BF16)
     digits[...] = jnp.zeros(digits.shape, F32)
     for s in range(z.subs):
         places = index[s : s + 1, :]
@@ -113,12 +114,6 @@
     for k in range(z.n):
         message[k, : z.modes, :] = modes
         message[k, z.modes :, :] = digits[...].astype(BF16)
-
-
-def stack_kernel(z, *refs):
-    *blocks, out = refs
-    for k, block in enumerate(blocks):
-        out[k] = block[...]
 
 
 def multiply(z, pieces, vector, store):
@@ -154,10 +149,17 @@
 
 def first_image_kernel(z, wait, *refs):
     inverse, stiffness = refs[: z.group], refs[z.group : 2 * z.group]
-    load_rows, basis_t, left_rows, right_rows = refs[2 * z.group : 2 * z.group + 4]
-    outs = refs[2 * z.group + 4 :]
-    solved, image, before, after, first_face, last_face, basis, image_basis, left_t, right_t, inner, start_modes = outs[:12]
-    rounded = outs[12]
+    pieces = refs[2 * z.group : 3 * z.group]
+    loads, left_rows, right_rows = refs[3 * z.group : 3 * z.group + 3]
+    load_rows, solved, image, before, after, first_face, last_face = refs[3 * z.group + 3 : 3 * z.group + 10]
+    basis, image_basis, left_t, right_t, inner, start_modes, rounded, basis_t = refs[3 * z.group + 10 :]
+    join_basis(z, pieces, basis_t)
+    packed = dot(loads[0], case_matrix(z, 0))
+    for s in range(1, z.subs):
+        packed = packed + dot(loads[s], case_matrix(z, s))
+    load_rows[...] = packed.astype(BF16)
+    for k in range(z.group):
+        wait(k)
 
     def store_solved(start, value):
         solved[pl.ds(start, z.own), :] = value
@@ -241,14 +243,9 @@
 def coarse_rows(z, ordered_inverse, arrived, message):
     flat = arrived[:, : z.modes, :].reshape(z.columns, z.lanes)
     rows = fold(z, select(z, [dot(ordered_inverse[s], flat) for s in range(z.subs)]))
-    for k in range(z.far):
-        place = lax.rem(lax.axis_index("sub") // z.near + k, z.far)
-        start = k * z.owned
-        packed = select(
-            z, [rows[start + s * z.modes : start + (s + 1) * z.modes, :] for s in range(z.subs)]
-        ).astype(BF16)
-        for a in range(z.near):
-            message[a, place] = packed
+    packed = select(z, [rows[s * z.modes : (s + 1) * z.modes, :] for s in range(z.subs)]).astype(BF16)
+    for k in range(z.n):
+        message[k] = packed
 
 
 def order_kernel(z, *refs):
@@ -263,15 +260,14 @@
         places = jnp.sum(spread * own_row[...], axis=0, keepdims=True).astype(jnp.int32)
         for at in range(0, z.columns, 768):
             wide = min(768, z.columns - at)
-            total = jnp.zeros((z.far * z.owned, wide), F32)
+            total = jnp.zeros((z.owned, wide), F32)
             for k, block in enumerate(blocks):
                 inside = places[:, at : at + wide] - piece_start(z, k, z.block)
                 for first in range(0, z.block, 768):
                     deep = min(768, z.block - first)
                     row = lax.broadcasted_iota(jnp.int32, (deep, wide), 0) + first
                     hot = jnp.where(row == inside, 1.0, 0.0).astype(BF16)
-                    rows = block[:, :, first : first + deep].reshape(z.far * z.owned, deep)
-                    total = total + dot(rows, hot)
+                    total = total + dot(block[:, first : first + deep], hot)
             ordered_inverse[s, :, at : at + wide] = total.astype(BF16)
     coarse_rows(z, ordered_inverse, arrived, message)
 
@@ -301,7 +297,7 @@
 
 
 def picked_rows(z, arrived, picks):
-    flat = jnp.concatenate([arrived[a, b] for b in range(z.far) for a in range(z.near)], axis=0)
+    flat = arrived[...].reshape(z.columns, z.lanes)
     return fold(z, select(z, [dot(picks[h], flat) for h in range(z.subs)])).astype(BF16)
 
 
@@ -424,40 +420,24 @@
     packed_f = shape((rows, lanes), F32)
     packed_b = shape((rows, lanes), BF16)
     copies = shape((n, modes, lanes), BF16)
-    few = shape((z.near, z.far, modes, lanes), BF16)
     tall = shape((subs, rows, modes), BF16)
     spread = functools.partial(lax.all_to_all, axis_name="sub", split_axis=0, concat_axis=0)
-    groups = [[a + z.near * b for a in range(z.near)] for b in range(z.far)]
-    spread_near = functools.partial(spread, axis_index_groups=groups)
     forward = [(i, (i + 1) % n) for i in range(n)]
     backward = [(target, source) for source, target in forward]
     work = 4 * subs * rows * rows * lanes
 
-    load_rows, basis_t, message = call(
+    (message,) = call(
         functools.partial(open_kernel, z),
-        [packed_b, shape((subs, modes, rows), BF16), shape((n, modes + DIGIT_ROWS, lanes), BF16)],
+        [shape((n, modes + DIGIT_ROWS, lanes), BF16)],
         [*basis_pieces, loads, coarse_index],
         4 * rows * lanes * lanes,
-        [pltpu.VMEM((DIGIT_ROWS, lanes), F32)],
+        [pltpu.VMEM((DIGIT_ROWS, lanes), F32), pltpu.VMEM((subs, modes, rows), BF16)],
         loose=range(1, group),
         name="open",
     )
     restricted = spread(message)
 
-    shared = [coarse_inverse]
-    for k in range(1, z.far):
-        shared.append(lax.ppermute(coarse_inverse, "sub", [((i + k * z.near) % n, i) for i in range(n)]))
-    (shared,) = call(
-        functools.partial(stack_kernel, z),
-        [shape((z.far, z.owned, z.block), BF16)],
-        shared,
-        0,
-        after=[message],
-        loose=range(1, z.far),
-        name="stack",
-    )
-    shared = pieces_of(shared, group)
-
+    inverse_columns = pieces_of(coarse_inverse, group)
     inverse_pieces = pieces_of(local_inverse, group)
     stiffness_pieces = pieces_of(stiffness, group)
     arrivals = [*range(1, group), *range(group + 1, 2 * group)]
@@ -465,31 +445,31 @@
     outer = shape((face, 2 * lanes), BF16)
     side = shape((subs, modes, face), BF16)
     (
-        solved, image, before, after, first_face, last_face, basis, image_basis, left_t, right_t, inner, start_modes
+        load_rows, solved, image, before, after, first_face, last_face, basis, image_basis, left_t, right_t, inner, start_modes
     ) = call(
         functools.partial(first_image_kernel, z),
         [
-            packed_f, packed_f, faces, faces, outer, outer, tall, tall, side, side,
+            packed_b, packed_f, packed_f, faces, faces, outer, outer, tall, tall, side, side,
             shape((subs, modes, modes), BF16), shape((modes, lanes), F32),
         ],
-        [*inverse_pieces, *stiffness_pieces, load_rows, basis_t, left_rows, right_rows],
+        [*inverse_pieces, *stiffness_pieces, *basis_pieces, loads, left_rows, right_rows],
         work,
-        [pltpu.VMEM((rows, lanes), BF16)],
-        late=range(group, 2 * group),
-        loose=arrivals,
+        [pltpu.VMEM((rows, lanes), BF16), pltpu.VMEM((subs, modes, rows), BF16)],
+        late=range(2 * group),
+        loose=[*arrivals, *range(2 * group + 1, 3 * group)],
         name="first_image",
     )
     outer_after = lax.ppermute(first_face, "sub", backward)
     ordered_inverse, index, message = call(
         functools.partial(order_kernel, z),
-        [shape((subs, z.far * z.owned, z.columns), BF16), shape((subs, n, lanes), F32), few],
-        [*shared, restricted, repeat, own_row],
-        2 * z.far * z.owned * z.total * z.total,
+        [shape((subs, z.owned, z.columns), BF16), shape((subs, n, lanes), F32), copies],
+        [*inverse_columns, restricted, repeat, own_row],
+        2 * z.owned * z.total * z.total,
         after=[first_face],
-        loose=range(1, group),
+        loose=range(1, group + 1),
         name="order",
     )
-    coarse = spread_near(message)
+    coarse = spread(message)
     picks, last_face = call(
         functools.partial(pick_kernel, z),
         [shape((subs, (subs + 2) * modes, z.columns), BF16), outer],
@@ -503,7 +483,7 @@
         [shape(((subs + 2) * modes, lanes), BF16), copies],
         [coarse, picks, start_modes, inner, left_t, right_t, before, after, outer_before, outer_after],
         work // 64,
-        loose=[8, 9],
+        loose=[0, 8, 9],
         name="update",
     )
     restricted = spread(message)
@@ -527,12 +507,13 @@
     outer_after = lax.ppermute(first_face, "sub", backward)
     message, last_face = call(
         functools.partial(coarse_kernel, z),
-        [few, outer],
+        [copies, outer],
         [restricted, ordered_inverse, last_face],
         work // 64,
+        loose=[0],
         name="coarse",
     )
-    coarse = spread_near(message)
+    coarse = spread(message)
     outer_before = lax.ppermute(last_face, "sub", forward)
     parts = call(
         functools.partial(last_kernel, z),
@@ -543,7 +524,7 @@
         ],
         work // 8,
         [pltpu.VMEM((2, rows, lanes), F32)],
-        loose=[9, 10, 13, 14],
+        loose=[0, 9, 10, 13, 14],
         name="last",
     )
     swapped = [parts[0]]

time: 110 us -> 100 us (0.909)
  local copies, waits for them, and re-layouts: 4.56 us -> 0.84 us
  Pallas kernels: 41.6 us -> 38.5 us
  waiting for transfers between devices: 21.2 us -> 19.3 us
    ppermute x3 -> x0, starting transfers between devices: 7.62 us -> none  [body(): lax.ppermute(coarse_inverse, 'sub', [((i + k * z.near) % n, i) for i in r...]
    ppermute x3 -> x0, waiting for transfers between devices: 6.6 us -> none  [body(): lax.ppermute(coarse_inverse, 'sub', [((i + k * z.near) % n, i) for i in r...]
    all_to_all x2, starting transfers between devices: 7.47 us -> 13.7 us  [body(): coarse = spread(message)]
    ppermute x4, waiting for transfers between devices: 1.28 us -> 5.96 us  [pieces_of(): lax.ppermute(block, GROUP, [((g + k) % group, g) for g in range(group)])]
    unnamed x14 -> x4, local copies, waits for them, and re-layouts: 4.56 us -> 0.84 us
    pallas_call x10 -> x9, Pallas kernels: 41.6 us -> 38.5 us  [call(): pl.pallas_call(whole, out_shape=[pltpu.HBM(o.shape, o.dtype) for o in out...]
    all_to_all x2, starting transfers between devices: 12.8 us -> 14.1 us  [body(): restricted = spread(message)]
  transfers between devices with their start and end apart: 16 -> 13, of which waited for: 7 -> 6; matrix products, arithmetic and copies ran while one was open for 0% -> 0% of each run, Pallas kernels for 22% -> 23%
where the time goes in v7:
time: 100 us; the launch traced here: 99.5 us
  starting transfers between devices  40.1 us (40%)
  Pallas kernels  38.5 us (38%)
  waiting for transfers between devices  19.3 us (19%)
    pallas_call x9, Pallas kernels, call(): pl.pallas_call(whole, out_shape=[pltpu.HBM(o.shape, o.dtype) for o in out...  38.5 us
    all_to_all x2, starting transfers between devices, body(): restricted = spread(message)  14.1 us
    all_to_all x2, starting transfers between devices, body(): coarse = spread(message)  13.7 us
    ppermute x2, starting transfers between devices, body(): outer_after = lax.ppermute(first_face, 'sub', backward)  9.23 us
    ppermute x2, waiting for transfers between devices, body(): outer_before = lax.ppermute(last_face, 'sub', forward)  9.2 us
    ppermute x4, waiting for transfers between devices, pieces_of(): lax.ppermute(block, GROUP, [((g + k) % group, g) for g in range(group)])  5.96 us
    ppermute x1, waiting for transfers between devices, body(): lax.ppermute(parts[k], GROUP, [(g, (g + k) % group) for g in range(group)])  2.11 us
  transfers between devices with their start and end apart: 13, of which 6 were waited for; matrix products, arithmetic and copies ran while one was open for 0% of the time, Pallas kernels for 23%

profile of v7, /device:TPU:0, one launch (start us, length us, event | category | flops | bytes accessed | tf_op | source)
XLA Modules:
  0.0 99.5 jit_solution(15963805063605416501)
XLA Ops:
  0.6 0.5 collective-permute-start.2
  1.1 0.1 collective-permute-start.3
  1.2 0.4 collective-permute-start.1
  1.7 6.0 %collective-permute-done.1.refs_1_.refs_5_ = bf16[2,48,512]{2,1,0:T(8,128)(2,1)S(1)} collective-permute-done((bf16[2,48,512]{2,1,0:T(8,128)(2,1)}, bf16[2,48,512]{2,1,0:T(8,128)(2,1)S(1)}, u32[]{:S(2)}, u32[]{:S(2)}) %collective-permute-start.1) | collective-permute-done | bytes 98336 | tf_op jit(solution)/shard_map/ppermute | solution.py:406
  7.6 2.3 %open.1 = bf16[16,64,128]{2,1,0:T(8,128)(2,1)} custom-call(bf16[2,48,512]{2,1,0:T(8,128)(2,1)} %bitcast.2, bf16[2,48,512]{2,1,0:T(8,128)(2,1)S(1)} %collective-permute-done.1.refs_1_.refs_5_, bf16[2,1024,128]{2,1,0:T(8,128)(2,1)} %refs_6_.1, s32[2,48]{1,0:T(2,128)} %refs_3_.2), custom_call_target="tpu_custom_call" | custom-call | flops 67108864 | bytes 983424 | tf_op jit(solution)/shard_map/open/pallas_call | solution.py:382
  9.9 8.2 %all-to-all-start = ((bf16[16,64,128]{2,1,0:T(8,128)(2,1)}), bf16[16,64,128]{2,1,0:T(8,128)(2,1)S(1)}, u32[]{:S(2)}, u32[]{:S(2)}) async-start(bf16[16,64,128]{2,1,0:T(8,128)(2,1)} %open.1), calls=%async_computation | async-start | bytes 524288 | tf_op jit(solution)/shard_map/all_to_all | solution.py:438
  18.1 0.1 collective-permute-start
  18.2 0.0 collective-permute-done.2.refs_1_
  18.2 0.0 collective-permute-done.3.refs_3_
  18.2 9.9 %first_image.1 = (bf16[1024,128]{1,0:T(8,128)(2,1)}, f32[1024,128]{1,0:T(8,128)}, f32[1024,128]{1,0:T(8,128)}, bf16[2,128,256]{2,1,0:T(8,128)(2,1)}, bf16[2,128,...) custom-call(bf16[2,512,1024]{2,1,0:T(8,128)(2,1)} %refs_0_.5, ...), custom_call_target="tpu_custom_call" | custom-call | flops 1073741824 | bytes 11291648 | tf_op jit(solution)/shard_map/first_image/pallas_call | solution.py:382
  28.2 0.1 all-to-all-done.refs_2_
  28.3 0.8 copy-done
  29.2 3.2 %order.1 = (bf16[2,96,768]{2,1,0:T(8,128)(2,1)}, f32[2,16,128]{2,1,0:T(8,128)}, bf16[16,48,128]{2,1,0:T(8,128)(2,1)}) custom-call(bf16[96,768]{1,0:T(8,128)(2,1)} %refs_0_.4, bf16[96,768]{1,0:T(8,128)(2,1)S(1)} %collective-permute-done.refs_1_, bf16[16,64,128]{2,1,0:T(8,128)(2,1)S(1)} %all-to-all-done.refs_2_, bf16[128,768]{1,0:T(8,128)(2,1)} %constant.6.clone.refs_3_, ...), custom_call_target="tpu_custom_call" | custom-call | flops 452984832 | bytes 1310720 | tf_op jit(solution)/shard_map/order/pallas_call | solution.py:382
  32.4 6.8 %all-to-all-start.1 = ((bf16[16,48,128]{2,1,0:T(8,128)(2,1)}), bf16[16,48,128]{2,1,0:T(8,128)(2,1)S(1)}, u32[]{:S(2)}, u32[]{:S(2)}) async-start(bf16[16,48,128]{2,1,0:T(8,128)(2,1)} %get-tuple-element.33), calls=%async_computation.1 | async-start | bytes 393216 | tf_op jit(solution)/shard_map/all_to_all | solution.py:472
  39.2 2.0 %picks.1 = (bf16[2,192,768]{2,1,0:T(8,128)(2,1)}, bf16[128,256]{1,0:T(8,128)(2,1)}) custom-call(f32[2,16,128]{2,1,0:T(8,128)} %get-tuple-element.34.refs_0_, s32[2,768]{1,0:T(2,128)} %constant.8.clone.refs_1_, bf16[128,256]{1,0:T(8,128)(2,1)} %get-tuple-element.35.refs_2_), custom_call_target="tpu_custom_call" | custom-call | flops 16777216 | bytes 743424 | tf_op jit(solution)/shard_map/picks/pallas_call | solution.py:382
  41.2 2.0 %collective-permute-start.4 = (bf16[128,256]{1,0:T(8,128)(2,1)}, bf16[128,256]{1,0:T(8,128)(2,1)S(1)}, u32[]{:S(2)}, u32[]{:S(2)}) collective-permute-start(bf16[128,256]{1,0:T(8,128)(2,1)} %get-tuple-element.43), channel_id=1, source_target_pairs={{0,2},{2,4},{4,6},{6,8},{8,10},{10,12},{12,14},{14,16},{16,18},{18... | collective-permute-start | bytes 196616 | tf_op jit(solution)/shard_map/ppermute | solution.py:480
  43.2 3.7 %collective-permute-start.5 = (bf16[128,256]{1,0:T(8,128)(2,1)S(1)}, bf16[128,256]{1,0:T(8,128)(2,1)S(1)}, u32[]{:S(2)}, u32[]{:S(2)}) collective-permute-start(bf16[128,256]{1,0:T(8,128)(2,1)S(1)} %copy-done.1), channel_id=1, source_target_pairs={{2,0},{4,2},{6,4},{8,6},{10,8},{12,10},{14,12},{16,14},{18,16},{20... | collective-permute-start | bytes 196616 | tf_op jit(solution)/shard_map/ppermute | solution.py:462
  46.9 3.4 %collective-permute-done.4.refs_8_.refs_12_.refs_13_ = bf16[128,256]{1,0:T(8,128)(2,1)S(1)} collective-permute-done((bf16[128,256]{1,0:T(8,128)(2,1)}, bf16[128,256]{1,0:T(8,128)(2,1)S(1)}, u32[]{:S(2)}, u32[]{:S(2)}) %collective-permute-start.4) | collective-permute-done | bytes 65568 | tf_op jit(solution)/shard_map/ppermute | solution.py:480
  50.3 0.0 collective-permute-done.5.refs_9_.refs_13_.refs_14_
  50.3 0.0 all-to-all-done.1.refs_0_
  50.3 2.9 %update.1 = (bf16[192,128]{1,0:T(8,128)(2,1)}, bf16[16,48,128]{2,1,0:T(8,128)(2,1)}) custom-call(bf16[16,48,128]{2,1,0:T(8,128)(2,1)S(1)} %all-to-all-done.1.refs_0_, bf16[2,192,768]{2,1,0:T(8,128)(2,1)} %get-tuple-element.36.refs_1_, f32[48,128]{1,0:T(8,128)} %get-tuple-element.37.refs_2_, bf16[2,48,48]{2,1,0:T(8,128)(2,1)} %get-tuple-element.38.refs_3_, ...), custom_call_target="tpu_custom_call" | custom-call | flops 16777216 | bytes 1508352 | tf_op jit(solution)/shard_map/update/pallas_call | solution.py:382
  53.2 5.8 %all-to-all-start.2 = ((bf16[16,48,128]{2,1,0:T(8,128)(2,1)}), bf16[16,48,128]{2,1,0:T(8,128)(2,1)S(1)}, u32[]{:S(2)}, u32[]{:S(2)}) async-start(bf16[16,48,128]{2,1,0:T(8,128)(2,1)} %get-tuple-element.44), calls=%async_computation.2 | async-start | bytes 393216 | tf_op jit(solution)/shard_map/all_to_all | solution.py:489
  59.1 8.7 %second_image.1 = (f32[1024,128]{1,0:T(8,128)}, f32[1024,128]{1,0:T(8,128)}, bf16[2,128,128]{2,1,0:T(8,128)(2,1)}, bf16[2,128,128]{2,1,0:T(8,128)(2,1)}, bf16[12...) custom-call(bf16[2,512,1024]{2,1,0:T(8,128)(2,1)} %refs_0_.5, bf16[2,512,1024]{2,1,0:T(8,128)(2,1)S(1)} %collective-permute-done.2.refs_1_, ...), custom_call_target="tpu_custom_call" | custom-call | flops 1073741824 | bytes 11782144 | tf_op jit(solution)/shard_map/second_image/pallas_call | solution.py:382
  67.8 2.2 %coarse.1 = (bf16[16,48,128]{2,1,0:T(8,128)(2,1)}, bf16[128,128]{1,0:T(8,128)(2,1)}) custom-call(bf16[16,48,128]{2,1,0:T(8,128)(2,1)S(1)} %all-to-all-done.2.refs_0_, bf16[2,96,768]{2,1,0:T(8,128)(2,1)} %get-tuple-element.45.refs_1_, bf16[128,128]{1,0:T(8,128)(2,1)} %get-tuple-element.52.refs_2_), custom_call_target="tpu_custom_call" | custom-call | flops 16777216 | bytes 753664 | tf_op jit(solution)/shard_map/coarse/pallas_call | solution.py:382
  70.0 6.9 %all-to-all-start.3 = ((bf16[16,48,128]{2,1,0:T(8,128)(2,1)}), bf16[16,48,128]{2,1,0:T(8,128)(2,1)S(1)}, u32[]{:S(2)}, u32[]{:S(2)}) async-start(bf16[16,48,128]{2,1,0:T(8,128)(2,1)} %get-tuple-element.53), calls=%async_computation.3 | async-start | bytes 393216 | tf_op jit(solution)/shard_map/all_to_all | solution.py:516
  77.0 5.5 %collective-permute-start.7 = (bf16[128,128]{1,0:T(8,128)(2,1)}, bf16[128,128]{1,0:T(8,128)(2,1)S(1)}, u32[]{:S(2)}, u32[]{:S(2)}) collective-permute-start(bf16[128,128]{1,0:T(8,128)(2,1)} %get-tuple-element.59), channel_id=1, source_target_pairs={{2,0},{4,2},{6,4},{8,6},{10,8},{12,10},{14,12},{16,14},{18,16},{20... | collective-permute-start | bytes 98312 | tf_op jit(solution)/shard_map/ppermute | solution.py:507
  82.5 1.9 %collective-permute-done.7.refs_10_ = bf16[128,128]{1,0:T(8,128)(2,1)S(1)} collective-permute-done((bf16[128,128]{1,0:T(8,128)(2,1)}, bf16[128,128]{1,0:T(8,128)(2,1)S(1)}, u32[]{:S(2)}, u32[]{:S(2)}) %collective-permute-start.7) | collective-permute-done | bytes 32800 | tf_op jit(solution)/shard_map/ppermute | solution.py:507
  84.4 5.8 %collective-permute-done.6.refs_9_ = bf16[128,128]{1,0:T(8,128)(2,1)S(1)} collective-permute-done((bf16[128,128]{1,0:T(8,128)(2,1)}, bf16[128,128]{1,0:T(8,128)(2,1)S(1)}, u32[]{:S(2)}, u32[]{:S(2)}) %collective-permute-start.6) | collective-permute-done | bytes 32800 | tf_op jit(solution)/shard_map/ppermute | solution.py:517
  90.2 4.6 %last.1 = (f32[2,512,128]{2,1,0:T(8,128)}, f32[2,512,128]{2,1,0:T(8,128)}) custom-call(bf16[16,48,128]{2,1,0:T(8,128)(2,1)S(1)} %all-to-all-done.3.refs_0_, bf16[2,192,768]{2,1,0:T(8,128)(2,1)} %get-tuple-element.36.refs_1_, bf16[1024,128]{1,0:T(8,128)(2,1)} %get-tuple-element.46.refs_4_.refs_2_, f32[1024,128]{1,0:T(8,128)} %get-tuple-element.54.refs_3_, ...), custom_call_target="tpu_custom_call" | custom-call | flops 134217728 | bytes 4130816 | tf_op jit(solution)/shard_map/last/pallas_call | solution.py:382
  94.9 0.1 collective-permute-start.8
  94.9 2.1 %collective-permute-done.8.refs_1_ = f32[2,512,128]{2,1,0:T(8,128)S(1)} collective-permute-done((f32[2,512,128]{2,1,0:T(8,128)}, f32[2,512,128]{2,1,0:T(8,128)S(1)}, u32[]{:S(2)}, u32[]{:S(2)}) %collective-permute-start.8) | collective-permute-done | bytes 524320 | tf_op jit(solution)/shard_map/ppermute | solution.py:532
  97.0 2.5 %unpack.1 = (f32[2,512,128]{2,1,0:T(8,128)}, f32[2,512,128]{2,1,0:T(8,128)}) custom-call(f32[2,512,128]{2,1,0:T(8,128)} %get-tuple-element.60.refs_0_, f32[2,512,128]{2,1,0:T(8,128)S(1)} %collective-permute-done.8.refs_1_), custom_call_target="tpu_custom_call" | custom-call | flops 16777216 | bytes 2097152 | tf_op jit(solution)/shard_map/unpack/pallas_call | solution.py:382
  (7 shorter events, 0.0 us)
Async XLA Ops:
  0.6 17.6 %collective-permute-start.2 = (bf16[2,512,1024]{2,1,0:T(8,128)(2,1)}, bf16[2,512,1024]{2,1,0:T(8,128)(2,1)S(1)}, u32[]{:S(2)}, u32[]{:S(2)}) collective-permute-start(bf16[2,512,1024]{2,1,0:T(8,128)(2,1)} %refs_0_.5), channel_id=1, source_target_pairs={{1,0},{0,1},{3,2},{2,3},{5,4},{4,5},{7,6},{6,7},{9,8},{8,9},{11,10... | collective-permute-start | bytes 6291464 | tf_op jit(solution)/shard_map/ppermute | solution.py:406
  1.1 17.1 %collective-permute-start.3 = (bf16[2,512,1024]{2,1,0:T(8,128)(2,1)}, bf16[2,512,1024]{2,1,0:T(8,128)(2,1)}, u32[]{:S(2)}, u32[]{:S(2)}) collective-permute-start(bf16[2,512,1024]{2,1,0:T(8,128)(2,1)} %refs_2_.5), channel_id=1, source_target_pairs={{1,0},{0,1},{3,2},{2,3},{5,4},{4,5},{7,6},{6,7},{9,8},{8,9},{11,10... | collective-permute-start | bytes 6291464 | tf_op jit(solution)/shard_map/ppermute | solution.py:406
  1.2 6.4 %collective-permute-start.1 = (bf16[2,48,512]{2,1,0:T(8,128)(2,1)}, bf16[2,48,512]{2,1,0:T(8,128)(2,1)S(1)}, u32[]{:S(2)}, u32[]{:S(2)}) collective-permute-start(bf16[2,48,512]{2,1,0:T(8,128)(2,1)} %bitcast.1), channel_id=1, source_target_pairs={{1,0},{0,1},{3,2},{2,3},{5,4},{4,5},{7,6},{6,7},{9,8},{8,9},{11,10... | collective-permute-start | bytes 294920 | tf_op jit(solution)/shard_map/ppermute | solution.py:406
  9.9 18.4 %all-to-all-start = ((bf16[16,64,128]{2,1,0:T(8,128)(2,1)}), bf16[16,64,128]{2,1,0:T(8,128)(2,1)S(1)}, u32[]{:S(2)}, u32[]{:S(2)}) async-start(bf16[16,64,128]{2,1,0:T(8,128)(2,1)} %open.1), calls=%async_computation | async-start | bytes 524288 | tf_op jit(solution)/shard_map/all_to_all | solution.py:438
  18.1 10.1 %collective-permute-start = (bf16[96,768]{1,0:T(8,128)(2,1)}, bf16[96,768]{1,0:T(8,128)(2,1)S(1)}, u32[]{:S(2)}, u32[]{:S(2)}) collective-permute-start(bf16[96,768]{1,0:T(8,128)(2,1)} %refs_0_.4), channel_id=1, source_target_pairs={{1,0},{0,1},{3,2},{2,3},{5,4},{4,5},{7,6},{6,7},{9,8},{8,9},{11,10... | collective-permute-start | bytes 442376 | tf_op jit(solution)/shard_map/ppermute | solution.py:406
  28.3 0.8 copy-start
  29.2 14.0 %copy-start.1 = (bf16[128,256]{1,0:T(8,128)(2,1)S(1)}, bf16[128,256]{1,0:T(8,128)(2,1)}, u32[]{:S(2)}) copy-start(bf16[128,256]{1,0:T(8,128)(2,1)} %get-tuple-element.32.refs_5_) | copy-start | bytes 196612
  32.4 17.9 %all-to-all-start.1 = ((bf16[16,48,128]{2,1,0:T(8,128)(2,1)}), bf16[16,48,128]{2,1,0:T(8,128)(2,1)S(1)}, u32[]{:S(2)}, u32[]{:S(2)}) async-start(bf16[16,48,128]{2,1,0:T(8,128)(2,1)} %get-tuple-element.33), calls=%async_computation.1 | async-start | bytes 393216 | tf_op jit(solution)/shard_map/all_to_all | solution.py:472
  41.2 9.1 %collective-permute-start.4 = (bf16[128,256]{1,0:T(8,128)(2,1)}, bf16[128,256]{1,0:T(8,128)(2,1)S(1)}, u32[]{:S(2)}, u32[]{:S(2)}) collective-permute-start(bf16[128,256]{1,0:T(8,128)(2,1)} %get-tuple-element.43), channel_id=1, source_target_pairs={{0,2},{2,4},{4,6},{6,8},{8,10},{10,12},{12,14},{14,16},{16,18},{18... | collective-permute-start | bytes 196616 | tf_op jit(solution)/shard_map/ppermute | solution.py:480
  43.2 7.1 %collective-permute-start.5 = (bf16[128,256]{1,0:T(8,128)(2,1)S(1)}, bf16[128,256]{1,0:T(8,128)(2,1)S(1)}, u32[]{:S(2)}, u32[]{:S(2)}) collective-permute-start(bf16[128,256]{1,0:T(8,128)(2,1)S(1)} %copy-done.1), channel_id=1, source_target_pairs={{2,0},{4,2},{6,4},{8,6},{10,8},{12,10},{14,12},{16,14},{18,16},{20... | collective-permute-start | bytes 196616 | tf_op jit(solution)/shard_map/ppermute | solution.py:462
  53.2 14.5 %all-to-all-start.2 = ((bf16[16,48,128]{2,1,0:T(8,128)(2,1)}), bf16[16,48,128]{2,1,0:T(8,128)(2,1)S(1)}, u32[]{:S(2)}, u32[]{:S(2)}) async-start(bf16[16,48,128]{2,1,0:T(8,128)(2,1)} %get-tuple-element.44), calls=%async_computation.2 | async-start | bytes 393216 | tf_op jit(solution)/shard_map/all_to_all | solution.py:489
  70.0 20.2 %all-to-all-start.3 = ((bf16[16,48,128]{2,1,0:T(8,128)(2,1)}), bf16[16,48,128]{2,1,0:T(8,128)(2,1)S(1)}, u32[]{:S(2)}, u32[]{:S(2)}) async-start(bf16[16,48,128]{2,1,0:T(8,128)(2,1)} %get-tuple-element.53), calls=%async_computation.3 | async-start | bytes 393216 | tf_op jit(solution)/shard_map/all_to_all | solution.py:516
  77.0 7.4 %collective-permute-start.7 = (bf16[128,128]{1,0:T(8,128)(2,1)}, bf16[128,128]{1,0:T(8,128)(2,1)S(1)}, u32[]{:S(2)}, u32[]{:S(2)}) collective-permute-start(bf16[128,128]{1,0:T(8,128)(2,1)} %get-tuple-element.59), channel_id=1, source_target_pairs={{2,0},{4,2},{6,4},{8,6},{10,8},{12,10},{14,12},{16,14},{18,16},{20... | collective-permute-start | bytes 98312 | tf_op jit(solution)/shard_map/ppermute | solution.py:507
  82.5 7.7 %collective-permute-start.6 = (bf16[128,128]{1,0:T(8,128)(2,1)}, bf16[128,128]{1,0:T(8,128)(2,1)S(1)}, u32[]{:S(2)}, u32[]{:S(2)}) collective-permute-start(bf16[128,128]{1,0:T(8,128)(2,1)} %get-tuple-element.58), channel_id=1, source_target_pairs={{0,2},{2,4},{4,6},{6,8},{8,10},{10,12},{12,14},{14,16},{16,18},{18... | collective-permute-start | bytes 98312 | tf_op jit(solution)/shard_map/ppermute | solution.py:517
  94.9 2.2 %collective-permute-start.8 = (f32[2,512,128]{2,1,0:T(8,128)}, f32[2,512,128]{2,1,0:T(8,128)S(1)}, u32[]{:S(2)}, u32[]{:S(2)}) collective-permute-start(f32[2,512,128]{2,1,0:T(8,128)} %get-tuple-element.61), channel_id=1, source_target_pairs={{0,1},{1,0},{2,3},{3,2},{4,5},{5,4},{6,7},{7,6},{8,9},{9,8},{10,11... | collective-permute-start | bytes 1572872 | tf_op jit(solution)/shard_map/ppermute | solution.py:532

commit v8 on v7

--- a/solution.py
+++ b/solution.py
@@ -86,6 +86,16 @@
     return jnp.where(row == rows_of, 1.0, 0.0).astype(BF16)
 
 
+def pick_matrix(z, rows_of):
+    column = jnp.transpose(jnp.broadcast_to(rows_of.astype(F32), (z.face, z.face)))[:, 0:1].astype(jnp.int32)
+    row = lax.broadcasted_iota(jnp.int32, (z.face, z.rows), 1)
+    return jnp.where(row == column, 1.0, 0.0).astype(BF16)
+
+
+def even():
+    return lax.rem(lax.axis_index("sub"), 2) == 0
+
+
 def case_matrix(z, s):
     row = lax.broadcasted_iota(jnp.int32, (z.cases, z.lanes), 0)
     lane = lax.broadcasted_iota(jnp.int32, (z.cases, z.lanes), 1)
@@ -123,12 +133,26 @@
 
 
 def face_rows(z, image_b, rows_ref, s, target):
-    picked = dot_tn(scatter_matrix(z, rows_ref[s : s + 1, :]), image_b).astype(BF16)
+    picked = dot(pick_matrix(z, rows_ref[s : s + 1, :]), image_b).astype(BF16)
     return dot(picked, shift_matrix(z, s, target)).astype(BF16)
 
 
-def sides(z, before, after, outer_before, outer_after, s):
-    return (outer_before if s == 0 else after.at[s - 1]), (outer_after if s == z.subs - 1 else before.at[s + 1])
+def store_faces(z, before, after, first_pair, second_pair):
+    first, last = before[0], after[z.subs - 1]
+    first_pair[...] = jnp.where(even(), last, first)
+    second_pair[...] = jnp.where(even(), first, last)
+
+
+def sides(z, before, after, first_pair, second_pair, s):
+    if s == 0:
+        from_before = jnp.where(even(), second_pair[...], first_pair[...])
+    else:
+        from_before = after[s - 1]
+    if s == z.subs - 1:
+        from_after = jnp.where(even(), first_pair[...], second_pair[...])
+    else:
+        from_after = before[s + 1]
+    return from_before, from_after
 
 
 def shares(z, s, chosen, values, bases):
@@ -151,8 +175,8 @@
     inverse, stiffness = refs[: z.group], refs[z.group : 2 * z.group]
     pieces = refs[2 * z.group : 3 * z.group]
     loads, left_rows, right_rows = refs[3 * z.group : 3 * z.group + 3]
-    load_rows, solved, image, before, after, first_face, last_face = refs[3 * z.group + 3 : 3 * z.group + 10]
-    basis, image_basis, left_t, right_t, inner, start_modes, rounded, basis_t = refs[3 * z.group + 10 :]
+    load_rows, solved, image, before, after, first_pair, second_pair = refs[3 * z.group + 3 : 3 * z.group + 10]
+    basis, image_basis, left_t, right_t, inner, start_modes, rounded, basis_t, both, images = refs[3 * z.group + 10 :]
     join_basis(z, pieces, basis_t)
     packed = dot(loads[0], case_matrix(z, 0))
     for s in range(1, z.subs):
@@ -166,45 +190,45 @@
         rounded[pl.ds(start, z.own), :] = value.astype(BF16)
 
     multiply(z, inverse, load_rows[...], store_solved)
+    solved_b = rounded[...]
     for s in range(z.subs):
         basis[s] = jnp.transpose(basis_t[s].astype(F32)).astype(BF16)
-
-    def store_image(start, value):
-        image[pl.ds(start, z.own), :] = value
-
-    for k in range(z.group):
+        both[s, :, : z.lanes] = solved_b
+        both[s, :, z.lanes : z.lanes + z.modes] = basis[s]
+        both[s, :, z.lanes + z.modes :] = jnp.zeros((z.rows, z.lanes - z.modes), BF16)
+    for k, piece in enumerate(stiffness):
         wait(z.group + k)
-    multiply(z, stiffness, rounded[...], store_image)
-    for s in range(z.subs):
-        for k, piece in enumerate(stiffness):
-            image_basis[s, pl.ds(piece_start(z, k, z.own), z.own), :] = dot(piece[s], basis[s]).astype(BF16)
-    image_b = image[...].astype(BF16)
+        start = piece_start(z, k, z.own)
+        parts = [dot(piece[s], both[s]) for s in range(z.subs)]
+        image[pl.ds(start, z.own), :] = select(z, [part[:, : z.lanes] for part in parts])
+        for s in range(z.subs):
+            images[s, pl.ds(start, z.own), :] = parts[s].astype(BF16)
     left = (load_rows[...].astype(F32) - image[...]).astype(BF16)
     start_modes[...] = select(z, [dot(basis_t[s], left) for s in range(z.subs)])
     for s in range(z.subs):
+        image_basis[s] = images[s, :, z.lanes : z.lanes + z.modes]
         inner[s] = dot(basis_t[s], image_basis[s]).astype(BF16)
         for rows_ref, out, side_t, target in (
             (left_rows, before, left_t, (s - 1) % z.subs),
             (right_rows, after, right_t, (s + 1) % z.subs),
         ):
-            scatter = scatter_matrix(z, rows_ref[s : s + 1, :])
-            side_t[s] = dot(basis_t[s], scatter).astype(BF16)
-            out[s, :, : z.lanes] = face_rows(z, image_b, rows_ref, s, target)
-            out[s, :, z.lanes : z.lanes + z.modes] = dot_tn(scatter, image_basis[s]).astype(BF16)
-            out[s, :, z.lanes + z.modes :] = jnp.zeros((z.face, z.lanes - z.modes), BF16)
-    first_face[...] = before[0]
-    last_face[...] = after[z.subs - 1]
+            pick = pick_matrix(z, rows_ref[s : s + 1, :])
+            side_t[s] = dot_nt(basis_t[s], pick).astype(BF16)
+            picked = dot(pick, images[s]).astype(BF16)
+            out[s, :, : z.lanes] = dot(picked[:, : z.lanes], shift_matrix(z, s, target)).astype(BF16)
+            out[s, :, z.lanes :] = picked[:, z.lanes :]
+    store_faces(z, before, after, first_pair, second_pair)
 
 
 def second_image_kernel(z, wait, *refs):
     inverse, stiffness = refs[: z.group], refs[z.group : 2 * z.group]
     rest = refs[2 * z.group :]
     load_rows, old_image, image_basis, old_solved, basis, chosen = rest[:6]
-    before, after, outer_before, outer_after, left_rows, right_rows = rest[6:12]
-    solved, image, new_before, new_after, first_face, last_face, rounded = rest[12:]
+    before, after, first_got, second_got, left_rows, right_rows = rest[6:12]
+    solved, image, new_before, new_after, first_pair, second_pair, rounded = rest[12:]
     parts = []
     for s in range(z.subs):
-        faces = sides(z, before, after, outer_before, outer_after, s)
+        faces = sides(z, before, after, first_got, second_got, s)
         both = shares(z, s, chosen, faces, faces)
         parts.append(correction(z, s, chosen, image_basis, both, left_rows, right_rows))
     residual = (load_rows[...].astype(F32) - old_image[...] - select(z, parts)).astype(BF16)
@@ -232,8 +256,7 @@
     for s in range(z.subs):
         new_before[s] = face_rows(z, image_b, left_rows, s, (s - 1) % z.subs)
         new_after[s] = face_rows(z, image_b, right_rows, s, (s + 1) % z.subs)
-    first_face[...] = new_before[0]
-    last_face[...] = new_after[z.subs - 1]
+    store_faces(z, new_before, new_after, first_pair, second_pair)
 
 
 def digit_row(shape, row):
@@ -272,13 +295,13 @@
     coarse_rows(z, ordered_inverse, arrived, message)
 
 
-def coarse_kernel(z, arrived, ordered_inverse, last_face, message, face):
+def coarse_kernel(z, arrived, ordered_inverse, pair, message, face):
     coarse_rows(z, ordered_inverse, arrived, message)
-    face[...] = last_face[...]
-
-
-def pick_kernel(z, index, place, last_face, picks, face):
-    face[...] = last_face[...]
+    face[...] = pair[...]
+
+
+def pick_kernel(z, index, place, pair, picks, face):
+    face[...] = pair[...]
     here = lax.axis_index("sub")
     device = lax.broadcasted_iota(jnp.int32, (z.n, z.lanes), 0)
     for t in range(z.subs + 2):
@@ -302,14 +325,14 @@
 
 
 def update_kernel(z, *refs):
-    arrived, picks, start_modes, inner, left_t, right_t, before, after, outer_before, outer_after = refs[:10]
+    arrived, picks, start_modes, inner, left_t, right_t, before, after, first_got, second_got = refs[:10]
     chosen, message = refs[10:]
     rows = picked_rows(z, arrived, picks)
     chosen[...] = rows
     m = z.modes
     parts = []
     for s in range(z.subs):
-        faces = sides(z, before, after, outer_before, outer_after, s)
+        faces = sides(z, before, after, first_got, second_got, s)
         both = shares(z, s, rows, faces, faces)
         total = dot(inner[s], rows[(s + 1) * m : (s + 2) * m])
         parts.append(total + dot(left_t[s], both[0]) + dot(right_t[s], both[1]))
@@ -320,15 +343,15 @@
 
 def last_kernel(z, *refs):
     arrived, picks, load_rows, image, image_basis, solved, basis = refs[:7]
-    before, after, outer_before, outer_after = refs[7:11]
-    base_before, base_after, base_outer_before, base_outer_after, left_rows, right_rows = refs[11:17]
+    before, after, first_got, second_got = refs[7:11]
+    base_before, base_after, base_first, base_second, left_rows, right_rows = refs[11:17]
     *outs, whole = refs[17:]
     chosen = picked_rows(z, arrived, picks)
     m = z.modes
     parts = []
     for s in range(z.subs):
-        values = sides(z, before, after, outer_before, outer_after, s)
-        bases = sides(z, base_before, base_after, base_outer_before, base_outer_after, s)
+        values = sides(z, before, after, first_got, second_got, s)
+        bases = sides(z, base_before, base_after, base_first, base_second, s)
         both = shares(z, s, chosen, values, bases)
         parts.append(correction(z, s, chosen, image_basis, both, left_rows, right_rows))
     whole[0] = solved[...] + select(
@@ -352,12 +375,12 @@
             out[s] = total[:, : z.cases]
 
 
-def call(kernel, outs, operands, flops, scratch=(), late=(), after=(), loose=(), name=None):
+def call(kernel, outs, operands, flops, scratch=(), late=(), loose=(), name=None):
     moved = sum(int(np.prod(x.shape)) * x.dtype.itemsize for x in (*operands, *outs))
     n_in, n_out = len(operands), len(outs)
 
     def whole(*refs):
-        hbm, refs = (*refs[:n_in], *refs[n_in + len(after) :][:n_out]), refs[n_in + len(after) + n_out :]
+        hbm, refs = refs[: n_in + n_out], refs[n_in + n_out :]
         vmem, refs = refs[: n_in + n_out], refs[n_in + n_out :]
         in_sems, out_sems, *rest = refs
         arriving = [pltpu.make_async_copy(hbm[i], vmem[i], in_sems.at[i]) for i in range(n_in)]
@@ -382,7 +405,7 @@
     return pl.pallas_call(
         whole,
         out_shape=[pltpu.HBM(o.shape, o.dtype) for o in outs],
-        in_specs=[*[any_spec if i in loose else hbm_spec for i in range(n_in)], *[any_spec] * len(after)],
+        in_specs=[any_spec if i in loose else hbm_spec for i in range(n_in)],
         out_specs=[hbm_spec] * n_out,
         scratch_shapes=[
             *[pltpu.VMEM(x.shape, x.dtype) for x in (*operands, *outs)],
@@ -393,7 +416,7 @@
         compiler_params=pltpu.CompilerParams(vmem_limit_bytes=VMEM_BYTES),
         cost_estimate=pl.CostEstimate(flops=flops, bytes_accessed=moved, transcendentals=0),
         name=name,
-    )(*placed, *after)
+    )(*placed)
 
 
 def shape(dims, dtype):
@@ -422,8 +445,8 @@
     copies = shape((n, modes, lanes), BF16)
     tall = shape((subs, rows, modes), BF16)
     spread = functools.partial(lax.all_to_all, axis_name="sub", split_axis=0, concat_axis=0)
-    forward = [(i, (i + 1) % n) for i in range(n)]
-    backward = [(target, source) for source, target in forward]
+    first_pairs = [(i, i + 1 if i % 2 == 0 else i - 1) for i in range(n)]
+    second_pairs = [(i, (i + (1 if i % 2 else -1)) % n) for i in range(n)]
     work = 4 * subs * rows * rows * lanes
 
     (message,) = call(
@@ -435,17 +458,17 @@
         loose=range(1, group),
         name="open",
     )
-    restricted = spread(message)
-
     inverse_columns = pieces_of(coarse_inverse, group)
+    message, local_inverse, stiffness = lax.optimization_barrier((message, local_inverse, stiffness))
     inverse_pieces = pieces_of(local_inverse, group)
     stiffness_pieces = pieces_of(stiffness, group)
+    restricted = spread(message)
     arrivals = [*range(1, group), *range(group + 1, 2 * group)]
     faces = shape((subs, face, 2 * lanes), BF16)
     outer = shape((face, 2 * lanes), BF16)
     side = shape((subs, modes, face), BF16)
     (
-        load_rows, solved, image, before, after, first_face, last_face, basis, image_basis, left_t, right_t, inner, start_modes
+        load_rows, solved, image, before, after, first_pair, second_pair, basis, image_basis, left_t, right_t, inner, start_modes
     ) = call(
         functools.partial(first_image_kernel, z),
         [
@@ -454,44 +477,47 @@
         ],
         [*inverse_pieces, *stiffness_pieces, *basis_pieces, loads, left_rows, right_rows],
         work,
-        [pltpu.VMEM((rows, lanes), BF16), pltpu.VMEM((subs, modes, rows), BF16)],
+        [
+            pltpu.VMEM((rows, lanes), BF16), pltpu.VMEM((subs, modes, rows), BF16),
+            pltpu.VMEM((subs, rows, 2 * lanes), BF16), pltpu.VMEM((subs, rows, 2 * lanes), BF16),
+        ],
         late=range(2 * group),
         loose=[*arrivals, *range(2 * group + 1, 3 * group)],
         name="first_image",
     )
-    outer_after = lax.ppermute(first_face, "sub", backward)
+    second_got = lax.ppermute(second_pair, "sub", second_pairs)
+    restricted, second_pair = lax.optimization_barrier((restricted, second_pair))
     ordered_inverse, index, message = call(
         functools.partial(order_kernel, z),
         [shape((subs, z.owned, z.columns), BF16), shape((subs, n, lanes), F32), copies],
         [*inverse_columns, restricted, repeat, own_row],
         2 * z.owned * z.total * z.total,
-        after=[first_face],
         loose=range(1, group + 1),
         name="order",
     )
     coarse = spread(message)
-    picks, last_face = call(
+    picks, first_pair = call(
         functools.partial(pick_kernel, z),
         [shape((subs, (subs + 2) * modes, z.columns), BF16), outer],
-        [index, place, last_face],
+        [index, place, first_pair],
         work // 64,
         name="picks",
     )
-    outer_before = lax.ppermute(last_face, "sub", forward)
+    first_got = lax.ppermute(first_pair, "sub", first_pairs)
     chosen, message = call(
         functools.partial(update_kernel, z),
         [shape(((subs + 2) * modes, lanes), BF16), copies],
-        [coarse, picks, start_modes, inner, left_t, right_t, before, after, outer_before, outer_after],
+        [coarse, picks, start_modes, inner, left_t, right_t, before, after, first_got, second_got],
         work // 64,
         loose=[0, 8, 9],
         name="update",
     )
     restricted = spread(message)
 
-    bases = [before, after, outer_before, outer_after]
+    bases = [before, after, first_got, second_got]
     faces = shape((subs, face, lanes), BF16)
     outer = shape((face, lanes), BF16)
-    solved, image, before, after, first_face, last_face = call(
+    solved, image, before, after, first_pair, second_pair = call(
         functools.partial(second_image_kernel, z),
         [packed_f, packed_f, faces, faces, outer, outer],
         [
@@ -504,23 +530,23 @@
         loose=[*arrivals, 2 * group + 8, 2 * group + 9],
         name="second_image",
     )
-    outer_after = lax.ppermute(first_face, "sub", backward)
-    message, last_face = call(
+    second_got = lax.ppermute(second_pair, "sub", second_pairs)
+    message, first_pair = call(
         functools.partial(coarse_kernel, z),
         [copies, outer],
-        [restricted, ordered_inverse, last_face],
+        [restricted, ordered_inverse, first_pair],
         work // 64,
         loose=[0],
         name="coarse",
     )
     coarse = spread(message)
-    outer_before = lax.ppermute(last_face, "sub", forward)
+    first_got = lax.ppermute(first_pair, "sub", first_pairs)
     parts = call(
         functools.partial(last_kernel, z),
         [shape((2, z.own, lanes), F32)] * group,
         [
             coarse, picks, load_rows, image, image_basis, solved, basis,
-            before, after, outer_before, outer_after, *bases, left_rows, right_rows,
+            before, after, first_got, second_got, *bases, left_rows, right_rows,
         ],
         work // 8,
         [pltpu.VMEM((2, rows, lanes), F32)],

time: 100 us -> 90.7 us (0.907)
  waiting for transfers between devices: 19.3 us -> 12.1 us
    ppermute x4, waiting for transfers between devices: 5.96 us -> 1.16 us  [pieces_of(): lax.ppermute(block, GROUP, [((g + k) % group, g) for g in range(group)])]
    ppermute x4, waiting for transfers between devices: 11.1 us -> 7.82 us  [the longest x2 7.36 us: body(): second_got = lax.ppermute(second_pair, 'sub', second_pairs)]
  transfers between devices with their start and end apart: 13 -> 13, of which waited for: 6 -> 6; matrix products, arithmetic and copies ran while one was open for 0% -> 0% of each run, Pallas kernels for 23% -> 22%
where the time goes in v8:
time: 90.7 us; the launch traced here: 90 us
  starting transfers between devices  39.6 us (44%)
  Pallas kernels  37.6 us (41%)
  waiting for transfers between devices  12.1 us (13%)
    pallas_call x9, Pallas kernels, call(): pl.pallas_call(whole, out_shape=[pltpu.HBM(o.shape, o.dtype) for o in out...  37.6 us
    all_to_all x2, starting transfers between devices, body(): restricted = spread(message)  13.8 us
    all_to_all x2, starting transfers between devices, body(): coarse = spread(message)  12.9 us
    ppermute x2, starting transfers between devices, body(): second_got = lax.ppermute(second_pair, 'sub', second_pairs)  9.69 us
    ppermute x2, waiting for transfers between devices, body(): second_got = lax.ppermute(second_pair, 'sub', second_pairs)  7.36 us
    ppermute x1, waiting for transfers between devices, body(): lax.ppermute(parts[k], GROUP, [(g, (g + k) % group) for g in range(group)])  2.11 us
    ppermute x2, starting transfers between devices, body(): first_got = lax.ppermute(first_pair, 'sub', first_pairs)  1.99 us
  transfers between devices with their start and end apart: 13, of which 6 were waited for; matrix products, arithmetic and copies ran while one was open for 0% of the time, Pallas kernels for 22%

profile of v8, /device:TPU:0, one launch (start us, length us, event | category | flops | bytes accessed | tf_op | source)
XLA Modules:
  0.0 90.0 jit_solution(1936804527491894563)
XLA Ops:
  0.6 0.5 collective-permute-start.1
  1.1 1.2 %collective-permute-done.1.refs_1_.refs_5_ = bf16[2,48,512]{2,1,0:T(8,128)(2,1)S(1)} collective-permute-done((bf16[2,48,512]{2,1,0:T(8,128)(2,1)}, bf16[2,48,512]{2,1,0:T(8,128)(2,1)S(1)}, u32[]{:S(2)}, u32[]{:S(2)}) %collective-permute-start.1) | collective-permute-done | bytes 98336 | tf_op jit(solution)/shard_map/ppermute | solution.py:429
  2.3 2.3 %open.1 = bf16[16,64,128]{2,1,0:T(8,128)(2,1)} custom-call(bf16[2,48,512]{2,1,0:T(8,128)(2,1)} %bitcast.2, bf16[2,48,512]{2,1,0:T(8,128)(2,1)S(1)} %collective-permute-done.1.refs_1_.refs_5_, bf16[2,1024,128]{2,1,0:T(8,128)(2,1)} %refs_6_.1, s32[2,48]{1,0:T(2,128)} %refs_3_.2), custom_call_target="tpu_custom_call" | custom-call | flops 67108864 | bytes 983424 | tf_op jit(solution)/shard_map/open/pallas_call | solution.py:405
  4.6 0.4 collective-permute-start.2
  5.0 0.1 collective-permute-start.3
  5.2 8.2 %all-to-all-start = ((bf16[16,64,128]{2,1,0:T(8,128)(2,1)}), bf16[16,64,128]{2,1,0:T(8,128)(2,1)S(1)}, u32[]{:S(2)}, u32[]{:S(2)}) async-start(bf16[16,64,128]{2,1,0:T(8,128)(2,1)} %open.1), calls=%async_computation | async-start | bytes 524288 | tf_op jit(solution)/shard_map/all_to_all | solution.py:465
  13.4 0.1 collective-permute-start
  13.5 0.0 collective-permute-done.3.refs_3_
  13.5 9.1 %first_image.1 = (bf16[1024,128]{1,0:T(8,128)(2,1)}, f32[1024,128]{1,0:T(8,128)}, f32[1024,128]{1,0:T(8,128)}, bf16[2,128,256]{2,1,0:T(8,128)(2,1)}, bf16[2,128,...) custom-call(bf16[2,512,1024]{2,1,0:T(8,128)(2,1)} %refs_0_.3, ...), custom_call_target="tpu_custom_call" | custom-call | flops 1073741824 | bytes 11291648 | tf_op jit(solution)/shard_map/first_image/pallas_call | solution.py:405
  22.6 1.0 %all-to-all-done.refs_2_ = bf16[16,64,128]{2,1,0:T(8,128)(2,1)S(1)} async-done(((bf16[16,64,128]{2,1,0:T(8,128)(2,1)}), bf16[16,64,128]{2,1,0:T(8,128)(2,1)S(1)}, u32[]{:S(2)}, u32[]{:S(2)}) %all-to-all-start) | async-done | bytes 262176 | tf_op jit(solution)/shard_map/all_to_all | solution.py:465
  23.6 0.0 collective-permute-done.refs_1_
  23.6 3.2 %order.1 = (bf16[2,96,768]{2,1,0:T(8,128)(2,1)}, f32[2,16,128]{2,1,0:T(8,128)}, bf16[16,48,128]{2,1,0:T(8,128)(2,1)}) custom-call(bf16[96,768]{1,0:T(8,128)(2,1)} %refs_0_.2, bf16[96,768]{1,0:T(8,128)(2,1)S(1)} %collective-permute-done.refs_1_, bf16[16,64,128]{2,1,0:T(8,128)(2,1)S(1)} %all-to-all-done.refs_2_, bf16[128,768]{1,0:T(8,128)(2,1)} %constant.6.clone.refs_3_, ...), custom_call_target="tpu_custom_call" | custom-call | flops 452984832 | bytes 1310720 | tf_op jit(solution)/shard_map/order/pallas_call | solution.py:405
  26.8 6.0 %all-to-all-start.1 = ((bf16[16,48,128]{2,1,0:T(8,128)(2,1)}), bf16[16,48,128]{2,1,0:T(8,128)(2,1)S(1)}, u32[]{:S(2)}, u32[]{:S(2)}) async-start(bf16[16,48,128]{2,1,0:T(8,128)(2,1)} %get-tuple-element.41), calls=%async_computation.1 | async-start | bytes 393216 | tf_op jit(solution)/shard_map/all_to_all | solution.py:498
  32.8 2.1 %picks.1 = (bf16[2,192,768]{2,1,0:T(8,128)(2,1)}, bf16[128,256]{1,0:T(8,128)(2,1)}) custom-call(f32[2,16,128]{2,1,0:T(8,128)} %get-tuple-element.42.refs_0_, s32[2,768]{1,0:T(2,128)} %constant.8.clone.refs_1_, bf16[128,256]{1,0:T(8,128)(2,1)} %get-tuple-element.43.refs_2_), custom_call_target="tpu_custom_call" | custom-call | flops 16777216 | bytes 743424 | tf_op jit(solution)/shard_map/picks/pallas_call | solution.py:405
  34.9 2.0 %collective-permute-start.4 = (bf16[128,256]{1,0:T(8,128)(2,1)}, bf16[128,256]{1,0:T(8,128)(2,1)S(1)}, u32[]{:S(2)}, u32[]{:S(2)}) collective-permute-start(bf16[128,256]{1,0:T(8,128)(2,1)} %get-tuple-element.51), channel_id=1, source_target_pairs={{0,2},{2,0},{4,6},{6,4},{8,10},{10,8},{12,14},{14,12},{16,18},{18,... | collective-permute-start | bytes 196616 | tf_op jit(solution)/shard_map/ppermute | solution.py:506
  36.8 4.2 %collective-permute-start.5 = (bf16[128,256]{1,0:T(8,128)(2,1)S(1)}, bf16[128,256]{1,0:T(8,128)(2,1)S(1)}, u32[]{:S(2)}, u32[]{:S(2)}) collective-permute-start(bf16[128,256]{1,0:T(8,128)(2,1)S(1)} %copy-done), channel_id=1, source_target_pairs={{0,30},{2,4},{4,2},{6,8},{8,6},{10,12},{12,10},{14,16},{16,14},{18... | collective-permute-start | bytes 196616 | tf_op jit(solution)/shard_map/ppermute | solution.py:488
  41.0 0.0 collective-permute-done.4.refs_8_.refs_12_.refs_13_
  41.0 3.7 %collective-permute-done.5.refs_9_.refs_13_.refs_14_ = bf16[128,256]{1,0:T(8,128)(2,1)S(1)} collective-permute-done((bf16[128,256]{1,0:T(8,128)(2,1)S(1)}, bf16[128,256]{1,0:T(8,128)(2,1)S(1)}, u32[]{:S(2)}, u32[]{:S(2)}) %collective-permute-start.5) | collective-permute-done | bytes 65568 | tf_op jit(solution)/shard_map/ppermute | solution.py:488
  44.7 2.9 %update.1 = (bf16[192,128]{1,0:T(8,128)(2,1)}, bf16[16,48,128]{2,1,0:T(8,128)(2,1)}) custom-call(bf16[16,48,128]{2,1,0:T(8,128)(2,1)S(1)} %all-to-all-done.1.refs_0_, bf16[2,192,768]{2,1,0:T(8,128)(2,1)} %get-tuple-element.44.refs_1_, f32[48,128]{1,0:T(8,128)} %get-tuple-element.45.refs_2_, bf16[2,48,48]{2,1,0:T(8,128)(2,1)} %get-tuple-element.46.refs_3_, ...), custom_call_target="tpu_custom_call" | custom-call | flops 16777216 | bytes 1508352 | tf_op jit(solution)/shard_map/update/pallas_call | solution.py:405
  47.6 5.6 %all-to-all-start.2 = ((bf16[16,48,128]{2,1,0:T(8,128)(2,1)}), bf16[16,48,128]{2,1,0:T(8,128)(2,1)S(1)}, u32[]{:S(2)}, u32[]{:S(2)}) async-start(bf16[16,48,128]{2,1,0:T(8,128)(2,1)} %get-tuple-element.52), calls=%async_computation.2 | async-start | bytes 393216 | tf_op jit(solution)/shard_map/all_to_all | solution.py:515
  53.2 8.7 %second_image.1 = (f32[1024,128]{1,0:T(8,128)}, f32[1024,128]{1,0:T(8,128)}, bf16[2,128,128]{2,1,0:T(8,128)(2,1)}, bf16[2,128,128]{2,1,0:T(8,128)(2,1)}, bf16[12...) custom-call(bf16[2,512,1024]{2,1,0:T(8,128)(2,1)} %refs_0_.3, bf16[2,512,1024]{2,1,0:T(8,128)(2,1)S(1)} %collective-permute-done.2.refs_1_, ...), custom_call_target="tpu_custom_call" | custom-call | flops 1073741824 | bytes 11782144 | tf_op jit(solution)/shard_map/second_image/pallas_call | solution.py:405
  61.9 2.2 %coarse.1 = (bf16[16,48,128]{2,1,0:T(8,128)(2,1)}, bf16[128,128]{1,0:T(8,128)(2,1)}) custom-call(bf16[16,48,128]{2,1,0:T(8,128)(2,1)S(1)} %all-to-all-done.2.refs_0_, bf16[2,96,768]{2,1,0:T(8,128)(2,1)} %get-tuple-element.53.refs_1_, bf16[128,128]{1,0:T(8,128)(2,1)} %get-tuple-element.60.refs_2_), custom_call_target="tpu_custom_call" | custom-call | flops 16777216 | bytes 753664 | tf_op jit(solution)/shard_map/coarse/pallas_call | solution.py:405
  64.1 6.9 %all-to-all-start.3 = ((bf16[16,48,128]{2,1,0:T(8,128)(2,1)}), bf16[16,48,128]{2,1,0:T(8,128)(2,1)S(1)}, u32[]{:S(2)}, u32[]{:S(2)}) async-start(bf16[16,48,128]{2,1,0:T(8,128)(2,1)} %get-tuple-element.61), calls=%async_computation.3 | async-start | bytes 393216 | tf_op jit(solution)/shard_map/all_to_all | solution.py:542
  71.1 5.5 %collective-permute-start.7 = (bf16[128,128]{1,0:T(8,128)(2,1)}, bf16[128,128]{1,0:T(8,128)(2,1)S(1)}, u32[]{:S(2)}, u32[]{:S(2)}) collective-permute-start(bf16[128,128]{1,0:T(8,128)(2,1)} %get-tuple-element.67), channel_id=1, source_target_pairs={{0,30},{2,4},{4,2},{6,8},{8,6},{10,12},{12,10},{14,16},{16,14},{18... | collective-permute-start | bytes 98312 | tf_op jit(solution)/shard_map/ppermute | solution.py:533
  76.6 0.0 collective-permute-start.6
  76.6 3.7 %collective-permute-done.7.refs_10_ = bf16[128,128]{1,0:T(8,128)(2,1)S(1)} collective-permute-done((bf16[128,128]{1,0:T(8,128)(2,1)}, bf16[128,128]{1,0:T(8,128)(2,1)S(1)}, u32[]{:S(2)}, u32[]{:S(2)}) %collective-permute-start.7) | collective-permute-done | bytes 32800 | tf_op jit(solution)/shard_map/ppermute | solution.py:533
  80.3 0.5 collective-permute-done.6.refs_9_
  80.7 0.0 all-to-all-done.3.refs_0_
  80.7 4.6 %last.1 = (f32[2,512,128]{2,1,0:T(8,128)}, f32[2,512,128]{2,1,0:T(8,128)}) custom-call(bf16[16,48,128]{2,1,0:T(8,128)(2,1)S(1)} %all-to-all-done.3.refs_0_, bf16[2,192,768]{2,1,0:T(8,128)(2,1)} %get-tuple-element.44.refs_1_, bf16[1024,128]{1,0:T(8,128)(2,1)} %get-tuple-element.54.refs_4_.refs_2_, f32[1024,128]{1,0:T(8,128)} %get-tuple-element.62.refs_3_, ...), custom_call_target="tpu_custom_call" | custom-call | flops 134217728 | bytes 4130816 | tf_op jit(solution)/shard_map/last/pallas_call | solution.py:405
  85.4 0.1 collective-permute-start.8
  85.4 2.1 %collective-permute-done.8.refs_1_ = f32[2,512,128]{2,1,0:T(8,128)S(1)} collective-permute-done((f32[2,512,128]{2,1,0:T(8,128)}, f32[2,512,128]{2,1,0:T(8,128)S(1)}, u32[]{:S(2)}, u32[]{:S(2)}) %collective-permute-start.8) | collective-permute-done | bytes 524320 | tf_op jit(solution)/shard_map/ppermute | solution.py:558
  87.5 2.5 %unpack.1 = (f32[2,512,128]{2,1,0:T(8,128)}, f32[2,512,128]{2,1,0:T(8,128)}) custom-call(f32[2,512,128]{2,1,0:T(8,128)} %get-tuple-element.68.refs_0_, f32[2,512,128]{2,1,0:T(8,128)S(1)} %collective-permute-done.8.refs_1_), custom_call_target="tpu_custom_call" | custom-call | flops 16777216 | bytes 2097152 | tf_op jit(solution)/shard_map/unpack/pallas_call | solution.py:405
  (5 shorter events, 0.0 us)
Async XLA Ops:
  0.6 1.7 %collective-permute-start.1 = (bf16[2,48,512]{2,1,0:T(8,128)(2,1)}, bf16[2,48,512]{2,1,0:T(8,128)(2,1)S(1)}, u32[]{:S(2)}, u32[]{:S(2)}) collective-permute-start(bf16[2,48,512]{2,1,0:T(8,128)(2,1)} %bitcast.1), channel_id=1, source_target_pairs={{1,0},{0,1},{3,2},{2,3},{5,4},{4,5},{7,6},{6,7},{9,8},{8,9},{11,10... | collective-permute-start | bytes 294920 | tf_op jit(solution)/shard_map/ppermute | solution.py:429
  4.6 8.9 %collective-permute-start.2 = (bf16[2,512,1024]{2,1,0:T(8,128)(2,1)}, bf16[2,512,1024]{2,1,0:T(8,128)(2,1)S(1)}, u32[]{:S(2)}, u32[]{:S(2)}) collective-permute-start(bf16[2,512,1024]{2,1,0:T(8,128)(2,1)} %refs_0_.3), channel_id=1, source_target_pairs={{1,0},{0,1},{3,2},{2,3},{5,4},{4,5},{7,6},{6,7},{9,8},{8,9},{11,10... | collective-permute-start | bytes 6291464 | tf_op jit(solution)/shard_map/ppermute | solution.py:429
  5.0 8.5 %collective-permute-start.3 = (bf16[2,512,1024]{2,1,0:T(8,128)(2,1)}, bf16[2,512,1024]{2,1,0:T(8,128)(2,1)}, u32[]{:S(2)}, u32[]{:S(2)}) collective-permute-start(bf16[2,512,1024]{2,1,0:T(8,128)(2,1)} %refs_2_.3), channel_id=1, source_target_pairs={{1,0},{0,1},{3,2},{2,3},{5,4},{4,5},{7,6},{6,7},{9,8},{8,9},{11,10... | collective-permute-start | bytes 6291464 | tf_op jit(solution)/shard_map/ppermute | solution.py:429
  5.2 18.4 %all-to-all-start = ((bf16[16,64,128]{2,1,0:T(8,128)(2,1)}), bf16[16,64,128]{2,1,0:T(8,128)(2,1)S(1)}, u32[]{:S(2)}, u32[]{:S(2)}) async-start(bf16[16,64,128]{2,1,0:T(8,128)(2,1)} %open.1), calls=%async_computation | async-start | bytes 524288 | tf_op jit(solution)/shard_map/all_to_all | solution.py:465
  13.4 10.2 %collective-permute-start = (bf16[96,768]{1,0:T(8,128)(2,1)}, bf16[96,768]{1,0:T(8,128)(2,1)S(1)}, u32[]{:S(2)}, u32[]{:S(2)}) collective-permute-start(bf16[96,768]{1,0:T(8,128)(2,1)} %refs_0_.2), channel_id=1, source_target_pairs={{1,0},{0,1},{3,2},{2,3},{5,4},{4,5},{7,6},{6,7},{9,8},{8,9},{11,10... | collective-permute-start | bytes 442376 | tf_op jit(solution)/shard_map/ppermute | solution.py:429
  22.6 14.3 %copy-start = (bf16[128,256]{1,0:T(8,128)(2,1)S(1)}, bf16[128,256]{1,0:T(8,128)(2,1)}, u32[]{:S(2)}) copy-start(bf16[128,256]{1,0:T(8,128)(2,1)} %get-tuple-element.39) | copy-start | bytes 196612
  26.8 17.9 %all-to-all-start.1 = ((bf16[16,48,128]{2,1,0:T(8,128)(2,1)}), bf16[16,48,128]{2,1,0:T(8,128)(2,1)S(1)}, u32[]{:S(2)}, u32[]{:S(2)}) async-start(bf16[16,48,128]{2,1,0:T(8,128)(2,1)} %get-tuple-element.41), calls=%async_computation.1 | async-start | bytes 393216 | tf_op jit(solution)/shard_map/all_to_all | solution.py:498
  34.9 6.2 %collective-permute-start.4 = (bf16[128,256]{1,0:T(8,128)(2,1)}, bf16[128,256]{1,0:T(8,128)(2,1)S(1)}, u32[]{:S(2)}, u32[]{:S(2)}) collective-permute-start(bf16[128,256]{1,0:T(8,128)(2,1)} %get-tuple-element.51), channel_id=1, source_target_pairs={{0,2},{2,0},{4,6},{6,4},{8,10},{10,8},{12,14},{14,12},{16,18},{18,... | collective-permute-start | bytes 196616 | tf_op jit(solution)/shard_map/ppermute | solution.py:506
  36.8 7.9 %collective-permute-start.5 = (bf16[128,256]{1,0:T(8,128)(2,1)S(1)}, bf16[128,256]{1,0:T(8,128)(2,1)S(1)}, u32[]{:S(2)}, u32[]{:S(2)}) collective-permute-start(bf16[128,256]{1,0:T(8,128)(2,1)S(1)} %copy-done), channel_id=1, source_target_pairs={{0,30},{2,4},{4,2},{6,8},{8,6},{10,12},{12,10},{14,16},{16,14},{18... | collective-permute-start | bytes 196616 | tf_op jit(solution)/shard_map/ppermute | solution.py:488
  47.6 14.2 %all-to-all-start.2 = ((bf16[16,48,128]{2,1,0:T(8,128)(2,1)}), bf16[16,48,128]{2,1,0:T(8,128)(2,1)S(1)}, u32[]{:S(2)}, u32[]{:S(2)}) async-start(bf16[16,48,128]{2,1,0:T(8,128)(2,1)} %get-tuple-element.52), calls=%async_computation.2 | async-start | bytes 393216 | tf_op jit(solution)/shard_map/all_to_all | solution.py:515
  64.1 16.6 %all-to-all-start.3 = ((bf16[16,48,128]{2,1,0:T(8,128)(2,1)}), bf16[16,48,128]{2,1,0:T(8,128)(2,1)S(1)}, u32[]{:S(2)}, u32[]{:S(2)}) async-start(bf16[16,48,128]{2,1,0:T(8,128)(2,1)} %get-tuple-element.61), calls=%async_computation.3 | async-start | bytes 393216 | tf_op jit(solution)/shard_map/all_to_all | solution.py:542
  71.1 9.2 %collective-permute-start.7 = (bf16[128,128]{1,0:T(8,128)(2,1)}, bf16[128,128]{1,0:T(8,128)(2,1)S(1)}, u32[]{:S(2)}, u32[]{:S(2)}) collective-permute-start(bf16[128,128]{1,0:T(8,128)(2,1)} %get-tuple-element.67), channel_id=1, source_target_pairs={{0,30},{2,4},{4,2},{6,8},{8,6},{10,12},{12,10},{14,16},{16,14},{18... | collective-permute-start | bytes 98312 | tf_op jit(solution)/shard_map/ppermute | solution.py:533
  76.6 4.1 %collective-permute-start.6 = (bf16[128,128]{1,0:T(8,128)(2,1)}, bf16[128,128]{1,0:T(8,128)(2,1)S(1)}, u32[]{:S(2)}, u32[]{:S(2)}) collective-permute-start(bf16[128,128]{1,0:T(8,128)(2,1)} %get-tuple-element.66), channel_id=1, source_target_pairs={{0,2},{2,0},{4,6},{6,4},{8,10},{10,8},{12,14},{14,12},{16,18},{18,... | collective-permute-start | bytes 98312 | tf_op jit(solution)/shard_map/ppermute | solution.py:543
  85.4 2.2 %collective-permute-start.8 = (f32[2,512,128]{2,1,0:T(8,128)}, f32[2,512,128]{2,1,0:T(8,128)S(1)}, u32[]{:S(2)}, u32[]{:S(2)}) collective-permute-start(f32[2,512,128]{2,1,0:T(8,128)} %get-tuple-element.69), channel_id=1, source_target_pairs={{0,1},{1,0},{2,3},{3,2},{4,5},{5,4},{6,7},{7,6},{8,9},{9,8},{10,11... | collective-permute-start | bytes 1572872 | tf_op jit(solution)/shard_map/ppermute | solution.py:558

commit v9 on v8

--- a/solution.py
+++ b/solution.py
@@ -165,10 +165,21 @@
     return out
 
 
-def correction(z, s, chosen, image_basis, both, left_rows, right_rows):
-    total = dot(image_basis[s], chosen[(s + 1) * z.modes : (s + 2) * z.modes])
-    total = total + dot(scatter_matrix(z, left_rows[s : s + 1, :]), both[0])
-    return total + dot(scatter_matrix(z, right_rows[s : s + 1, :]), both[1])
+def corrected(z, chosen, tall, both, left_rows, right_rows):
+    images, steps = [], []
+    m, at = z.modes, z.lanes // 2
+    for s in range(z.subs):
+        own = chosen[(s + 1) * m : (s + 2) * m]
+        none = jnp.zeros((at - m, z.lanes), BF16)
+        nil = jnp.zeros((at, z.lanes), BF16)
+        left = jnp.concatenate([tall[s], scatter_matrix(z, left_rows[s : s + 1, :])], axis=1)
+        right = scatter_matrix(z, right_rows[s : s + 1, :])
+        image = jnp.concatenate([own, none, nil, both[s][0]], axis=0)
+        step = jnp.concatenate([nil, own, none, jnp.zeros((z.face, z.lanes), BF16)], axis=0)
+        total = dot(left, jnp.concatenate([image, step], axis=1))
+        images.append(total[:, : z.lanes] + dot(right, both[s][1]))
+        steps.append(total[:, z.lanes :])
+    return select(z, steps), select(z, images)
 
 
 def first_image_kernel(z, wait, *refs):
@@ -176,7 +187,7 @@
     pieces = refs[2 * z.group : 3 * z.group]
     loads, left_rows, right_rows = refs[3 * z.group : 3 * z.group + 3]
     load_rows, solved, image, before, after, first_pair, second_pair = refs[3 * z.group + 3 : 3 * z.group + 10]
-    basis, image_basis, left_t, right_t, inner, start_modes, rounded, basis_t, both, images = refs[3 * z.group + 10 :]
+    tall, left_t, right_t, inner, start_modes, rounded, basis_t, both, images = refs[3 * z.group + 10 :]
     join_basis(z, pieces, basis_t)
     packed = dot(loads[0], case_matrix(z, 0))
     for s in range(1, z.subs):
@@ -191,10 +202,13 @@
 
     multiply(z, inverse, load_rows[...], store_solved)
     solved_b = rounded[...]
-    for s in range(z.subs):
-        basis[s] = jnp.transpose(basis_t[s].astype(F32)).astype(BF16)
+    half = z.lanes // 2
+    for s in range(z.subs):
+        basis = jnp.transpose(basis_t[s].astype(F32)).astype(BF16)
+        tall[s, :, half : half + z.modes] = basis
+        tall[s, :, half + z.modes :] = jnp.zeros((z.rows, half - z.modes), BF16)
         both[s, :, : z.lanes] = solved_b
-        both[s, :, z.lanes : z.lanes + z.modes] = basis[s]
+        both[s, :, z.lanes : z.lanes + z.modes] = basis
         both[s, :, z.lanes + z.modes :] = jnp.zeros((z.rows, z.lanes - z.modes), BF16)
     for k, piece in enumerate(stiffness):
         wait(z.group + k)
@@ -206,8 +220,9 @@
     left = (load_rows[...].astype(F32) - image[...]).astype(BF16)
     start_modes[...] = select(z, [dot(basis_t[s], left) for s in range(z.subs)])
     for s in range(z.subs):
-        image_basis[s] = images[s, :, z.lanes : z.lanes + z.modes]
-        inner[s] = dot(basis_t[s], image_basis[s]).astype(BF16)
+        image_basis = images[s, :, z.lanes :]
+        tall[s, :, :half] = image_basis[:, :half]
+        inner[s] = dot(basis_t[s], image_basis)[:, : z.modes].astype(BF16)
         for rows_ref, out, side_t, target in (
             (left_rows, before, left_t, (s - 1) % z.subs),
             (right_rows, after, right_t, (s + 1) % z.subs),
@@ -223,19 +238,16 @@
 def second_image_kernel(z, wait, *refs):
     inverse, stiffness = refs[: z.group], refs[z.group : 2 * z.group]
     rest = refs[2 * z.group :]
-    load_rows, old_image, image_basis, old_solved, basis, chosen = rest[:6]
-    before, after, first_got, second_got, left_rows, right_rows = rest[6:12]
-    solved, image, new_before, new_after, first_pair, second_pair, rounded = rest[12:]
-    parts = []
+    load_rows, old_image, tall, old_solved, chosen = rest[:5]
+    before, after, first_got, second_got, left_rows, right_rows = rest[5:11]
+    solved, remaining, new_before, new_after, first_pair, second_pair, rounded, image = rest[11:]
+    both = []
     for s in range(z.subs):
         faces = sides(z, before, after, first_got, second_got, s)
-        both = shares(z, s, chosen, faces, faces)
-        parts.append(correction(z, s, chosen, image_basis, both, left_rows, right_rows))
-    residual = (load_rows[...].astype(F32) - old_image[...] - select(z, parts)).astype(BF16)
-    m = z.modes
-    solved[...] = old_solved[...] + select(
-        z, [dot(basis[s], chosen[(s + 1) * m : (s + 2) * m]) for s in range(z.subs)]
-    )
+        both.append(shares(z, s, chosen, faces, faces))
+    step, added = corrected(z, chosen, tall, both, left_rows, right_rows)
+    residual = (load_rows[...].astype(F32) - old_image[...] - added).astype(BF16)
+    solved[...] = old_solved[...] + step
     for k in range(z.group):
         wait(k)
 
@@ -247,12 +259,14 @@
     multiply(z, inverse, residual, store_solved)
 
     def store_image(start, value):
-        image[pl.ds(start, z.own), :] = value
+        place = pl.ds(start, z.own)
+        remaining[place, :] = load_rows[place, :].astype(F32) - value
+        image[place, :] = value.astype(BF16)
 
     for k in range(z.group):
         wait(z.group + k)
     multiply(z, stiffness, rounded[...], store_image)
-    image_b = image[...].astype(BF16)
+    image_b = image[...]
     for s in range(z.subs):
         new_before[s] = face_rows(z, image_b, left_rows, s, (s - 1) % z.subs)
         new_after[s] = face_rows(z, image_b, right_rows, s, (s + 1) % z.subs)
@@ -273,12 +287,13 @@
 
 def order_kernel(z, *refs):
     blocks = refs[: z.group]
-    arrived, repeat, own_row, ordered_inverse, index, message = refs[z.group :]
+    arrived, repeat, own_row, place, ordered_inverse, picks, message = refs[z.group :]
     digits = arrived[:, z.modes :, :].astype(F32)
+    index = []
     for s in range(z.subs):
         high = jnp.sum(jnp.where(digit_row(digits.shape, 2 * s), digits, 0.0), axis=1)
         low = jnp.sum(jnp.where(digit_row(digits.shape, 2 * s + 1), digits, 0.0), axis=1)
-        index[s] = high * DIGIT + low
+        index.append(high * DIGIT + low)
         spread = dot(high.astype(BF16), repeat[...]) * DIGIT + dot(low.astype(BF16), repeat[...])
         places = jnp.sum(spread * own_row[...], axis=0, keepdims=True).astype(jnp.int32)
         for at in range(0, z.columns, 768):
@@ -293,15 +308,6 @@
                     total = total + dot(block[:, first : first + deep], hot)
             ordered_inverse[s, :, at : at + wide] = total.astype(BF16)
     coarse_rows(z, ordered_inverse, arrived, message)
-
-
-def coarse_kernel(z, arrived, ordered_inverse, pair, message, face):
-    coarse_rows(z, ordered_inverse, arrived, message)
-    face[...] = pair[...]
-
-
-def pick_kernel(z, index, place, pair, picks, face):
-    face[...] = pair[...]
     here = lax.axis_index("sub")
     device = lax.broadcasted_iota(jnp.int32, (z.n, z.lanes), 0)
     for t in range(z.subs + 2):
@@ -312,11 +318,14 @@
         else:
             s, owner = t - 1, here
         row = jnp.sum(jnp.where(device == owner, index[s], 0.0), axis=0, keepdims=True)
-        column = jnp.transpose(jnp.broadcast_to(row, (z.lanes, z.lanes)))[: z.modes, 0:1]
-        column = column.astype(jnp.int32)
+        column = jnp.transpose(jnp.broadcast_to(row, (z.lanes, z.lanes)))[: z.modes, 0:1].astype(jnp.int32)
         for h in range(z.subs):
             hit = column == place[h : h + 1, :]
             picks[h, t * z.modes : (t + 1) * z.modes, :] = jnp.where(hit, 1.0, 0.0).astype(BF16)
+
+
+def coarse_kernel(z, arrived, ordered_inverse, message):
+    coarse_rows(z, ordered_inverse, arrived, message)
 
 
 def picked_rows(z, arrived, picks):
@@ -342,22 +351,19 @@
 
 
 def last_kernel(z, *refs):
-    arrived, picks, load_rows, image, image_basis, solved, basis = refs[:7]
-    before, after, first_got, second_got = refs[7:11]
-    base_before, base_after, base_first, base_second, left_rows, right_rows = refs[11:17]
-    *outs, whole = refs[17:]
+    arrived, picks, remaining, solved, tall = refs[:5]
+    before, after, first_got, second_got = refs[5:9]
+    base_before, base_after, base_first, base_second, left_rows, right_rows = refs[9:15]
+    *outs, whole = refs[15:]
     chosen = picked_rows(z, arrived, picks)
-    m = z.modes
-    parts = []
+    both = []
     for s in range(z.subs):
         values = sides(z, before, after, first_got, second_got, s)
         bases = sides(z, base_before, base_after, base_first, base_second, s)
-        both = shares(z, s, chosen, values, bases)
-        parts.append(correction(z, s, chosen, image_basis, both, left_rows, right_rows))
-    whole[0] = solved[...] + select(
-        z, [dot(basis[s], chosen[(s + 1) * m : (s + 2) * m]) for s in range(z.subs)]
-    )
-    whole[1] = load_rows[...].astype(F32) - image[...] - select(z, parts)
+        both.append(shares(z, s, chosen, values, bases))
+    step, added = corrected(z, chosen, tall, both, left_rows, right_rows)
+    whole[0] = solved[...] + step
+    whole[1] = remaining[...] - added
     for k, out in enumerate(outs):
         out[...] = whole[:, pl.ds(piece_start(z, k, z.own), z.own), :]
 
@@ -384,8 +390,8 @@
         vmem, refs = refs[: n_in + n_out], refs[n_in + n_out :]
         in_sems, out_sems, *rest = refs
         arriving = [pltpu.make_async_copy(hbm[i], vmem[i], in_sems.at[i]) for i in range(n_in)]
-        for copy in arriving:
-            copy.start()
+        for i in sorted(range(n_in), key=lambda i: i in late):
+            arriving[i].start()
         for i, copy in enumerate(arriving):
             if i not in late:
                 copy.wait()
@@ -443,7 +449,7 @@
     packed_f = shape((rows, lanes), F32)
     packed_b = shape((rows, lanes), BF16)
     copies = shape((n, modes, lanes), BF16)
-    tall = shape((subs, rows, modes), BF16)
+    tall = shape((subs, rows, lanes), BF16)
     spread = functools.partial(lax.all_to_all, axis_name="sub", split_axis=0, concat_axis=0)
     first_pairs = [(i, i + 1 if i % 2 == 0 else i - 1) for i in range(n)]
     second_pairs = [(i, (i + (1 if i % 2 else -1)) % n) for i in range(n)]
@@ -468,11 +474,11 @@
     outer = shape((face, 2 * lanes), BF16)
     side = shape((subs, modes, face), BF16)
     (
-        load_rows, solved, image, before, after, first_pair, second_pair, basis, image_basis, left_t, right_t, inner, start_modes
+        load_rows, solved, image, before, after, first_pair, second_pair, tall, left_t, right_t, inner, start_modes
     ) = call(
         functools.partial(first_image_kernel, z),
         [
-            packed_b, packed_f, packed_f, faces, faces, outer, outer, tall, tall, side, side,
+            packed_b, packed_f, packed_f, faces, faces, outer, outer, tall, side, side,
             shape((subs, modes, modes), BF16), shape((modes, lanes), F32),
         ],
         [*inverse_pieces, *stiffness_pieces, *basis_pieces, loads, left_rows, right_rows],
@@ -487,26 +493,20 @@
     )
     second_got = lax.ppermute(second_pair, "sub", second_pairs)
     restricted, second_pair = lax.optimization_barrier((restricted, second_pair))
-    ordered_inverse, index, message = call(
+    near = (subs + 2) * modes
+    ordered_inverse, picks, message = call(
         functools.partial(order_kernel, z),
-        [shape((subs, z.owned, z.columns), BF16), shape((subs, n, lanes), F32), copies],
-        [*inverse_columns, restricted, repeat, own_row],
+        [shape((subs, z.owned, z.columns), BF16), shape((subs, near, z.columns), BF16), copies],
+        [*inverse_columns, restricted, repeat, own_row, place],
         2 * z.owned * z.total * z.total,
         loose=range(1, group + 1),
         name="order",
     )
     coarse = spread(message)
-    picks, first_pair = call(
-        functools.partial(pick_kernel, z),
-        [shape((subs, (subs + 2) * modes, z.columns), BF16), outer],
-        [index, place, first_pair],
-        work // 64,
-        name="picks",
-    )
     first_got = lax.ppermute(first_pair, "sub", first_pairs)
     chosen, message = call(
         functools.partial(update_kernel, z),
-        [shape(((subs + 2) * modes, lanes), BF16), copies],
+        [shape((near, lanes), BF16), copies],
         [coarse, picks, start_modes, inner, left_t, right_t, before, after, first_got, second_got],
         work // 64,
         loose=[0, 8, 9],
@@ -517,24 +517,24 @@
     bases = [before, after, first_got, second_got]
     faces = shape((subs, face, lanes), BF16)
     outer = shape((face, lanes), BF16)
-    solved, image, before, after, first_pair, second_pair = call(
+    solved, remaining, before, after, first_pair, second_pair = call(
         functools.partial(second_image_kernel, z),
         [packed_f, packed_f, faces, faces, outer, outer],
         [
-            *inverse_pieces, *stiffness_pieces, load_rows, image, image_basis, solved, basis, chosen,
+            *inverse_pieces, *stiffness_pieces, load_rows, image, tall, solved, chosen,
             *bases, left_rows, right_rows,
         ],
         work,
-        [pltpu.VMEM((rows, lanes), BF16)],
+        [pltpu.VMEM((rows, lanes), BF16), pltpu.VMEM((rows, lanes), BF16)],
         late=range(2 * group),
-        loose=[*arrivals, 2 * group + 8, 2 * group + 9],
+        loose=[*arrivals, 2 * group + 7, 2 * group + 8],
         name="second_image",
     )
     second_got = lax.ppermute(second_pair, "sub", second_pairs)
-    message, first_pair = call(
+    (message,) = call(
         functools.partial(coarse_kernel, z),
-        [copies, outer],
-        [restricted, ordered_inverse, first_pair],
+        [copies],
+        [restricted, ordered_inverse],
         work // 64,
         loose=[0],
         name="coarse",
@@ -545,12 +545,12 @@
         functools.partial(last_kernel, z),
         [shape((2, z.own, lanes), F32)] * group,
         [
-            coarse, picks, load_rows, image, image_basis, solved, basis,
+            coarse, picks, remaining, solved, tall,
             before, after, first_got, second_got, *bases, left_rows, right_rows,
         ],
         work // 8,
         [pltpu.VMEM((2, rows, lanes), F32)],
-        loose=[0, 9, 10, 13, 14],
+        loose=[0, 7, 8, 11, 12],
         name="last",
     )
     swapped = [parts[0]]

time: 90.7 us -> 89.5 us (0.987)
  blocking collectives: 0 us -> 12.6 us
  starting transfers between devices: 39.6 us -> 29.3 us
  Pallas kernels: 37.6 us -> 31.5 us
  waiting for transfers between devices: 12.1 us -> 14.5 us
    all_to_all x0 -> x1, blocking collectives: none -> 12.6 us  [body(): restricted = spread(message)]
    pallas_call x9 -> x8, Pallas kernels: 37.6 us -> 31.5 us  [call(): pl.pallas_call(whole, out_shape=[pltpu.HBM(o.shape, o.dtype) for o in out...]
    all_to_all x2 -> x1, starting transfers between devices: 13.8 us -> 8.22 us  [body(): restricted = spread(message)]
    all_to_all x2, starting transfers between devices: 12.9 us -> 7.8 us  [body(): coarse = spread(message)]
    all_to_all x2 -> x1, waiting for transfers between devices: 0.97 us -> 2.8 us  [body(): restricted = spread(message)]
    ppermute x2, starting transfers between devices: 1.99 us -> 3.63 us  [body(): first_got = lax.ppermute(first_pair, 'sub', first_pairs)]
    ppermute x2, starting transfers between devices: 9.69 us -> 8.4 us  [body(): second_got = lax.ppermute(second_pair, 'sub', second_pairs)]
    ppermute x2, waiting for transfers between devices: 7.36 us -> 8.44 us  [body(): second_got = lax.ppermute(second_pair, 'sub', second_pairs)]
  transfers between devices with their start and end apart: 13 -> 12, of which waited for: 6 -> 5; matrix products, arithmetic and copies ran while one was open for 0% -> 0% of each run, Pallas kernels for 22% -> 16%
where the time goes in v9:
time: 89.5 us; the launch traced here: 88.8 us
  Pallas kernels  31.5 us (35%)
  starting transfers between devices  29.3 us (33%)
  waiting for transfers between devices  14.5 us (16%)
  blocking collectives  12.6 us (14%)
  between operations  0.91 us (1%)
    pallas_call x8, Pallas kernels, call(): pl.pallas_call(whole, out_shape=[pltpu.HBM(o.shape, o.dtype) for o in out...  31.5 us
    all_to_all x1, blocking collectives, body(): restricted = spread(message)  12.6 us
    ppermute x2, waiting for transfers between devices, body(): second_got = lax.ppermute(second_pair, 'sub', second_pairs)  8.44 us
    ppermute x2, starting transfers between devices, body(): second_got = lax.ppermute(second_pair, 'sub', second_pairs)  8.4 us
    all_to_all x1, starting transfers between devices, body(): restricted = spread(message)  8.22 us
    all_to_all x2, starting transfers between devices, body(): coarse = spread(message)  7.8 us
    ppermute x2, starting transfers between devices, body(): first_got = lax.ppermute(first_pair, 'sub', first_pairs)  3.63 us
    all_to_all x1, waiting for transfers between devices, body(): restricted = spread(message)  2.8 us
  transfers between devices with their start and end apart: 12, of which 5 were waited for; matrix products, arithmetic and copies ran while one was open for 0% of the time, Pallas kernels for 16%

profile of v9, /device:TPU:0, one launch (start us, length us, event | category | flops | bytes accessed | tf_op | source)
XLA Modules:
  0.0 88.8 jit_solution(9672390196172884403)
XLA Ops:
  0.6 0.5 collective-permute-start.1
  1.1 1.2 %collective-permute-done.1.refs_1_.refs_5_ = bf16[2,48,512]{2,1,0:T(8,128)(2,1)S(1)} collective-permute-done((bf16[2,48,512]{2,1,0:T(8,128)(2,1)}, bf16[2,48,512]{2,1,0:T(8,128)(2,1)S(1)}, u32[]{:S(2)}, u32[]{:S(2)}) %collective-permute-start.1) | collective-permute-done | bytes 98336 | tf_op jit(solution)/shard_map/ppermute | solution.py:435
  2.3 2.3 %open.1 = bf16[16,64,128]{2,1,0:T(8,128)(2,1)} custom-call(bf16[2,48,512]{2,1,0:T(8,128)(2,1)} %bitcast.2, bf16[2,48,512]{2,1,0:T(8,128)(2,1)S(1)} %collective-permute-done.1.refs_1_.refs_5_, bf16[2,1024,128]{2,1,0:T(8,128)(2,1)} %refs_6_.1, s32[2,48]{1,0:T(2,128)} %refs_3_.2), custom_call_target="tpu_custom_call" | custom-call | flops 67108864 | bytes 983424 | tf_op jit(solution)/shard_map/open/pallas_call | solution.py:411
  4.6 0.4 collective-permute-start.2
  5.0 0.1 collective-permute-start.3
  5.2 8.2 %all-to-all-start = ((bf16[16,64,128]{2,1,0:T(8,128)(2,1)}), bf16[16,64,128]{2,1,0:T(8,128)(2,1)S(1)}, u32[]{:S(2)}, u32[]{:S(2)}) async-start(bf16[16,64,128]{2,1,0:T(8,128)(2,1)} %open.1), calls=%async_computation | async-start | bytes 524288 | tf_op jit(solution)/shard_map/all_to_all | solution.py:471
  13.4 0.1 collective-permute-start
  13.5 0.0 collective-permute-done.2.refs_1_
  13.5 7.3 %first_image.1 = (bf16[1024,128]{1,0:T(8,128)(2,1)}, f32[1024,128]{1,0:T(8,128)}, f32[1024,128]{1,0:T(8,128)}, bf16[2,128,256]{2,1,0:T(8,128)(2,1)}, bf16[2,128,...) custom-call(bf16[2,512,1024]{2,1,0:T(8,128)(2,1)} %refs_0_.3, ...), custom_call_target="tpu_custom_call" | custom-call | flops 1073741824 | bytes 11422720 | tf_op jit(solution)/shard_map/first_image/pallas_call | solution.py:411
  20.8 2.8 %all-to-all-done.refs_2_ = bf16[16,64,128]{2,1,0:T(8,128)(2,1)S(1)} async-done(((bf16[16,64,128]{2,1,0:T(8,128)(2,1)}), bf16[16,64,128]{2,1,0:T(8,128)(2,1)S(1)}, u32[]{:S(2)}, u32[]{:S(2)}) %all-to-all-start) | async-done | bytes 262176 | tf_op jit(solution)/shard_map/all_to_all | solution.py:471
  23.6 0.0 collective-permute-done.refs_1_
  23.6 3.5 %order.1 = (bf16[2,96,768]{2,1,0:T(8,128)(2,1)}, bf16[2,192,768]{2,1,0:T(8,128)(2,1)}, bf16[16,48,128]{2,1,0:T(8,128)(2,1)}) custom-call(bf16[96,768]{1,0:T(8,128)(2,1)} %refs_0_.2, bf16[96,768]{1,0:T(8,128)(2,1)S(1)} %collective-permute-done.refs_1_, bf16[16,64,128]{2,1,0:T(8,128)(2,1)S(1)} %all-to-all-done.refs_2_, ...), custom_call_target="tpu_custom_call" | custom-call | flops 452984832 | bytes 1890304 | tf_op jit(solution)/shard_map/order/pallas_call | solution.py:411
  27.1 4.1 %all-to-all-start.1 = ((bf16[16,48,128]{2,1,0:T(8,128)(2,1)}), bf16[16,48,128]{2,1,0:T(8,128)(2,1)S(1)}, u32[]{:S(2)}, u32[]{:S(2)}) async-start(bf16[16,48,128]{2,1,0:T(8,128)(2,1)} %get-tuple-element.36), calls=%async_computation.1 | async-start | bytes 393216 | tf_op jit(solution)/shard_map/all_to_all | solution.py:505
  31.2 1.9 %collective-permute-start.4 = (bf16[128,256]{1,0:T(8,128)(2,1)}, bf16[128,256]{1,0:T(8,128)(2,1)S(1)}, u32[]{:S(2)}, u32[]{:S(2)}) collective-permute-start(bf16[128,256]{1,0:T(8,128)(2,1)} %get-tuple-element.44), channel_id=1, source_target_pairs={{0,2},{2,0},{4,6},{6,4},{8,10},{10,8},{12,14},{14,12},{16,18},{18,... | collective-permute-start | bytes 196616 | tf_op jit(solution)/shard_map/ppermute | solution.py:506
  33.1 4.2 %collective-permute-start.5 = (bf16[128,256]{1,0:T(8,128)(2,1)}, bf16[128,256]{1,0:T(8,128)(2,1)S(1)}, u32[]{:S(2)}, u32[]{:S(2)}) collective-permute-start(bf16[128,256]{1,0:T(8,128)(2,1)} %get-tuple-element.34), channel_id=1, source_target_pairs={{0,30},{2,4},{4,2},{6,8},{8,6},{10,12},{12,10},{14,16},{16,14},{18... | collective-permute-start | bytes 196616 | tf_op jit(solution)/shard_map/ppermute | solution.py:494
  37.3 0.0 collective-permute-done.4.refs_8_.refs_11_
  37.3 5.0 %collective-permute-done.5.refs_9_.refs_12_ = bf16[128,256]{1,0:T(8,128)(2,1)S(1)} collective-permute-done((bf16[128,256]{1,0:T(8,128)(2,1)}, bf16[128,256]{1,0:T(8,128)(2,1)S(1)}, u32[]{:S(2)}, u32[]{:S(2)}) %collective-permute-start.5) | collective-permute-done | bytes 65568 | tf_op jit(solution)/shard_map/ppermute | solution.py:494
  42.2 0.0 all-to-all-done.1.refs_0_
  42.2 2.9 %update.1 = (bf16[192,128]{1,0:T(8,128)(2,1)}, bf16[16,48,128]{2,1,0:T(8,128)(2,1)}) custom-call(bf16[16,48,128]{2,1,0:T(8,128)(2,1)S(1)} %all-to-all-done.1.refs_0_, bf16[2,192,768]{2,1,0:T(8,128)(2,1)} %get-tuple-element.37.refs_1_, f32[48,128]{1,0:T(8,128)} %get-tuple-element.38.refs_2_, bf16[2,48,48]{2,1,0:T(8,128)(2,1)} %get-tuple-element.39.refs_3_, ...), custom_call_target="tpu_custom_call" | custom-call | flops 16777216 | bytes 1508352 | tf_op jit(solution)/shard_map/update/pallas_call | solution.py:411
  45.2 12.6 %all_to_all.20.refs_0_ = bf16[16,48,128]{2,1,0:T(8,128)(2,1)S(1)} all-to-all(bf16[16,48,128]{2,1,0:T(8,128)(2,1)} %get-tuple-element.45), channel_id=1, replica_groups=mesh['sub'=16,'crow'=2,'ccol'=1] {'sub'}, dimensions={0} | all-to-all | bytes 393216 | tf_op jit(solution)/shard_map/all_to_all | solution.py:515
  57.7 2.2 %coarse.1 = bf16[16,48,128]{2,1,0:T(8,128)(2,1)} custom-call(bf16[16,48,128]{2,1,0:T(8,128)(2,1)S(1)} %all_to_all.20.refs_0_, bf16[2,96,768]{2,1,0:T(8,128)(2,1)} %get-tuple-element.46.refs_1_), custom_call_target="tpu_custom_call" | custom-call | flops 16777216 | bytes 688128 | tf_op jit(solution)/shard_map/coarse/pallas_call | solution.py:411
  59.9 3.7 %all-to-all-start.3 = ((bf16[16,48,128]{2,1,0:T(8,128)(2,1)}), bf16[16,48,128]{2,1,0:T(8,128)(2,1)S(1)}, u32[]{:S(2)}, u32[]{:S(2)}) async-start(bf16[16,48,128]{2,1,0:T(8,128)(2,1)} %coarse.1), calls=%async_computation.3 | async-start | bytes 393216 | tf_op jit(solution)/shard_map/all_to_all | solution.py:542
  63.7 6.6 %second_image.1 = (f32[1024,128]{1,0:T(8,128)}, f32[1024,128]{1,0:T(8,128)}, bf16[2,128,128]{2,1,0:T(8,128)(2,1)}, bf16[2,128,128]{2,1,0:T(8,128)(2,1)}, bf16[12...) custom-call(bf16[2,512,1024]{2,1,0:T(8,128)(2,1)} %refs_0_.3, bf16[2,512,1024]{2,1,0:T(8,128)(2,1)S(1)} %collective-permute-done.2.refs_1_, ...), custom_call_target="tpu_custom_call" | custom-call | flops 1073741824 | bytes 11913216 | tf_op jit(solution)/shard_map/second_image/pallas_call | solution.py:411
  70.3 1.7 %collective-permute-start.6 = (bf16[128,128]{1,0:T(8,128)(2,1)}, bf16[128,128]{1,0:T(8,128)(2,1)S(1)}, u32[]{:S(2)}, u32[]{:S(2)}) collective-permute-start(bf16[128,128]{1,0:T(8,128)(2,1)} %get-tuple-element.56), channel_id=1, source_target_pairs={{0,2},{2,0},{4,6},{6,4},{8,10},{10,8},{12,14},{14,12},{16,18},{18,... | collective-permute-start | bytes 98312 | tf_op jit(solution)/shard_map/ppermute | solution.py:543
  71.9 4.2 %collective-permute-start.7 = (bf16[128,128]{1,0:T(8,128)(2,1)}, bf16[128,128]{1,0:T(8,128)(2,1)S(1)}, u32[]{:S(2)}, u32[]{:S(2)}) collective-permute-start(bf16[128,128]{1,0:T(8,128)(2,1)} %get-tuple-element.57), channel_id=1, source_target_pairs={{0,30},{2,4},{4,2},{6,8},{8,6},{10,12},{12,10},{14,16},{16,14},{18... | collective-permute-start | bytes 98312 | tf_op jit(solution)/shard_map/ppermute | solution.py:533
  76.2 0.0 collective-permute-done.6.refs_7_
  76.2 3.5 %collective-permute-done.7.refs_8_ = bf16[128,128]{1,0:T(8,128)(2,1)S(1)} collective-permute-done((bf16[128,128]{1,0:T(8,128)(2,1)}, bf16[128,128]{1,0:T(8,128)(2,1)S(1)}, u32[]{:S(2)}, u32[]{:S(2)}) %collective-permute-start.7) | collective-permute-done | bytes 32800 | tf_op jit(solution)/shard_map/ppermute | solution.py:533
  79.7 0.0 all-to-all-done.3.refs_0_
  79.7 4.3 %last.1 = (f32[2,512,128]{2,1,0:T(8,128)}, f32[2,512,128]{2,1,0:T(8,128)}) custom-call(bf16[16,48,128]{2,1,0:T(8,128)(2,1)S(1)} %all-to-all-done.3.refs_0_, bf16[2,192,768]{2,1,0:T(8,128)(2,1)} %get-tuple-element.37.refs_1_, f32[1024,128]{1,0:T(8,128)} %get-tuple-element.52.refs_2_, f32[1024,128]{1,0:T(8,128)} %get-tuple-element.53.refs_3_, ...), custom_call_target="tpu_custom_call" | custom-call | flops 134217728 | bytes 3999744 | tf_op jit(solution)/shard_map/last/pallas_call | solution.py:411
  84.0 0.1 collective-permute-start.8
  84.1 2.1 %collective-permute-done.8.refs_1_ = f32[2,512,128]{2,1,0:T(8,128)S(1)} collective-permute-done((f32[2,512,128]{2,1,0:T(8,128)}, f32[2,512,128]{2,1,0:T(8,128)S(1)}, u32[]{:S(2)}, u32[]{:S(2)}) %collective-permute-start.8) | collective-permute-done | bytes 524320 | tf_op jit(solution)/shard_map/ppermute | solution.py:558
  86.2 2.5 %unpack.1 = (f32[2,512,128]{2,1,0:T(8,128)}, f32[2,512,128]{2,1,0:T(8,128)}) custom-call(f32[2,512,128]{2,1,0:T(8,128)} %get-tuple-element.58.refs_0_, f32[2,512,128]{2,1,0:T(8,128)S(1)} %collective-permute-done.8.refs_1_), custom_call_target="tpu_custom_call" | custom-call | flops 16777216 | bytes 2097152 | tf_op jit(solution)/shard_map/unpack/pallas_call | solution.py:411
  (1 shorter events, 0.0 us)
Async XLA Ops:
  0.6 1.7 %collective-permute-start.1 = (bf16[2,48,512]{2,1,0:T(8,128)(2,1)}, bf16[2,48,512]{2,1,0:T(8,128)(2,1)S(1)}, u32[]{:S(2)}, u32[]{:S(2)}) collective-permute-start(bf16[2,48,512]{2,1,0:T(8,128)(2,1)} %bitcast.1), channel_id=1, source_target_pairs={{1,0},{0,1},{3,2},{2,3},{5,4},{4,5},{7,6},{6,7},{9,8},{8,9},{11,10... | collective-permute-start | bytes 294920 | tf_op jit(solution)/shard_map/ppermute | solution.py:435
  4.6 8.9 %collective-permute-start.2 = (bf16[2,512,1024]{2,1,0:T(8,128)(2,1)}, bf16[2,512,1024]{2,1,0:T(8,128)(2,1)S(1)}, u32[]{:S(2)}, u32[]{:S(2)}) collective-permute-start(bf16[2,512,1024]{2,1,0:T(8,128)(2,1)} %refs_0_.3), channel_id=1, source_target_pairs={{1,0},{0,1},{3,2},{2,3},{5,4},{4,5},{7,6},{6,7},{9,8},{8,9},{11,10... | collective-permute-start | bytes 6291464 | tf_op jit(solution)/shard_map/ppermute | solution.py:435
  5.0 8.5 %collective-permute-start.3 = (bf16[2,512,1024]{2,1,0:T(8,128)(2,1)}, bf16[2,512,1024]{2,1,0:T(8,128)(2,1)}, u32[]{:S(2)}, u32[]{:S(2)}) collective-permute-start(bf16[2,512,1024]{2,1,0:T(8,128)(2,1)} %refs_2_.3), channel_id=1, source_target_pairs={{1,0},{0,1},{3,2},{2,3},{5,4},{4,5},{7,6},{6,7},{9,8},{8,9},{11,10... | collective-permute-start | bytes 6291464 | tf_op jit(solution)/shard_map/ppermute | solution.py:435
  5.2 18.4 %all-to-all-start = ((bf16[16,64,128]{2,1,0:T(8,128)(2,1)}), bf16[16,64,128]{2,1,0:T(8,128)(2,1)S(1)}, u32[]{:S(2)}, u32[]{:S(2)}) async-start(bf16[16,64,128]{2,1,0:T(8,128)(2,1)} %open.1), calls=%async_computation | async-start | bytes 524288 | tf_op jit(solution)/shard_map/all_to_all | solution.py:471
  13.4 10.2 %collective-permute-start = (bf16[96,768]{1,0:T(8,128)(2,1)}, bf16[96,768]{1,0:T(8,128)(2,1)S(1)}, u32[]{:S(2)}, u32[]{:S(2)}) collective-permute-start(bf16[96,768]{1,0:T(8,128)(2,1)} %refs_0_.2), channel_id=1, source_target_pairs={{1,0},{0,1},{3,2},{2,3},{5,4},{4,5},{7,6},{6,7},{9,8},{8,9},{11,10... | collective-permute-start | bytes 442376 | tf_op jit(solution)/shard_map/ppermute | solution.py:435
  27.1 15.2 %all-to-all-start.1 = ((bf16[16,48,128]{2,1,0:T(8,128)(2,1)}), bf16[16,48,128]{2,1,0:T(8,128)(2,1)S(1)}, u32[]{:S(2)}, u32[]{:S(2)}) async-start(bf16[16,48,128]{2,1,0:T(8,128)(2,1)} %get-tuple-element.36), calls=%async_computation.1 | async-start | bytes 393216 | tf_op jit(solution)/shard_map/all_to_all | solution.py:505
  31.2 6.1 %collective-permute-start.4 = (bf16[128,256]{1,0:T(8,128)(2,1)}, bf16[128,256]{1,0:T(8,128)(2,1)S(1)}, u32[]{:S(2)}, u32[]{:S(2)}) collective-permute-start(bf16[128,256]{1,0:T(8,128)(2,1)} %get-tuple-element.44), channel_id=1, source_target_pairs={{0,2},{2,0},{4,6},{6,4},{8,10},{10,8},{12,14},{14,12},{16,18},{18,... | collective-permute-start | bytes 196616 | tf_op jit(solution)/shard_map/ppermute | solution.py:506
  33.1 9.1 %collective-permute-start.5 = (bf16[128,256]{1,0:T(8,128)(2,1)}, bf16[128,256]{1,0:T(8,128)(2,1)S(1)}, u32[]{:S(2)}, u32[]{:S(2)}) collective-permute-start(bf16[128,256]{1,0:T(8,128)(2,1)} %get-tuple-element.34), channel_id=1, source_target_pairs={{0,30},{2,4},{4,2},{6,8},{8,6},{10,12},{12,10},{14,16},{16,14},{18... | collective-permute-start | bytes 196616 | tf_op jit(solution)/shard_map/ppermute | solution.py:494
  59.9 19.7 %all-to-all-start.3 = ((bf16[16,48,128]{2,1,0:T(8,128)(2,1)}), bf16[16,48,128]{2,1,0:T(8,128)(2,1)S(1)}, u32[]{:S(2)}, u32[]{:S(2)}) async-start(bf16[16,48,128]{2,1,0:T(8,128)(2,1)} %coarse.1), calls=%async_computation.3 | async-start | bytes 393216 | tf_op jit(solution)/shard_map/all_to_all | solution.py:542
  70.3 5.9 %collective-permute-start.6 = (bf16[128,128]{1,0:T(8,128)(2,1)}, bf16[128,128]{1,0:T(8,128)(2,1)S(1)}, u32[]{:S(2)}, u32[]{:S(2)}) collective-permute-start(bf16[128,128]{1,0:T(8,128)(2,1)} %get-tuple-element.56), channel_id=1, source_target_pairs={{0,2},{2,0},{4,6},{6,4},{8,10},{10,8},{12,14},{14,12},{16,18},{18,... | collective-permute-start | bytes 98312 | tf_op jit(solution)/shard_map/ppermute | solution.py:543
  71.9 7.7 %collective-permute-start.7 = (bf16[128,128]{1,0:T(8,128)(2,1)}, bf16[128,128]{1,0:T(8,128)(2,1)S(1)}, u32[]{:S(2)}, u32[]{:S(2)}) collective-permute-start(bf16[128,128]{1,0:T(8,128)(2,1)} %get-tuple-element.57), channel_id=1, source_target_pairs={{0,30},{2,4},{4,2},{6,8},{8,6},{10,12},{12,10},{14,16},{16,14},{18... | collective-permute-start | bytes 98312 | tf_op jit(solution)/shard_map/ppermute | solution.py:533
  84.0 2.2 %collective-permute-start.8 = (f32[2,512,128]{2,1,0:T(8,128)}, f32[2,512,128]{2,1,0:T(8,128)S(1)}, u32[]{:S(2)}, u32[]{:S(2)}) collective-permute-start(f32[2,512,128]{2,1,0:T(8,128)} %get-tuple-element.59), channel_id=1, source_target_pairs={{0,1},{1,0},{2,3},{3,2},{4,5},{5,4},{6,7},{7,6},{8,9},{9,8},{10,11... | collective-permute-start | bytes 1572872 | tf_op jit(solution)/shard_map/ppermute | solution.py:558

commit v10 on v9

--- a/solution.py
+++ b/solution.py
@@ -69,10 +69,10 @@
     return out
 
 
-def shift_matrix(z, source, target):
+def lane_matrix(z, source, target):
     row = lax.broadcasted_iota(jnp.int32, (z.lanes, z.lanes), 0)
     lane = lax.broadcasted_iota(jnp.int32, (z.lanes, z.lanes), 1)
-    hit = (row - source * z.width == lane - target * z.width) & lane_mask(z, target, (z.lanes, z.lanes))
+    hit = (row - source == lane - target) & (lane >= target) & (lane < target + z.width)
     return jnp.where(hit, 1.0, 0.0).astype(BF16)
 
 
@@ -132,9 +132,8 @@
         store(piece_start(z, k, z.own), select(z, parts))
 
 
-def face_rows(z, image_b, rows_ref, s, target):
-    picked = dot(pick_matrix(z, rows_ref[s : s + 1, :]), image_b).astype(BF16)
-    return dot(picked, shift_matrix(z, s, target)).astype(BF16)
+def face_rows(z, pick, image_b, s):
+    return dot(dot(pick, image_b).astype(BF16), lane_matrix(z, s * z.width, 0))
 
 
 def store_faces(z, before, after, first_pair, second_pair):
@@ -155,12 +154,18 @@
     return from_before, from_after
 
 
-def shares(z, s, chosen, values, bases):
-    m = z.modes
+def shares(z, s, chosen, faces, bases=None):
+    m, half = z.modes, z.lanes // 2
+    moved = lane_matrix(z, 0, s * z.width)
     out = []
-    for value, base, at in ((values[0], bases[0], s), (values[1], bases[1], s + 2)):
-        total = value[:, : z.lanes].astype(F32)
-        total = total + dot(base[:, z.lanes : z.lanes + m], chosen[at * m : (at + 1) * m])
+    for side, at in ((0, s), (1, s + 2)):
+        own = chosen[at * m : (at + 1) * m]
+        below = jnp.concatenate([own, jnp.zeros((half - m, z.lanes), BF16)], axis=0)
+        if bases is None:
+            total = dot(faces[side], jnp.concatenate([moved[:half], below], axis=0))
+        else:
+            above = jnp.zeros((half, z.lanes), BF16)
+            total = dot(faces[side], moved) + dot(bases[side], jnp.concatenate([above, below], axis=0))
         out.append(total.astype(BF16))
     return out
 
@@ -223,15 +228,11 @@
         image_basis = images[s, :, z.lanes :]
         tall[s, :, :half] = image_basis[:, :half]
         inner[s] = dot(basis_t[s], image_basis)[:, : z.modes].astype(BF16)
-        for rows_ref, out, side_t, target in (
-            (left_rows, before, left_t, (s - 1) % z.subs),
-            (right_rows, after, right_t, (s + 1) % z.subs),
-        ):
+        placed = jnp.concatenate([jnp.zeros((z.rows, half), BF16), image_basis[:, :half]], axis=1)
+        for rows_ref, out, side_t in ((left_rows, before, left_t), (right_rows, after, right_t)):
             pick = pick_matrix(z, rows_ref[s : s + 1, :])
             side_t[s] = dot_nt(basis_t[s], pick).astype(BF16)
-            picked = dot(pick, images[s]).astype(BF16)
-            out[s, :, : z.lanes] = dot(picked[:, : z.lanes], shift_matrix(z, s, target)).astype(BF16)
-            out[s, :, z.lanes :] = picked[:, z.lanes :]
+            out[s] = (face_rows(z, pick, images[s, :, : z.lanes], s) + dot(pick, placed)).astype(BF16)
     store_faces(z, before, after, first_pair, second_pair)
 
 
@@ -244,7 +245,7 @@
     both = []
     for s in range(z.subs):
         faces = sides(z, before, after, first_got, second_got, s)
-        both.append(shares(z, s, chosen, faces, faces))
+        both.append(shares(z, s, chosen, faces))
     step, added = corrected(z, chosen, tall, both, left_rows, right_rows)
     residual = (load_rows[...].astype(F32) - old_image[...] - added).astype(BF16)
     solved[...] = old_solved[...] + step
@@ -268,8 +269,8 @@
     multiply(z, stiffness, rounded[...], store_image)
     image_b = image[...]
     for s in range(z.subs):
-        new_before[s] = face_rows(z, image_b, left_rows, s, (s - 1) % z.subs)
-        new_after[s] = face_rows(z, image_b, right_rows, s, (s + 1) % z.subs)
+        new_before[s] = face_rows(z, pick_matrix(z, left_rows[s : s + 1, :]), image_b, s).astype(BF16)
+        new_after[s] = face_rows(z, pick_matrix(z, right_rows[s : s + 1, :]), image_b, s).astype(BF16)
     store_faces(z, new_before, new_after, first_pair, second_pair)
 
 
@@ -342,7 +343,7 @@
     parts = []
     for s in range(z.subs):
         faces = sides(z, before, after, first_got, second_got, s)
-        both = shares(z, s, rows, faces, faces)
+        both = shares(z, s, rows, faces)
         total = dot(inner[s], rows[(s + 1) * m : (s + 2) * m])
         parts.append(total + dot(left_t[s], both[0]) + dot(right_t[s], both[1]))
     modes = (start_modes[...] - select(z, parts)).astype(BF16)
@@ -440,6 +441,7 @@
     z = Sizes(loads, stiffness, coarse_basis, coarse_inverse, left_rows)
     n, group, subs, rows, lanes, modes, face = z.n, z.group, z.subs, z.rows, z.lanes, z.modes, z.face
     basis_pieces = pieces_of(jnp.swapaxes(coarse_basis, 1, 2), group)
+    basis_pieces, local_inverse, stiffness = lax.optimization_barrier((basis_pieces, local_inverse, stiffness))
     column = np.arange(z.columns)
     repeat = jnp.asarray(np.arange(lanes)[:, None] == column[None, :] % modes, BF16)
     own_row = jnp.asarray(np.arange(n)[:, None] == column[None, :] // modes, F32)
@@ -465,13 +467,12 @@
         name="open",
     )
     inverse_columns = pieces_of(coarse_inverse, group)
-    message, local_inverse, stiffness = lax.optimization_barrier((message, local_inverse, stiffness))
     inverse_pieces = pieces_of(local_inverse, group)
     stiffness_pieces = pieces_of(stiffness, group)
     restricted = spread(message)
     arrivals = [*range(1, group), *range(group + 1, 2 * group)]
-    faces = shape((subs, face, 2 * lanes), BF16)
-    outer = shape((face, 2 * lanes), BF16)
+    faces = shape((subs, face, lanes), BF16)
+    outer = shape((face, lanes), BF16)
     side = shape((subs, modes, face), BF16)
     (
         load_rows, solved, image, before, after, first_pair, second_pair, tall, left_t, right_t, inner, start_modes
@@ -515,8 +516,6 @@
     restricted = spread(message)
 
     bases = [before, after, first_got, second_got]
-    faces = shape((subs, face, lanes), BF16)
-    outer = shape((face, lanes), BF16)
     solved, remaining, before, after, first_pair, second_pair = call(
         functools.partial(second_image_kernel, z),
         [packed_f, packed_f, faces, faces, outer, outer],
@@ -531,6 +530,7 @@
         name="second_image",
     )
     second_got = lax.ppermute(second_pair, "sub", second_pairs)
+    restricted, remaining = lax.optimization_barrier((restricted, remaining))
     (message,) = call(
         functools.partial(coarse_kernel, z),
         [copies],

time: 89.5 us -> 84.4 us (0.943)
  blocking collectives: 12.6 us -> 0 us
  starting transfers between devices: 29.3 us -> 36.2 us
    all_to_all x1 -> x0, blocking collectives: 12.6 us -> none  [body(): restricted = spread(message)]
    all_to_all x1 -> x2, starting transfers between devices: 8.22 us -> 13.1 us  [body(): restricted = spread(message)]
    all_to_all x2, starting transfers between devices: 7.8 us -> 9.74 us  [body(): coarse = spread(message)]
    all_to_all x1 -> x2, waiting for transfers between devices: 2.8 us -> 4.1 us  [body(): restricted = spread(message)]
  transfers between devices with their start and end apart: 12 -> 13, of which waited for: 5 -> 6; matrix products, arithmetic and copies ran while one was open for 0% -> 0% of each run, Pallas kernels for 16% -> 20%
where the time goes in v10:
time: 84.4 us; the launch traced here: 83.7 us
  starting transfers between devices  36.2 us (43%)
  Pallas kernels  31.6 us (37%)
  waiting for transfers between devices  15.2 us (18%)
    pallas_call x8, Pallas kernels, call(): pl.pallas_call(whole, out_shape=[pltpu.HBM(o.shape, o.dtype) for o in out...  31.6 us
    all_to_all x2, starting transfers between devices, body(): restricted = spread(message)  13.1 us
    all_to_all x2, starting transfers between devices, body(): coarse = spread(message)  9.74 us
    ppermute x2, starting transfers between devices, body(): second_got = lax.ppermute(second_pair, 'sub', second_pairs)  8.32 us
    ppermute x2, waiting for transfers between devices, body(): second_got = lax.ppermute(second_pair, 'sub', second_pairs)  7.82 us
    all_to_all x2, waiting for transfers between devices, body(): restricted = spread(message)  4.1 us
    ppermute x2, starting transfers between devices, body(): first_got = lax.ppermute(first_pair, 'sub', first_pairs)  3.87 us
    ppermute x1, waiting for transfers between devices, body(): lax.ppermute(parts[k], GROUP, [(g, (g + k) % group) for g in range(group)])  2.11 us
  transfers between devices with their start and end apart: 13, of which 6 were waited for; matrix products, arithmetic and copies ran while one was open for 0% of the time, Pallas kernels for 20%

profile of v10, /device:TPU:0, one launch (start us, length us, event | category | flops | bytes accessed | tf_op | source)
XLA Modules:
  0.0 83.7 jit_solution(7413039185664974482)
XLA Ops:
  0.6 0.5 collective-permute-start.1
  1.1 1.2 %collective-permute-done.1.refs_1_.refs_5_ = bf16[2,48,512]{2,1,0:T(8,128)(2,1)S(1)} collective-permute-done((bf16[2,48,512]{2,1,0:T(8,128)(2,1)}, bf16[2,48,512]{2,1,0:T(8,128)(2,1)S(1)}, u32[]{:S(2)}, u32[]{:S(2)}) %collective-permute-start.1) | collective-permute-done | bytes 98336 | tf_op jit(solution)/shard_map/ppermute | solution.py:436
  2.3 0.4 collective-permute-start.2
  2.7 0.2 collective-permute-start.3
  2.8 2.3 %open.1 = bf16[16,64,128]{2,1,0:T(8,128)(2,1)} custom-call(bf16[2,48,512]{2,1,0:T(8,128)(2,1)} %bitcast.2, bf16[2,48,512]{2,1,0:T(8,128)(2,1)S(1)} %collective-permute-done.1.refs_1_.refs_5_, bf16[2,1024,128]{2,1,0:T(8,128)(2,1)} %refs_6_.1, s32[2,48]{1,0:T(2,128)} %refs_3_.2), custom_call_target="tpu_custom_call" | custom-call | flops 67108864 | bytes 983424 | tf_op jit(solution)/shard_map/open/pallas_call | solution.py:412
  5.1 8.2 %all-to-all-start = ((bf16[16,64,128]{2,1,0:T(8,128)(2,1)}), bf16[16,64,128]{2,1,0:T(8,128)(2,1)S(1)}, u32[]{:S(2)}, u32[]{:S(2)}) async-start(bf16[16,64,128]{2,1,0:T(8,128)(2,1)} %open.1), calls=%async_computation | async-start | bytes 524288 | tf_op jit(solution)/shard_map/all_to_all | solution.py:472
  13.3 0.1 collective-permute-start
  13.4 0.0 collective-permute-done.2.refs_1_
  13.4 0.0 collective-permute-done.3.refs_3_
  13.4 7.5 %first_image.1 = (bf16[1024,128]{1,0:T(8,128)(2,1)}, f32[1024,128]{1,0:T(8,128)}, f32[1024,128]{1,0:T(8,128)}, bf16[2,128,128]{2,1,0:T(8,128)(2,1)}, bf16[2,128,...) custom-call(bf16[2,512,1024]{2,1,0:T(8,128)(2,1)} %refs_0_.3, ...), custom_call_target="tpu_custom_call" | custom-call | flops 1073741824 | bytes 11226112 | tf_op jit(solution)/shard_map/first_image/pallas_call | solution.py:412
  20.9 2.6 %all-to-all-done.refs_2_ = bf16[16,64,128]{2,1,0:T(8,128)(2,1)S(1)} async-done(((bf16[16,64,128]{2,1,0:T(8,128)(2,1)}), bf16[16,64,128]{2,1,0:T(8,128)(2,1)S(1)}, u32[]{:S(2)}, u32[]{:S(2)}) %all-to-all-start) | async-done | bytes 262176 | tf_op jit(solution)/shard_map/all_to_all | solution.py:472
  23.5 3.5 %order.1 = (bf16[2,96,768]{2,1,0:T(8,128)(2,1)}, bf16[2,192,768]{2,1,0:T(8,128)(2,1)}, bf16[16,48,128]{2,1,0:T(8,128)(2,1)}) custom-call(bf16[96,768]{1,0:T(8,128)(2,1)} %refs_0_.2, bf16[96,768]{1,0:T(8,128)(2,1)S(1)} %collective-permute-done.refs_1_, bf16[16,64,128]{2,1,0:T(8,128)(2,1)S(1)} %all-to-all-done.refs_2_, ...), custom_call_target="tpu_custom_call" | custom-call | flops 452984832 | bytes 1890304 | tf_op jit(solution)/shard_map/order/pallas_call | solution.py:412
  27.0 4.3 %all-to-all-start.1 = ((bf16[16,48,128]{2,1,0:T(8,128)(2,1)}), bf16[16,48,128]{2,1,0:T(8,128)(2,1)S(1)}, u32[]{:S(2)}, u32[]{:S(2)}) async-start(bf16[16,48,128]{2,1,0:T(8,128)(2,1)} %get-tuple-element.40), calls=%async_computation.1 | async-start | bytes 393216 | tf_op jit(solution)/shard_map/all_to_all | solution.py:506
  31.3 1.9 %collective-permute-start.4 = (bf16[128,128]{1,0:T(8,128)(2,1)}, bf16[128,128]{1,0:T(8,128)(2,1)S(1)}, u32[]{:S(2)}, u32[]{:S(2)}) collective-permute-start(bf16[128,128]{1,0:T(8,128)(2,1)} %get-tuple-element.48), channel_id=1, source_target_pairs={{0,2},{2,0},{4,6},{6,4},{8,10},{10,8},{12,14},{14,12},{16,18},{18,... | collective-permute-start | bytes 98312 | tf_op jit(solution)/shard_map/ppermute | solution.py:507
  33.3 4.2 %collective-permute-start.5 = (bf16[128,128]{1,0:T(8,128)(2,1)}, bf16[128,128]{1,0:T(8,128)(2,1)S(1)}, u32[]{:S(2)}, u32[]{:S(2)}) collective-permute-start(bf16[128,128]{1,0:T(8,128)(2,1)} %get-tuple-element.38), channel_id=1, source_target_pairs={{0,30},{2,4},{4,2},{6,8},{8,6},{10,12},{12,10},{14,16},{16,14},{18... | collective-permute-start | bytes 98312 | tf_op jit(solution)/shard_map/ppermute | solution.py:495
  37.4 0.0 collective-permute-done.4.refs_8_.refs_11_
  37.4 4.3 %collective-permute-done.5.refs_9_.refs_12_ = bf16[128,128]{1,0:T(8,128)(2,1)S(1)} collective-permute-done((bf16[128,128]{1,0:T(8,128)(2,1)}, bf16[128,128]{1,0:T(8,128)(2,1)S(1)}, u32[]{:S(2)}, u32[]{:S(2)}) %collective-permute-start.5) | collective-permute-done | bytes 32800 | tf_op jit(solution)/shard_map/ppermute | solution.py:495
  41.7 2.8 %update.1 = (bf16[192,128]{1,0:T(8,128)(2,1)}, bf16[16,48,128]{2,1,0:T(8,128)(2,1)}) custom-call(bf16[16,48,128]{2,1,0:T(8,128)(2,1)S(1)} %all-to-all-done.1.refs_0_, bf16[2,192,768]{2,1,0:T(8,128)(2,1)} %get-tuple-element.41.refs_1_, f32[48,128]{1,0:T(8,128)} %get-tuple-element.42.refs_2_, bf16[2,48,48]{2,1,0:T(8,128)(2,1)} %get-tuple-element.43.refs_3_, ...), custom_call_target="tpu_custom_call" | custom-call | flops 16777216 | bytes 1311744 | tf_op jit(solution)/shard_map/update/pallas_call | solution.py:412
  44.6 4.8 %all-to-all-start.2 = ((bf16[16,48,128]{2,1,0:T(8,128)(2,1)}), bf16[16,48,128]{2,1,0:T(8,128)(2,1)S(1)}, u32[]{:S(2)}, u32[]{:S(2)}) async-start(bf16[16,48,128]{2,1,0:T(8,128)(2,1)} %get-tuple-element.49), calls=%async_computation.2 | async-start | bytes 393216 | tf_op jit(solution)/shard_map/all_to_all | solution.py:516
  49.4 6.6 %second_image.1 = (f32[1024,128]{1,0:T(8,128)}, f32[1024,128]{1,0:T(8,128)}, bf16[2,128,128]{2,1,0:T(8,128)(2,1)}, bf16[2,128,128]{2,1,0:T(8,128)(2,1)}, bf16[12...) custom-call(bf16[2,512,1024]{2,1,0:T(8,128)(2,1)} %refs_0_.3, bf16[2,512,1024]{2,1,0:T(8,128)(2,1)S(1)} %collective-permute-done.2.refs_1_, ...), custom_call_target="tpu_custom_call" | custom-call | flops 1073741824 | bytes 11716608 | tf_op jit(solution)/shard_map/second_image/pallas_call | solution.py:412
  56.0 1.5 %all-to-all-done.2.refs_0_ = bf16[16,48,128]{2,1,0:T(8,128)(2,1)S(1)} async-done(((bf16[16,48,128]{2,1,0:T(8,128)(2,1)}), bf16[16,48,128]{2,1,0:T(8,128)(2,1)S(1)}, u32[]{:S(2)}, u32[]{:S(2)}) %all-to-all-start.2) | async-done | bytes 196640 | tf_op jit(solution)/shard_map/all_to_all | solution.py:516
  57.5 2.2 %coarse.1 = bf16[16,48,128]{2,1,0:T(8,128)(2,1)} custom-call(bf16[16,48,128]{2,1,0:T(8,128)(2,1)S(1)} %all-to-all-done.2.refs_0_, bf16[2,96,768]{2,1,0:T(8,128)(2,1)} %get-tuple-element.57.refs_1_), custom_call_target="tpu_custom_call" | custom-call | flops 16777216 | bytes 688128 | tf_op jit(solution)/shard_map/coarse/pallas_call | solution.py:412
  59.7 5.4 %all-to-all-start.3 = ((bf16[16,48,128]{2,1,0:T(8,128)(2,1)}), bf16[16,48,128]{2,1,0:T(8,128)(2,1)S(1)}, u32[]{:S(2)}, u32[]{:S(2)}) async-start(bf16[16,48,128]{2,1,0:T(8,128)(2,1)} %coarse.1), calls=%async_computation.3 | async-start | bytes 393216 | tf_op jit(solution)/shard_map/all_to_all | solution.py:542
  65.1 1.9 %collective-permute-start.6 = (bf16[128,128]{1,0:T(8,128)(2,1)}, bf16[128,128]{1,0:T(8,128)(2,1)S(1)}, u32[]{:S(2)}, u32[]{:S(2)}) collective-permute-start(bf16[128,128]{1,0:T(8,128)(2,1)} %get-tuple-element.62), channel_id=1, source_target_pairs={{0,2},{2,0},{4,6},{6,4},{8,10},{10,8},{12,14},{14,12},{16,18},{18,... | collective-permute-start | bytes 98312 | tf_op jit(solution)/shard_map/ppermute | solution.py:543
  67.0 4.2 %collective-permute-start.7 = (bf16[128,128]{1,0:T(8,128)(2,1)}, bf16[128,128]{1,0:T(8,128)(2,1)S(1)}, u32[]{:S(2)}, u32[]{:S(2)}) collective-permute-start(bf16[128,128]{1,0:T(8,128)(2,1)} %get-tuple-element.63), channel_id=1, source_target_pairs={{0,30},{2,4},{4,2},{6,8},{8,6},{10,12},{12,10},{14,16},{16,14},{18... | collective-permute-start | bytes 98312 | tf_op jit(solution)/shard_map/ppermute | solution.py:532
  71.2 0.0 collective-permute-done.6.refs_7_
  71.2 3.6 %collective-permute-done.7.refs_8_ = bf16[128,128]{1,0:T(8,128)(2,1)S(1)} collective-permute-done((bf16[128,128]{1,0:T(8,128)(2,1)}, bf16[128,128]{1,0:T(8,128)(2,1)S(1)}, u32[]{:S(2)}, u32[]{:S(2)}) %collective-permute-start.7) | collective-permute-done | bytes 32800 | tf_op jit(solution)/shard_map/ppermute | solution.py:532
  74.8 0.0 all-to-all-done.3.refs_0_
  74.8 4.3 %last.1 = (f32[2,512,128]{2,1,0:T(8,128)}, f32[2,512,128]{2,1,0:T(8,128)}) custom-call(bf16[16,48,128]{2,1,0:T(8,128)(2,1)S(1)} %all-to-all-done.3.refs_0_, bf16[2,192,768]{2,1,0:T(8,128)(2,1)} %get-tuple-element.41.refs_1_, f32[1024,128]{1,0:T(8,128)} %get-tuple-element.58.refs_2_, f32[1024,128]{1,0:T(8,128)} %get-tuple-element.59.refs_3_, ...), custom_call_target="tpu_custom_call" | custom-call | flops 134217728 | bytes 3803136 | tf_op jit(solution)/shard_map/last/pallas_call | solution.py:412
  79.0 0.1 collective-permute-start.8
  79.1 2.1 %collective-permute-done.8.refs_1_ = f32[2,512,128]{2,1,0:T(8,128)S(1)} collective-permute-done((f32[2,512,128]{2,1,0:T(8,128)}, f32[2,512,128]{2,1,0:T(8,128)S(1)}, u32[]{:S(2)}, u32[]{:S(2)}) %collective-permute-start.8) | collective-permute-done | bytes 524320 | tf_op jit(solution)/shard_map/ppermute | solution.py:558
  81.2 2.5 %unpack.1 = (f32[2,512,128]{2,1,0:T(8,128)}, f32[2,512,128]{2,1,0:T(8,128)}) custom-call(f32[2,512,128]{2,1,0:T(8,128)} %get-tuple-element.64.refs_0_, f32[2,512,128]{2,1,0:T(8,128)S(1)} %collective-permute-done.8.refs_1_), custom_call_target="tpu_custom_call" | custom-call | flops 16777216 | bytes 2097152 | tf_op jit(solution)/shard_map/unpack/pallas_call | solution.py:412
  (2 shorter events, 0.0 us)
Async XLA Ops:
  0.6 1.7 %collective-permute-start.1 = (bf16[2,48,512]{2,1,0:T(8,128)(2,1)}, bf16[2,48,512]{2,1,0:T(8,128)(2,1)S(1)}, u32[]{:S(2)}, u32[]{:S(2)}) collective-permute-start(bf16[2,48,512]{2,1,0:T(8,128)(2,1)} %bitcast.1), channel_id=1, source_target_pairs={{1,0},{0,1},{3,2},{2,3},{5,4},{4,5},{7,6},{6,7},{9,8},{8,9},{11,10... | collective-permute-start | bytes 294920 | tf_op jit(solution)/shard_map/ppermute | solution.py:436
  2.3 11.1 %collective-permute-start.2 = (bf16[2,512,1024]{2,1,0:T(8,128)(2,1)}, bf16[2,512,1024]{2,1,0:T(8,128)(2,1)S(1)}, u32[]{:S(2)}, u32[]{:S(2)}) collective-permute-start(bf16[2,512,1024]{2,1,0:T(8,128)(2,1)} %refs_0_.3), channel_id=1, source_target_pairs={{1,0},{0,1},{3,2},{2,3},{5,4},{4,5},{7,6},{6,7},{9,8},{8,9},{11,10... | collective-permute-start | bytes 6291464 | tf_op jit(solution)/shard_map/ppermute | solution.py:436
  2.7 10.8 %collective-permute-start.3 = (bf16[2,512,1024]{2,1,0:T(8,128)(2,1)}, bf16[2,512,1024]{2,1,0:T(8,128)(2,1)}, u32[]{:S(2)}, u32[]{:S(2)}) collective-permute-start(bf16[2,512,1024]{2,1,0:T(8,128)(2,1)} %refs_2_.3), channel_id=1, source_target_pairs={{1,0},{0,1},{3,2},{2,3},{5,4},{4,5},{7,6},{6,7},{9,8},{8,9},{11,10... | collective-permute-start | bytes 6291464 | tf_op jit(solution)/shard_map/ppermute | solution.py:436
  5.1 18.4 %all-to-all-start = ((bf16[16,64,128]{2,1,0:T(8,128)(2,1)}), bf16[16,64,128]{2,1,0:T(8,128)(2,1)S(1)}, u32[]{:S(2)}, u32[]{:S(2)}) async-start(bf16[16,64,128]{2,1,0:T(8,128)(2,1)} %open.1), calls=%async_computation | async-start | bytes 524288 | tf_op jit(solution)/shard_map/all_to_all | solution.py:472
  13.3 10.2 %collective-permute-start = (bf16[96,768]{1,0:T(8,128)(2,1)}, bf16[96,768]{1,0:T(8,128)(2,1)S(1)}, u32[]{:S(2)}, u32[]{:S(2)}) collective-permute-start(bf16[96,768]{1,0:T(8,128)(2,1)} %refs_0_.2), channel_id=1, source_target_pairs={{1,0},{0,1},{3,2},{2,3},{5,4},{4,5},{7,6},{6,7},{9,8},{8,9},{11,10... | collective-permute-start | bytes 442376 | tf_op jit(solution)/shard_map/ppermute | solution.py:436
  27.0 14.7 %all-to-all-start.1 = ((bf16[16,48,128]{2,1,0:T(8,128)(2,1)}), bf16[16,48,128]{2,1,0:T(8,128)(2,1)S(1)}, u32[]{:S(2)}, u32[]{:S(2)}) async-start(bf16[16,48,128]{2,1,0:T(8,128)(2,1)} %get-tuple-element.40), calls=%async_computation.1 | async-start | bytes 393216 | tf_op jit(solution)/shard_map/all_to_all | solution.py:506
  31.3 6.1 %collective-permute-start.4 = (bf16[128,128]{1,0:T(8,128)(2,1)}, bf16[128,128]{1,0:T(8,128)(2,1)S(1)}, u32[]{:S(2)}, u32[]{:S(2)}) collective-permute-start(bf16[128,128]{1,0:T(8,128)(2,1)} %get-tuple-element.48), channel_id=1, source_target_pairs={{0,2},{2,0},{4,6},{6,4},{8,10},{10,8},{12,14},{14,12},{16,18},{18,... | collective-permute-start | bytes 98312 | tf_op jit(solution)/shard_map/ppermute | solution.py:507
  33.3 8.4 %collective-permute-start.5 = (bf16[128,128]{1,0:T(8,128)(2,1)}, bf16[128,128]{1,0:T(8,128)(2,1)S(1)}, u32[]{:S(2)}, u32[]{:S(2)}) collective-permute-start(bf16[128,128]{1,0:T(8,128)(2,1)} %get-tuple-element.38), channel_id=1, source_target_pairs={{0,30},{2,4},{4,2},{6,8},{8,6},{10,12},{12,10},{14,16},{16,14},{18... | collective-permute-start | bytes 98312 | tf_op jit(solution)/shard_map/ppermute | solution.py:495
  44.6 12.9 %all-to-all-start.2 = ((bf16[16,48,128]{2,1,0:T(8,128)(2,1)}), bf16[16,48,128]{2,1,0:T(8,128)(2,1)S(1)}, u32[]{:S(2)}, u32[]{:S(2)}) async-start(bf16[16,48,128]{2,1,0:T(8,128)(2,1)} %get-tuple-element.49), calls=%async_computation.2 | async-start | bytes 393216 | tf_op jit(solution)/shard_map/all_to_all | solution.py:516
  59.7 15.1 %all-to-all-start.3 = ((bf16[16,48,128]{2,1,0:T(8,128)(2,1)}), bf16[16,48,128]{2,1,0:T(8,128)(2,1)S(1)}, u32[]{:S(2)}, u32[]{:S(2)}) async-start(bf16[16,48,128]{2,1,0:T(8,128)(2,1)} %coarse.1), calls=%async_computation.3 | async-start | bytes 393216 | tf_op jit(solution)/shard_map/all_to_all | solution.py:542
  65.1 6.1 %collective-permute-start.6 = (bf16[128,128]{1,0:T(8,128)(2,1)}, bf16[128,128]{1,0:T(8,128)(2,1)S(1)}, u32[]{:S(2)}, u32[]{:S(2)}) collective-permute-start(bf16[128,128]{1,0:T(8,128)(2,1)} %get-tuple-element.62), channel_id=1, source_target_pairs={{0,2},{2,0},{4,6},{6,4},{8,10},{10,8},{12,14},{14,12},{16,18},{18,... | collective-permute-start | bytes 98312 | tf_op jit(solution)/shard_map/ppermute | solution.py:543
  67.0 7.7 %collective-permute-start.7 = (bf16[128,128]{1,0:T(8,128)(2,1)}, bf16[128,128]{1,0:T(8,128)(2,1)S(1)}, u32[]{:S(2)}, u32[]{:S(2)}) collective-permute-start(bf16[128,128]{1,0:T(8,128)(2,1)} %get-tuple-element.63), channel_id=1, source_target_pairs={{0,30},{2,4},{4,2},{6,8},{8,6},{10,12},{12,10},{14,16},{16,14},{18... | collective-permute-start | bytes 98312 | tf_op jit(solution)/shard_map/ppermute | solution.py:532
  79.0 2.2 %collective-permute-start.8 = (f32[2,512,128]{2,1,0:T(8,128)}, f32[2,512,128]{2,1,0:T(8,128)S(1)}, u32[]{:S(2)}, u32[]{:S(2)}) collective-permute-start(f32[2,512,128]{2,1,0:T(8,128)} %get-tuple-element.65), channel_id=1, source_target_pairs={{0,1},{1,0},{2,3},{3,2},{4,5},{5,4},{6,7},{7,6},{8,9},{9,8},{10,11... | collective-permute-start | bytes 1572872 | tf_op jit(solution)/shard_map/ppermute | solution.py:558

commit v11 on v10

--- a/solution.py
+++ b/solution.py
@@ -69,21 +69,16 @@
     return out
 
 
-def lane_matrix(z, source, target):
+def lane_matrix(z, source, target, width=None):
     row = lax.broadcasted_iota(jnp.int32, (z.lanes, z.lanes), 0)
     lane = lax.broadcasted_iota(jnp.int32, (z.lanes, z.lanes), 1)
-    hit = (row - source == lane - target) & (lane >= target) & (lane < target + z.width)
+    hit = (row - source == lane - target) & (lane >= target) & (lane < target + (width or z.width))
     return jnp.where(hit, 1.0, 0.0).astype(BF16)
 
 
 def piece_start(z, k, size):
     place = lax.rem(lax.axis_index(GROUP) + k, z.group)
     return pl.multiple_of(place * size, size)
-
-
-def scatter_matrix(z, rows_of):
-    row = lax.broadcasted_iota(jnp.int32, (z.rows, z.face), 0)
-    return jnp.where(row == rows_of, 1.0, 0.0).astype(BF16)
 
 
 def pick_matrix(z, rows_of):
@@ -129,11 +124,13 @@
 def multiply(z, pieces, vector, store):
     for k, piece in enumerate(pieces):
         parts = [dot(piece[s], vector) for s in range(z.subs)]
-        store(piece_start(z, k, z.own), select(z, parts))
-
-
-def face_rows(z, pick, image_b, s):
-    return dot(dot(pick, image_b).astype(BF16), lane_matrix(z, s * z.width, 0))
+        store(k, piece_start(z, k, z.own), select(z, parts))
+
+
+def pick_both(z, left_rows, right_rows, s):
+    return jnp.concatenate(
+        [pick_matrix(z, left_rows[s : s + 1, :]), pick_matrix(z, right_rows[s : s + 1, :])], axis=0
+    )
 
 
 def store_faces(z, before, after, first_pair, second_pair):
@@ -166,25 +163,23 @@
         else:
             above = jnp.zeros((half, z.lanes), BF16)
             total = dot(faces[side], moved) + dot(bases[side], jnp.concatenate([above, below], axis=0))
-        out.append(total.astype(BF16))
+        out.append(total)
     return out
 
 
-def corrected(z, chosen, tall, both, left_rows, right_rows):
-    images, steps = [], []
-    m, at = z.modes, z.lanes // 2
-    for s in range(z.subs):
-        own = chosen[(s + 1) * m : (s + 2) * m]
-        none = jnp.zeros((at - m, z.lanes), BF16)
-        nil = jnp.zeros((at, z.lanes), BF16)
-        left = jnp.concatenate([tall[s], scatter_matrix(z, left_rows[s : s + 1, :])], axis=1)
-        right = scatter_matrix(z, right_rows[s : s + 1, :])
-        image = jnp.concatenate([own, none, nil, both[s][0]], axis=0)
-        step = jnp.concatenate([nil, own, none, jnp.zeros((z.face, z.lanes), BF16)], axis=0)
-        total = dot(left, jnp.concatenate([image, step], axis=1))
-        images.append(total[:, : z.lanes] + dot(right, both[s][1]))
-        steps.append(total[:, z.lanes :])
-    return select(z, steps), select(z, images)
+def correction_side(z, chosen, s, share):
+    m, half = z.modes, z.lanes // 2
+    own = chosen[(s + 1) * m : (s + 2) * m]
+    none = jnp.zeros((half - m, z.lanes), BF16)
+    nil = jnp.zeros((half, z.lanes), BF16)
+    image = jnp.concatenate([own, none, nil, share], axis=0)
+    step = jnp.concatenate([nil, own, none, jnp.zeros((z.face, z.lanes), BF16)], axis=0)
+    return jnp.concatenate([image, step], axis=1)
+
+
+def scatter_matrix(z, rows_of, start, count):
+    row = lax.broadcasted_iota(jnp.int32, (count, z.face), 0) + start
+    return jnp.where(row == rows_of, 1.0, 0.0).astype(BF16)
 
 
 def first_image_kernel(z, wait, *refs):
@@ -201,7 +196,7 @@
     for k in range(z.group):
         wait(k)
 
-    def store_solved(start, value):
+    def store_solved(k, start, value):
         solved[pl.ds(start, z.own), :] = value
         rounded[pl.ds(start, z.own), :] = value.astype(BF16)
 
@@ -223,16 +218,23 @@
         for s in range(z.subs):
             images[s, pl.ds(start, z.own), :] = parts[s].astype(BF16)
     left = (load_rows[...].astype(F32) - image[...]).astype(BF16)
-    start_modes[...] = select(z, [dot(basis_t[s], left) for s in range(z.subs)])
+    begun = []
     for s in range(z.subs):
         image_basis = images[s, :, z.lanes :]
         tall[s, :, :half] = image_basis[:, :half]
-        inner[s] = dot(basis_t[s], image_basis)[:, : z.modes].astype(BF16)
-        placed = jnp.concatenate([jnp.zeros((z.rows, half), BF16), image_basis[:, :half]], axis=1)
-        for rows_ref, out, side_t in ((left_rows, before, left_t), (right_rows, after, right_t)):
-            pick = pick_matrix(z, rows_ref[s : s + 1, :])
-            side_t[s] = dot_nt(basis_t[s], pick).astype(BF16)
-            out[s] = (face_rows(z, pick, images[s, :, : z.lanes], s) + dot(pick, placed)).astype(BF16)
+        restricted = dot(basis_t[s], jnp.concatenate([left, image_basis], axis=1))
+        begun.append(restricted[:, : z.lanes])
+        inner[s] = restricted[:, z.lanes : z.lanes + z.modes].astype(BF16)
+        pick = pick_both(z, left_rows, right_rows, s)
+        sides_t = dot_nt(basis_t[s], pick).astype(BF16)
+        left_t[s] = sides_t[:, : z.face]
+        right_t[s] = sides_t[:, z.face :]
+        picked = dot(pick, images[s]).astype(BF16)
+        faces = dot(picked[:, : z.lanes], lane_matrix(z, s * z.width, 0))
+        faces = (faces + dot(picked[:, z.lanes :], lane_matrix(z, 0, half, z.modes))).astype(BF16)
+        before[s] = faces[: z.face]
+        after[s] = faces[z.face :]
+    start_modes[...] = select(z, begun)
     store_faces(z, before, after, first_pair, second_pair)
 
 
@@ -241,36 +243,44 @@
     rest = refs[2 * z.group :]
     load_rows, old_image, tall, old_solved, chosen = rest[:5]
     before, after, first_got, second_got, left_rows, right_rows = rest[5:11]
-    solved, remaining, new_before, new_after, first_pair, second_pair, rounded, image = rest[11:]
-    both = []
+    new_before, new_after, first_pair, second_pair = rest[11:15]
+    values = rest[15 : 15 + z.group]
+    base, rounded, image = rest[15 + z.group :]
+    steps, images = [], []
     for s in range(z.subs):
         faces = sides(z, before, after, first_got, second_got, s)
-        both.append(shares(z, s, chosen, faces))
-    step, added = corrected(z, chosen, tall, both, left_rows, right_rows)
-    residual = (load_rows[...].astype(F32) - old_image[...] - added).astype(BF16)
-    solved[...] = old_solved[...] + step
+        both = [share.astype(BF16) for share in shares(z, s, chosen, faces)]
+        left = jnp.concatenate([tall[s], scatter_matrix(z, left_rows[s : s + 1, :], 0, z.rows)], axis=1)
+        total = dot(left, correction_side(z, chosen, s, both[0]))
+        steps.append(total[:, z.lanes :])
+        images.append(total[:, : z.lanes] + dot(scatter_matrix(z, right_rows[s : s + 1, :], 0, z.rows), both[1]))
+    residual = (load_rows[...].astype(F32) - old_image[...] - select(z, images)).astype(BF16)
+    base[...] = old_solved[...] + select(z, steps)
     for k in range(z.group):
         wait(k)
 
-    def store_solved(start, value):
-        value = value + solved[pl.ds(start, z.own), :]
-        solved[pl.ds(start, z.own), :] = value
+    def store_solved(k, start, value):
+        value = value + base[pl.ds(start, z.own), :]
+        values[k][0] = value
         rounded[pl.ds(start, z.own), :] = value.astype(BF16)
 
     multiply(z, inverse, residual, store_solved)
 
-    def store_image(start, value):
+    def store_image(k, start, value):
         place = pl.ds(start, z.own)
-        remaining[place, :] = load_rows[place, :].astype(F32) - value
+        values[k][1] = load_rows[place, :].astype(F32) - value
         image[place, :] = value.astype(BF16)
 
     for k in range(z.group):
         wait(z.group + k)
     multiply(z, stiffness, rounded[...], store_image)
-    image_b = image[...]
-    for s in range(z.subs):
-        new_before[s] = face_rows(z, pick_matrix(z, left_rows[s : s + 1, :]), image_b, s).astype(BF16)
-        new_after[s] = face_rows(z, pick_matrix(z, right_rows[s : s + 1, :]), image_b, s).astype(BF16)
+    pick = jnp.concatenate([pick_both(z, left_rows, right_rows, s) for s in range(z.subs)], axis=0)
+    picked = dot(pick, image[...]).astype(BF16)
+    for s in range(z.subs):
+        own = picked[2 * s * z.face : 2 * (s + 1) * z.face]
+        faces = dot(own, lane_matrix(z, s * z.width, 0)).astype(BF16)
+        new_before[s] = faces[: z.face]
+        new_after[s] = faces[z.face :]
     store_faces(z, new_before, new_after, first_pair, second_pair)
 
 
@@ -345,41 +355,59 @@
         faces = sides(z, before, after, first_got, second_got, s)
         both = shares(z, s, rows, faces)
         total = dot(inner[s], rows[(s + 1) * m : (s + 2) * m])
-        parts.append(total + dot(left_t[s], both[0]) + dot(right_t[s], both[1]))
+        parts.append(total + dot(left_t[s], both[0].astype(BF16)) + dot(right_t[s], both[1].astype(BF16)))
     modes = (start_modes[...] - select(z, parts)).astype(BF16)
     for k in range(z.n):
         message[k] = modes
 
 
-def last_kernel(z, *refs):
-    arrived, picks, remaining, solved, tall = refs[:5]
-    before, after, first_got, second_got = refs[5:9]
-    base_before, base_after, base_first, base_second, left_rows, right_rows = refs[9:15]
-    *outs, whole = refs[15:]
+def pick_kernel(z, *refs):
+    arrived, picks, before, after, first_got, second_got = refs[:6]
+    base_before, base_after, base_first, base_second, out = refs[6:]
     chosen = picked_rows(z, arrived, picks)
-    both = []
+    near = chosen.shape[0]
+    lefts, rights = [], []
     for s in range(z.subs):
         values = sides(z, before, after, first_got, second_got, s)
         bases = sides(z, base_before, base_after, base_first, base_second, s)
-        both.append(shares(z, s, chosen, values, bases))
-    step, added = corrected(z, chosen, tall, both, left_rows, right_rows)
-    whole[0] = solved[...] + step
-    whole[1] = remaining[...] - added
-    for k, out in enumerate(outs):
-        out[...] = whole[:, pl.ds(piece_start(z, k, z.own), z.own), :]
-
-
-def unpack_kernel(z, *refs):
-    pieces, outs = refs[: z.group], refs[z.group :]
-    for at, out in enumerate(outs):
+        left, right = shares(z, s, chosen, values, bases)
+        lefts.append(left)
+        rights.append(right)
+    out[:near] = chosen
+    out[near : near + z.face] = select(z, lefts).astype(BF16)
+    out[near + z.face :] = select(z, rights).astype(BF16)
+
+
+def last_kernel(z, *refs):
+    chosen, values = refs[: z.group], refs[z.group : 2 * z.group]
+    tall, left_rows, right_rows, second_pass, final_residual = refs[2 * z.group :]
+    start = piece_start(z, 0, z.own)
+    near = (z.subs + 2) * z.modes
+    lefts, rights = [], []
+    for s in range(z.subs):
+        scatter = scatter_matrix(z, left_rows[s : s + 1, :], start, z.own)
+        lefts.append(jnp.concatenate([tall[s, pl.ds(start, z.own), :], scatter], axis=1))
+        rights.append(scatter_matrix(z, right_rows[s : s + 1, :], start, z.own))
+    done = [jnp.zeros((z.own, z.lanes), F32) for _ in range(2 * z.subs)]
+    for k in range(z.group):
+        rows = chosen[k][:near]
+        left, right = chosen[k][near : near + z.face], chosen[k][near + z.face :]
+        steps, images = [], []
         for s in range(z.subs):
-            total = jnp.zeros((z.own, z.lanes), F32)
-            for k, piece in enumerate(pieces):
-                place = lax.rem(lax.axis_index(GROUP) + k, z.group)
+            total = dot(lefts[s], correction_side(z, rows, s, left))
+            steps.append(total[:, z.lanes :])
+            images.append(total[:, : z.lanes] + dot(rights[s], right))
+        pair = values[k][0] + select(z, steps), values[k][1] - select(z, images)
+        place = lax.rem(lax.axis_index(GROUP) + k, z.group)
+        for at, packed in enumerate(pair):
+            for s in range(z.subs):
                 turn = lax.rem((place - s + z.subs * z.group) * z.width, z.lanes)
-                turned = pltpu.roll(piece[at], turn, 1)
-                total = jnp.where(lane_mask(z, place, turned.shape), turned, total)
-            out[s] = total[:, : z.cases]
+                turned = pltpu.roll(packed, turn, 1)
+                here = at * z.subs + s
+                done[here] = jnp.where(lane_mask(z, place, turned.shape), turned, done[here])
+    for s in range(z.subs):
+        second_pass[s] = done[s][:, : z.cases]
+        final_residual[s] = done[z.subs + s][:, : z.cases]
 
 
 def call(kernel, outs, operands, flops, scratch=(), late=(), loose=(), name=None):
@@ -516,21 +544,21 @@
     restricted = spread(message)
 
     bases = [before, after, first_got, second_got]
-    solved, remaining, before, after, first_pair, second_pair = call(
+    before, after, first_pair, second_pair, *values = call(
         functools.partial(second_image_kernel, z),
-        [packed_f, packed_f, faces, faces, outer, outer],
+        [faces, faces, outer, outer, *[shape((2, z.own, lanes), F32)] * group],
         [
             *inverse_pieces, *stiffness_pieces, load_rows, image, tall, solved, chosen,
             *bases, left_rows, right_rows,
         ],
         work,
-        [pltpu.VMEM((rows, lanes), BF16), pltpu.VMEM((rows, lanes), BF16)],
+        [pltpu.VMEM((rows, lanes), F32), pltpu.VMEM((rows, lanes), BF16), pltpu.VMEM((rows, lanes), BF16)],
         late=range(2 * group),
         loose=[*arrivals, 2 * group + 7, 2 * group + 8],
         name="second_image",
     )
     second_got = lax.ppermute(second_pair, "sub", second_pairs)
-    restricted, remaining = lax.optimization_barrier((restricted, remaining))
+    restricted, before = lax.optimization_barrier((restricted, before))
     (message,) = call(
         functools.partial(coarse_kernel, z),
         [copies],
@@ -541,26 +569,27 @@
     )
     coarse = spread(message)
     first_got = lax.ppermute(first_pair, "sub", first_pairs)
-    parts = call(
-        functools.partial(last_kernel, z),
-        [shape((2, z.own, lanes), F32)] * group,
-        [
-            coarse, picks, remaining, solved, tall,
-            before, after, first_got, second_got, *bases, left_rows, right_rows,
-        ],
-        work // 8,
-        [pltpu.VMEM((2, rows, lanes), F32)],
-        loose=[0, 7, 8, 11, 12],
-        name="last",
-    )
-    swapped = [parts[0]]
+    swapped = [values[0]]
     for k in range(1, group):
-        swapped.append(lax.ppermute(parts[k], GROUP, [(g, (g + k) % group) for g in range(group)]))
+        swapped.append(lax.ppermute(values[k], GROUP, [(g, (g + k) % group) for g in range(group)]))
     swapped = [swapped[(group - k) % group] for k in range(group)]
+    (chosen,) = call(
+        functools.partial(pick_kernel, z),
+        [shape((near + 2 * face, lanes), BF16)],
+        [coarse, picks, before, after, first_got, second_got, *bases],
+        work // 64,
+        loose=[0, 4, 5, 8, 9],
+        name="pick",
+    )
     out = shape((subs, z.own, z.cases), F32)
     return tuple(
         call(
-            functools.partial(unpack_kernel, z), [out, out], swapped, work // 64, loose=range(1, group), name="unpack"
+            functools.partial(last_kernel, z),
+            [out, out],
+            [*pieces_of(chosen, group), *swapped, tall, left_rows, right_rows],
+            work // 8,
+            loose=[*range(1, group), *range(group + 1, 2 * group)],
+            name="last",
         )
     )
 

time: 84.4 us -> 83.8 us (level)
    ppermute x1, waiting for transfers between devices: 2.11 us -> 0.01 us  [body(): lax.ppermute(values[k], GROUP, [(g, (g + k) % group) for g in range(group)])]
    ppermute x4 -> x5, waiting for transfers between devices: 1.16 us -> 2.67 us  [pieces_of(): lax.ppermute(block, GROUP, [((g + k) % group, g) for g in range(group)])]
  transfers between devices with their start and end apart: 13 -> 14, of which waited for: 6 -> 6; matrix products, arithmetic and copies ran while one was open for 0% -> 0% of each run, Pallas kernels for 20% -> 25%
where the time goes in v11:
time: 83.8 us; the launch traced here: 83.2 us
  starting transfers between devices  36.4 us (43%)
  Pallas kernels  30.8 us (37%)
  waiting for transfers between devices  15.2 us (18%)
    pallas_call x8, Pallas kernels, call(): pl.pallas_call(whole, out_shape=[pltpu.HBM(o.shape, o.dtype) for o in out...  30.8 us
    all_to_all x2, starting transfers between devices, body(): restricted = spread(message)  13 us
    all_to_all x2, starting transfers between devices, body(): coarse = spread(message)  9.9 us
    ppermute x2, waiting for transfers between devices, body(): second_got = lax.ppermute(second_pair, 'sub', second_pairs)  8.6 us
    ppermute x2, starting transfers between devices, body(): second_got = lax.ppermute(second_pair, 'sub', second_pairs)  8.3 us
    all_to_all x2, waiting for transfers between devices, body(): restricted = spread(message)  3.95 us
    ppermute x2, starting transfers between devices, body(): first_got = lax.ppermute(first_pair, 'sub', first_pairs)  3.88 us
    ppermute x5, waiting for transfers between devices, pieces_of(): lax.ppermute(block, GROUP, [((g + k) % group, g) for g in range(group)])  2.67 us
  transfers between devices with their start and end apart: 14, of which 6 were waited for; matrix products, arithmetic and copies ran while one was open for 0% of the time, Pallas kernels for 25%

profile of v11, /device:TPU:0, one launch (start us, length us, event | category | flops | bytes accessed | tf_op | source)
XLA Modules:
  0.0 83.2 jit_solution(7288999857116716106)
XLA Ops:
  0.6 0.5 collective-permute-start.1
  1.1 1.2 %collective-permute-done.1.refs_1_.refs_5_ = bf16[2,48,512]{2,1,0:T(8,128)(2,1)S(1)} collective-permute-done((bf16[2,48,512]{2,1,0:T(8,128)(2,1)}, bf16[2,48,512]{2,1,0:T(8,128)(2,1)S(1)}, u32[]{:S(2)}, u32[]{:S(2)}) %collective-permute-start.1) | collective-permute-done | bytes 98336 | tf_op jit(solution)/shard_map/ppermute | solution.py:464
  2.3 0.4 collective-permute-start.2
  2.7 0.2 collective-permute-start.3
  2.8 2.3 %open.1 = bf16[16,64,128]{2,1,0:T(8,128)(2,1)} custom-call(bf16[2,48,512]{2,1,0:T(8,128)(2,1)} %bitcast.2, bf16[2,48,512]{2,1,0:T(8,128)(2,1)S(1)} %collective-permute-done.1.refs_1_.refs_5_, bf16[2,1024,128]{2,1,0:T(8,128)(2,1)} %refs_6_.2, s32[2,48]{1,0:T(2,128)} %refs_3_.2), custom_call_target="tpu_custom_call" | custom-call | flops 67108864 | bytes 983424 | tf_op jit(solution)/shard_map/open/pallas_call | solution.py:440
  5.1 8.2 %all-to-all-start = ((bf16[16,64,128]{2,1,0:T(8,128)(2,1)}), bf16[16,64,128]{2,1,0:T(8,128)(2,1)S(1)}, u32[]{:S(2)}, u32[]{:S(2)}) async-start(bf16[16,64,128]{2,1,0:T(8,128)(2,1)} %open.1), calls=%async_computation | async-start | bytes 524288 | tf_op jit(solution)/shard_map/all_to_all | solution.py:500
  13.3 0.1 collective-permute-start
  13.4 0.0 collective-permute-done.2.refs_1_
  13.4 0.0 collective-permute-done.3.refs_3_
  13.4 7.2 %first_image.1 = (bf16[1024,128]{1,0:T(8,128)(2,1)}, f32[1024,128]{1,0:T(8,128)}, f32[1024,128]{1,0:T(8,128)}, bf16[2,128,128]{2,1,0:T(8,128)(2,1)}, bf16[2,128,...) custom-call(bf16[2,512,1024]{2,1,0:T(8,128)(2,1)} %refs_0_.3, ...), custom_call_target="tpu_custom_call" | custom-call | flops 1073741824 | bytes 11226112 | tf_op jit(solution)/shard_map/first_image/pallas_call | solution.py:440
  20.6 2.9 %all-to-all-done.refs_2_ = bf16[16,64,128]{2,1,0:T(8,128)(2,1)S(1)} async-done(((bf16[16,64,128]{2,1,0:T(8,128)(2,1)}), bf16[16,64,128]{2,1,0:T(8,128)(2,1)S(1)}, u32[]{:S(2)}, u32[]{:S(2)}) %all-to-all-start) | async-done | bytes 262176 | tf_op jit(solution)/shard_map/all_to_all | solution.py:500
  23.5 3.5 %order.1 = (bf16[2,96,768]{2,1,0:T(8,128)(2,1)}, bf16[2,192,768]{2,1,0:T(8,128)(2,1)}, bf16[16,48,128]{2,1,0:T(8,128)(2,1)}) custom-call(bf16[96,768]{1,0:T(8,128)(2,1)} %refs_0_.2, bf16[96,768]{1,0:T(8,128)(2,1)S(1)} %collective-permute-done.refs_1_, bf16[16,64,128]{2,1,0:T(8,128)(2,1)S(1)} %all-to-all-done.refs_2_, ...), custom_call_target="tpu_custom_call" | custom-call | flops 452984832 | bytes 1890304 | tf_op jit(solution)/shard_map/order/pallas_call | solution.py:440
  27.0 4.0 %all-to-all-start.1 = ((bf16[16,48,128]{2,1,0:T(8,128)(2,1)}), bf16[16,48,128]{2,1,0:T(8,128)(2,1)S(1)}, u32[]{:S(2)}, u32[]{:S(2)}) async-start(bf16[16,48,128]{2,1,0:T(8,128)(2,1)} %get-tuple-element.38), calls=%async_computation.1 | async-start | bytes 393216 | tf_op jit(solution)/shard_map/all_to_all | solution.py:534
  31.0 1.9 %collective-permute-start.4 = (bf16[128,128]{1,0:T(8,128)(2,1)}, bf16[128,128]{1,0:T(8,128)(2,1)S(1)}, u32[]{:S(2)}, u32[]{:S(2)}) collective-permute-start(bf16[128,128]{1,0:T(8,128)(2,1)} %get-tuple-element.46), channel_id=1, source_target_pairs={{0,2},{2,0},{4,6},{6,4},{8,10},{10,8},{12,14},{14,12},{16,18},{18,... | collective-permute-start | bytes 98312 | tf_op jit(solution)/shard_map/ppermute | solution.py:535
  33.0 4.2 %collective-permute-start.5 = (bf16[128,128]{1,0:T(8,128)(2,1)}, bf16[128,128]{1,0:T(8,128)(2,1)S(1)}, u32[]{:S(2)}, u32[]{:S(2)}) collective-permute-start(bf16[128,128]{1,0:T(8,128)(2,1)} %get-tuple-element.36), channel_id=1, source_target_pairs={{0,30},{2,4},{4,2},{6,8},{8,6},{10,12},{12,10},{14,16},{16,14},{18... | collective-permute-start | bytes 98312 | tf_op jit(solution)/shard_map/ppermute | solution.py:523
  37.1 4.3 %collective-permute-done.5.refs_9_.refs_12_ = bf16[128,128]{1,0:T(8,128)(2,1)S(1)} collective-permute-done((bf16[128,128]{1,0:T(8,128)(2,1)}, bf16[128,128]{1,0:T(8,128)(2,1)S(1)}, u32[]{:S(2)}, u32[]{:S(2)}) %collective-permute-start.5) | collective-permute-done | bytes 32800 | tf_op jit(solution)/shard_map/ppermute | solution.py:523
  41.4 0.0 all-to-all-done.1.refs_0_
  41.4 2.8 %update.1 = (bf16[192,128]{1,0:T(8,128)(2,1)}, bf16[16,48,128]{2,1,0:T(8,128)(2,1)}) custom-call(bf16[16,48,128]{2,1,0:T(8,128)(2,1)S(1)} %all-to-all-done.1.refs_0_, bf16[2,192,768]{2,1,0:T(8,128)(2,1)} %get-tuple-element.39.refs_1_, f32[48,128]{1,0:T(8,128)} %get-tuple-element.40.refs_2_, bf16[2,48,48]{2,1,0:T(8,128)(2,1)} %get-tuple-element.41.refs_3_, ...), custom_call_target="tpu_custom_call" | custom-call | flops 16777216 | bytes 1311744 | tf_op jit(solution)/shard_map/update/pallas_call | solution.py:440
  44.3 4.8 %all-to-all-start.2 = ((bf16[16,48,128]{2,1,0:T(8,128)(2,1)}), bf16[16,48,128]{2,1,0:T(8,128)(2,1)S(1)}, u32[]{:S(2)}, u32[]{:S(2)}) async-start(bf16[16,48,128]{2,1,0:T(8,128)(2,1)} %get-tuple-element.47), calls=%async_computation.2 | async-start | bytes 393216 | tf_op jit(solution)/shard_map/all_to_all | solution.py:544
  49.1 6.9 %second_image.1 = (bf16[2,128,128]{2,1,0:T(8,128)(2,1)}, bf16[2,128,128]{2,1,0:T(8,128)(2,1)}, bf16[128,128]{1,0:T(8,128)(2,1)}, bf16[128,128]{1,0:T(8,128)(2,1)...) custom-call(bf16[2,512,1024]{2,1,0:T(8,128)(2,1)} %refs_0_.3, ...), custom_call_target="tpu_custom_call" | custom-call | flops 1073741824 | bytes 11716608 | tf_op jit(solution)/shard_map/second_image/pallas_call | solution.py:440
  56.0 0.1 collective-permute-start.9
  56.1 1.0 %all-to-all-done.2.refs_0_ = bf16[16,48,128]{2,1,0:T(8,128)(2,1)S(1)} async-done(((bf16[16,48,128]{2,1,0:T(8,128)(2,1)}), bf16[16,48,128]{2,1,0:T(8,128)(2,1)S(1)}, u32[]{:S(2)}, u32[]{:S(2)}) %all-to-all-start.2) | async-done | bytes 196640 | tf_op jit(solution)/shard_map/all_to_all | solution.py:544
  57.2 2.2 %coarse.1 = bf16[16,48,128]{2,1,0:T(8,128)(2,1)} custom-call(bf16[16,48,128]{2,1,0:T(8,128)(2,1)S(1)} %all-to-all-done.2.refs_0_, bf16[2,96,768]{2,1,0:T(8,128)(2,1)} %get-tuple-element.55.refs_1_), custom_call_target="tpu_custom_call" | custom-call | flops 16777216 | bytes 688128 | tf_op jit(solution)/shard_map/coarse/pallas_call | solution.py:440
  59.4 5.9 %all-to-all-start.3 = ((bf16[16,48,128]{2,1,0:T(8,128)(2,1)}), bf16[16,48,128]{2,1,0:T(8,128)(2,1)S(1)}, u32[]{:S(2)}, u32[]{:S(2)}) async-start(bf16[16,48,128]{2,1,0:T(8,128)(2,1)} %coarse.1), calls=%async_computation.3 | async-start | bytes 393216 | tf_op jit(solution)/shard_map/all_to_all | solution.py:570
  65.3 1.9 %collective-permute-start.6 = (bf16[128,128]{1,0:T(8,128)(2,1)}, bf16[128,128]{1,0:T(8,128)(2,1)S(1)}, u32[]{:S(2)}, u32[]{:S(2)}) collective-permute-start(bf16[128,128]{1,0:T(8,128)(2,1)} %get-tuple-element.58), channel_id=1, source_target_pairs={{0,2},{2,0},{4,6},{6,4},{8,10},{10,8},{12,14},{14,12},{16,18},{18,... | collective-permute-start | bytes 98312 | tf_op jit(solution)/shard_map/ppermute | solution.py:571
  67.2 4.2 %collective-permute-start.7 = (bf16[128,128]{1,0:T(8,128)(2,1)}, bf16[128,128]{1,0:T(8,128)(2,1)S(1)}, u32[]{:S(2)}, u32[]{:S(2)}) collective-permute-start(bf16[128,128]{1,0:T(8,128)(2,1)} %get-tuple-element.59), channel_id=1, source_target_pairs={{0,30},{2,4},{4,2},{6,8},{8,6},{10,12},{12,10},{14,16},{16,14},{18... | collective-permute-start | bytes 98312 | tf_op jit(solution)/shard_map/ppermute | solution.py:560
  71.4 0.0 collective-permute-done.6.refs_4_
  71.4 4.3 %collective-permute-done.7.refs_5_ = bf16[128,128]{1,0:T(8,128)(2,1)S(1)} collective-permute-done((bf16[128,128]{1,0:T(8,128)(2,1)}, bf16[128,128]{1,0:T(8,128)(2,1)S(1)}, u32[]{:S(2)}, u32[]{:S(2)}) %collective-permute-start.7) | collective-permute-done | bytes 32800 | tf_op jit(solution)/shard_map/ppermute | solution.py:560
  75.7 2.6 %pick.1.refs_0_ = bf16[448,128]{1,0:T(8,128)(2,1)} custom-call(bf16[16,48,128]{2,1,0:T(8,128)(2,1)S(1)} %all-to-all-done.3.refs_0_, bf16[2,192,768]{2,1,0:T(8,128)(2,1)} %get-tuple-element.39.refs_1_, bf16[2,128,128]{2,1,0:T(8,128)(2,1)} %get-tuple-element.56.refs_2_, bf16[2,128,128]{2,1,0:T(8,128)(2,1)} %get-tuple-element.57.refs_3_, ...), custom_call_target="tpu_custom_call" | custom-call | flops 16777216 | bytes 1294336 | tf_op jit(solution)/shard_map/pick/pallas_call | solution.py:440
  78.3 0.1 collective-permute-start.8
  78.4 1.5 %collective-permute-done.8.refs_1_ = bf16[448,128]{1,0:T(8,128)(2,1)S(1)} collective-permute-done((bf16[448,128]{1,0:T(8,128)(2,1)}, bf16[448,128]{1,0:T(8,128)(2,1)S(1)}, u32[]{:S(2)}, u32[]{:S(2)}) %collective-permute-start.8) | collective-permute-done | bytes 114720 | tf_op jit(solution)/shard_map/ppermute | solution.py:464
  79.9 3.3 %last.1 = (f32[2,512,128]{2,1,0:T(8,128)}, f32[2,512,128]{2,1,0:T(8,128)}) custom-call(bf16[448,128]{1,0:T(8,128)(2,1)} %pick.1.refs_0_, bf16[448,128]{1,0:T(8,128)(2,1)S(1)} %collective-permute-done.8.refs_1_, f32[2,512,128]{2,1,0:T(8,128)} %get-tuple-element.60.refs_2_, f32[2,512,128]{2,1,0:T(8,128)S(1)} %collective-permute-done.9.refs_3_, ...), custom_call_target="tpu_custom_call" | custom-call | flops 134217728 | bytes 2852864 | tf_op jit(solution)/shard_map/last/pallas_call | solution.py:440
  (4 shorter events, 0.0 us)
Async XLA Ops:
  0.6 1.7 %collective-permute-start.1 = (bf16[2,48,512]{2,1,0:T(8,128)(2,1)}, bf16[2,48,512]{2,1,0:T(8,128)(2,1)S(1)}, u32[]{:S(2)}, u32[]{:S(2)}) collective-permute-start(bf16[2,48,512]{2,1,0:T(8,128)(2,1)} %bitcast.1), channel_id=1, source_target_pairs={{1,0},{0,1},{3,2},{2,3},{5,4},{4,5},{7,6},{6,7},{9,8},{8,9},{11,10... | collective-permute-start | bytes 294920 | tf_op jit(solution)/shard_map/ppermute | solution.py:464
  2.3 11.1 %collective-permute-start.2 = (bf16[2,512,1024]{2,1,0:T(8,128)(2,1)}, bf16[2,512,1024]{2,1,0:T(8,128)(2,1)S(1)}, u32[]{:S(2)}, u32[]{:S(2)}) collective-permute-start(bf16[2,512,1024]{2,1,0:T(8,128)(2,1)} %refs_0_.3), channel_id=1, source_target_pairs={{1,0},{0,1},{3,2},{2,3},{5,4},{4,5},{7,6},{6,7},{9,8},{8,9},{11,10... | collective-permute-start | bytes 6291464 | tf_op jit(solution)/shard_map/ppermute | solution.py:464
  2.7 10.8 %collective-permute-start.3 = (bf16[2,512,1024]{2,1,0:T(8,128)(2,1)}, bf16[2,512,1024]{2,1,0:T(8,128)(2,1)}, u32[]{:S(2)}, u32[]{:S(2)}) collective-permute-start(bf16[2,512,1024]{2,1,0:T(8,128)(2,1)} %refs_2_.3), channel_id=1, source_target_pairs={{1,0},{0,1},{3,2},{2,3},{5,4},{4,5},{7,6},{6,7},{9,8},{8,9},{11,10... | collective-permute-start | bytes 6291464 | tf_op jit(solution)/shard_map/ppermute | solution.py:464
  5.1 18.4 %all-to-all-start = ((bf16[16,64,128]{2,1,0:T(8,128)(2,1)}), bf16[16,64,128]{2,1,0:T(8,128)(2,1)S(1)}, u32[]{:S(2)}, u32[]{:S(2)}) async-start(bf16[16,64,128]{2,1,0:T(8,128)(2,1)} %open.1), calls=%async_computation | async-start | bytes 524288 | tf_op jit(solution)/shard_map/all_to_all | solution.py:500
  13.3 10.2 %collective-permute-start = (bf16[96,768]{1,0:T(8,128)(2,1)}, bf16[96,768]{1,0:T(8,128)(2,1)S(1)}, u32[]{:S(2)}, u32[]{:S(2)}) collective-permute-start(bf16[96,768]{1,0:T(8,128)(2,1)} %refs_0_.2), channel_id=1, source_target_pairs={{1,0},{0,1},{3,2},{2,3},{5,4},{4,5},{7,6},{6,7},{9,8},{8,9},{11,10... | collective-permute-start | bytes 442376 | tf_op jit(solution)/shard_map/ppermute | solution.py:464
  27.0 14.4 %all-to-all-start.1 = ((bf16[16,48,128]{2,1,0:T(8,128)(2,1)}), bf16[16,48,128]{2,1,0:T(8,128)(2,1)S(1)}, u32[]{:S(2)}, u32[]{:S(2)}) async-start(bf16[16,48,128]{2,1,0:T(8,128)(2,1)} %get-tuple-element.38), calls=%async_computation.1 | async-start | bytes 393216 | tf_op jit(solution)/shard_map/all_to_all | solution.py:534
  31.0 6.1 %collective-permute-start.4 = (bf16[128,128]{1,0:T(8,128)(2,1)}, bf16[128,128]{1,0:T(8,128)(2,1)S(1)}, u32[]{:S(2)}, u32[]{:S(2)}) collective-permute-start(bf16[128,128]{1,0:T(8,128)(2,1)} %get-tuple-element.46), channel_id=1, source_target_pairs={{0,2},{2,0},{4,6},{6,4},{8,10},{10,8},{12,14},{14,12},{16,18},{18,... | collective-permute-start | bytes 98312 | tf_op jit(solution)/shard_map/ppermute | solution.py:535
  33.0 8.5 %collective-permute-start.5 = (bf16[128,128]{1,0:T(8,128)(2,1)}, bf16[128,128]{1,0:T(8,128)(2,1)S(1)}, u32[]{:S(2)}, u32[]{:S(2)}) collective-permute-start(bf16[128,128]{1,0:T(8,128)(2,1)} %get-tuple-element.36), channel_id=1, source_target_pairs={{0,30},{2,4},{4,2},{6,8},{8,6},{10,12},{12,10},{14,16},{16,14},{18... | collective-permute-start | bytes 98312 | tf_op jit(solution)/shard_map/ppermute | solution.py:523
  44.3 12.9 %all-to-all-start.2 = ((bf16[16,48,128]{2,1,0:T(8,128)(2,1)}), bf16[16,48,128]{2,1,0:T(8,128)(2,1)S(1)}, u32[]{:S(2)}, u32[]{:S(2)}) async-start(bf16[16,48,128]{2,1,0:T(8,128)(2,1)} %get-tuple-element.47), calls=%async_computation.2 | async-start | bytes 393216 | tf_op jit(solution)/shard_map/all_to_all | solution.py:544
  56.0 22.4 %collective-permute-start.9 = (f32[2,512,128]{2,1,0:T(8,128)}, f32[2,512,128]{2,1,0:T(8,128)S(1)}, u32[]{:S(2)}, u32[]{:S(2)}) collective-permute-start(f32[2,512,128]{2,1,0:T(8,128)} %get-tuple-element.61), channel_id=1, source_target_pairs={{0,1},{1,0},{2,3},{3,2},{4,5},{5,4},{6,7},{7,6},{8,9},{9,8},{10,11... | collective-permute-start | bytes 1572872 | tf_op jit(solution)/shard_map/ppermute | solution.py:574
  59.4 16.3 %all-to-all-start.3 = ((bf16[16,48,128]{2,1,0:T(8,128)(2,1)}), bf16[16,48,128]{2,1,0:T(8,128)(2,1)S(1)}, u32[]{:S(2)}, u32[]{:S(2)}) async-start(bf16[16,48,128]{2,1,0:T(8,128)(2,1)} %coarse.1), calls=%async_computation.3 | async-start | bytes 393216 | tf_op jit(solution)/shard_map/all_to_all | solution.py:570
  65.3 6.1 %collective-permute-start.6 = (bf16[128,128]{1,0:T(8,128)(2,1)}, bf16[128,128]{1,0:T(8,128)(2,1)S(1)}, u32[]{:S(2)}, u32[]{:S(2)}) collective-permute-start(bf16[128,128]{1,0:T(8,128)(2,1)} %get-tuple-element.58), channel_id=1, source_target_pairs={{0,2},{2,0},{4,6},{6,4},{8,10},{10,8},{12,14},{14,12},{16,18},{18,... | collective-permute-start | bytes 98312 | tf_op jit(solution)/shard_map/ppermute | solution.py:571
  67.2 8.5 %collective-permute-start.7 = (bf16[128,128]{1,0:T(8,128)(2,1)}, bf16[128,128]{1,0:T(8,128)(2,1)S(1)}, u32[]{:S(2)}, u32[]{:S(2)}) collective-permute-start(bf16[128,128]{1,0:T(8,128)(2,1)} %get-tuple-element.59), channel_id=1, source_target_pairs={{0,30},{2,4},{4,2},{6,8},{8,6},{10,12},{12,10},{14,16},{16,14},{18... | collective-permute-start | bytes 98312 | tf_op jit(solution)/shard_map/ppermute | solution.py:560
  78.3 1.6 %collective-permute-start.8 = (bf16[448,128]{1,0:T(8,128)(2,1)}, bf16[448,128]{1,0:T(8,128)(2,1)S(1)}, u32[]{:S(2)}, u32[]{:S(2)}) collective-permute-start(bf16[448,128]{1,0:T(8,128)(2,1)} %pick.1.refs_0_), channel_id=1, source_target_pairs={{1,0},{0,1},{3,2},{2,3},{5,4},{4,5},{7,6},{6,7},{9,8},{8,9},{11,10... | collective-permute-start | bytes 344072 | tf_op jit(solution)/shard_map/ppermute | solution.py:464

commit v12 on v11

--- a/solution.py
+++ b/solution.py
@@ -11,7 +11,7 @@
 GROUP = ("crow", "ccol")
 F32 = jnp.float32
 BF16 = jnp.bfloat16
-VMEM_BYTES = 48 * 1024 * 1024
+VMEM_BYTES = 28 * 1024 * 1024
 DIGIT_ROWS = 16
 DIGIT_BITS = 8
 DIGIT = 1 << DIGIT_BITS
@@ -193,13 +193,12 @@
     for s in range(1, z.subs):
         packed = packed + dot(loads[s], case_matrix(z, s))
     load_rows[...] = packed.astype(BF16)
-    for k in range(z.group):
-        wait(k)
 
     def store_solved(k, start, value):
         solved[pl.ds(start, z.own), :] = value
         rounded[pl.ds(start, z.own), :] = value.astype(BF16)
 
+    wait(0)
     multiply(z, inverse, load_rows[...], store_solved)
     solved_b = rounded[...]
     half = z.lanes // 2
@@ -210,8 +209,8 @@
         both[s, :, : z.lanes] = solved_b
         both[s, :, z.lanes : z.lanes + z.modes] = basis
         both[s, :, z.lanes + z.modes :] = jnp.zeros((z.rows, z.lanes - z.modes), BF16)
+    wait(z.group)
     for k, piece in enumerate(stiffness):
-        wait(z.group + k)
         start = piece_start(z, k, z.own)
         parts = [dot(piece[s], both[s]) for s in range(z.subs)]
         image[pl.ds(start, z.own), :] = select(z, [part[:, : z.lanes] for part in parts])
@@ -256,14 +255,13 @@
         images.append(total[:, : z.lanes] + dot(scatter_matrix(z, right_rows[s : s + 1, :], 0, z.rows), both[1]))
     residual = (load_rows[...].astype(F32) - old_image[...] - select(z, images)).astype(BF16)
     base[...] = old_solved[...] + select(z, steps)
-    for k in range(z.group):
-        wait(k)
 
     def store_solved(k, start, value):
         value = value + base[pl.ds(start, z.own), :]
         values[k][0] = value
         rounded[pl.ds(start, z.own), :] = value.astype(BF16)
 
+    wait(0)
     multiply(z, inverse, residual, store_solved)
 
     def store_image(k, start, value):
@@ -271,8 +269,7 @@
         values[k][1] = load_rows[place, :].astype(F32) - value
         image[place, :] = value.astype(BF16)
 
-    for k in range(z.group):
-        wait(z.group + k)
+    wait(z.group)
     multiply(z, stiffness, rounded[...], store_image)
     pick = jnp.concatenate([pick_both(z, left_rows, right_rows, s) for s in range(z.subs)], axis=0)
     picked = dot(pick, image[...]).astype(BF16)
@@ -410,23 +407,27 @@
         final_residual[s] = done[z.subs + s][:, : z.cases]
 
 
-def call(kernel, outs, operands, flops, scratch=(), late=(), loose=(), name=None):
+def call(kernel, outs, operands, flops, scratch=(), late=(), resident=(), loose=(), name=None):
     moved = sum(int(np.prod(x.shape)) * x.dtype.itemsize for x in (*operands, *outs))
     n_in, n_out = len(operands), len(outs)
 
+    brought = [i for i in range(n_in) if i not in resident]
+
     def whole(*refs):
-        hbm, refs = refs[: n_in + n_out], refs[n_in + n_out :]
-        vmem, refs = refs[: n_in + n_out], refs[n_in + n_out :]
+        given, refs = refs[: n_in + n_out], refs[n_in + n_out :]
+        inside, refs = list(given), list(refs)
+        for i in [*brought, *range(n_in, n_in + n_out)]:
+            inside[i] = refs.pop(0)
         in_sems, out_sems, *rest = refs
-        arriving = [pltpu.make_async_copy(hbm[i], vmem[i], in_sems.at[i]) for i in range(n_in)]
-        for i in sorted(range(n_in), key=lambda i: i in late):
+        arriving = {i: pltpu.make_async_copy(given[i], inside[i], in_sems.at[i]) for i in brought}
+        for i in sorted(brought, key=lambda i: i in late):
             arriving[i].start()
-        for i, copy in enumerate(arriving):
+        for i in brought:
             if i not in late:
-                copy.wait()
+                arriving[i].wait()
         extra = [lambda i: arriving[i].wait()] if late else []
-        kernel(*extra, *vmem, *rest)
-        leaving = [pltpu.make_async_copy(vmem[n_in + i], hbm[n_in + i], out_sems.at[i]) for i in range(n_out)]
+        kernel(*extra, *inside, *rest)
+        leaving = [pltpu.make_async_copy(inside[n_in + i], given[n_in + i], out_sems.at[i]) for i in range(n_out)]
         for copy in leaving:
             copy.start()
         for copy in leaving:
@@ -434,16 +435,19 @@
 
     hbm_spec = pl.BlockSpec(memory_space=pltpu.HBM)
     any_spec = pl.BlockSpec(memory_space=pl.ANY)
+    vmem_spec = pl.BlockSpec(memory_space=pltpu.VMEM)
     placed = [
-        x if i in loose else pltpu.with_memory_space_constraint(x, pltpu.HBM) for i, x in enumerate(operands)
+        x if i in loose or i in resident else pltpu.with_memory_space_constraint(x, pltpu.HBM) for i, x in enumerate(operands)
     ]
     return pl.pallas_call(
         whole,
         out_shape=[pltpu.HBM(o.shape, o.dtype) for o in outs],
-        in_specs=[any_spec if i in loose else hbm_spec for i in range(n_in)],
+        in_specs=[
+            vmem_spec if i in resident else any_spec if i in loose else hbm_spec for i in range(n_in)
+        ],
         out_specs=[hbm_spec] * n_out,
         scratch_shapes=[
-            *[pltpu.VMEM(x.shape, x.dtype) for x in (*operands, *outs)],
+            *[pltpu.VMEM(x.shape, x.dtype) for x in (*[operands[i] for i in brought], *outs)],
             pltpu.SemaphoreType.DMA((n_in,)),
             pltpu.SemaphoreType.DMA((n_out,)),
             *scratch,
@@ -498,7 +502,6 @@
     inverse_pieces = pieces_of(local_inverse, group)
     stiffness_pieces = pieces_of(stiffness, group)
     restricted = spread(message)
-    arrivals = [*range(1, group), *range(group + 1, 2 * group)]
     faces = shape((subs, face, lanes), BF16)
     outer = shape((face, lanes), BF16)
     side = shape((subs, modes, face), BF16)
@@ -516,8 +519,9 @@
             pltpu.VMEM((rows, lanes), BF16), pltpu.VMEM((subs, modes, rows), BF16),
             pltpu.VMEM((subs, rows, 2 * lanes), BF16), pltpu.VMEM((subs, rows, 2 * lanes), BF16),
         ],
-        late=range(2 * group),
-        loose=[*arrivals, *range(2 * group + 1, 3 * group)],
+        late=[0, group],
+        resident=[*range(1, group), *range(group + 1, 2 * group)],
+        loose=range(2 * group + 1, 3 * group),
         name="first_image",
     )
     second_got = lax.ppermute(second_pair, "sub", second_pairs)
@@ -553,8 +557,9 @@
         ],
         work,
         [pltpu.VMEM((rows, lanes), F32), pltpu.VMEM((rows, lanes), BF16), pltpu.VMEM((rows, lanes), BF16)],
-        late=range(2 * group),
-        loose=[*arrivals, 2 * group + 7, 2 * group + 8],
+        late=[0, group],
+        resident=[*range(1, group), *range(group + 1, 2 * group)],
+        loose=[2 * group + 7, 2 * group + 8],
         name="second_image",
     )
     second_got = lax.ppermute(second_pair, "sub", second_pairs)

time: 83.8 us -> 86.8 us (1.036)
  Pallas kernels: 30.8 us -> 33.8 us
  starting transfers between devices: 36.4 us -> 38.8 us
  waiting for transfers between devices: 15.2 us -> 12.8 us
    pallas_call x8, Pallas kernels: 30.8 us -> 33.8 us  [call(): pl.pallas_call(whole, out_shape=[pltpu.HBM(o.shape, o.dtype) for o in out...]
    all_to_all x2, waiting for transfers between devices: 3.95 us -> 1.54 us  [body(): restricted = spread(message)]
    all_to_all x2, starting transfers between devices: 9.9 us -> 12.3 us  [body(): coarse = spread(message)]
  transfers between devices with their start and end apart: 14 -> 14, of which waited for: 6 -> 5; matrix products, arithmetic and copies ran while one was open for 0% -> 0% of each run, Pallas kernels for 25% -> 28%
where the time goes in v12:
time: 86.8 us; the launch traced here: 86.1 us
  starting transfers between devices  38.8 us (45%)
  Pallas kernels  33.8 us (39%)
  waiting for transfers between devices  12.8 us (15%)
    pallas_call x8, Pallas kernels, call(): pl.pallas_call(whole, out_shape=[pltpu.HBM(o.shape, o.dtype) for o in out...  33.8 us
    all_to_all x2, starting transfers between devices, body(): restricted = spread(message)  13.1 us
    all_to_all x2, starting transfers between devices, body(): coarse = spread(message)  12.3 us
    ppermute x2, waiting for transfers between devices, body(): second_got = lax.ppermute(second_pair, 'sub', second_pairs)  8.56 us
    ppermute x2, starting transfers between devices, body(): second_got = lax.ppermute(second_pair, 'sub', second_pairs)  8.3 us
    ppermute x2, starting transfers between devices, body(): first_got = lax.ppermute(first_pair, 'sub', first_pairs)  3.88 us
    ppermute x5, waiting for transfers between devices, pieces_of(): lax.ppermute(block, GROUP, [((g + k) % group, g) for g in range(group)])  2.67 us
  transfers between devices with their start and end apart: 14, of which 5 were waited for; matrix products, arithmetic and copies ran while one was open for 0% of the time, Pallas kernels for 28%

profile of v12, /device:TPU:0, one launch (start us, length us, event | category | flops | bytes accessed | tf_op | source)
XLA Modules:
  0.0 86.1 jit_solution(5240738905392878613)
XLA Ops:
  0.6 0.5 collective-permute-start.1
  1.1 1.2 %collective-permute-done.1.refs_1_.refs_5_ = bf16[2,48,512]{2,1,0:T(8,128)(2,1)S(1)} collective-permute-done((bf16[2,48,512]{2,1,0:T(8,128)(2,1)}, bf16[2,48,512]{2,1,0:T(8,128)(2,1)S(1)}, u32[]{:S(2)}, u32[]{:S(2)}) %collective-permute-start.1) | collective-permute-done | bytes 98336 | tf_op jit(solution)/shard_map/ppermute | solution.py:468
  2.3 0.4 collective-permute-start.2
  2.7 0.2 collective-permute-start.3
  2.8 2.3 %open.1 = bf16[16,64,128]{2,1,0:T(8,128)(2,1)} custom-call(bf16[2,48,512]{2,1,0:T(8,128)(2,1)} %bitcast.2, bf16[2,48,512]{2,1,0:T(8,128)(2,1)S(1)} %collective-permute-done.1.refs_1_.refs_5_, bf16[2,1024,128]{2,1,0:T(8,128)(2,1)} %refs_6_.2, s32[2,48]{1,0:T(2,128)} %refs_3_.2), custom_call_target="tpu_custom_call" | custom-call | flops 67108864 | bytes 983424 | tf_op jit(solution)/shard_map/open/pallas_call | solution.py:442
  5.1 8.2 %all-to-all-start = ((bf16[16,64,128]{2,1,0:T(8,128)(2,1)}), bf16[16,64,128]{2,1,0:T(8,128)(2,1)S(1)}, u32[]{:S(2)}, u32[]{:S(2)}) async-start(bf16[16,64,128]{2,1,0:T(8,128)(2,1)} %open.1), calls=%async_computation | async-start | bytes 524288 | tf_op jit(solution)/shard_map/all_to_all | solution.py:504
  13.3 0.1 collective-permute-start
  13.4 0.0 collective-permute-done.2.refs_1_
  13.4 8.6 %first_image.1 = (bf16[1024,128]{1,0:T(8,128)(2,1)}, f32[1024,128]{1,0:T(8,128)}, f32[1024,128]{1,0:T(8,128)}, bf16[2,128,128]{2,1,0:T(8,128)(2,1)}, bf16[2,128,...) custom-call(bf16[2,512,1024]{2,1,0:T(8,128)(2,1)} %refs_0_.3, ...), custom_call_target="tpu_custom_call" | custom-call | flops 1073741824 | bytes 11226112 | tf_op jit(solution)/shard_map/first_image/pallas_call | solution.py:442
  22.0 1.5 %all-to-all-done.refs_2_ = bf16[16,64,128]{2,1,0:T(8,128)(2,1)S(1)} async-done(((bf16[16,64,128]{2,1,0:T(8,128)(2,1)}), bf16[16,64,128]{2,1,0:T(8,128)(2,1)S(1)}, u32[]{:S(2)}, u32[]{:S(2)}) %all-to-all-start) | async-done | bytes 262176 | tf_op jit(solution)/shard_map/all_to_all | solution.py:504
  23.5 3.5 %order.1 = (bf16[2,96,768]{2,1,0:T(8,128)(2,1)}, bf16[2,192,768]{2,1,0:T(8,128)(2,1)}, bf16[16,48,128]{2,1,0:T(8,128)(2,1)}) custom-call(bf16[96,768]{1,0:T(8,128)(2,1)} %refs_0_.2, bf16[96,768]{1,0:T(8,128)(2,1)S(1)} %collective-permute-done.refs_1_, bf16[16,64,128]{2,1,0:T(8,128)(2,1)S(1)} %all-to-all-done.refs_2_, ...), custom_call_target="tpu_custom_call" | custom-call | flops 452984832 | bytes 1890304 | tf_op jit(solution)/shard_map/order/pallas_call | solution.py:442
  27.0 5.4 %all-to-all-start.1 = ((bf16[16,48,128]{2,1,0:T(8,128)(2,1)}), bf16[16,48,128]{2,1,0:T(8,128)(2,1)S(1)}, u32[]{:S(2)}, u32[]{:S(2)}) async-start(bf16[16,48,128]{2,1,0:T(8,128)(2,1)} %get-tuple-element.38), calls=%async_computation.1 | async-start | bytes 393216 | tf_op jit(solution)/shard_map/all_to_all | solution.py:538
  32.4 1.9 %collective-permute-start.4 = (bf16[128,128]{1,0:T(8,128)(2,1)}, bf16[128,128]{1,0:T(8,128)(2,1)S(1)}, u32[]{:S(2)}, u32[]{:S(2)}) collective-permute-start(bf16[128,128]{1,0:T(8,128)(2,1)} %get-tuple-element.46), channel_id=1, source_target_pairs={{0,2},{2,0},{4,6},{6,4},{8,10},{10,8},{12,14},{14,12},{16,18},{18,... | collective-permute-start | bytes 98312 | tf_op jit(solution)/shard_map/ppermute | solution.py:539
  34.3 4.2 %collective-permute-start.5 = (bf16[128,128]{1,0:T(8,128)(2,1)}, bf16[128,128]{1,0:T(8,128)(2,1)S(1)}, u32[]{:S(2)}, u32[]{:S(2)}) collective-permute-start(bf16[128,128]{1,0:T(8,128)(2,1)} %get-tuple-element.36), channel_id=1, source_target_pairs={{0,30},{2,4},{4,2},{6,8},{8,6},{10,12},{12,10},{14,16},{16,14},{18... | collective-permute-start | bytes 98312 | tf_op jit(solution)/shard_map/ppermute | solution.py:527
  38.5 0.0 collective-permute-done.4.refs_8_.refs_11_
  38.5 4.3 %collective-permute-done.5.refs_9_.refs_12_ = bf16[128,128]{1,0:T(8,128)(2,1)S(1)} collective-permute-done((bf16[128,128]{1,0:T(8,128)(2,1)}, bf16[128,128]{1,0:T(8,128)(2,1)S(1)}, u32[]{:S(2)}, u32[]{:S(2)}) %collective-permute-start.5) | collective-permute-done | bytes 32800 | tf_op jit(solution)/shard_map/ppermute | solution.py:527
  42.8 2.8 %update.1 = (bf16[192,128]{1,0:T(8,128)(2,1)}, bf16[16,48,128]{2,1,0:T(8,128)(2,1)}) custom-call(bf16[16,48,128]{2,1,0:T(8,128)(2,1)S(1)} %all-to-all-done.1.refs_0_, bf16[2,192,768]{2,1,0:T(8,128)(2,1)} %get-tuple-element.39.refs_1_, f32[48,128]{1,0:T(8,128)} %get-tuple-element.40.refs_2_, bf16[2,48,48]{2,1,0:T(8,128)(2,1)} %get-tuple-element.41.refs_3_, ...), custom_call_target="tpu_custom_call" | custom-call | flops 16777216 | bytes 1311744 | tf_op jit(solution)/shard_map/update/pallas_call | solution.py:442
  45.6 4.8 %all-to-all-start.2 = ((bf16[16,48,128]{2,1,0:T(8,128)(2,1)}), bf16[16,48,128]{2,1,0:T(8,128)(2,1)S(1)}, u32[]{:S(2)}, u32[]{:S(2)}) async-start(bf16[16,48,128]{2,1,0:T(8,128)(2,1)} %get-tuple-element.47), calls=%async_computation.2 | async-start | bytes 393216 | tf_op jit(solution)/shard_map/all_to_all | solution.py:548
  50.5 8.5 %second_image.1 = (bf16[2,128,128]{2,1,0:T(8,128)(2,1)}, bf16[2,128,128]{2,1,0:T(8,128)(2,1)}, bf16[128,128]{1,0:T(8,128)(2,1)}, bf16[128,128]{1,0:T(8,128)(2,1)...) custom-call(bf16[2,512,1024]{2,1,0:T(8,128)(2,1)} %refs_0_.3, ...), custom_call_target="tpu_custom_call" | custom-call | flops 1073741824 | bytes 11716608 | tf_op jit(solution)/shard_map/second_image/pallas_call | solution.py:442
  59.0 0.1 collective-permute-start.9
  59.1 0.0 all-to-all-done.2.refs_0_
  59.1 2.2 %coarse.1 = bf16[16,48,128]{2,1,0:T(8,128)(2,1)} custom-call(bf16[16,48,128]{2,1,0:T(8,128)(2,1)S(1)} %all-to-all-done.2.refs_0_, bf16[2,96,768]{2,1,0:T(8,128)(2,1)} %get-tuple-element.55.refs_1_), custom_call_target="tpu_custom_call" | custom-call | flops 16777216 | bytes 688128 | tf_op jit(solution)/shard_map/coarse/pallas_call | solution.py:442
  61.3 6.9 %all-to-all-start.3 = ((bf16[16,48,128]{2,1,0:T(8,128)(2,1)}), bf16[16,48,128]{2,1,0:T(8,128)(2,1)S(1)}, u32[]{:S(2)}, u32[]{:S(2)}) async-start(bf16[16,48,128]{2,1,0:T(8,128)(2,1)} %coarse.1), calls=%async_computation.3 | async-start | bytes 393216 | tf_op jit(solution)/shard_map/all_to_all | solution.py:575
  68.2 1.9 %collective-permute-start.6 = (bf16[128,128]{1,0:T(8,128)(2,1)}, bf16[128,128]{1,0:T(8,128)(2,1)S(1)}, u32[]{:S(2)}, u32[]{:S(2)}) collective-permute-start(bf16[128,128]{1,0:T(8,128)(2,1)} %get-tuple-element.58), channel_id=1, source_target_pairs={{0,2},{2,0},{4,6},{6,4},{8,10},{10,8},{12,14},{14,12},{16,18},{18,... | collective-permute-start | bytes 98312 | tf_op jit(solution)/shard_map/ppermute | solution.py:576
  70.2 4.2 %collective-permute-start.7 = (bf16[128,128]{1,0:T(8,128)(2,1)}, bf16[128,128]{1,0:T(8,128)(2,1)S(1)}, u32[]{:S(2)}, u32[]{:S(2)}) collective-permute-start(bf16[128,128]{1,0:T(8,128)(2,1)} %get-tuple-element.59), channel_id=1, source_target_pairs={{0,30},{2,4},{4,2},{6,8},{8,6},{10,12},{12,10},{14,16},{16,14},{18... | collective-permute-start | bytes 98312 | tf_op jit(solution)/shard_map/ppermute | solution.py:565
  74.3 0.0 collective-permute-done.6.refs_4_
  74.3 4.3 %collective-permute-done.7.refs_5_ = bf16[128,128]{1,0:T(8,128)(2,1)S(1)} collective-permute-done((bf16[128,128]{1,0:T(8,128)(2,1)}, bf16[128,128]{1,0:T(8,128)(2,1)S(1)}, u32[]{:S(2)}, u32[]{:S(2)}) %collective-permute-start.7) | collective-permute-done | bytes 32800 | tf_op jit(solution)/shard_map/ppermute | solution.py:565
  78.6 0.0 all-to-all-done.3.refs_0_
  78.6 2.6 %pick.1.refs_0_ = bf16[448,128]{1,0:T(8,128)(2,1)} custom-call(bf16[16,48,128]{2,1,0:T(8,128)(2,1)S(1)} %all-to-all-done.3.refs_0_, bf16[2,192,768]{2,1,0:T(8,128)(2,1)} %get-tuple-element.39.refs_1_, bf16[2,128,128]{2,1,0:T(8,128)(2,1)} %get-tuple-element.56.refs_2_, bf16[2,128,128]{2,1,0:T(8,128)(2,1)} %get-tuple-element.57.refs_3_, ...), custom_call_target="tpu_custom_call" | custom-call | flops 16777216 | bytes 1294336 | tf_op jit(solution)/shard_map/pick/pallas_call | solution.py:442
  81.3 0.1 collective-permute-start.8
  81.3 1.5 %collective-permute-done.8.refs_1_ = bf16[448,128]{1,0:T(8,128)(2,1)S(1)} collective-permute-done((bf16[448,128]{1,0:T(8,128)(2,1)}, bf16[448,128]{1,0:T(8,128)(2,1)S(1)}, u32[]{:S(2)}, u32[]{:S(2)}) %collective-permute-start.8) | collective-permute-done | bytes 114720 | tf_op jit(solution)/shard_map/ppermute | solution.py:468
  82.9 3.3 %last.1 = (f32[2,512,128]{2,1,0:T(8,128)}, f32[2,512,128]{2,1,0:T(8,128)}) custom-call(bf16[448,128]{1,0:T(8,128)(2,1)} %pick.1.refs_0_, bf16[448,128]{1,0:T(8,128)(2,1)S(1)} %collective-permute-done.8.refs_1_, f32[2,512,128]{2,1,0:T(8,128)} %get-tuple-element.60.refs_2_, f32[2,512,128]{2,1,0:T(8,128)S(1)} %collective-permute-done.9.refs_3_, ...), custom_call_target="tpu_custom_call" | custom-call | flops 134217728 | bytes 2852864 | tf_op jit(solution)/shard_map/last/pallas_call | solution.py:442
  (4 shorter events, 0.0 us)
Async XLA Ops:
  0.6 1.7 %collective-permute-start.1 = (bf16[2,48,512]{2,1,0:T(8,128)(2,1)}, bf16[2,48,512]{2,1,0:T(8,128)(2,1)S(1)}, u32[]{:S(2)}, u32[]{:S(2)}) collective-permute-start(bf16[2,48,512]{2,1,0:T(8,128)(2,1)} %bitcast.1), channel_id=1, source_target_pairs={{1,0},{0,1},{3,2},{2,3},{5,4},{4,5},{7,6},{6,7},{9,8},{8,9},{11,10... | collective-permute-start | bytes 294920 | tf_op jit(solution)/shard_map/ppermute | solution.py:468
  2.3 11.1 %collective-permute-start.2 = (bf16[2,512,1024]{2,1,0:T(8,128)(2,1)}, bf16[2,512,1024]{2,1,0:T(8,128)(2,1)S(1)}, u32[]{:S(2)}, u32[]{:S(2)}) collective-permute-start(bf16[2,512,1024]{2,1,0:T(8,128)(2,1)} %refs_0_.3), channel_id=1, source_target_pairs={{1,0},{0,1},{3,2},{2,3},{5,4},{4,5},{7,6},{6,7},{9,8},{8,9},{11,10... | collective-permute-start | bytes 6291464 | tf_op jit(solution)/shard_map/ppermute | solution.py:468
  2.7 10.8 %collective-permute-start.3 = (bf16[2,512,1024]{2,1,0:T(8,128)(2,1)}, bf16[2,512,1024]{2,1,0:T(8,128)(2,1)}, u32[]{:S(2)}, u32[]{:S(2)}) collective-permute-start(bf16[2,512,1024]{2,1,0:T(8,128)(2,1)} %refs_2_.3), channel_id=1, source_target_pairs={{1,0},{0,1},{3,2},{2,3},{5,4},{4,5},{7,6},{6,7},{9,8},{8,9},{11,10... | collective-permute-start | bytes 6291464 | tf_op jit(solution)/shard_map/ppermute | solution.py:468
  5.1 18.4 %all-to-all-start = ((bf16[16,64,128]{2,1,0:T(8,128)(2,1)}), bf16[16,64,128]{2,1,0:T(8,128)(2,1)S(1)}, u32[]{:S(2)}, u32[]{:S(2)}) async-start(bf16[16,64,128]{2,1,0:T(8,128)(2,1)} %open.1), calls=%async_computation | async-start | bytes 524288 | tf_op jit(solution)/shard_map/all_to_all | solution.py:504
  13.3 10.2 %collective-permute-start = (bf16[96,768]{1,0:T(8,128)(2,1)}, bf16[96,768]{1,0:T(8,128)(2,1)S(1)}, u32[]{:S(2)}, u32[]{:S(2)}) collective-permute-start(bf16[96,768]{1,0:T(8,128)(2,1)} %refs_0_.2), channel_id=1, source_target_pairs={{1,0},{0,1},{3,2},{2,3},{5,4},{4,5},{7,6},{6,7},{9,8},{8,9},{11,10... | collective-permute-start | bytes 442376 | tf_op jit(solution)/shard_map/ppermute | solution.py:468
  27.0 15.7 %all-to-all-start.1 = ((bf16[16,48,128]{2,1,0:T(8,128)(2,1)}), bf16[16,48,128]{2,1,0:T(8,128)(2,1)S(1)}, u32[]{:S(2)}, u32[]{:S(2)}) async-start(bf16[16,48,128]{2,1,0:T(8,128)(2,1)} %get-tuple-element.38), calls=%async_computation.1 | async-start | bytes 393216 | tf_op jit(solution)/shard_map/all_to_all | solution.py:538
  32.4 6.1 %collective-permute-start.4 = (bf16[128,128]{1,0:T(8,128)(2,1)}, bf16[128,128]{1,0:T(8,128)(2,1)S(1)}, u32[]{:S(2)}, u32[]{:S(2)}) collective-permute-start(bf16[128,128]{1,0:T(8,128)(2,1)} %get-tuple-element.46), channel_id=1, source_target_pairs={{0,2},{2,0},{4,6},{6,4},{8,10},{10,8},{12,14},{14,12},{16,18},{18,... | collective-permute-start | bytes 98312 | tf_op jit(solution)/shard_map/ppermute | solution.py:539
  34.3 8.4 %collective-permute-start.5 = (bf16[128,128]{1,0:T(8,128)(2,1)}, bf16[128,128]{1,0:T(8,128)(2,1)S(1)}, u32[]{:S(2)}, u32[]{:S(2)}) collective-permute-start(bf16[128,128]{1,0:T(8,128)(2,1)} %get-tuple-element.36), channel_id=1, source_target_pairs={{0,30},{2,4},{4,2},{6,8},{8,6},{10,12},{12,10},{14,16},{16,14},{18... | collective-permute-start | bytes 98312 | tf_op jit(solution)/shard_map/ppermute | solution.py:527
  45.6 13.5 %all-to-all-start.2 = ((bf16[16,48,128]{2,1,0:T(8,128)(2,1)}), bf16[16,48,128]{2,1,0:T(8,128)(2,1)S(1)}, u32[]{:S(2)}, u32[]{:S(2)}) async-start(bf16[16,48,128]{2,1,0:T(8,128)(2,1)} %get-tuple-element.47), calls=%async_computation.2 | async-start | bytes 393216 | tf_op jit(solution)/shard_map/all_to_all | solution.py:548
  59.0 22.3 %collective-permute-start.9 = (f32[2,512,128]{2,1,0:T(8,128)}, f32[2,512,128]{2,1,0:T(8,128)S(1)}, u32[]{:S(2)}, u32[]{:S(2)}) collective-permute-start(f32[2,512,128]{2,1,0:T(8,128)} %get-tuple-element.61), channel_id=1, source_target_pairs={{0,1},{1,0},{2,3},{3,2},{4,5},{5,4},{6,7},{7,6},{8,9},{9,8},{10,11... | collective-permute-start | bytes 1572872 | tf_op jit(solution)/shard_map/ppermute | solution.py:579
  61.3 17.3 %all-to-all-start.3 = ((bf16[16,48,128]{2,1,0:T(8,128)(2,1)}), bf16[16,48,128]{2,1,0:T(8,128)(2,1)S(1)}, u32[]{:S(2)}, u32[]{:S(2)}) async-start(bf16[16,48,128]{2,1,0:T(8,128)(2,1)} %coarse.1), calls=%async_computation.3 | async-start | bytes 393216 | tf_op jit(solution)/shard_map/all_to_all | solution.py:575
  68.2 6.1 %collective-permute-start.6 = (bf16[128,128]{1,0:T(8,128)(2,1)}, bf16[128,128]{1,0:T(8,128)(2,1)S(1)}, u32[]{:S(2)}, u32[]{:S(2)}) collective-permute-start(bf16[128,128]{1,0:T(8,128)(2,1)} %get-tuple-element.58), channel_id=1, source_target_pairs={{0,2},{2,0},{4,6},{6,4},{8,10},{10,8},{12,14},{14,12},{16,18},{18,... | collective-permute-start | bytes 98312 | tf_op jit(solution)/shard_map/ppermute | solution.py:576
  70.2 8.5 %collective-permute-start.7 = (bf16[128,128]{1,0:T(8,128)(2,1)}, bf16[128,128]{1,0:T(8,128)(2,1)S(1)}, u32[]{:S(2)}, u32[]{:S(2)}) collective-permute-start(bf16[128,128]{1,0:T(8,128)(2,1)} %get-tuple-element.59), channel_id=1, source_target_pairs={{0,30},{2,4},{4,2},{6,8},{8,6},{10,12},{12,10},{14,16},{16,14},{18... | collective-permute-start | bytes 98312 | tf_op jit(solution)/shard_map/ppermute | solution.py:565
  81.3 1.6 %collective-permute-start.8 = (bf16[448,128]{1,0:T(8,128)(2,1)}, bf16[448,128]{1,0:T(8,128)(2,1)S(1)}, u32[]{:S(2)}, u32[]{:S(2)}) collective-permute-start(bf16[448,128]{1,0:T(8,128)(2,1)} %pick.1.refs_0_), channel_id=1, source_target_pairs={{1,0},{0,1},{3,2},{2,3},{5,4},{4,5},{7,6},{6,7},{9,8},{8,9},{11,10... | collective-permute-start | bytes 344072 | tf_op jit(solution)/shard_map/ppermute | solution.py:468

commit v13 on v11

--- a/solution.py
+++ b/solution.py
@@ -121,8 +121,9 @@
         message[k, z.modes :, :] = digits[...].astype(BF16)
 
 
-def multiply(z, pieces, vector, store):
+def multiply(z, pieces, vector, store, wait):
     for k, piece in enumerate(pieces):
+        wait(k)
         parts = [dot(piece[s], vector) for s in range(z.subs)]
         store(k, piece_start(z, k, z.own), select(z, parts))
 
@@ -187,20 +188,18 @@
     pieces = refs[2 * z.group : 3 * z.group]
     loads, left_rows, right_rows = refs[3 * z.group : 3 * z.group + 3]
     load_rows, solved, image, before, after, first_pair, second_pair = refs[3 * z.group + 3 : 3 * z.group + 10]
-    tall, left_t, right_t, inner, start_modes, rounded, basis_t, both, images = refs[3 * z.group + 10 :]
+    tall, basis_t, rounded, both, images = refs[3 * z.group + 10 :]
     join_basis(z, pieces, basis_t)
     packed = dot(loads[0], case_matrix(z, 0))
     for s in range(1, z.subs):
         packed = packed + dot(loads[s], case_matrix(z, s))
     load_rows[...] = packed.astype(BF16)
-    for k in range(z.group):
-        wait(k)
 
     def store_solved(k, start, value):
         solved[pl.ds(start, z.own), :] = value
         rounded[pl.ds(start, z.own), :] = value.astype(BF16)
 
-    multiply(z, inverse, load_rows[...], store_solved)
+    multiply(z, inverse, load_rows[...], store_solved, wait)
     solved_b = rounded[...]
     half = z.lanes // 2
     for s in range(z.subs):
@@ -217,25 +216,27 @@
         image[pl.ds(start, z.own), :] = select(z, [part[:, : z.lanes] for part in parts])
         for s in range(z.subs):
             images[s, pl.ds(start, z.own), :] = parts[s].astype(BF16)
-    left = (load_rows[...].astype(F32) - image[...]).astype(BF16)
-    begun = []
-    for s in range(z.subs):
-        image_basis = images[s, :, z.lanes :]
-        tall[s, :, :half] = image_basis[:, :half]
-        restricted = dot(basis_t[s], jnp.concatenate([left, image_basis], axis=1))
-        begun.append(restricted[:, : z.lanes])
-        inner[s] = restricted[:, z.lanes : z.lanes + z.modes].astype(BF16)
-        pick = pick_both(z, left_rows, right_rows, s)
-        sides_t = dot_nt(basis_t[s], pick).astype(BF16)
-        left_t[s] = sides_t[:, : z.face]
-        right_t[s] = sides_t[:, z.face :]
-        picked = dot(pick, images[s]).astype(BF16)
+    for s in range(z.subs):
+        tall[s, :, :half] = images[s, :, z.lanes : z.lanes + half]
+        picked = dot(pick_both(z, left_rows, right_rows, s), images[s]).astype(BF16)
         faces = dot(picked[:, : z.lanes], lane_matrix(z, s * z.width, 0))
         faces = (faces + dot(picked[:, z.lanes :], lane_matrix(z, 0, half, z.modes))).astype(BF16)
         before[s] = faces[: z.face]
         after[s] = faces[z.face :]
+    store_faces(z, before, after, first_pair, second_pair)
+
+
+def begin_kernel(z, load_rows, image, tall, basis_t, left_rows, right_rows, left_t, right_t, inner, start_modes):
+    left = (load_rows[...].astype(F32) - image[...]).astype(BF16)
+    begun = []
+    for s in range(z.subs):
+        restricted = dot(basis_t[s], jnp.concatenate([left, tall[s]], axis=1))
+        begun.append(restricted[:, : z.lanes])
+        inner[s] = restricted[:, z.lanes : z.lanes + z.modes].astype(BF16)
+        sides_t = dot_nt(basis_t[s], pick_both(z, left_rows, right_rows, s)).astype(BF16)
+        left_t[s] = sides_t[:, : z.face]
+        right_t[s] = sides_t[:, z.face :]
     start_modes[...] = select(z, begun)
-    store_faces(z, before, after, first_pair, second_pair)
 
 
 def second_image_kernel(z, wait, *refs):
@@ -256,24 +257,20 @@
         images.append(total[:, : z.lanes] + dot(scatter_matrix(z, right_rows[s : s + 1, :], 0, z.rows), both[1]))
     residual = (load_rows[...].astype(F32) - old_image[...] - select(z, images)).astype(BF16)
     base[...] = old_solved[...] + select(z, steps)
-    for k in range(z.group):
-        wait(k)
 
     def store_solved(k, start, value):
         value = value + base[pl.ds(start, z.own), :]
         values[k][0] = value
         rounded[pl.ds(start, z.own), :] = value.astype(BF16)
 
-    multiply(z, inverse, residual, store_solved)
+    multiply(z, inverse, residual, store_solved, wait)
 
     def store_image(k, start, value):
         place = pl.ds(start, z.own)
         values[k][1] = load_rows[place, :].astype(F32) - value
         image[place, :] = value.astype(BF16)
 
-    for k in range(z.group):
-        wait(z.group + k)
-    multiply(z, stiffness, rounded[...], store_image)
+    multiply(z, stiffness, rounded[...], store_image, lambda k: wait(z.group + k))
     pick = jnp.concatenate([pick_both(z, left_rows, right_rows, s) for s in range(z.subs)], axis=0)
     picked = dot(pick, image[...]).astype(BF16)
     for s in range(z.subs):
@@ -311,11 +308,11 @@
             wide = min(768, z.columns - at)
             total = jnp.zeros((z.owned, wide), F32)
             for k, block in enumerate(blocks):
-                inside = places[:, at : at + wide] - piece_start(z, k, z.block)
+                inside = (places[:, at : at + wide] - piece_start(z, k, z.block)).astype(jnp.int16)
                 for first in range(0, z.block, 768):
                     deep = min(768, z.block - first)
-                    row = lax.broadcasted_iota(jnp.int32, (deep, wide), 0) + first
-                    hot = jnp.where(row == inside, 1.0, 0.0).astype(BF16)
+                    row = lax.broadcasted_iota(jnp.int16, (deep, wide), 0) + jnp.int16(first)
+                    hot = jnp.where(row == inside, jnp.ones((), BF16), jnp.zeros((), BF16))
                     total = total + dot(block[:, first : first + deep], hot)
             ordered_inverse[s, :, at : at + wide] = total.astype(BF16)
     coarse_rows(z, ordered_inverse, arrived, message)
@@ -469,7 +466,10 @@
     z = Sizes(loads, stiffness, coarse_basis, coarse_inverse, left_rows)
     n, group, subs, rows, lanes, modes, face = z.n, z.group, z.subs, z.rows, z.lanes, z.modes, z.face
     basis_pieces = pieces_of(jnp.swapaxes(coarse_basis, 1, 2), group)
-    basis_pieces, local_inverse, stiffness = lax.optimization_barrier((basis_pieces, local_inverse, stiffness))
+    inverse_columns = pieces_of(coarse_inverse, group)
+    basis_pieces, inverse_columns, local_inverse, stiffness = lax.optimization_barrier(
+        (basis_pieces, inverse_columns, local_inverse, stiffness)
+    )
     column = np.arange(z.columns)
     repeat = jnp.asarray(np.arange(lanes)[:, None] == column[None, :] % modes, BF16)
     own_row = jnp.asarray(np.arange(n)[:, None] == column[None, :] // modes, F32)
@@ -494,26 +494,23 @@
         loose=range(1, group),
         name="open",
     )
-    inverse_columns = pieces_of(coarse_inverse, group)
     inverse_pieces = pieces_of(local_inverse, group)
     stiffness_pieces = pieces_of(stiffness, group)
     restricted = spread(message)
     arrivals = [*range(1, group), *range(group + 1, 2 * group)]
     faces = shape((subs, face, lanes), BF16)
     outer = shape((face, lanes), BF16)
-    side = shape((subs, modes, face), BF16)
     (
-        load_rows, solved, image, before, after, first_pair, second_pair, tall, left_t, right_t, inner, start_modes
+        load_rows, solved, image, before, after, first_pair, second_pair, tall, basis_t
     ) = call(
         functools.partial(first_image_kernel, z),
         [
-            packed_b, packed_f, packed_f, faces, faces, outer, outer, tall, side, side,
-            shape((subs, modes, modes), BF16), shape((modes, lanes), F32),
+            packed_b, packed_f, packed_f, faces, faces, outer, outer, tall, shape((subs, modes, rows), BF16),
         ],
         [*inverse_pieces, *stiffness_pieces, *basis_pieces, loads, left_rows, right_rows],
         work,
         [
-            pltpu.VMEM((rows, lanes), BF16), pltpu.VMEM((subs, modes, rows), BF16),
+            pltpu.VMEM((rows, lanes), BF16),
             pltpu.VMEM((subs, rows, 2 * lanes), BF16), pltpu.VMEM((subs, rows, 2 * lanes), BF16),
         ],
         late=range(2 * group),
@@ -521,6 +518,14 @@
         name="first_image",
     )
     second_got = lax.ppermute(second_pair, "sub", second_pairs)
+    side = shape((subs, modes, face), BF16)
+    left_t, right_t, inner, start_modes = call(
+        functools.partial(begin_kernel, z),
+        [side, side, shape((subs, modes, modes), BF16), shape((modes, lanes), F32)],
+        [load_rows, image, tall, basis_t, left_rows, right_rows],
+        work // 16,
+        name="begin",
+    )
     restricted, second_pair = lax.optimization_barrier((restricted, second_pair))
     near = (subs + 2) * modes
     ordered_inverse, picks, message = call(

time: 83.8 us -> 84.3 us (level)
  waiting for transfers between devices: 15.2 us -> 11.9 us
  Pallas kernels: 30.8 us -> 33.9 us
    ppermute x2, waiting for transfers between devices: 8.6 us -> 4.97 us  [body(): second_got = lax.ppermute(second_pair, 'sub', second_pairs)]
    pallas_call x8 -> x9, Pallas kernels: 30.8 us -> 33.9 us  [call(): pl.pallas_call(whole, out_shape=[pltpu.HBM(o.shape, o.dtype) for o in out...]
  transfers between devices with their start and end apart: 14 -> 14, of which waited for: 6 -> 6; matrix products, arithmetic and copies ran while one was open for 0% -> 0% of each run, Pallas kernels for 25% -> 29%
where the time goes in v13:
time: 84.3 us; the launch traced here: 83.6 us
  starting transfers between devices  37 us (44%)
  Pallas kernels  33.9 us (40%)
  waiting for transfers between devices  11.9 us (14%)
    pallas_call x9, Pallas kernels, call(): pl.pallas_call(whole, out_shape=[pltpu.HBM(o.shape, o.dtype) for o in out...  33.9 us
    all_to_all x2, starting transfers between devices, body(): restricted = spread(message)  13.6 us
    all_to_all x2, starting transfers between devices, body(): coarse = spread(message)  9.97 us
    ppermute x2, starting transfers between devices, body(): second_got = lax.ppermute(second_pair, 'sub', second_pairs)  8.32 us
    ppermute x2, waiting for transfers between devices, body(): second_got = lax.ppermute(second_pair, 'sub', second_pairs)  4.97 us
    all_to_all x2, waiting for transfers between devices, body(): restricted = spread(message)  3.94 us
    ppermute x2, starting transfers between devices, body(): first_got = lax.ppermute(first_pair, 'sub', first_pairs)  3.87 us
    ppermute x5, waiting for transfers between devices, pieces_of(): lax.ppermute(block, GROUP, [((g + k) % group, g) for g in range(group)])  2.95 us
  transfers between devices with their start and end apart: 14, of which 6 were waited for; matrix products, arithmetic and copies ran while one was open for 0% of the time, Pallas kernels for 29%

profile of v13, /device:TPU:0, one launch (start us, length us, event | category | flops | bytes accessed | tf_op | source)
XLA Modules:
  0.0 83.6 jit_solution(14276568886704669074)
XLA Ops:
  0.6 0.5 collective-permute-start.1
  1.1 0.1 collective-permute-start
  1.2 1.4 %collective-permute-done.refs_1_.refs_5_ = bf16[2,48,512]{2,1,0:T(8,128)(2,1)S(1)} collective-permute-done((bf16[2,48,512]{2,1,0:T(8,128)(2,1)}, bf16[2,48,512]{2,1,0:T(8,128)(2,1)S(1)}, u32[]{:S(2)}, u32[]{:S(2)}) %collective-permute-start) | collective-permute-done | bytes 98336 | tf_op jit(solution)/shard_map/ppermute | solution.py:461
  2.7 0.0 collective-permute-done.1.refs_1_
  2.7 0.2 collective-permute-start.2
  2.9 0.3 collective-permute-start.3
  3.2 2.3 %open.1 = bf16[16,64,128]{2,1,0:T(8,128)(2,1)} custom-call(bf16[2,48,512]{2,1,0:T(8,128)(2,1)} %bitcast.2, bf16[2,48,512]{2,1,0:T(8,128)(2,1)S(1)} %collective-permute-done.refs_1_.refs_5_, bf16[2,1024,128]{2,1,0:T(8,128)(2,1)} %refs_6_.2, s32[2,48]{1,0:T(2,128)} %refs_3_.2), custom_call_target="tpu_custom_call" | custom-call | flops 67108864 | bytes 983424 | tf_op jit(solution)/shard_map/open/pallas_call | solution.py:437
  5.5 8.1 %all-to-all-start = ((bf16[16,64,128]{2,1,0:T(8,128)(2,1)}), bf16[16,64,128]{2,1,0:T(8,128)(2,1)S(1)}, u32[]{:S(2)}, u32[]{:S(2)}) async-start(bf16[16,64,128]{2,1,0:T(8,128)(2,1)} %open.1), calls=%async_computation | async-start | bytes 524288 | tf_op jit(solution)/shard_map/all_to_all | solution.py:499
  13.6 0.0 collective-permute-done.2.refs_1_
  13.6 0.0 collective-permute-done.3.refs_3_
  13.6 7.0 %first_image.1 = (bf16[1024,128]{1,0:T(8,128)(2,1)}, f32[1024,128]{1,0:T(8,128)}, f32[1024,128]{1,0:T(8,128)}, bf16[2,128,128]{2,1,0:T(8,128)(2,1)}, bf16[2,128,...) custom-call(bf16[2,512,1024]{2,1,0:T(8,128)(2,1)} %refs_0_.2, ...), custom_call_target="tpu_custom_call" | custom-call | flops 1073741824 | bytes 11339776 | tf_op jit(solution)/shard_map/first_image/pallas_call | solution.py:437
  20.6 3.3 %all-to-all-done.refs_2_ = bf16[16,64,128]{2,1,0:T(8,128)(2,1)S(1)} async-done(((bf16[16,64,128]{2,1,0:T(8,128)(2,1)}), bf16[16,64,128]{2,1,0:T(8,128)(2,1)S(1)}, u32[]{:S(2)}, u32[]{:S(2)}) %all-to-all-start) | async-done | bytes 262176 | tf_op jit(solution)/shard_map/all_to_all | solution.py:499
  23.9 3.5 %order.1 = (bf16[2,96,768]{2,1,0:T(8,128)(2,1)}, bf16[2,192,768]{2,1,0:T(8,128)(2,1)}, bf16[16,48,128]{2,1,0:T(8,128)(2,1)}) custom-call(bf16[96,768]{1,0:T(8,128)(2,1)} %refs_0_.1, bf16[96,768]{1,0:T(8,128)(2,1)S(1)} %collective-permute-done.1.refs_1_, bf16[16,64,128]{2,1,0:T(8,128)(2,1)S(1)} %all-to-all-done.refs_2_, ...), custom_call_target="tpu_custom_call" | custom-call | flops 452984832 | bytes 1890304 | tf_op jit(solution)/shard_map/order/pallas_call | solution.py:437
  27.4 3.6 %all-to-all-start.1 = ((bf16[16,48,128]{2,1,0:T(8,128)(2,1)}), bf16[16,48,128]{2,1,0:T(8,128)(2,1)S(1)}, u32[]{:S(2)}, u32[]{:S(2)}) async-start(bf16[16,48,128]{2,1,0:T(8,128)(2,1)} %get-tuple-element.43), calls=%async_computation.1 | async-start | bytes 393216 | tf_op jit(solution)/shard_map/all_to_all | solution.py:539
  31.0 1.9 %collective-permute-start.4 = (bf16[128,128]{1,0:T(8,128)(2,1)}, bf16[128,128]{1,0:T(8,128)(2,1)S(1)}, u32[]{:S(2)}, u32[]{:S(2)}) collective-permute-start(bf16[128,128]{1,0:T(8,128)(2,1)} %get-tuple-element.55), channel_id=1, source_target_pairs={{0,2},{2,0},{4,6},{6,4},{8,10},{10,8},{12,14},{14,12},{16,18},{18,... | collective-permute-start | bytes 98312 | tf_op jit(solution)/shard_map/ppermute | solution.py:540
  33.0 4.2 %collective-permute-start.5 = (bf16[128,128]{1,0:T(8,128)(2,1)}, bf16[128,128]{1,0:T(8,128)(2,1)S(1)}, u32[]{:S(2)}, u32[]{:S(2)}) collective-permute-start(bf16[128,128]{1,0:T(8,128)(2,1)} %get-tuple-element.41), channel_id=1, source_target_pairs={{0,30},{2,4},{4,2},{6,8},{8,6},{10,12},{12,10},{14,16},{16,14},{18... | collective-permute-start | bytes 98312 | tf_op jit(solution)/shard_map/ppermute | solution.py:520
  37.1 2.9 %begin.1 = (bf16[2,48,128]{2,1,0:T(8,128)(2,1)}, bf16[2,48,128]{2,1,0:T(8,128)(2,1)}, bf16[2,48,48]{2,1,0:T(8,128)(2,1)}, f32[48,128]{1,0:T(8,128)}) custom-call(bf16[1024,128]{1,0:T(8,128)(2,1)} %get-tuple-element.45.refs_0_.refs_4_, f32[1024,128]{1,0:T(8,128)} %get-tuple-element.46.refs_1_.refs_5_, ...), custom_call_target="tpu_custom_call" | custom-call | flops 67108864 | bytes 1592320 | tf_op jit(solution)/shard_map/begin/pallas_call | solution.py:437
  40.0 0.7 collective-permute-done.5.refs_9_.refs_12_
  40.7 2.8 %update.1 = (bf16[192,128]{1,0:T(8,128)(2,1)}, bf16[16,48,128]{2,1,0:T(8,128)(2,1)}) custom-call(bf16[16,48,128]{2,1,0:T(8,128)(2,1)S(1)} %all-to-all-done.1.refs_0_, bf16[2,192,768]{2,1,0:T(8,128)(2,1)} %get-tuple-element.44.refs_1_, f32[48,128]{1,0:T(8,128)} %get-tuple-element.49.refs_2_, bf16[2,48,48]{2,1,0:T(8,128)(2,1)} %get-tuple-element.50.refs_3_, ...), custom_call_target="tpu_custom_call" | custom-call | flops 16777216 | bytes 1311744 | tf_op jit(solution)/shard_map/update/pallas_call | solution.py:437
  43.5 5.6 %all-to-all-start.2 = ((bf16[16,48,128]{2,1,0:T(8,128)(2,1)}), bf16[16,48,128]{2,1,0:T(8,128)(2,1)S(1)}, u32[]{:S(2)}, u32[]{:S(2)}) async-start(bf16[16,48,128]{2,1,0:T(8,128)(2,1)} %get-tuple-element.56), calls=%async_computation.2 | async-start | bytes 393216 | tf_op jit(solution)/shard_map/all_to_all | solution.py:549
  49.1 7.4 %second_image.1 = (bf16[2,128,128]{2,1,0:T(8,128)(2,1)}, bf16[2,128,128]{2,1,0:T(8,128)(2,1)}, bf16[128,128]{1,0:T(8,128)(2,1)}, bf16[128,128]{1,0:T(8,128)(2,1)...) custom-call(bf16[2,512,1024]{2,1,0:T(8,128)(2,1)} %refs_0_.2, ...), custom_call_target="tpu_custom_call" | custom-call | flops 1073741824 | bytes 11716608 | tf_op jit(solution)/shard_map/second_image/pallas_call | solution.py:437
  56.5 0.1 collective-permute-start.9
  56.6 0.6 all-to-all-done.2.refs_0_
  57.2 2.2 %coarse.1 = bf16[16,48,128]{2,1,0:T(8,128)(2,1)} custom-call(bf16[16,48,128]{2,1,0:T(8,128)(2,1)S(1)} %all-to-all-done.2.refs_0_, bf16[2,96,768]{2,1,0:T(8,128)(2,1)} %get-tuple-element.61.refs_1_), custom_call_target="tpu_custom_call" | custom-call | flops 16777216 | bytes 688128 | tf_op jit(solution)/shard_map/coarse/pallas_call | solution.py:437
  59.4 6.3 %all-to-all-start.3 = ((bf16[16,48,128]{2,1,0:T(8,128)(2,1)}), bf16[16,48,128]{2,1,0:T(8,128)(2,1)S(1)}, u32[]{:S(2)}, u32[]{:S(2)}) async-start(bf16[16,48,128]{2,1,0:T(8,128)(2,1)} %coarse.1), calls=%async_computation.3 | async-start | bytes 393216 | tf_op jit(solution)/shard_map/all_to_all | solution.py:575
  65.7 1.9 %collective-permute-start.6 = (bf16[128,128]{1,0:T(8,128)(2,1)}, bf16[128,128]{1,0:T(8,128)(2,1)S(1)}, u32[]{:S(2)}, u32[]{:S(2)}) collective-permute-start(bf16[128,128]{1,0:T(8,128)(2,1)} %get-tuple-element.64), channel_id=1, source_target_pairs={{0,2},{2,0},{4,6},{6,4},{8,10},{10,8},{12,14},{14,12},{16,18},{18,... | collective-permute-start | bytes 98312 | tf_op jit(solution)/shard_map/ppermute | solution.py:576
  67.7 4.2 %collective-permute-start.7 = (bf16[128,128]{1,0:T(8,128)(2,1)}, bf16[128,128]{1,0:T(8,128)(2,1)S(1)}, u32[]{:S(2)}, u32[]{:S(2)}) collective-permute-start(bf16[128,128]{1,0:T(8,128)(2,1)} %get-tuple-element.65), channel_id=1, source_target_pairs={{0,30},{2,4},{4,2},{6,8},{8,6},{10,12},{12,10},{14,16},{16,14},{18... | collective-permute-start | bytes 98312 | tf_op jit(solution)/shard_map/ppermute | solution.py:565
  71.8 4.3 %collective-permute-done.7.refs_5_ = bf16[128,128]{1,0:T(8,128)(2,1)S(1)} collective-permute-done((bf16[128,128]{1,0:T(8,128)(2,1)}, bf16[128,128]{1,0:T(8,128)(2,1)S(1)}, u32[]{:S(2)}, u32[]{:S(2)}) %collective-permute-start.7) | collective-permute-done | bytes 32800 | tf_op jit(solution)/shard_map/ppermute | solution.py:565
  76.1 2.6 %pick.1.refs_0_ = bf16[448,128]{1,0:T(8,128)(2,1)} custom-call(bf16[16,48,128]{2,1,0:T(8,128)(2,1)S(1)} %all-to-all-done.3.refs_0_, bf16[2,192,768]{2,1,0:T(8,128)(2,1)} %get-tuple-element.44.refs_1_, bf16[2,128,128]{2,1,0:T(8,128)(2,1)} %get-tuple-element.62.refs_2_, bf16[2,128,128]{2,1,0:T(8,128)(2,1)} %get-tuple-element.63.refs_3_, ...), custom_call_target="tpu_custom_call" | custom-call | flops 16777216 | bytes 1294336 | tf_op jit(solution)/shard_map/pick/pallas_call | solution.py:437
  78.7 0.1 collective-permute-start.8
  78.8 1.5 %collective-permute-done.8.refs_1_ = bf16[448,128]{1,0:T(8,128)(2,1)S(1)} collective-permute-done((bf16[448,128]{1,0:T(8,128)(2,1)}, bf16[448,128]{1,0:T(8,128)(2,1)S(1)}, u32[]{:S(2)}, u32[]{:S(2)}) %collective-permute-start.8) | collective-permute-done | bytes 114720 | tf_op jit(solution)/shard_map/ppermute | solution.py:461
  80.3 3.3 %last.1 = (f32[2,512,128]{2,1,0:T(8,128)}, f32[2,512,128]{2,1,0:T(8,128)}) custom-call(bf16[448,128]{1,0:T(8,128)(2,1)} %pick.1.refs_0_, bf16[448,128]{1,0:T(8,128)(2,1)S(1)} %collective-permute-done.8.refs_1_, f32[2,512,128]{2,1,0:T(8,128)} %get-tuple-element.66.refs_2_, f32[2,512,128]{2,1,0:T(8,128)S(1)} %collective-permute-done.9.refs_3_, ...), custom_call_target="tpu_custom_call" | custom-call | flops 134217728 | bytes 2852864 | tf_op jit(solution)/shard_map/last/pallas_call | solution.py:437
  (5 shorter events, 0.0 us)
Async XLA Ops:
  0.6 2.0 %collective-permute-start.1 = (bf16[96,768]{1,0:T(8,128)(2,1)}, bf16[96,768]{1,0:T(8,128)(2,1)S(1)}, u32[]{:S(2)}, u32[]{:S(2)}) collective-permute-start(bf16[96,768]{1,0:T(8,128)(2,1)} %refs_0_.1), channel_id=1, source_target_pairs={{1,0},{0,1},{3,2},{2,3},{5,4},{4,5},{7,6},{6,7},{9,8},{8,9},{11,10... | collective-permute-start | bytes 442376 | tf_op jit(solution)/shard_map/ppermute | solution.py:461
  1.1 1.5 %collective-permute-start = (bf16[2,48,512]{2,1,0:T(8,128)(2,1)}, bf16[2,48,512]{2,1,0:T(8,128)(2,1)S(1)}, u32[]{:S(2)}, u32[]{:S(2)}) collective-permute-start(bf16[2,48,512]{2,1,0:T(8,128)(2,1)} %bitcast.1), channel_id=1, source_target_pairs={{1,0},{0,1},{3,2},{2,3},{5,4},{4,5},{7,6},{6,7},{9,8},{8,9},{11,10... | collective-permute-start | bytes 294920 | tf_op jit(solution)/shard_map/ppermute | solution.py:461
  2.7 10.9 %collective-permute-start.2 = (bf16[2,512,1024]{2,1,0:T(8,128)(2,1)}, bf16[2,512,1024]{2,1,0:T(8,128)(2,1)S(1)}, u32[]{:S(2)}, u32[]{:S(2)}) collective-permute-start(bf16[2,512,1024]{2,1,0:T(8,128)(2,1)} %refs_0_.2), channel_id=1, source_target_pairs={{1,0},{0,1},{3,2},{2,3},{5,4},{4,5},{7,6},{6,7},{9,8},{8,9},{11,10... | collective-permute-start | bytes 6291464 | tf_op jit(solution)/shard_map/ppermute | solution.py:461
  2.9 10.7 %collective-permute-start.3 = (bf16[2,512,1024]{2,1,0:T(8,128)(2,1)}, bf16[2,512,1024]{2,1,0:T(8,128)(2,1)}, u32[]{:S(2)}, u32[]{:S(2)}) collective-permute-start(bf16[2,512,1024]{2,1,0:T(8,128)(2,1)} %refs_2_.3), channel_id=1, source_target_pairs={{1,0},{0,1},{3,2},{2,3},{5,4},{4,5},{7,6},{6,7},{9,8},{8,9},{11,10... | collective-permute-start | bytes 6291464 | tf_op jit(solution)/shard_map/ppermute | solution.py:461
  5.5 18.4 %all-to-all-start = ((bf16[16,64,128]{2,1,0:T(8,128)(2,1)}), bf16[16,64,128]{2,1,0:T(8,128)(2,1)S(1)}, u32[]{:S(2)}, u32[]{:S(2)}) async-start(bf16[16,64,128]{2,1,0:T(8,128)(2,1)} %open.1), calls=%async_computation | async-start | bytes 524288 | tf_op jit(solution)/shard_map/all_to_all | solution.py:499
  27.4 13.3 %all-to-all-start.1 = ((bf16[16,48,128]{2,1,0:T(8,128)(2,1)}), bf16[16,48,128]{2,1,0:T(8,128)(2,1)S(1)}, u32[]{:S(2)}, u32[]{:S(2)}) async-start(bf16[16,48,128]{2,1,0:T(8,128)(2,1)} %get-tuple-element.43), calls=%async_computation.1 | async-start | bytes 393216 | tf_op jit(solution)/shard_map/all_to_all | solution.py:539
  31.0 9.0 %collective-permute-start.4 = (bf16[128,128]{1,0:T(8,128)(2,1)}, bf16[128,128]{1,0:T(8,128)(2,1)S(1)}, u32[]{:S(2)}, u32[]{:S(2)}) collective-permute-start(bf16[128,128]{1,0:T(8,128)(2,1)} %get-tuple-element.55), channel_id=1, source_target_pairs={{0,2},{2,0},{4,6},{6,4},{8,10},{10,8},{12,14},{14,12},{16,18},{18,... | collective-permute-start | bytes 98312 | tf_op jit(solution)/shard_map/ppermute | solution.py:540
  33.0 7.7 %collective-permute-start.5 = (bf16[128,128]{1,0:T(8,128)(2,1)}, bf16[128,128]{1,0:T(8,128)(2,1)S(1)}, u32[]{:S(2)}, u32[]{:S(2)}) collective-permute-start(bf16[128,128]{1,0:T(8,128)(2,1)} %get-tuple-element.41), channel_id=1, source_target_pairs={{0,30},{2,4},{4,2},{6,8},{8,6},{10,12},{12,10},{14,16},{16,14},{18... | collective-permute-start | bytes 98312 | tf_op jit(solution)/shard_map/ppermute | solution.py:520
  43.5 13.6 %all-to-all-start.2 = ((bf16[16,48,128]{2,1,0:T(8,128)(2,1)}), bf16[16,48,128]{2,1,0:T(8,128)(2,1)S(1)}, u32[]{:S(2)}, u32[]{:S(2)}) async-start(bf16[16,48,128]{2,1,0:T(8,128)(2,1)} %get-tuple-element.56), calls=%async_computation.2 | async-start | bytes 393216 | tf_op jit(solution)/shard_map/all_to_all | solution.py:549
  56.5 22.3 %collective-permute-start.9 = (f32[2,512,128]{2,1,0:T(8,128)}, f32[2,512,128]{2,1,0:T(8,128)S(1)}, u32[]{:S(2)}, u32[]{:S(2)}) collective-permute-start(f32[2,512,128]{2,1,0:T(8,128)} %get-tuple-element.67), channel_id=1, source_target_pairs={{0,1},{1,0},{2,3},{3,2},{4,5},{5,4},{6,7},{7,6},{8,9},{9,8},{10,11... | collective-permute-start | bytes 1572872 | tf_op jit(solution)/shard_map/ppermute | solution.py:579
  59.4 16.7 %all-to-all-start.3 = ((bf16[16,48,128]{2,1,0:T(8,128)(2,1)}), bf16[16,48,128]{2,1,0:T(8,128)(2,1)S(1)}, u32[]{:S(2)}, u32[]{:S(2)}) async-start(bf16[16,48,128]{2,1,0:T(8,128)(2,1)} %coarse.1), calls=%async_computation.3 | async-start | bytes 393216 | tf_op jit(solution)/shard_map/all_to_all | solution.py:575
  65.7 6.1 %collective-permute-start.6 = (bf16[128,128]{1,0:T(8,128)(2,1)}, bf16[128,128]{1,0:T(8,128)(2,1)S(1)}, u32[]{:S(2)}, u32[]{:S(2)}) collective-permute-start(bf16[128,128]{1,0:T(8,128)(2,1)} %get-tuple-element.64), channel_id=1, source_target_pairs={{0,2},{2,0},{4,6},{6,4},{8,10},{10,8},{12,14},{14,12},{16,18},{18,... | collective-permute-start | bytes 98312 | tf_op jit(solution)/shard_map/ppermute | solution.py:576
  67.7 8.5 %collective-permute-start.7 = (bf16[128,128]{1,0:T(8,128)(2,1)}, bf16[128,128]{1,0:T(8,128)(2,1)S(1)}, u32[]{:S(2)}, u32[]{:S(2)}) collective-permute-start(bf16[128,128]{1,0:T(8,128)(2,1)} %get-tuple-element.65), channel_id=1, source_target_pairs={{0,30},{2,4},{4,2},{6,8},{8,6},{10,12},{12,10},{14,16},{16,14},{18... | collective-permute-start | bytes 98312 | tf_op jit(solution)/shard_map/ppermute | solution.py:565
  78.7 1.6 %collective-permute-start.8 = (bf16[448,128]{1,0:T(8,128)(2,1)}, bf16[448,128]{1,0:T(8,128)(2,1)S(1)}, u32[]{:S(2)}, u32[]{:S(2)}) collective-permute-start(bf16[448,128]{1,0:T(8,128)(2,1)} %pick.1.refs_0_), channel_id=1, source_target_pairs={{1,0},{0,1},{3,2},{2,3},{5,4},{4,5},{7,6},{6,7},{9,8},{8,9},{11,10... | collective-permute-start | bytes 344072 | tf_op jit(solution)/shard_map/ppermute | solution.py:461

commit v14 on v13

--- a/solution.py
+++ b/solution.py
@@ -122,8 +122,9 @@
 
 
 def multiply(z, pieces, vector, store, wait):
+    for k in range(z.group):
+        wait(k)
     for k, piece in enumerate(pieces):
-        wait(k)
         parts = [dot(piece[s], vector) for s in range(z.subs)]
         store(k, piece_start(z, k, z.own), select(z, parts))
 
@@ -358,14 +359,13 @@
         message[k] = modes
 
 
-def pick_kernel(z, *refs):
-    arrived, picks, before, after, first_got, second_got = refs[:6]
-    base_before, base_after, base_first, base_second, out = refs[6:]
+def pick_kernel(z, arrived, picks, before, after, base_before, base_after, base_first, base_second, out):
     chosen = picked_rows(z, arrived, picks)
     near = chosen.shape[0]
+    none = jnp.zeros((z.face, z.lanes), BF16)
     lefts, rights = [], []
     for s in range(z.subs):
-        values = sides(z, before, after, first_got, second_got, s)
+        values = (none if s == 0 else after[s - 1]), (none if s == z.subs - 1 else before[s + 1])
         bases = sides(z, base_before, base_after, base_first, base_second, s)
         left, right = shares(z, s, chosen, values, bases)
         lefts.append(left)
@@ -377,7 +377,8 @@
 
 def last_kernel(z, *refs):
     chosen, values = refs[: z.group], refs[z.group : 2 * z.group]
-    tall, left_rows, right_rows, second_pass, final_residual = refs[2 * z.group :]
+    firsts, seconds = refs[2 * z.group : 3 * z.group], refs[3 * z.group : 4 * z.group]
+    tall, left_rows, right_rows, second_pass, final_residual = refs[4 * z.group :]
     start = piece_start(z, 0, z.own)
     near = (z.subs + 2) * z.modes
     lefts, rights = [], []
@@ -388,7 +389,12 @@
     done = [jnp.zeros((z.own, z.lanes), F32) for _ in range(2 * z.subs)]
     for k in range(z.group):
         rows = chosen[k][:near]
-        left, right = chosen[k][near : near + z.face], chosen[k][near + z.face :]
+        from_before = dot(jnp.where(even(), seconds[k][...], firsts[k][...]), lane_matrix(z, 0, 0))
+        from_after = dot(
+            jnp.where(even(), firsts[k][...], seconds[k][...]), lane_matrix(z, 0, (z.subs - 1) * z.width)
+        )
+        left = (chosen[k][near : near + z.face].astype(F32) + from_before).astype(BF16)
+        right = (chosen[k][near + z.face :].astype(F32) + from_after).astype(BF16)
         steps, images = [], []
         for s in range(z.subs):
             total = dot(lefts[s], correction_side(z, rows, s, left))
@@ -581,9 +587,9 @@
     (chosen,) = call(
         functools.partial(pick_kernel, z),
         [shape((near + 2 * face, lanes), BF16)],
-        [coarse, picks, before, after, first_got, second_got, *bases],
+        [coarse, picks, before, after, *bases],
         work // 64,
-        loose=[0, 4, 5, 8, 9],
+        loose=[0, 6, 7],
         name="pick",
     )
     out = shape((subs, z.own, z.cases), F32)
@@ -591,9 +597,12 @@
         call(
             functools.partial(last_kernel, z),
             [out, out],
-            [*pieces_of(chosen, group), *swapped, tall, left_rows, right_rows],
+            [
+                *pieces_of(chosen, group), *swapped, *pieces_of(first_got, group), *pieces_of(second_got, group),
+                tall, left_rows, right_rows,
+            ],
             work // 8,
-            loose=[*range(1, group), *range(group + 1, 2 * group)],
+            loose=[*range(1, group), *range(group + 1, 4 * group)],
             name="last",
         )
     )

time: 84.3 us -> 91.2 us (1.082)
  blocking collectives: 0 us -> 14.9 us
  starting transfers between devices: 37 us -> 28.4 us
    all_to_all x0 -> x1, blocking collectives: none -> 14.9 us  [body(): coarse = spread(message)]
    all_to_all x2 -> x1, starting transfers between devices: 9.97 us -> 3.55 us  [body(): coarse = spread(message)]
    ppermute x2, starting transfers between devices: 8.32 us -> 6.67 us  [body(): second_got = lax.ppermute(second_pair, 'sub', second_pairs)]
    ppermute x5 -> x7, waiting for transfers between devices: 2.95 us -> 2.65 us  [pieces_of(): lax.ppermute(block, GROUP, [((g + k) % group, g) for g in range(group)])]
  transfers between devices with their start and end apart: 14 -> 15, of which waited for: 6 -> 7; matrix products, arithmetic and copies ran while one was open for 0% -> 0% of each run, Pallas kernels for 29% -> 26%
where the time goes in v14:
time: 91.2 us; the launch traced here: 90.6 us
  Pallas kernels  33.7 us (37%)
  starting transfers between devices  28.4 us (31%)
  blocking collectives  14.9 us (16%)
  waiting for transfers between devices  12.8 us (14%)
    pallas_call x9, Pallas kernels, call(): pl.pallas_call(whole, out_shape=[pltpu.HBM(o.shape, o.dtype) for o in out...  33.7 us
    all_to_all x1, blocking collectives, body(): coarse = spread(message)  14.9 us
    all_to_all x2, starting transfers between devices, body(): restricted = spread(message)  13.6 us
    ppermute x2, starting transfers between devices, body(): second_got = lax.ppermute(second_pair, 'sub', second_pairs)  6.67 us
    ppermute x2, waiting for transfers between devices, body(): second_got = lax.ppermute(second_pair, 'sub', second_pairs)  5.55 us
    all_to_all x2, waiting for transfers between devices, body(): restricted = spread(message)  4.44 us
    all_to_all x1, starting transfers between devices, body(): coarse = spread(message)  3.55 us
    ppermute x2, starting transfers between devices, body(): first_got = lax.ppermute(first_pair, 'sub', first_pairs)  3.28 us
  transfers between devices with their start and end apart: 15, of which 7 were waited for; matrix products, arithmetic and copies ran while one was open for 0% of the time, Pallas kernels for 26%

profile of v14, /device:TPU:0, one launch (start us, length us, event | category | flops | bytes accessed | tf_op | source)
XLA Modules:
  0.0 90.6 jit_solution(11503004255619262087)
XLA Ops:
  0.6 0.5 collective-permute-start.1
  1.1 0.1 collective-permute-start
  1.2 1.4 %collective-permute-done.refs_1_.refs_5_ = bf16[2,48,512]{2,1,0:T(8,128)(2,1)S(1)} collective-permute-done((bf16[2,48,512]{2,1,0:T(8,128)(2,1)}, bf16[2,48,512]{2,1,0:T(8,128)(2,1)S(1)}, u32[]{:S(2)}, u32[]{:S(2)}) %collective-permute-start) | collective-permute-done | bytes 98336 | tf_op jit(solution)/shard_map/ppermute | solution.py:467
  2.7 0.2 collective-permute-start.2
  2.9 0.3 collective-permute-start.3
  3.2 2.3 %open.1 = bf16[16,64,128]{2,1,0:T(8,128)(2,1)} custom-call(bf16[2,48,512]{2,1,0:T(8,128)(2,1)} %bitcast.2, bf16[2,48,512]{2,1,0:T(8,128)(2,1)S(1)} %collective-permute-done.refs_1_.refs_5_, bf16[2,1024,128]{2,1,0:T(8,128)(2,1)} %refs_6_.1, s32[2,48]{1,0:T(2,128)} %refs_3_.2), custom_call_target="tpu_custom_call" | custom-call | flops 67108864 | bytes 983424 | tf_op jit(solution)/shard_map/open/pallas_call | solution.py:443
  5.5 8.1 %all-to-all-start = ((bf16[16,64,128]{2,1,0:T(8,128)(2,1)}), bf16[16,64,128]{2,1,0:T(8,128)(2,1)S(1)}, u32[]{:S(2)}, u32[]{:S(2)}) async-start(bf16[16,64,128]{2,1,0:T(8,128)(2,1)} %open.1), calls=%async_computation | async-start | bytes 524288 | tf_op jit(solution)/shard_map/all_to_all | solution.py:505
  13.5 0.0 collective-permute-done.2.refs_1_
  13.6 6.8 %first_image.1 = (bf16[1024,128]{1,0:T(8,128)(2,1)}, f32[1024,128]{1,0:T(8,128)}, f32[1024,128]{1,0:T(8,128)}, bf16[2,128,128]{2,1,0:T(8,128)(2,1)}, bf16[2,128,...) custom-call(bf16[2,512,1024]{2,1,0:T(8,128)(2,1)} %refs_0_.2, ...), custom_call_target="tpu_custom_call" | custom-call | flops 1073741824 | bytes 11339776 | tf_op jit(solution)/shard_map/first_image/pallas_call | solution.py:443
  20.4 3.5 %all-to-all-done.refs_2_ = bf16[16,64,128]{2,1,0:T(8,128)(2,1)S(1)} async-done(((bf16[16,64,128]{2,1,0:T(8,128)(2,1)}), bf16[16,64,128]{2,1,0:T(8,128)(2,1)S(1)}, u32[]{:S(2)}, u32[]{:S(2)}) %all-to-all-start) | async-done | bytes 262176 | tf_op jit(solution)/shard_map/all_to_all | solution.py:505
  23.9 3.5 %order.1 = (bf16[2,96,768]{2,1,0:T(8,128)(2,1)}, bf16[2,192,768]{2,1,0:T(8,128)(2,1)}, bf16[16,48,128]{2,1,0:T(8,128)(2,1)}) custom-call(bf16[96,768]{1,0:T(8,128)(2,1)} %refs_0_.1, bf16[96,768]{1,0:T(8,128)(2,1)S(1)} %collective-permute-done.1.refs_1_, bf16[16,64,128]{2,1,0:T(8,128)(2,1)S(1)} %all-to-all-done.refs_2_, ...), custom_call_target="tpu_custom_call" | custom-call | flops 452984832 | bytes 1890304 | tf_op jit(solution)/shard_map/order/pallas_call | solution.py:443
  27.4 3.6 %all-to-all-start.1 = ((bf16[16,48,128]{2,1,0:T(8,128)(2,1)}), bf16[16,48,128]{2,1,0:T(8,128)(2,1)S(1)}, u32[]{:S(2)}, u32[]{:S(2)}) async-start(bf16[16,48,128]{2,1,0:T(8,128)(2,1)} %get-tuple-element.43), calls=%async_computation.1 | async-start | bytes 393216 | tf_op jit(solution)/shard_map/all_to_all | solution.py:545
  30.9 1.9 %collective-permute-start.4 = (bf16[128,128]{1,0:T(8,128)(2,1)}, bf16[128,128]{1,0:T(8,128)(2,1)S(1)}, u32[]{:S(2)}, u32[]{:S(2)}) collective-permute-start(bf16[128,128]{1,0:T(8,128)(2,1)} %get-tuple-element.55), channel_id=1, source_target_pairs={{0,2},{2,0},{4,6},{6,4},{8,10},{10,8},{12,14},{14,12},{16,18},{18,... | collective-permute-start | bytes 98312 | tf_op jit(solution)/shard_map/ppermute | solution.py:546
  32.9 4.2 %collective-permute-start.5 = (bf16[128,128]{1,0:T(8,128)(2,1)}, bf16[128,128]{1,0:T(8,128)(2,1)S(1)}, u32[]{:S(2)}, u32[]{:S(2)}) collective-permute-start(bf16[128,128]{1,0:T(8,128)(2,1)} %get-tuple-element.41), channel_id=1, source_target_pairs={{0,30},{2,4},{4,2},{6,8},{8,6},{10,12},{12,10},{14,16},{16,14},{18... | collective-permute-start | bytes 98312 | tf_op jit(solution)/shard_map/ppermute | solution.py:526
  37.0 2.9 %begin.1 = (bf16[2,48,128]{2,1,0:T(8,128)(2,1)}, bf16[2,48,128]{2,1,0:T(8,128)(2,1)}, bf16[2,48,48]{2,1,0:T(8,128)(2,1)}, f32[48,128]{1,0:T(8,128)}) custom-call(bf16[1024,128]{1,0:T(8,128)(2,1)} %get-tuple-element.45.refs_0_.refs_4_, f32[1024,128]{1,0:T(8,128)} %get-tuple-element.46.refs_1_.refs_5_, ...), custom_call_target="tpu_custom_call" | custom-call | flops 67108864 | bytes 1592320 | tf_op jit(solution)/shard_map/begin/pallas_call | solution.py:443
  39.9 0.7 collective-permute-done.5.refs_9_.refs_12_.refs_7_
  40.6 0.0 all-to-all-done.1.refs_0_
  40.6 2.8 %update.1 = (bf16[192,128]{1,0:T(8,128)(2,1)}, bf16[16,48,128]{2,1,0:T(8,128)(2,1)}) custom-call(bf16[16,48,128]{2,1,0:T(8,128)(2,1)S(1)} %all-to-all-done.1.refs_0_, bf16[2,192,768]{2,1,0:T(8,128)(2,1)} %get-tuple-element.44.refs_1_, f32[48,128]{1,0:T(8,128)} %get-tuple-element.49.refs_2_, bf16[2,48,48]{2,1,0:T(8,128)(2,1)} %get-tuple-element.50.refs_3_, ...), custom_call_target="tpu_custom_call" | custom-call | flops 16777216 | bytes 1311744 | tf_op jit(solution)/shard_map/update/pallas_call | solution.py:443
  43.4 5.6 %all-to-all-start.2 = ((bf16[16,48,128]{2,1,0:T(8,128)(2,1)}), bf16[16,48,128]{2,1,0:T(8,128)(2,1)S(1)}, u32[]{:S(2)}, u32[]{:S(2)}) async-start(bf16[16,48,128]{2,1,0:T(8,128)(2,1)} %get-tuple-element.56), calls=%async_computation.2 | async-start | bytes 393216 | tf_op jit(solution)/shard_map/all_to_all | solution.py:555
  49.0 7.0 %second_image.1 = (bf16[2,128,128]{2,1,0:T(8,128)(2,1)}, bf16[2,128,128]{2,1,0:T(8,128)(2,1)}, bf16[128,128]{1,0:T(8,128)(2,1)}, bf16[128,128]{1,0:T(8,128)(2,1)...) custom-call(bf16[2,512,1024]{2,1,0:T(8,128)(2,1)} %refs_0_.2, ...), custom_call_target="tpu_custom_call" | custom-call | flops 1073741824 | bytes 11716608 | tf_op jit(solution)/shard_map/second_image/pallas_call | solution.py:443
  56.1 0.1 collective-permute-start.7
  56.1 0.9 %all-to-all-done.2.refs_0_ = bf16[16,48,128]{2,1,0:T(8,128)(2,1)S(1)} async-done(((bf16[16,48,128]{2,1,0:T(8,128)(2,1)}), bf16[16,48,128]{2,1,0:T(8,128)(2,1)S(1)}, u32[]{:S(2)}, u32[]{:S(2)}) %all-to-all-start.2) | async-done | bytes 196640 | tf_op jit(solution)/shard_map/all_to_all | solution.py:555
  57.1 2.2 %coarse.1 = bf16[16,48,128]{2,1,0:T(8,128)(2,1)} custom-call(bf16[16,48,128]{2,1,0:T(8,128)(2,1)S(1)} %all-to-all-done.2.refs_0_, bf16[2,96,768]{2,1,0:T(8,128)(2,1)} %get-tuple-element.61.refs_1_), custom_call_target="tpu_custom_call" | custom-call | flops 16777216 | bytes 688128 | tf_op jit(solution)/shard_map/coarse/pallas_call | solution.py:443
  59.3 14.9 %all_to_all.20.refs_0_ = bf16[16,48,128]{2,1,0:T(8,128)(2,1)S(1)} all-to-all(bf16[16,48,128]{2,1,0:T(8,128)(2,1)} %coarse.1), channel_id=1, replica_groups=mesh['sub'=16,'crow'=2,'ccol'=1] {'sub'}, dimensions={0} | all-to-all | bytes 393216 | tf_op jit(solution)/shard_map/all_to_all | solution.py:581
  74.2 2.6 %pick.1.refs_0_ = bf16[448,128]{1,0:T(8,128)(2,1)} custom-call(bf16[16,48,128]{2,1,0:T(8,128)(2,1)S(1)} %all_to_all.20.refs_0_, bf16[2,192,768]{2,1,0:T(8,128)(2,1)} %get-tuple-element.44.refs_1_, bf16[2,128,128]{2,1,0:T(8,128)(2,1)} %get-tuple-element.62.refs_2_, bf16[2,128,128]{2,1,0:T(8,128)(2,1)} %get-tuple-element.63.refs_3_, ...), custom_call_target="tpu_custom_call" | custom-call | flops 16777216 | bytes 1228800 | tf_op jit(solution)/shard_map/pick/pallas_call | solution.py:443
  76.8 0.1 collective-permute-start.6
  76.9 1.4 %collective-permute-start.8 = (bf16[128,128]{1,0:T(8,128)(2,1)S(1)}, bf16[128,128]{1,0:T(8,128)(2,1)S(1)}, u32[]{:S(2)}, u32[]{:S(2)}) collective-permute-start(bf16[128,128]{1,0:T(8,128)(2,1)S(1)} %copy-done.1), channel_id=1, source_target_pairs={{0,2},{2,0},{4,6},{6,4},{8,10},{10,8},{12,14},{14,12},{16,18},{18,... | collective-permute-start | bytes 98312 | tf_op jit(solution)/shard_map/ppermute | solution.py:582
  78.2 2.5 %collective-permute-start.10 = (bf16[128,128]{1,0:T(8,128)(2,1)S(1)}, bf16[128,128]{1,0:T(8,128)(2,1)S(1)}, u32[]{:S(2)}, u32[]{:S(2)}) collective-permute-start(bf16[128,128]{1,0:T(8,128)(2,1)S(1)} %copy-done), channel_id=1, source_target_pairs={{0,30},{2,4},{4,2},{6,8},{8,6},{10,12},{12,10},{14,16},{16,14},{18... | collective-permute-start | bytes 98312 | tf_op jit(solution)/shard_map/ppermute | solution.py:571
  80.8 0.1 collective-permute-done.8.refs_4_
  80.9 4.9 %collective-permute-done.10.refs_6_ = bf16[128,128]{1,0:T(8,128)(2,1)S(1)} collective-permute-done((bf16[128,128]{1,0:T(8,128)(2,1)S(1)}, bf16[128,128]{1,0:T(8,128)(2,1)S(1)}, u32[]{:S(2)}, u32[]{:S(2)}) %collective-permute-start.10) | collective-permute-done | bytes 32800 | tf_op jit(solution)/shard_map/ppermute | solution.py:571
  85.8 1.2 %collective-permute-done.11.refs_7_ = bf16[128,128]{1,0:T(8,128)(2,1)S(1)} collective-permute-done((bf16[128,128]{1,0:T(8,128)(2,1)S(1)}, bf16[128,128]{1,0:T(8,128)(2,1)S(1)}, u32[]{:S(2)}, u32[]{:S(2)}) %collective-permute-start.11) | collective-permute-done | bytes 32800 | tf_op jit(solution)/shard_map/ppermute | solution.py:467
  87.0 3.6 %last.1 = (f32[2,512,128]{2,1,0:T(8,128)}, f32[2,512,128]{2,1,0:T(8,128)}) custom-call(bf16[448,128]{1,0:T(8,128)(2,1)} %pick.1.refs_0_, bf16[448,128]{1,0:T(8,128)(2,1)S(1)} %collective-permute-done.6.refs_1_, f32[2,512,128]{2,1,0:T(8,128)} %get-tuple-element.64.refs_2_, f32[2,512,128]{2,1,0:T(8,128)S(1)} %collective-permute-done.7.refs_3_, ...), custom_call_target="tpu_custom_call" | custom-call | flops 134217728 | bytes 2983936 | tf_op jit(solution)/shard_map/last/pallas_call | solution.py:443
  (12 shorter events, 0.0 us)
Async XLA Ops:
  0.6 2.0 %collective-permute-start.1 = (bf16[96,768]{1,0:T(8,128)(2,1)}, bf16[96,768]{1,0:T(8,128)(2,1)S(1)}, u32[]{:S(2)}, u32[]{:S(2)}) collective-permute-start(bf16[96,768]{1,0:T(8,128)(2,1)} %refs_0_.1), channel_id=1, source_target_pairs={{1,0},{0,1},{3,2},{2,3},{5,4},{4,5},{7,6},{6,7},{9,8},{8,9},{11,10... | collective-permute-start | bytes 442376 | tf_op jit(solution)/shard_map/ppermute | solution.py:467
  1.1 1.5 %collective-permute-start = (bf16[2,48,512]{2,1,0:T(8,128)(2,1)}, bf16[2,48,512]{2,1,0:T(8,128)(2,1)S(1)}, u32[]{:S(2)}, u32[]{:S(2)}) collective-permute-start(bf16[2,48,512]{2,1,0:T(8,128)(2,1)} %bitcast.1), channel_id=1, source_target_pairs={{1,0},{0,1},{3,2},{2,3},{5,4},{4,5},{7,6},{6,7},{9,8},{8,9},{11,10... | collective-permute-start | bytes 294920 | tf_op jit(solution)/shard_map/ppermute | solution.py:467
  2.7 10.9 %collective-permute-start.2 = (bf16[2,512,1024]{2,1,0:T(8,128)(2,1)}, bf16[2,512,1024]{2,1,0:T(8,128)(2,1)S(1)}, u32[]{:S(2)}, u32[]{:S(2)}) collective-permute-start(bf16[2,512,1024]{2,1,0:T(8,128)(2,1)} %refs_0_.2), channel_id=1, source_target_pairs={{1,0},{0,1},{3,2},{2,3},{5,4},{4,5},{7,6},{6,7},{9,8},{8,9},{11,10... | collective-permute-start | bytes 6291464 | tf_op jit(solution)/shard_map/ppermute | solution.py:467
  2.9 10.7 %collective-permute-start.3 = (bf16[2,512,1024]{2,1,0:T(8,128)(2,1)}, bf16[2,512,1024]{2,1,0:T(8,128)(2,1)}, u32[]{:S(2)}, u32[]{:S(2)}) collective-permute-start(bf16[2,512,1024]{2,1,0:T(8,128)(2,1)} %refs_2_.3), channel_id=1, source_target_pairs={{1,0},{0,1},{3,2},{2,3},{5,4},{4,5},{7,6},{6,7},{9,8},{8,9},{11,10... | collective-permute-start | bytes 6291464 | tf_op jit(solution)/shard_map/ppermute | solution.py:467
  5.5 18.4 %all-to-all-start = ((bf16[16,64,128]{2,1,0:T(8,128)(2,1)}), bf16[16,64,128]{2,1,0:T(8,128)(2,1)S(1)}, u32[]{:S(2)}, u32[]{:S(2)}) async-start(bf16[16,64,128]{2,1,0:T(8,128)(2,1)} %open.1), calls=%async_computation | async-start | bytes 524288 | tf_op jit(solution)/shard_map/all_to_all | solution.py:505
  27.4 13.2 %all-to-all-start.1 = ((bf16[16,48,128]{2,1,0:T(8,128)(2,1)}), bf16[16,48,128]{2,1,0:T(8,128)(2,1)S(1)}, u32[]{:S(2)}, u32[]{:S(2)}) async-start(bf16[16,48,128]{2,1,0:T(8,128)(2,1)} %get-tuple-element.43), calls=%async_computation.1 | async-start | bytes 393216 | tf_op jit(solution)/shard_map/all_to_all | solution.py:545
  30.9 9.0 %collective-permute-start.4 = (bf16[128,128]{1,0:T(8,128)(2,1)}, bf16[128,128]{1,0:T(8,128)(2,1)S(1)}, u32[]{:S(2)}, u32[]{:S(2)}) collective-permute-start(bf16[128,128]{1,0:T(8,128)(2,1)} %get-tuple-element.55), channel_id=1, source_target_pairs={{0,2},{2,0},{4,6},{6,4},{8,10},{10,8},{12,14},{14,12},{16,18},{18,... | collective-permute-start | bytes 98312 | tf_op jit(solution)/shard_map/ppermute | solution.py:546
  32.9 7.7 %collective-permute-start.5 = (bf16[128,128]{1,0:T(8,128)(2,1)}, bf16[128,128]{1,0:T(8,128)(2,1)S(1)}, u32[]{:S(2)}, u32[]{:S(2)}) collective-permute-start(bf16[128,128]{1,0:T(8,128)(2,1)} %get-tuple-element.41), channel_id=1, source_target_pairs={{0,30},{2,4},{4,2},{6,8},{8,6},{10,12},{12,10},{14,16},{16,14},{18... | collective-permute-start | bytes 98312 | tf_op jit(solution)/shard_map/ppermute | solution.py:526
  43.4 13.6 %all-to-all-start.2 = ((bf16[16,48,128]{2,1,0:T(8,128)(2,1)}), bf16[16,48,128]{2,1,0:T(8,128)(2,1)S(1)}, u32[]{:S(2)}, u32[]{:S(2)}) async-start(bf16[16,48,128]{2,1,0:T(8,128)(2,1)} %get-tuple-element.56), calls=%async_computation.2 | async-start | bytes 393216 | tf_op jit(solution)/shard_map/all_to_all | solution.py:555
  56.0 20.8 %copy-start.1 = (bf16[128,128]{1,0:T(8,128)(2,1)S(1)}, bf16[128,128]{1,0:T(8,128)(2,1)}, u32[]{:S(2)}) copy-start(bf16[128,128]{1,0:T(8,128)(2,1)} %get-tuple-element.66) | copy-start | bytes 98308
  56.1 22.2 %copy-start = (bf16[128,128]{1,0:T(8,128)(2,1)S(1)}, bf16[128,128]{1,0:T(8,128)(2,1)}, u32[]{:S(2)}) copy-start(bf16[128,128]{1,0:T(8,128)(2,1)} %get-tuple-element.67) | copy-start | bytes 98308
  56.1 30.9 %collective-permute-start.7 = (f32[2,512,128]{2,1,0:T(8,128)}, f32[2,512,128]{2,1,0:T(8,128)S(1)}, u32[]{:S(2)}, u32[]{:S(2)}) collective-permute-start(f32[2,512,128]{2,1,0:T(8,128)} %get-tuple-element.65), channel_id=1, source_target_pairs={{0,1},{1,0},{2,3},{3,2},{4,5},{5,4},{6,7},{7,6},{8,9},{9,8},{10,11... | collective-permute-start | bytes 1572872 | tf_op jit(solution)/shard_map/ppermute | solution.py:585
  76.8 10.2 %collective-permute-start.6 = (bf16[448,128]{1,0:T(8,128)(2,1)}, bf16[448,128]{1,0:T(8,128)(2,1)S(1)}, u32[]{:S(2)}, u32[]{:S(2)}) collective-permute-start(bf16[448,128]{1,0:T(8,128)(2,1)} %pick.1.refs_0_), channel_id=1, source_target_pairs={{1,0},{0,1},{3,2},{2,3},{5,4},{4,5},{7,6},{6,7},{9,8},{8,9},{11,10... | collective-permute-start | bytes 344072 | tf_op jit(solution)/shard_map/ppermute | solution.py:467
  76.9 4.0 %collective-permute-start.8 = (bf16[128,128]{1,0:T(8,128)(2,1)S(1)}, bf16[128,128]{1,0:T(8,128)(2,1)S(1)}, u32[]{:S(2)}, u32[]{:S(2)}) collective-permute-start(bf16[128,128]{1,0:T(8,128)(2,1)S(1)} %copy-done.1), channel_id=1, source_target_pairs={{0,2},{2,0},{4,6},{6,4},{8,10},{10,8},{12,14},{14,12},{16,18},{18,... | collective-permute-start | bytes 98312 | tf_op jit(solution)/shard_map/ppermute | solution.py:582
  78.2 7.5 %collective-permute-start.10 = (bf16[128,128]{1,0:T(8,128)(2,1)S(1)}, bf16[128,128]{1,0:T(8,128)(2,1)S(1)}, u32[]{:S(2)}, u32[]{:S(2)}) collective-permute-start(bf16[128,128]{1,0:T(8,128)(2,1)S(1)} %copy-done), channel_id=1, source_target_pairs={{0,30},{2,4},{4,2},{6,8},{8,6},{10,12},{12,10},{14,16},{16,14},{18... | collective-permute-start | bytes 98312 | tf_op jit(solution)/shard_map/ppermute | solution.py:571
  80.9 4.9 %collective-permute-start.9 = (bf16[128,128]{1,0:T(8,128)(2,1)S(1)}, bf16[128,128]{1,0:T(8,128)(2,1)S(1)}, u32[]{:S(2)}, u32[]{:S(2)}) collective-permute-start(bf16[128,128]{1,0:T(8,128)(2,1)S(1)} %collective-permute-done.8.refs_4_), channel_id=1, source_target_pairs={{1,0},{0,1},{3,2},{2,3},{5,4},{4,5},{7,6},{6,7},{9,8},{8,9},{11,10... | collective-permute-start | bytes 98312 | tf_op jit(solution)/shard_map/ppermute | solution.py:467
  85.8 1.2 %collective-permute-start.11 = (bf16[128,128]{1,0:T(8,128)(2,1)S(1)}, bf16[128,128]{1,0:T(8,128)(2,1)S(1)}, u32[]{:S(2)}, u32[]{:S(2)}) collective-permute-start(bf16[128,128]{1,0:T(8,128)(2,1)S(1)} %collective-permute-done.10.refs_6_), channel_id=1, source_target_pairs={{1,0},{0,1},{3,2},{2,3},{5,4},{4,5},{7,6},{6,7},{9,8},{8,9},{11,10... | collective-permute-start | bytes 98312 | tf_op jit(solution)/shard_map/ppermute | solution.py:467

commit v15 on v13

--- a/solution.py
+++ b/solution.py
@@ -122,8 +122,9 @@
 
 
 def multiply(z, pieces, vector, store, wait):
+    for k in range(z.group):
+        wait(k)
     for k, piece in enumerate(pieces):
-        wait(k)
         parts = [dot(piece[s], vector) for s in range(z.subs)]
         store(k, piece_start(z, k, z.own), select(z, parts))
 
@@ -226,7 +227,9 @@
     store_faces(z, before, after, first_pair, second_pair)
 
 
-def begin_kernel(z, load_rows, image, tall, basis_t, left_rows, right_rows, left_t, right_t, inner, start_modes):
+def begin_kernel(z, *refs):
+    load_rows, image, tall, basis_t, left_rows, right_rows, index, place = refs[:8]
+    left_t, right_t, inner, start_modes, picks = refs[8:]
     left = (load_rows[...].astype(F32) - image[...]).astype(BF16)
     begun = []
     for s in range(z.subs):
@@ -237,6 +240,20 @@
         left_t[s] = sides_t[:, : z.face]
         right_t[s] = sides_t[:, z.face :]
     start_modes[...] = select(z, begun)
+    here = lax.axis_index("sub")
+    device = lax.broadcasted_iota(jnp.int32, (z.n, z.lanes), 0)
+    for t in range(z.subs + 2):
+        if t == 0:
+            s, owner = z.subs - 1, lax.rem(here + z.n - 1, z.n)
+        elif t == z.subs + 1:
+            s, owner = 0, lax.rem(here + 1, z.n)
+        else:
+            s, owner = t - 1, here
+        row = jnp.sum(jnp.where(device == owner, index[s], 0.0), axis=0, keepdims=True)
+        column = jnp.transpose(jnp.broadcast_to(row, (z.lanes, z.lanes)))[: z.modes, 0:1].astype(jnp.int32)
+        for h in range(z.subs):
+            hit = column == place[h : h + 1, :]
+            picks[h, t * z.modes : (t + 1) * z.modes, :] = jnp.where(hit, 1.0, 0.0).astype(BF16)
 
 
 def second_image_kernel(z, wait, *refs):
@@ -295,13 +312,12 @@
 
 def order_kernel(z, *refs):
     blocks = refs[: z.group]
-    arrived, repeat, own_row, place, ordered_inverse, picks, message = refs[z.group :]
+    arrived, repeat, own_row, ordered_inverse, index, message = refs[z.group :]
     digits = arrived[:, z.modes :, :].astype(F32)
-    index = []
     for s in range(z.subs):
         high = jnp.sum(jnp.where(digit_row(digits.shape, 2 * s), digits, 0.0), axis=1)
         low = jnp.sum(jnp.where(digit_row(digits.shape, 2 * s + 1), digits, 0.0), axis=1)
-        index.append(high * DIGIT + low)
+        index[s] = high * DIGIT + low
         spread = dot(high.astype(BF16), repeat[...]) * DIGIT + dot(low.astype(BF16), repeat[...])
         places = jnp.sum(spread * own_row[...], axis=0, keepdims=True).astype(jnp.int32)
         for at in range(0, z.columns, 768):
@@ -316,20 +332,6 @@
                     total = total + dot(block[:, first : first + deep], hot)
             ordered_inverse[s, :, at : at + wide] = total.astype(BF16)
     coarse_rows(z, ordered_inverse, arrived, message)
-    here = lax.axis_index("sub")
-    device = lax.broadcasted_iota(jnp.int32, (z.n, z.lanes), 0)
-    for t in range(z.subs + 2):
-        if t == 0:
-            s, owner = z.subs - 1, lax.rem(here + z.n - 1, z.n)
-        elif t == z.subs + 1:
-            s, owner = 0, lax.rem(here + 1, z.n)
-        else:
-            s, owner = t - 1, here
-        row = jnp.sum(jnp.where(device == owner, index[s], 0.0), axis=0, keepdims=True)
-        column = jnp.transpose(jnp.broadcast_to(row, (z.lanes, z.lanes)))[: z.modes, 0:1].astype(jnp.int32)
-        for h in range(z.subs):
-            hit = column == place[h : h + 1, :]
-            picks[h, t * z.modes : (t + 1) * z.modes, :] = jnp.where(hit, 1.0, 0.0).astype(BF16)
 
 
 def coarse_kernel(z, arrived, ordered_inverse, message):
@@ -518,26 +520,29 @@
         name="first_image",
     )
     second_got = lax.ppermute(second_pair, "sub", second_pairs)
-    side = shape((subs, modes, face), BF16)
-    left_t, right_t, inner, start_modes = call(
-        functools.partial(begin_kernel, z),
-        [side, side, shape((subs, modes, modes), BF16), shape((modes, lanes), F32)],
-        [load_rows, image, tall, basis_t, left_rows, right_rows],
-        work // 16,
-        name="begin",
-    )
     restricted, second_pair = lax.optimization_barrier((restricted, second_pair))
     near = (subs + 2) * modes
-    ordered_inverse, picks, message = call(
+    ordered_inverse, index, message = call(
         functools.partial(order_kernel, z),
-        [shape((subs, z.owned, z.columns), BF16), shape((subs, near, z.columns), BF16), copies],
-        [*inverse_columns, restricted, repeat, own_row, place],
+        [shape((subs, z.owned, z.columns), BF16), shape((subs, n, lanes), F32), copies],
+        [*inverse_columns, restricted, repeat, own_row],
         2 * z.owned * z.total * z.total,
         loose=range(1, group + 1),
         name="order",
     )
     coarse = spread(message)
     first_got = lax.ppermute(first_pair, "sub", first_pairs)
+    side = shape((subs, modes, face), BF16)
+    left_t, right_t, inner, start_modes, picks = call(
+        functools.partial(begin_kernel, z),
+        [
+            side, side, shape((subs, modes, modes), BF16), shape((modes, lanes), F32),
+            shape((subs, near, z.columns), BF16),
+        ],
+        [load_rows, image, tall, basis_t, left_rows, right_rows, index, place],
+        work // 16,
+        name="begin",
+    )
     chosen, message = call(
         functools.partial(update_kernel, z),
         [shape((near, lanes), BF16), copies],

time: 84.3 us -> 83.6 us (level)
  no operation moved by 1% of the time
where the time goes in v15:
time: 83.6 us; the launch traced here: 82.9 us
  starting transfers between devices  36.6 us (44%)
  Pallas kernels  33.4 us (40%)
  waiting for transfers between devices  12.1 us (14%)
    pallas_call x9, Pallas kernels, call(): pl.pallas_call(whole, out_shape=[pltpu.HBM(o.shape, o.dtype) for o in out...  33.4 us
    all_to_all x2, starting transfers between devices, body(): restricted = spread(message)  13.6 us
    all_to_all x2, starting transfers between devices, body(): coarse = spread(message)  9.55 us
    ppermute x2, starting transfers between devices, body(): second_got = lax.ppermute(second_pair, 'sub', second_pairs)  8.32 us
    ppermute x2, waiting for transfers between devices, body(): second_got = lax.ppermute(second_pair, 'sub', second_pairs)  4.71 us
    all_to_all x2, waiting for transfers between devices, body(): restricted = spread(message)  4.46 us
    ppermute x2, starting transfers between devices, body(): first_got = lax.ppermute(first_pair, 'sub', first_pairs)  3.86 us
    ppermute x5, waiting for transfers between devices, pieces_of(): lax.ppermute(block, GROUP, [((g + k) % group, g) for g in range(group)])  2.95 us
  transfers between devices with their start and end apart: 14, of which 6 were waited for; matrix products, arithmetic and copies ran while one was open for 0% of the time, Pallas kernels for 29%

profile of v15, /device:TPU:0, one launch (start us, length us, event | category | flops | bytes accessed | tf_op | source)
XLA Modules:
  0.0 82.9 jit_solution(4541899554348376201)
XLA Ops:
  0.6 0.5 collective-permute-start.1
  1.1 0.1 collective-permute-start
  1.2 1.4 %collective-permute-done.refs_1_.refs_5_ = bf16[2,48,512]{2,1,0:T(8,128)(2,1)S(1)} collective-permute-done((bf16[2,48,512]{2,1,0:T(8,128)(2,1)}, bf16[2,48,512]{2,1,0:T(8,128)(2,1)S(1)}, u32[]{:S(2)}, u32[]{:S(2)}) %collective-permute-start) | collective-permute-done | bytes 98336 | tf_op jit(solution)/shard_map/ppermute | solution.py:463
  2.7 0.0 collective-permute-done.1.refs_1_
  2.7 0.2 collective-permute-start.2
  2.9 0.3 collective-permute-start.3
  3.2 2.3 %open.1 = bf16[16,64,128]{2,1,0:T(8,128)(2,1)} custom-call(bf16[2,48,512]{2,1,0:T(8,128)(2,1)} %bitcast.2, bf16[2,48,512]{2,1,0:T(8,128)(2,1)S(1)} %collective-permute-done.refs_1_.refs_5_, bf16[2,1024,128]{2,1,0:T(8,128)(2,1)} %refs_6_.2, s32[2,48]{1,0:T(2,128)} %refs_3_.2), custom_call_target="tpu_custom_call" | custom-call | flops 67108864 | bytes 983424 | tf_op jit(solution)/shard_map/open/pallas_call | solution.py:439
  5.5 8.1 %all-to-all-start = ((bf16[16,64,128]{2,1,0:T(8,128)(2,1)}), bf16[16,64,128]{2,1,0:T(8,128)(2,1)S(1)}, u32[]{:S(2)}, u32[]{:S(2)}) async-start(bf16[16,64,128]{2,1,0:T(8,128)(2,1)} %open.1), calls=%async_computation | async-start | bytes 524288 | tf_op jit(solution)/shard_map/all_to_all | solution.py:501
  13.6 0.0 collective-permute-done.2.refs_1_
  13.6 0.0 collective-permute-done.3.refs_3_
  13.6 6.8 %first_image.1 = (bf16[1024,128]{1,0:T(8,128)(2,1)}, f32[1024,128]{1,0:T(8,128)}, f32[1024,128]{1,0:T(8,128)}, bf16[2,128,128]{2,1,0:T(8,128)(2,1)}, bf16[2,128,...) custom-call(bf16[2,512,1024]{2,1,0:T(8,128)(2,1)} %refs_0_.2, ...), custom_call_target="tpu_custom_call" | custom-call | flops 1073741824 | bytes 11339776 | tf_op jit(solution)/shard_map/first_image/pallas_call | solution.py:439
  20.4 3.5 %all-to-all-done.refs_2_ = bf16[16,64,128]{2,1,0:T(8,128)(2,1)S(1)} async-done(((bf16[16,64,128]{2,1,0:T(8,128)(2,1)}), bf16[16,64,128]{2,1,0:T(8,128)(2,1)S(1)}, u32[]{:S(2)}, u32[]{:S(2)}) %all-to-all-start) | async-done | bytes 262176 | tf_op jit(solution)/shard_map/all_to_all | solution.py:501
  23.9 3.2 %order.1 = (bf16[2,96,768]{2,1,0:T(8,128)(2,1)}, f32[2,16,128]{2,1,0:T(8,128)}, bf16[16,48,128]{2,1,0:T(8,128)(2,1)}) custom-call(bf16[96,768]{1,0:T(8,128)(2,1)} %refs_0_.1, bf16[96,768]{1,0:T(8,128)(2,1)S(1)} %collective-permute-done.1.refs_1_, bf16[16,64,128]{2,1,0:T(8,128)(2,1)S(1)} %all-to-all-done.refs_2_, bf16[128,768]{1,0:T(8,128)(2,1)} %constant.6.clone.refs_3_, ...), custom_call_target="tpu_custom_call" | custom-call | flops 452984832 | bytes 1310720 | tf_op jit(solution)/shard_map/order/pallas_call | solution.py:439
  27.1 3.6 %all-to-all-start.1 = ((bf16[16,48,128]{2,1,0:T(8,128)(2,1)}), bf16[16,48,128]{2,1,0:T(8,128)(2,1)S(1)}, u32[]{:S(2)}, u32[]{:S(2)}) async-start(bf16[16,48,128]{2,1,0:T(8,128)(2,1)} %get-tuple-element.44), calls=%async_computation.1 | async-start | bytes 393216 | tf_op jit(solution)/shard_map/all_to_all | solution.py:533
  30.7 1.9 %collective-permute-start.4 = (bf16[128,128]{1,0:T(8,128)(2,1)}, bf16[128,128]{1,0:T(8,128)(2,1)S(1)}, u32[]{:S(2)}, u32[]{:S(2)}) collective-permute-start(bf16[128,128]{1,0:T(8,128)(2,1)} %get-tuple-element.57), channel_id=1, source_target_pairs={{0,2},{2,0},{4,6},{6,4},{8,10},{10,8},{12,14},{14,12},{16,18},{18,... | collective-permute-start | bytes 98312 | tf_op jit(solution)/shard_map/ppermute | solution.py:534
  32.6 4.2 %collective-permute-start.5 = (bf16[128,128]{1,0:T(8,128)(2,1)}, bf16[128,128]{1,0:T(8,128)(2,1)S(1)}, u32[]{:S(2)}, u32[]{:S(2)}) collective-permute-start(bf16[128,128]{1,0:T(8,128)(2,1)} %get-tuple-element.42), channel_id=1, source_target_pairs={{0,30},{2,4},{4,2},{6,8},{8,6},{10,12},{12,10},{14,16},{16,14},{18... | collective-permute-start | bytes 98312 | tf_op jit(solution)/shard_map/ppermute | solution.py:522
  36.8 3.1 %begin.1 = (bf16[2,48,128]{2,1,0:T(8,128)(2,1)}, bf16[2,48,128]{2,1,0:T(8,128)(2,1)}, bf16[2,48,48]{2,1,0:T(8,128)(2,1)}, f32[48,128]{1,0:T(8,128)}, bf16[2,192,768]{2,1,0:T(8,128)(2,1)}) custom-call(bf16[1024,128]{1,0:T(8,128)(2,1)} %get-tuple-element.45.refs_0_.refs_4_, f32[1024,128]{1,0:T(8,128)} %get-tuple-element.46.refs_1_.refs_5_, ...), custom_call_target="tpu_custom_call" | custom-call | flops 67108864 | bytes 2204672 | tf_op jit(solution)/shard_map/begin/pallas_call | solution.py:439
  39.9 0.4 collective-permute-done.5.refs_9_.refs_12_
  40.4 2.8 %update.1 = (bf16[192,128]{1,0:T(8,128)(2,1)}, bf16[16,48,128]{2,1,0:T(8,128)(2,1)}) custom-call(bf16[16,48,128]{2,1,0:T(8,128)(2,1)S(1)} %all-to-all-done.1.refs_0_, bf16[2,192,768]{2,1,0:T(8,128)(2,1)} %get-tuple-element.50.refs_1_, f32[48,128]{1,0:T(8,128)} %get-tuple-element.51.refs_2_, bf16[2,48,48]{2,1,0:T(8,128)(2,1)} %get-tuple-element.52.refs_3_, ...), custom_call_target="tpu_custom_call" | custom-call | flops 16777216 | bytes 1311744 | tf_op jit(solution)/shard_map/update/pallas_call | solution.py:439
  43.2 5.6 %all-to-all-start.2 = ((bf16[16,48,128]{2,1,0:T(8,128)(2,1)}), bf16[16,48,128]{2,1,0:T(8,128)(2,1)S(1)}, u32[]{:S(2)}, u32[]{:S(2)}) async-start(bf16[16,48,128]{2,1,0:T(8,128)(2,1)} %get-tuple-element.58), calls=%async_computation.2 | async-start | bytes 393216 | tf_op jit(solution)/shard_map/all_to_all | solution.py:554
  48.8 7.0 %second_image.1 = (bf16[2,128,128]{2,1,0:T(8,128)(2,1)}, bf16[2,128,128]{2,1,0:T(8,128)(2,1)}, bf16[128,128]{1,0:T(8,128)(2,1)}, bf16[128,128]{1,0:T(8,128)(2,1)...) custom-call(bf16[2,512,1024]{2,1,0:T(8,128)(2,1)} %refs_0_.2, ...), custom_call_target="tpu_custom_call" | custom-call | flops 1073741824 | bytes 11716608 | tf_op jit(solution)/shard_map/second_image/pallas_call | solution.py:439
  55.8 0.1 collective-permute-start.9
  55.9 1.0 %all-to-all-done.2.refs_0_ = bf16[16,48,128]{2,1,0:T(8,128)(2,1)S(1)} async-done(((bf16[16,48,128]{2,1,0:T(8,128)(2,1)}), bf16[16,48,128]{2,1,0:T(8,128)(2,1)S(1)}, u32[]{:S(2)}, u32[]{:S(2)}) %all-to-all-start.2) | async-done | bytes 196640 | tf_op jit(solution)/shard_map/all_to_all | solution.py:554
  56.8 2.2 %coarse.1 = bf16[16,48,128]{2,1,0:T(8,128)(2,1)} custom-call(bf16[16,48,128]{2,1,0:T(8,128)(2,1)S(1)} %all-to-all-done.2.refs_0_, bf16[2,96,768]{2,1,0:T(8,128)(2,1)} %get-tuple-element.63.refs_1_), custom_call_target="tpu_custom_call" | custom-call | flops 16777216 | bytes 688128 | tf_op jit(solution)/shard_map/coarse/pallas_call | solution.py:439
  59.0 6.0 %all-to-all-start.3 = ((bf16[16,48,128]{2,1,0:T(8,128)(2,1)}), bf16[16,48,128]{2,1,0:T(8,128)(2,1)S(1)}, u32[]{:S(2)}, u32[]{:S(2)}) async-start(bf16[16,48,128]{2,1,0:T(8,128)(2,1)} %coarse.1), calls=%async_computation.3 | async-start | bytes 393216 | tf_op jit(solution)/shard_map/all_to_all | solution.py:580
  65.0 1.9 %collective-permute-start.6 = (bf16[128,128]{1,0:T(8,128)(2,1)}, bf16[128,128]{1,0:T(8,128)(2,1)S(1)}, u32[]{:S(2)}, u32[]{:S(2)}) collective-permute-start(bf16[128,128]{1,0:T(8,128)(2,1)} %get-tuple-element.66), channel_id=1, source_target_pairs={{0,2},{2,0},{4,6},{6,4},{8,10},{10,8},{12,14},{14,12},{16,18},{18,... | collective-permute-start | bytes 98312 | tf_op jit(solution)/shard_map/ppermute | solution.py:581
  67.0 4.2 %collective-permute-start.7 = (bf16[128,128]{1,0:T(8,128)(2,1)}, bf16[128,128]{1,0:T(8,128)(2,1)S(1)}, u32[]{:S(2)}, u32[]{:S(2)}) collective-permute-start(bf16[128,128]{1,0:T(8,128)(2,1)} %get-tuple-element.67), channel_id=1, source_target_pairs={{0,30},{2,4},{4,2},{6,8},{8,6},{10,12},{12,10},{14,16},{16,14},{18... | collective-permute-start | bytes 98312 | tf_op jit(solution)/shard_map/ppermute | solution.py:570
  71.1 4.3 %collective-permute-done.7.refs_5_ = bf16[128,128]{1,0:T(8,128)(2,1)S(1)} collective-permute-done((bf16[128,128]{1,0:T(8,128)(2,1)}, bf16[128,128]{1,0:T(8,128)(2,1)S(1)}, u32[]{:S(2)}, u32[]{:S(2)}) %collective-permute-start.7) | collective-permute-done | bytes 32800 | tf_op jit(solution)/shard_map/ppermute | solution.py:570
  75.4 2.6 %pick.1.refs_0_ = bf16[448,128]{1,0:T(8,128)(2,1)} custom-call(bf16[16,48,128]{2,1,0:T(8,128)(2,1)S(1)} %all-to-all-done.3.refs_0_, bf16[2,192,768]{2,1,0:T(8,128)(2,1)} %get-tuple-element.50.refs_1_, bf16[2,128,128]{2,1,0:T(8,128)(2,1)} %get-tuple-element.64.refs_2_, bf16[2,128,128]{2,1,0:T(8,128)(2,1)} %get-tuple-element.65.refs_3_, ...), custom_call_target="tpu_custom_call" | custom-call | flops 16777216 | bytes 1294336 | tf_op jit(solution)/shard_map/pick/pallas_call | solution.py:439
  78.1 0.1 collective-permute-start.8
  78.1 1.5 %collective-permute-done.8.refs_1_ = bf16[448,128]{1,0:T(8,128)(2,1)S(1)} collective-permute-done((bf16[448,128]{1,0:T(8,128)(2,1)}, bf16[448,128]{1,0:T(8,128)(2,1)S(1)}, u32[]{:S(2)}, u32[]{:S(2)}) %collective-permute-start.8) | collective-permute-done | bytes 114720 | tf_op jit(solution)/shard_map/ppermute | solution.py:463
  79.7 3.3 %last.1 = (f32[2,512,128]{2,1,0:T(8,128)}, f32[2,512,128]{2,1,0:T(8,128)}) custom-call(bf16[448,128]{1,0:T(8,128)(2,1)} %pick.1.refs_0_, bf16[448,128]{1,0:T(8,128)(2,1)S(1)} %collective-permute-done.8.refs_1_, f32[2,512,128]{2,1,0:T(8,128)} %get-tuple-element.68.refs_2_, f32[2,512,128]{2,1,0:T(8,128)S(1)} %collective-permute-done.9.refs_3_, ...), custom_call_target="tpu_custom_call" | custom-call | flops 134217728 | bytes 2852864 | tf_op jit(solution)/shard_map/last/pallas_call | solution.py:439
  (5 shorter events, 0.0 us)
Async XLA Ops:
  0.6 2.0 %collective-permute-start.1 = (bf16[96,768]{1,0:T(8,128)(2,1)}, bf16[96,768]{1,0:T(8,128)(2,1)S(1)}, u32[]{:S(2)}, u32[]{:S(2)}) collective-permute-start(bf16[96,768]{1,0:T(8,128)(2,1)} %refs_0_.1), channel_id=1, source_target_pairs={{1,0},{0,1},{3,2},{2,3},{5,4},{4,5},{7,6},{6,7},{9,8},{8,9},{11,10... | collective-permute-start | bytes 442376 | tf_op jit(solution)/shard_map/ppermute | solution.py:463
  1.1 1.5 %collective-permute-start = (bf16[2,48,512]{2,1,0:T(8,128)(2,1)}, bf16[2,48,512]{2,1,0:T(8,128)(2,1)S(1)}, u32[]{:S(2)}, u32[]{:S(2)}) collective-permute-start(bf16[2,48,512]{2,1,0:T(8,128)(2,1)} %bitcast.1), channel_id=1, source_target_pairs={{1,0},{0,1},{3,2},{2,3},{5,4},{4,5},{7,6},{6,7},{9,8},{8,9},{11,10... | collective-permute-start | bytes 294920 | tf_op jit(solution)/shard_map/ppermute | solution.py:463
  2.7 10.9 %collective-permute-start.2 = (bf16[2,512,1024]{2,1,0:T(8,128)(2,1)}, bf16[2,512,1024]{2,1,0:T(8,128)(2,1)S(1)}, u32[]{:S(2)}, u32[]{:S(2)}) collective-permute-start(bf16[2,512,1024]{2,1,0:T(8,128)(2,1)} %refs_0_.2), channel_id=1, source_target_pairs={{1,0},{0,1},{3,2},{2,3},{5,4},{4,5},{7,6},{6,7},{9,8},{8,9},{11,10... | collective-permute-start | bytes 6291464 | tf_op jit(solution)/shard_map/ppermute | solution.py:463
  2.9 10.7 %collective-permute-start.3 = (bf16[2,512,1024]{2,1,0:T(8,128)(2,1)}, bf16[2,512,1024]{2,1,0:T(8,128)(2,1)}, u32[]{:S(2)}, u32[]{:S(2)}) collective-permute-start(bf16[2,512,1024]{2,1,0:T(8,128)(2,1)} %refs_2_.3), channel_id=1, source_target_pairs={{1,0},{0,1},{3,2},{2,3},{5,4},{4,5},{7,6},{6,7},{9,8},{8,9},{11,10... | collective-permute-start | bytes 6291464 | tf_op jit(solution)/shard_map/ppermute | solution.py:463
  5.5 18.4 %all-to-all-start = ((bf16[16,64,128]{2,1,0:T(8,128)(2,1)}), bf16[16,64,128]{2,1,0:T(8,128)(2,1)S(1)}, u32[]{:S(2)}, u32[]{:S(2)}) async-start(bf16[16,64,128]{2,1,0:T(8,128)(2,1)} %open.1), calls=%async_computation | async-start | bytes 524288 | tf_op jit(solution)/shard_map/all_to_all | solution.py:501
  27.1 13.2 %all-to-all-start.1 = ((bf16[16,48,128]{2,1,0:T(8,128)(2,1)}), bf16[16,48,128]{2,1,0:T(8,128)(2,1)S(1)}, u32[]{:S(2)}, u32[]{:S(2)}) async-start(bf16[16,48,128]{2,1,0:T(8,128)(2,1)} %get-tuple-element.44), calls=%async_computation.1 | async-start | bytes 393216 | tf_op jit(solution)/shard_map/all_to_all | solution.py:533
  30.7 9.2 %collective-permute-start.4 = (bf16[128,128]{1,0:T(8,128)(2,1)}, bf16[128,128]{1,0:T(8,128)(2,1)S(1)}, u32[]{:S(2)}, u32[]{:S(2)}) collective-permute-start(bf16[128,128]{1,0:T(8,128)(2,1)} %get-tuple-element.57), channel_id=1, source_target_pairs={{0,2},{2,0},{4,6},{6,4},{8,10},{10,8},{12,14},{14,12},{16,18},{18,... | collective-permute-start | bytes 98312 | tf_op jit(solution)/shard_map/ppermute | solution.py:534
  32.6 7.7 %collective-permute-start.5 = (bf16[128,128]{1,0:T(8,128)(2,1)}, bf16[128,128]{1,0:T(8,128)(2,1)S(1)}, u32[]{:S(2)}, u32[]{:S(2)}) collective-permute-start(bf16[128,128]{1,0:T(8,128)(2,1)} %get-tuple-element.42), channel_id=1, source_target_pairs={{0,30},{2,4},{4,2},{6,8},{8,6},{10,12},{12,10},{14,16},{16,14},{18... | collective-permute-start | bytes 98312 | tf_op jit(solution)/shard_map/ppermute | solution.py:522
  43.2 13.6 %all-to-all-start.2 = ((bf16[16,48,128]{2,1,0:T(8,128)(2,1)}), bf16[16,48,128]{2,1,0:T(8,128)(2,1)S(1)}, u32[]{:S(2)}, u32[]{:S(2)}) async-start(bf16[16,48,128]{2,1,0:T(8,128)(2,1)} %get-tuple-element.58), calls=%async_computation.2 | async-start | bytes 393216 | tf_op jit(solution)/shard_map/all_to_all | solution.py:554
  55.8 22.3 %collective-permute-start.9 = (f32[2,512,128]{2,1,0:T(8,128)}, f32[2,512,128]{2,1,0:T(8,128)S(1)}, u32[]{:S(2)}, u32[]{:S(2)}) collective-permute-start(f32[2,512,128]{2,1,0:T(8,128)} %get-tuple-element.69), channel_id=1, source_target_pairs={{0,1},{1,0},{2,3},{3,2},{4,5},{5,4},{6,7},{7,6},{8,9},{9,8},{10,11... | collective-permute-start | bytes 1572872 | tf_op jit(solution)/shard_map/ppermute | solution.py:584
  59.0 16.4 %all-to-all-start.3 = ((bf16[16,48,128]{2,1,0:T(8,128)(2,1)}), bf16[16,48,128]{2,1,0:T(8,128)(2,1)S(1)}, u32[]{:S(2)}, u32[]{:S(2)}) async-start(bf16[16,48,128]{2,1,0:T(8,128)(2,1)} %coarse.1), calls=%async_computation.3 | async-start | bytes 393216 | tf_op jit(solution)/shard_map/all_to_all | solution.py:580
  65.0 6.1 %collective-permute-start.6 = (bf16[128,128]{1,0:T(8,128)(2,1)}, bf16[128,128]{1,0:T(8,128)(2,1)S(1)}, u32[]{:S(2)}, u32[]{:S(2)}) collective-permute-start(bf16[128,128]{1,0:T(8,128)(2,1)} %get-tuple-element.66), channel_id=1, source_target_pairs={{0,2},{2,0},{4,6},{6,4},{8,10},{10,8},{12,14},{14,12},{16,18},{18,... | collective-permute-start | bytes 98312 | tf_op jit(solution)/shard_map/ppermute | solution.py:581
  67.0 8.5 %collective-permute-start.7 = (bf16[128,128]{1,0:T(8,128)(2,1)}, bf16[128,128]{1,0:T(8,128)(2,1)S(1)}, u32[]{:S(2)}, u32[]{:S(2)}) collective-permute-start(bf16[128,128]{1,0:T(8,128)(2,1)} %get-tuple-element.67), channel_id=1, source_target_pairs={{0,30},{2,4},{4,2},{6,8},{8,6},{10,12},{12,10},{14,16},{16,14},{18... | collective-permute-start | bytes 98312 | tf_op jit(solution)/shard_map/ppermute | solution.py:570
  78.1 1.6 %collective-permute-start.8 = (bf16[448,128]{1,0:T(8,128)(2,1)}, bf16[448,128]{1,0:T(8,128)(2,1)S(1)}, u32[]{:S(2)}, u32[]{:S(2)}) collective-permute-start(bf16[448,128]{1,0:T(8,128)(2,1)} %pick.1.refs_0_), channel_id=1, source_target_pairs={{1,0},{0,1},{3,2},{2,3},{5,4},{4,5},{7,6},{6,7},{9,8},{8,9},{11,10... | collective-permute-start | bytes 344072 | tf_op jit(solution)/shard_map/ppermute | solution.py:463

commit v16 on v15

--- a/solution.py
+++ b/solution.py
@@ -377,36 +377,42 @@
     out[near + z.face :] = select(z, rights).astype(BF16)
 
 
+def base_kernel(z, *refs):
+    *values, out = refs
+    for at in range(2):
+        for s in range(z.subs):
+            total = jnp.zeros((z.own, z.lanes), F32)
+            for k, value in enumerate(values):
+                place = lax.rem(lax.axis_index(GROUP) + k, z.group)
+                turn = lax.rem((place - s + z.subs * z.group) * z.width, z.lanes)
+                turned = pltpu.roll(value[at], turn, 1)
+                total = jnp.where(lane_mask(z, place, turned.shape), turned, total)
+            out[at, s] = total
+
+
 def last_kernel(z, *refs):
-    chosen, values = refs[: z.group], refs[z.group : 2 * z.group]
-    tall, left_rows, right_rows, second_pass, final_residual = refs[2 * z.group :]
+    chosen = refs[: z.group]
+    base, tall, left_rows, right_rows, second_pass, final_residual = refs[z.group :]
     start = piece_start(z, 0, z.own)
     near = (z.subs + 2) * z.modes
-    lefts, rights = [], []
-    for s in range(z.subs):
+
+    def all_cases(rows, source):
+        total = jnp.zeros((rows.stop - rows.start, z.lanes), F32)
+        for k, piece in enumerate(chosen):
+            place = lax.rem(lax.axis_index(GROUP) + k, z.group)
+            total = total + dot(piece[rows, :], lane_matrix(z, source, place * z.width))
+        return total.astype(BF16)
+
+    modes = all_cases(slice(0, near), 0)
+    for s in range(z.subs):
+        left = all_cases(slice(near, near + z.face), s * z.width)
+        right = all_cases(slice(near + z.face, near + 2 * z.face), s * z.width)
         scatter = scatter_matrix(z, left_rows[s : s + 1, :], start, z.own)
-        lefts.append(jnp.concatenate([tall[s, pl.ds(start, z.own), :], scatter], axis=1))
-        rights.append(scatter_matrix(z, right_rows[s : s + 1, :], start, z.own))
-    done = [jnp.zeros((z.own, z.lanes), F32) for _ in range(2 * z.subs)]
-    for k in range(z.group):
-        rows = chosen[k][:near]
-        left, right = chosen[k][near : near + z.face], chosen[k][near + z.face :]
-        steps, images = [], []
-        for s in range(z.subs):
-            total = dot(lefts[s], correction_side(z, rows, s, left))
-            steps.append(total[:, z.lanes :])
-            images.append(total[:, : z.lanes] + dot(rights[s], right))
-        pair = values[k][0] + select(z, steps), values[k][1] - select(z, images)
-        place = lax.rem(lax.axis_index(GROUP) + k, z.group)
-        for at, packed in enumerate(pair):
-            for s in range(z.subs):
-                turn = lax.rem((place - s + z.subs * z.group) * z.width, z.lanes)
-                turned = pltpu.roll(packed, turn, 1)
-                here = at * z.subs + s
-                done[here] = jnp.where(lane_mask(z, place, turned.shape), turned, done[here])
-    for s in range(z.subs):
-        second_pass[s] = done[s][:, : z.cases]
-        final_residual[s] = done[z.subs + s][:, : z.cases]
+        wide = jnp.concatenate([tall[s, pl.ds(start, z.own), :], scatter], axis=1)
+        total = dot(wide, correction_side(z, modes, s, left))
+        image = total[:, : z.lanes] + dot(scatter_matrix(z, right_rows[s : s + 1, :], start, z.own), right)
+        second_pass[s] = (base[0, s] + total[:, z.lanes :])[:, : z.cases]
+        final_residual[s] = (base[1, s] - image)[:, : z.cases]
 
 
 def call(kernel, outs, operands, flops, scratch=(), late=(), loose=(), name=None):
@@ -583,6 +589,15 @@
     for k in range(1, group):
         swapped.append(lax.ppermute(values[k], GROUP, [(g, (g + k) % group) for g in range(group)]))
     swapped = [swapped[(group - k) % group] for k in range(group)]
+    (base,) = call(
+        functools.partial(base_kernel, z),
+        [shape((2, subs, z.own, lanes), F32)],
+        swapped,
+        work // 64,
+        loose=range(1, group),
+        name="base",
+    )
+    coarse, base = lax.optimization_barrier((coarse, base))
     (chosen,) = call(
         functools.partial(pick_kernel, z),
         [shape((near + 2 * face, lanes), BF16)],
@@ -596,9 +611,9 @@
         call(
             functools.partial(last_kernel, z),
             [out, out],
-            [*pieces_of(chosen, group), *swapped, tall, left_rows, right_rows],
+            [*pieces_of(chosen, group), base, tall, left_rows, right_rows],
             work // 8,
-            loose=[*range(1, group), *range(group + 1, 2 * group)],
+            loose=range(1, group),
             name="last",
         )
     )

time: 83.6 us -> 83.6 us (level)
  Pallas kernels: 33.4 us -> 36.1 us
  waiting for transfers between devices: 12.1 us -> 9.45 us
    ppermute x2, waiting for transfers between devices: 4.71 us -> 1.88 us  [body(): second_got = lax.ppermute(second_pair, 'sub', second_pairs)]
    pallas_call x9 -> x10, Pallas kernels: 33.4 us -> 36.1 us  [call(): pl.pallas_call(whole, out_shape=[pltpu.HBM(o.shape, o.dtype) for o in out...]
  transfers between devices with their start and end apart: 14 -> 14, of which waited for: 6 -> 7; matrix products, arithmetic and copies ran while one was open for 0% -> 0% of each run, Pallas kernels for 29% -> 29%
where the time goes in v16:
time: 83.6 us; the launch traced here: 82.9 us
  starting transfers between devices  36.6 us (44%)
  Pallas kernels  36.1 us (43%)
  waiting for transfers between devices  9.45 us (11%)
    pallas_call x10, Pallas kernels, call(): pl.pallas_call(whole, out_shape=[pltpu.HBM(o.shape, o.dtype) for o in out...  36.1 us
    all_to_all x2, starting transfers between devices, body(): restricted = spread(message)  13.6 us
    all_to_all x2, starting transfers between devices, body(): coarse = spread(message)  9.55 us
    ppermute x2, starting transfers between devices, body(): second_got = lax.ppermute(second_pair, 'sub', second_pairs)  8.32 us
    all_to_all x2, waiting for transfers between devices, body(): restricted = spread(message)  4.46 us
    ppermute x2, starting transfers between devices, body(): first_got = lax.ppermute(first_pair, 'sub', first_pairs)  3.86 us
    ppermute x5, waiting for transfers between devices, pieces_of(): lax.ppermute(block, GROUP, [((g + k) % group, g) for g in range(group)])  2.96 us
    ppermute x2, waiting for transfers between devices, body(): second_got = lax.ppermute(second_pair, 'sub', second_pairs)  1.88 us
  transfers between devices with their start and end apart: 14, of which 7 were waited for; matrix products, arithmetic and copies ran while one was open for 0% of the time, Pallas kernels for 29%

profile of v16, /device:TPU:0, one launch (start us, length us, event | category | flops | bytes accessed | tf_op | source)
XLA Modules:
  0.0 82.9 jit_solution(9437440001855619162)
XLA Ops:
  0.6 0.5 collective-permute-start.1
  1.1 0.1 collective-permute-start
  1.2 1.4 %collective-permute-done.refs_1_.refs_5_ = bf16[2,48,512]{2,1,0:T(8,128)(2,1)S(1)} collective-permute-done((bf16[2,48,512]{2,1,0:T(8,128)(2,1)}, bf16[2,48,512]{2,1,0:T(8,128)(2,1)S(1)}, u32[]{:S(2)}, u32[]{:S(2)}) %collective-permute-start) | collective-permute-done | bytes 98336 | tf_op jit(solution)/shard_map/ppermute | solution.py:469
  2.7 0.0 collective-permute-done.1.refs_1_
  2.7 0.2 collective-permute-start.2
  2.9 0.3 collective-permute-start.3
  3.2 2.3 %open.1 = bf16[16,64,128]{2,1,0:T(8,128)(2,1)} custom-call(bf16[2,48,512]{2,1,0:T(8,128)(2,1)} %bitcast.2, bf16[2,48,512]{2,1,0:T(8,128)(2,1)S(1)} %collective-permute-done.refs_1_.refs_5_, bf16[2,1024,128]{2,1,0:T(8,128)(2,1)} %refs_6_.1, s32[2,48]{1,0:T(2,128)} %refs_3_.2), custom_call_target="tpu_custom_call" | custom-call | flops 67108864 | bytes 983424 | tf_op jit(solution)/shard_map/open/pallas_call | solution.py:445
  5.5 8.1 %all-to-all-start = ((bf16[16,64,128]{2,1,0:T(8,128)(2,1)}), bf16[16,64,128]{2,1,0:T(8,128)(2,1)S(1)}, u32[]{:S(2)}, u32[]{:S(2)}) async-start(bf16[16,64,128]{2,1,0:T(8,128)(2,1)} %open.1), calls=%async_computation | async-start | bytes 524288 | tf_op jit(solution)/shard_map/all_to_all | solution.py:507
  13.6 6.8 %first_image.1 = (bf16[1024,128]{1,0:T(8,128)(2,1)}, f32[1024,128]{1,0:T(8,128)}, f32[1024,128]{1,0:T(8,128)}, bf16[2,128,128]{2,1,0:T(8,128)(2,1)}, bf16[2,128,...) custom-call(bf16[2,512,1024]{2,1,0:T(8,128)(2,1)} %refs_0_.2, ...), custom_call_target="tpu_custom_call" | custom-call | flops 1073741824 | bytes 11339776 | tf_op jit(solution)/shard_map/first_image/pallas_call | solution.py:445
  20.4 3.5 %all-to-all-done.refs_2_ = bf16[16,64,128]{2,1,0:T(8,128)(2,1)S(1)} async-done(((bf16[16,64,128]{2,1,0:T(8,128)(2,1)}), bf16[16,64,128]{2,1,0:T(8,128)(2,1)S(1)}, u32[]{:S(2)}, u32[]{:S(2)}) %all-to-all-start) | async-done | bytes 262176 | tf_op jit(solution)/shard_map/all_to_all | solution.py:507
  23.9 3.2 %order.1 = (bf16[2,96,768]{2,1,0:T(8,128)(2,1)}, f32[2,16,128]{2,1,0:T(8,128)}, bf16[16,48,128]{2,1,0:T(8,128)(2,1)}) custom-call(bf16[96,768]{1,0:T(8,128)(2,1)} %refs_0_.1, bf16[96,768]{1,0:T(8,128)(2,1)S(1)} %collective-permute-done.1.refs_1_, bf16[16,64,128]{2,1,0:T(8,128)(2,1)S(1)} %all-to-all-done.refs_2_, bf16[128,768]{1,0:T(8,128)(2,1)} %constant.6.clone.refs_3_, ...), custom_call_target="tpu_custom_call" | custom-call | flops 452984832 | bytes 1310720 | tf_op jit(solution)/shard_map/order/pallas_call | solution.py:445
  27.1 3.6 %all-to-all-start.1 = ((bf16[16,48,128]{2,1,0:T(8,128)(2,1)}), bf16[16,48,128]{2,1,0:T(8,128)(2,1)S(1)}, u32[]{:S(2)}, u32[]{:S(2)}) async-start(bf16[16,48,128]{2,1,0:T(8,128)(2,1)} %get-tuple-element.46), calls=%async_computation.1 | async-start | bytes 393216 | tf_op jit(solution)/shard_map/all_to_all | solution.py:539
  30.7 1.9 %collective-permute-start.4 = (bf16[128,128]{1,0:T(8,128)(2,1)}, bf16[128,128]{1,0:T(8,128)(2,1)S(1)}, u32[]{:S(2)}, u32[]{:S(2)}) collective-permute-start(bf16[128,128]{1,0:T(8,128)(2,1)} %get-tuple-element.59), channel_id=1, source_target_pairs={{0,2},{2,0},{4,6},{6,4},{8,10},{10,8},{12,14},{14,12},{16,18},{18,... | collective-permute-start | bytes 98312 | tf_op jit(solution)/shard_map/ppermute | solution.py:540
  32.6 4.2 %collective-permute-start.5 = (bf16[128,128]{1,0:T(8,128)(2,1)}, bf16[128,128]{1,0:T(8,128)(2,1)S(1)}, u32[]{:S(2)}, u32[]{:S(2)}) collective-permute-start(bf16[128,128]{1,0:T(8,128)(2,1)} %get-tuple-element.44), channel_id=1, source_target_pairs={{0,30},{2,4},{4,2},{6,8},{8,6},{10,12},{12,10},{14,16},{16,14},{18... | collective-permute-start | bytes 98312 | tf_op jit(solution)/shard_map/ppermute | solution.py:528
  36.8 3.1 %begin.1 = (bf16[2,48,128]{2,1,0:T(8,128)(2,1)}, bf16[2,48,128]{2,1,0:T(8,128)(2,1)}, bf16[2,48,48]{2,1,0:T(8,128)(2,1)}, f32[48,128]{1,0:T(8,128)}, bf16[2,192,768]{2,1,0:T(8,128)(2,1)}) custom-call(bf16[1024,128]{1,0:T(8,128)(2,1)} %get-tuple-element.47.refs_0_.refs_4_, f32[1024,128]{1,0:T(8,128)} %get-tuple-element.48.refs_1_.refs_5_, ...), custom_call_target="tpu_custom_call" | custom-call | flops 67108864 | bytes 2204672 | tf_op jit(solution)/shard_map/begin/pallas_call | solution.py:445
  39.9 0.4 collective-permute-done.5.refs_9_.refs_12_
  40.4 2.8 %update.1 = (bf16[192,128]{1,0:T(8,128)(2,1)}, bf16[16,48,128]{2,1,0:T(8,128)(2,1)}) custom-call(bf16[16,48,128]{2,1,0:T(8,128)(2,1)S(1)} %all-to-all-done.1.refs_0_, bf16[2,192,768]{2,1,0:T(8,128)(2,1)} %get-tuple-element.52.refs_1_, f32[48,128]{1,0:T(8,128)} %get-tuple-element.53.refs_2_, bf16[2,48,48]{2,1,0:T(8,128)(2,1)} %get-tuple-element.54.refs_3_, ...), custom_call_target="tpu_custom_call" | custom-call | flops 16777216 | bytes 1311744 | tf_op jit(solution)/shard_map/update/pallas_call | solution.py:445
  43.2 5.6 %all-to-all-start.2 = ((bf16[16,48,128]{2,1,0:T(8,128)(2,1)}), bf16[16,48,128]{2,1,0:T(8,128)(2,1)S(1)}, u32[]{:S(2)}, u32[]{:S(2)}) async-start(bf16[16,48,128]{2,1,0:T(8,128)(2,1)} %get-tuple-element.60), calls=%async_computation.2 | async-start | bytes 393216 | tf_op jit(solution)/shard_map/all_to_all | solution.py:560
  48.8 7.0 %second_image.1 = (bf16[2,128,128]{2,1,0:T(8,128)(2,1)}, bf16[2,128,128]{2,1,0:T(8,128)(2,1)}, bf16[128,128]{1,0:T(8,128)(2,1)}, bf16[128,128]{1,0:T(8,128)(2,1)...) custom-call(bf16[2,512,1024]{2,1,0:T(8,128)(2,1)} %refs_0_.2, ...), custom_call_target="tpu_custom_call" | custom-call | flops 1073741824 | bytes 11716608 | tf_op jit(solution)/shard_map/second_image/pallas_call | solution.py:445
  55.8 0.1 collective-permute-start.6
  55.9 1.0 %all-to-all-done.2.refs_0_ = bf16[16,48,128]{2,1,0:T(8,128)(2,1)S(1)} async-done(((bf16[16,48,128]{2,1,0:T(8,128)(2,1)}), bf16[16,48,128]{2,1,0:T(8,128)(2,1)S(1)}, u32[]{:S(2)}, u32[]{:S(2)}) %all-to-all-start.2) | async-done | bytes 196640 | tf_op jit(solution)/shard_map/all_to_all | solution.py:560
  56.8 2.2 %coarse.1 = bf16[16,48,128]{2,1,0:T(8,128)(2,1)} custom-call(bf16[16,48,128]{2,1,0:T(8,128)(2,1)S(1)} %all-to-all-done.2.refs_0_, bf16[2,96,768]{2,1,0:T(8,128)(2,1)} %get-tuple-element.65.refs_1_), custom_call_target="tpu_custom_call" | custom-call | flops 16777216 | bytes 688128 | tf_op jit(solution)/shard_map/coarse/pallas_call | solution.py:445
  59.0 6.0 %all-to-all-start.3 = ((bf16[16,48,128]{2,1,0:T(8,128)(2,1)}), bf16[16,48,128]{2,1,0:T(8,128)(2,1)S(1)}, u32[]{:S(2)}, u32[]{:S(2)}) async-start(bf16[16,48,128]{2,1,0:T(8,128)(2,1)} %coarse.1), calls=%async_computation.3 | async-start | bytes 393216 | tf_op jit(solution)/shard_map/all_to_all | solution.py:586
  65.0 1.9 %collective-permute-start.7 = (bf16[128,128]{1,0:T(8,128)(2,1)}, bf16[128,128]{1,0:T(8,128)(2,1)S(1)}, u32[]{:S(2)}, u32[]{:S(2)}) collective-permute-start(bf16[128,128]{1,0:T(8,128)(2,1)} %get-tuple-element.71), channel_id=1, source_target_pairs={{0,2},{2,0},{4,6},{6,4},{8,10},{10,8},{12,14},{14,12},{16,18},{18,... | collective-permute-start | bytes 98312 | tf_op jit(solution)/shard_map/ppermute | solution.py:587
  67.0 4.2 %collective-permute-start.8 = (bf16[128,128]{1,0:T(8,128)(2,1)}, bf16[128,128]{1,0:T(8,128)(2,1)S(1)}, u32[]{:S(2)}, u32[]{:S(2)}) collective-permute-start(bf16[128,128]{1,0:T(8,128)(2,1)} %get-tuple-element.72), channel_id=1, source_target_pairs={{0,30},{2,4},{4,2},{6,8},{8,6},{10,12},{12,10},{14,16},{16,14},{18... | collective-permute-start | bytes 98312 | tf_op jit(solution)/shard_map/ppermute | solution.py:576
  71.1 2.7 %base.1.refs_2_ = f32[2,2,512,128]{3,2,1,0:T(8,128)} custom-call(f32[2,512,128]{2,1,0:T(8,128)} %get-tuple-element.66.refs_0_, f32[2,512,128]{2,1,0:T(8,128)S(1)} %collective-permute-done.6.refs_1_), custom_call_target="tpu_custom_call" | custom-call | flops 16777216 | bytes 2097152 | tf_op jit(solution)/shard_map/base/pallas_call | solution.py:445
  73.8 0.1 all-to-all-done.3.refs_0_
  74.0 1.5 %collective-permute-done.8.refs_5_ = bf16[128,128]{1,0:T(8,128)(2,1)S(1)} collective-permute-done((bf16[128,128]{1,0:T(8,128)(2,1)}, bf16[128,128]{1,0:T(8,128)(2,1)S(1)}, u32[]{:S(2)}, u32[]{:S(2)}) %collective-permute-start.8) | collective-permute-done | bytes 32800 | tf_op jit(solution)/shard_map/ppermute | solution.py:576
  75.4 2.6 %pick.1.refs_0_ = bf16[448,128]{1,0:T(8,128)(2,1)} custom-call(bf16[16,48,128]{2,1,0:T(8,128)(2,1)S(1)} %all-to-all-done.3.refs_0_, bf16[2,192,768]{2,1,0:T(8,128)(2,1)} %get-tuple-element.52.refs_1_, bf16[2,128,128]{2,1,0:T(8,128)(2,1)} %get-tuple-element.69.refs_2_, bf16[2,128,128]{2,1,0:T(8,128)(2,1)} %get-tuple-element.70.refs_3_, ...), custom_call_target="tpu_custom_call" | custom-call | flops 16777216 | bytes 1294336 | tf_op jit(solution)/shard_map/pick/pallas_call | solution.py:445
  78.1 0.1 collective-permute-start.9
  78.1 1.5 %collective-permute-done.9.refs_1_ = bf16[448,128]{1,0:T(8,128)(2,1)S(1)} collective-permute-done((bf16[448,128]{1,0:T(8,128)(2,1)}, bf16[448,128]{1,0:T(8,128)(2,1)S(1)}, u32[]{:S(2)}, u32[]{:S(2)}) %collective-permute-start.9) | collective-permute-done | bytes 114720 | tf_op jit(solution)/shard_map/ppermute | solution.py:469
  79.7 3.3 %last.1 = (f32[2,512,128]{2,1,0:T(8,128)}, f32[2,512,128]{2,1,0:T(8,128)}) custom-call(bf16[448,128]{1,0:T(8,128)(2,1)} %pick.1.refs_0_, bf16[448,128]{1,0:T(8,128)(2,1)S(1)} %collective-permute-done.9.refs_1_, f32[2,2,512,128]{3,2,1,0:T(8,128)} %base.1.refs_2_, bf16[2,1024,128]{2,1,0:T(8,128)(2,1)} %get-tuple-element.49.refs_2_.refs_6_.refs_3_, ...), custom_call_target="tpu_custom_call" | custom-call | flops 134217728 | bytes 2852864 | tf_op jit(solution)/shard_map/last/pallas_call | solution.py:445
  (6 shorter events, 0.0 us)
Async XLA Ops:
  0.6 2.0 %collective-permute-start.1 = (bf16[96,768]{1,0:T(8,128)(2,1)}, bf16[96,768]{1,0:T(8,128)(2,1)S(1)}, u32[]{:S(2)}, u32[]{:S(2)}) collective-permute-start(bf16[96,768]{1,0:T(8,128)(2,1)} %refs_0_.1), channel_id=1, source_target_pairs={{1,0},{0,1},{3,2},{2,3},{5,4},{4,5},{7,6},{6,7},{9,8},{8,9},{11,10... | collective-permute-start | bytes 442376 | tf_op jit(solution)/shard_map/ppermute | solution.py:469
  1.1 1.5 %collective-permute-start = (bf16[2,48,512]{2,1,0:T(8,128)(2,1)}, bf16[2,48,512]{2,1,0:T(8,128)(2,1)S(1)}, u32[]{:S(2)}, u32[]{:S(2)}) collective-permute-start(bf16[2,48,512]{2,1,0:T(8,128)(2,1)} %bitcast.1), channel_id=1, source_target_pairs={{1,0},{0,1},{3,2},{2,3},{5,4},{4,5},{7,6},{6,7},{9,8},{8,9},{11,10... | collective-permute-start | bytes 294920 | tf_op jit(solution)/shard_map/ppermute | solution.py:469
  2.7 10.9 %collective-permute-start.2 = (bf16[2,512,1024]{2,1,0:T(8,128)(2,1)}, bf16[2,512,1024]{2,1,0:T(8,128)(2,1)S(1)}, u32[]{:S(2)}, u32[]{:S(2)}) collective-permute-start(bf16[2,512,1024]{2,1,0:T(8,128)(2,1)} %refs_0_.2), channel_id=1, source_target_pairs={{1,0},{0,1},{3,2},{2,3},{5,4},{4,5},{7,6},{6,7},{9,8},{8,9},{11,10... | collective-permute-start | bytes 6291464 | tf_op jit(solution)/shard_map/ppermute | solution.py:469
  2.9 10.7 %collective-permute-start.3 = (bf16[2,512,1024]{2,1,0:T(8,128)(2,1)}, bf16[2,512,1024]{2,1,0:T(8,128)(2,1)}, u32[]{:S(2)}, u32[]{:S(2)}) collective-permute-start(bf16[2,512,1024]{2,1,0:T(8,128)(2,1)} %refs_2_.3), channel_id=1, source_target_pairs={{1,0},{0,1},{3,2},{2,3},{5,4},{4,5},{7,6},{6,7},{9,8},{8,9},{11,10... | collective-permute-start | bytes 6291464 | tf_op jit(solution)/shard_map/ppermute | solution.py:469
  5.5 18.4 %all-to-all-start = ((bf16[16,64,128]{2,1,0:T(8,128)(2,1)}), bf16[16,64,128]{2,1,0:T(8,128)(2,1)S(1)}, u32[]{:S(2)}, u32[]{:S(2)}) async-start(bf16[16,64,128]{2,1,0:T(8,128)(2,1)} %open.1), calls=%async_computation | async-start | bytes 524288 | tf_op jit(solution)/shard_map/all_to_all | solution.py:507
  27.1 13.2 %all-to-all-start.1 = ((bf16[16,48,128]{2,1,0:T(8,128)(2,1)}), bf16[16,48,128]{2,1,0:T(8,128)(2,1)S(1)}, u32[]{:S(2)}, u32[]{:S(2)}) async-start(bf16[16,48,128]{2,1,0:T(8,128)(2,1)} %get-tuple-element.46), calls=%async_computation.1 | async-start | bytes 393216 | tf_op jit(solution)/shard_map/all_to_all | solution.py:539
  30.7 9.2 %collective-permute-start.4 = (bf16[128,128]{1,0:T(8,128)(2,1)}, bf16[128,128]{1,0:T(8,128)(2,1)S(1)}, u32[]{:S(2)}, u32[]{:S(2)}) collective-permute-start(bf16[128,128]{1,0:T(8,128)(2,1)} %get-tuple-element.59), channel_id=1, source_target_pairs={{0,2},{2,0},{4,6},{6,4},{8,10},{10,8},{12,14},{14,12},{16,18},{18,... | collective-permute-start | bytes 98312 | tf_op jit(solution)/shard_map/ppermute | solution.py:540
  32.6 7.7 %collective-permute-start.5 = (bf16[128,128]{1,0:T(8,128)(2,1)}, bf16[128,128]{1,0:T(8,128)(2,1)S(1)}, u32[]{:S(2)}, u32[]{:S(2)}) collective-permute-start(bf16[128,128]{1,0:T(8,128)(2,1)} %get-tuple-element.44), channel_id=1, source_target_pairs={{0,30},{2,4},{4,2},{6,8},{8,6},{10,12},{12,10},{14,16},{16,14},{18... | collective-permute-start | bytes 98312 | tf_op jit(solution)/shard_map/ppermute | solution.py:528
  43.2 13.6 %all-to-all-start.2 = ((bf16[16,48,128]{2,1,0:T(8,128)(2,1)}), bf16[16,48,128]{2,1,0:T(8,128)(2,1)S(1)}, u32[]{:S(2)}, u32[]{:S(2)}) async-start(bf16[16,48,128]{2,1,0:T(8,128)(2,1)} %get-tuple-element.60), calls=%async_computation.2 | async-start | bytes 393216 | tf_op jit(solution)/shard_map/all_to_all | solution.py:560
  55.8 15.3 %collective-permute-start.6 = (f32[2,512,128]{2,1,0:T(8,128)}, f32[2,512,128]{2,1,0:T(8,128)S(1)}, u32[]{:S(2)}, u32[]{:S(2)}) collective-permute-start(f32[2,512,128]{2,1,0:T(8,128)} %get-tuple-element.67), channel_id=1, source_target_pairs={{0,1},{1,0},{2,3},{3,2},{4,5},{5,4},{6,7},{7,6},{8,9},{9,8},{10,11... | collective-permute-start | bytes 1572872 | tf_op jit(solution)/shard_map/ppermute | solution.py:590
  59.0 14.9 %all-to-all-start.3 = ((bf16[16,48,128]{2,1,0:T(8,128)(2,1)}), bf16[16,48,128]{2,1,0:T(8,128)(2,1)S(1)}, u32[]{:S(2)}, u32[]{:S(2)}) async-start(bf16[16,48,128]{2,1,0:T(8,128)(2,1)} %coarse.1), calls=%async_computation.3 | async-start | bytes 393216 | tf_op jit(solution)/shard_map/all_to_all | solution.py:586
  65.0 8.9 %collective-permute-start.7 = (bf16[128,128]{1,0:T(8,128)(2,1)}, bf16[128,128]{1,0:T(8,128)(2,1)S(1)}, u32[]{:S(2)}, u32[]{:S(2)}) collective-permute-start(bf16[128,128]{1,0:T(8,128)(2,1)} %get-tuple-element.71), channel_id=1, source_target_pairs={{0,2},{2,0},{4,6},{6,4},{8,10},{10,8},{12,14},{14,12},{16,18},{18,... | collective-permute-start | bytes 98312 | tf_op jit(solution)/shard_map/ppermute | solution.py:587
  67.0 8.5 %collective-permute-start.8 = (bf16[128,128]{1,0:T(8,128)(2,1)}, bf16[128,128]{1,0:T(8,128)(2,1)S(1)}, u32[]{:S(2)}, u32[]{:S(2)}) collective-permute-start(bf16[128,128]{1,0:T(8,128)(2,1)} %get-tuple-element.72), channel_id=1, source_target_pairs={{0,30},{2,4},{4,2},{6,8},{8,6},{10,12},{12,10},{14,16},{16,14},{18... | collective-permute-start | bytes 98312 | tf_op jit(solution)/shard_map/ppermute | solution.py:576
  78.1 1.6 %collective-permute-start.9 = (bf16[448,128]{1,0:T(8,128)(2,1)}, bf16[448,128]{1,0:T(8,128)(2,1)S(1)}, u32[]{:S(2)}, u32[]{:S(2)}) collective-permute-start(bf16[448,128]{1,0:T(8,128)(2,1)} %pick.1.refs_0_), channel_id=1, source_target_pairs={{1,0},{0,1},{3,2},{2,3},{5,4},{4,5},{7,6},{6,7},{9,8},{8,9},{11,10... | collective-permute-start | bytes 344072 | tf_op jit(solution)/shard_map/ppermute | solution.py:469

commit v17 on v16

--- a/solution.py
+++ b/solution.py
@@ -261,9 +261,9 @@
     rest = refs[2 * z.group :]
     load_rows, old_image, tall, old_solved, chosen = rest[:5]
     before, after, first_got, second_got, left_rows, right_rows = rest[5:11]
-    new_before, new_after, first_pair, second_pair = rest[11:15]
-    values = rest[15 : 15 + z.group]
-    base, rounded, image = rest[15 + z.group :]
+    first_pair, second_pair = rest[11:13]
+    values = rest[13 : 13 + z.group]
+    base, rounded, image, new_before, new_after = rest[13 + z.group :]
     steps, images = [], []
     for s in range(z.subs):
         faces = sides(z, before, after, first_got, second_got, s)
@@ -296,6 +296,20 @@
         new_before[s] = faces[: z.face]
         new_after[s] = faces[z.face :]
     store_faces(z, new_before, new_after, first_pair, second_pair)
+    inner = []
+    for s in range(z.subs):
+        move = lane_matrix(z, 0, s * z.width)
+        total = jnp.zeros((z.rows, z.lanes), F32)
+        if s > 0:
+            share = dot(new_after[s - 1], move).astype(BF16)
+            total = total + dot(scatter_matrix(z, left_rows[s : s + 1, :], 0, z.rows), share)
+        if s < z.subs - 1:
+            share = dot(new_before[s + 1], move).astype(BF16)
+            total = total + dot(scatter_matrix(z, right_rows[s : s + 1, :], 0, z.rows), share)
+        inner.append(total)
+    base[...] = select(z, inner)
+    for k in range(z.group):
+        values[k][1] = values[k][1] - base[pl.ds(piece_start(z, k, z.own), z.own), :]
 
 
 def digit_row(shape, row):
@@ -360,23 +374,6 @@
         message[k] = modes
 
 
-def pick_kernel(z, *refs):
-    arrived, picks, before, after, first_got, second_got = refs[:6]
-    base_before, base_after, base_first, base_second, out = refs[6:]
-    chosen = picked_rows(z, arrived, picks)
-    near = chosen.shape[0]
-    lefts, rights = [], []
-    for s in range(z.subs):
-        values = sides(z, before, after, first_got, second_got, s)
-        bases = sides(z, base_before, base_after, base_first, base_second, s)
-        left, right = shares(z, s, chosen, values, bases)
-        lefts.append(left)
-        rights.append(right)
-    out[:near] = chosen
-    out[near : near + z.face] = select(z, lefts).astype(BF16)
-    out[near + z.face :] = select(z, rights).astype(BF16)
-
-
 def base_kernel(z, *refs):
     *values, out = refs
     for at in range(2):
@@ -390,28 +387,43 @@
             out[at, s] = total
 
 
-def last_kernel(z, *refs):
-    chosen = refs[: z.group]
-    base, tall, left_rows, right_rows, second_pass, final_residual = refs[z.group :]
+def last_kernel(z, wait, *refs):
+    arrived, firsts, seconds = refs[: z.group], refs[z.group : 2 * z.group], refs[2 * z.group : 3 * z.group]
+    picks, face_before, face_after, face_first, face_second, left_rows, right_rows = refs[3 * z.group : 3 * z.group + 7]
+    tall, base, second_pass, final_residual = refs[3 * z.group + 7 :]
     start = piece_start(z, 0, z.own)
-    near = (z.subs + 2) * z.modes
-
-    def all_cases(rows, source):
-        total = jnp.zeros((rows.stop - rows.start, z.lanes), F32)
-        for k, piece in enumerate(chosen):
-            place = lax.rem(lax.axis_index(GROUP) + k, z.group)
-            total = total + dot(piece[rows, :], lane_matrix(z, source, place * z.width))
-        return total.astype(BF16)
-
-    modes = all_cases(slice(0, near), 0)
-    for s in range(z.subs):
-        left = all_cases(slice(near, near + z.face), s * z.width)
-        right = all_cases(slice(near + z.face, near + 2 * z.face), s * z.width)
+    m, half = z.modes, z.lanes // 2
+    places = [lax.rem(lax.axis_index(GROUP) + k, z.group) * z.width for k in range(z.group)]
+    moves = [lane_matrix(z, 0, place) for place in places]
+
+    def all_cases(parts):
+        return sum(dot(part, move) for part, move in zip(parts, moves))
+
+    modes = all_cases([picked_rows(z, piece, picks) for piece in arrived]).astype(BF16)
+    swaps = list(zip(firsts, seconds))
+    outer_before = all_cases([jnp.where(even(), b[...], a[...]) for a, b in swaps])
+    outer_after = all_cases([jnp.where(even(), a[...], b[...]) for a, b in swaps])
+    wait(3 * z.group + 7)
+    totals = []
+    for s in range(z.subs):
+        faces = sides(z, face_before, face_after, face_first, face_second, s)
+        both = []
+        for side, at in ((0, s), (1, s + 2)):
+            above = jnp.zeros((half, z.lanes), BF16)
+            below = jnp.zeros((half - m, z.lanes), BF16)
+            both.append(dot(faces[side], jnp.concatenate([above, modes[at * m : (at + 1) * m], below], axis=0)))
+        if s == 0:
+            both[0] = both[0] + outer_before
+        if s == z.subs - 1:
+            both[1] = both[1] + outer_after
         scatter = scatter_matrix(z, left_rows[s : s + 1, :], start, z.own)
         wide = jnp.concatenate([tall[s, pl.ds(start, z.own), :], scatter], axis=1)
-        total = dot(wide, correction_side(z, modes, s, left))
-        image = total[:, : z.lanes] + dot(scatter_matrix(z, right_rows[s : s + 1, :], start, z.own), right)
-        second_pass[s] = (base[0, s] + total[:, z.lanes :])[:, : z.cases]
+        total = dot(wide, correction_side(z, modes, s, both[0].astype(BF16)))
+        image = dot(scatter_matrix(z, right_rows[s : s + 1, :], start, z.own), both[1].astype(BF16))
+        totals.append((total[:, z.lanes :], total[:, : z.lanes] + image))
+    wait(3 * z.group + 8)
+    for s, (step, image) in enumerate(totals):
+        second_pass[s] = (base[0, s] + step)[:, : z.cases]
         final_residual[s] = (base[1, s] - image)[:, : z.cases]
 
 
@@ -560,21 +572,24 @@
     restricted = spread(message)
 
     bases = [before, after, first_got, second_got]
-    before, after, first_pair, second_pair, *values = call(
+    first_pair, second_pair, *values = call(
         functools.partial(second_image_kernel, z),
-        [faces, faces, outer, outer, *[shape((2, z.own, lanes), F32)] * group],
+        [outer, outer, *[shape((2, z.own, lanes), F32)] * group],
         [
             *inverse_pieces, *stiffness_pieces, load_rows, image, tall, solved, chosen,
             *bases, left_rows, right_rows,
         ],
         work,
-        [pltpu.VMEM((rows, lanes), F32), pltpu.VMEM((rows, lanes), BF16), pltpu.VMEM((rows, lanes), BF16)],
+        [
+            pltpu.VMEM((rows, lanes), F32), pltpu.VMEM((rows, lanes), BF16), pltpu.VMEM((rows, lanes), BF16),
+            pltpu.VMEM((subs, face, lanes), BF16), pltpu.VMEM((subs, face, lanes), BF16),
+        ],
         late=range(2 * group),
         loose=[*arrivals, 2 * group + 7, 2 * group + 8],
         name="second_image",
     )
     second_got = lax.ppermute(second_pair, "sub", second_pairs)
-    restricted, before = lax.optimization_barrier((restricted, before))
+    restricted, second_pair = lax.optimization_barrier((restricted, second_pair))
     (message,) = call(
         functools.partial(coarse_kernel, z),
         [copies],
@@ -597,23 +612,19 @@
         loose=range(1, group),
         name="base",
     )
-    coarse, base = lax.optimization_barrier((coarse, base))
-    (chosen,) = call(
-        functools.partial(pick_kernel, z),
-        [shape((near + 2 * face, lanes), BF16)],
-        [coarse, picks, before, after, first_got, second_got, *bases],
-        work // 64,
-        loose=[0, 4, 5, 8, 9],
-        name="pick",
-    )
+    coarse, base, first_got, second_got = lax.optimization_barrier((coarse, base, first_got, second_got))
     out = shape((subs, z.own, z.cases), F32)
     return tuple(
         call(
             functools.partial(last_kernel, z),
             [out, out],
-            [*pieces_of(chosen, group), base, tall, left_rows, right_rows],
+            [
+                *pieces_of(coarse, group), *pieces_of(first_got, group), *pieces_of(second_got, group),
+                picks, *bases, left_rows, right_rows, tall, base,
+            ],
             work // 8,
-            loose=range(1, group),
+            late=[3 * group + 7, 3 * group + 8],
+            loose=[*range(3 * group), 3 * group + 3, 3 * group + 4],
             name="last",
         )
     )

time: 83.6 us -> 82.6 us (0.988)
  Pallas kernels: 36.1 us -> 34.9 us
  starting transfers between devices: 36.6 us -> 37.5 us
    pallas_call x10 -> x9, Pallas kernels: 36.1 us -> 34.9 us  [call(): pl.pallas_call(whole, out_shape=[pltpu.HBM(o.shape, o.dtype) for o in out...]
    ppermute x5 -> x7, waiting for transfers between devices: 2.96 us -> 2.65 us  [pieces_of(): lax.ppermute(block, GROUP, [((g + k) % group, g) for g in range(group)])]
  transfers between devices with their start and end apart: 14 -> 16, of which waited for: 7 -> 7; matrix products, arithmetic and copies ran while one was open for 0% -> 0% of each run, Pallas kernels for 29% -> 30%
where the time goes in v17:
time: 82.6 us; the launch traced here: 81.9 us
  starting transfers between devices  37.5 us (45%)
  Pallas kernels  34.9 us (42%)
  waiting for transfers between devices  8.66 us (10%)
    pallas_call x9, Pallas kernels, call(): pl.pallas_call(whole, out_shape=[pltpu.HBM(o.shape, o.dtype) for o in out...  34.9 us
    all_to_all x2, starting transfers between devices, body(): restricted = spread(message)  13.6 us
    all_to_all x2, starting transfers between devices, body(): coarse = spread(message)  10 us
    ppermute x2, starting transfers between devices, body(): second_got = lax.ppermute(second_pair, 'sub', second_pairs)  8.32 us
    all_to_all x2, waiting for transfers between devices, body(): restricted = spread(message)  3.99 us
    ppermute x2, starting transfers between devices, body(): first_got = lax.ppermute(first_pair, 'sub', first_pairs)  3.86 us
    ppermute x7, waiting for transfers between devices, pieces_of(): lax.ppermute(block, GROUP, [((g + k) % group, g) for g in range(group)])  2.65 us
    ppermute x2, waiting for transfers between devices, body(): second_got = lax.ppermute(second_pair, 'sub', second_pairs)  2.01 us
  transfers between devices with their start and end apart: 16, of which 7 were waited for; matrix products, arithmetic and copies ran while one was open for 0% of the time, Pallas kernels for 30%

profile of v17, /device:TPU:0, one launch (start us, length us, event | category | flops | bytes accessed | tf_op | source)
XLA Modules:
  0.0 81.9 jit_solution(6671422688146786662)
XLA Ops:
  0.6 0.5 collective-permute-start.1
  1.1 0.1 collective-permute-start
  1.2 1.4 %collective-permute-done.refs_1_.refs_5_ = bf16[2,48,512]{2,1,0:T(8,128)(2,1)S(1)} collective-permute-done((bf16[2,48,512]{2,1,0:T(8,128)(2,1)}, bf16[2,48,512]{2,1,0:T(8,128)(2,1)S(1)}, u32[]{:S(2)}, u32[]{:S(2)}) %collective-permute-start) | collective-permute-done | bytes 98336 | tf_op jit(solution)/shard_map/ppermute | solution.py:481
  2.7 0.0 collective-permute-done.1.refs_1_
  2.7 0.2 collective-permute-start.2
  2.9 0.3 collective-permute-start.3
  3.2 2.3 %open.1 = bf16[16,64,128]{2,1,0:T(8,128)(2,1)} custom-call(bf16[2,48,512]{2,1,0:T(8,128)(2,1)} %bitcast.2, bf16[2,48,512]{2,1,0:T(8,128)(2,1)S(1)} %collective-permute-done.refs_1_.refs_5_, bf16[2,1024,128]{2,1,0:T(8,128)(2,1)} %refs_6_.1, s32[2,48]{1,0:T(2,128)} %refs_3_.2), custom_call_target="tpu_custom_call" | custom-call | flops 67108864 | bytes 983424 | tf_op jit(solution)/shard_map/open/pallas_call | solution.py:457
  5.5 8.1 %all-to-all-start = ((bf16[16,64,128]{2,1,0:T(8,128)(2,1)}), bf16[16,64,128]{2,1,0:T(8,128)(2,1)S(1)}, u32[]{:S(2)}, u32[]{:S(2)}) async-start(bf16[16,64,128]{2,1,0:T(8,128)(2,1)} %open.1), calls=%async_computation | async-start | bytes 524288 | tf_op jit(solution)/shard_map/all_to_all | solution.py:519
  13.6 6.8 %first_image.1 = (bf16[1024,128]{1,0:T(8,128)(2,1)}, f32[1024,128]{1,0:T(8,128)}, f32[1024,128]{1,0:T(8,128)}, bf16[2,128,128]{2,1,0:T(8,128)(2,1)}, bf16[2,128,...) custom-call(bf16[2,512,1024]{2,1,0:T(8,128)(2,1)} %refs_0_.2, ...), custom_call_target="tpu_custom_call" | custom-call | flops 1073741824 | bytes 11339776 | tf_op jit(solution)/shard_map/first_image/pallas_call | solution.py:457
  20.4 3.5 %all-to-all-done.refs_2_ = bf16[16,64,128]{2,1,0:T(8,128)(2,1)S(1)} async-done(((bf16[16,64,128]{2,1,0:T(8,128)(2,1)}), bf16[16,64,128]{2,1,0:T(8,128)(2,1)S(1)}, u32[]{:S(2)}, u32[]{:S(2)}) %all-to-all-start) | async-done | bytes 262176 | tf_op jit(solution)/shard_map/all_to_all | solution.py:519
  23.9 3.2 %order.1 = (bf16[2,96,768]{2,1,0:T(8,128)(2,1)}, f32[2,16,128]{2,1,0:T(8,128)}, bf16[16,48,128]{2,1,0:T(8,128)(2,1)}) custom-call(bf16[96,768]{1,0:T(8,128)(2,1)} %refs_0_.1, bf16[96,768]{1,0:T(8,128)(2,1)S(1)} %collective-permute-done.1.refs_1_, bf16[16,64,128]{2,1,0:T(8,128)(2,1)S(1)} %all-to-all-done.refs_2_, bf16[128,768]{1,0:T(8,128)(2,1)} %constant.6.clone.refs_3_, ...), custom_call_target="tpu_custom_call" | custom-call | flops 452984832 | bytes 1310720 | tf_op jit(solution)/shard_map/order/pallas_call | solution.py:457
  27.1 3.6 %all-to-all-start.1 = ((bf16[16,48,128]{2,1,0:T(8,128)(2,1)}), bf16[16,48,128]{2,1,0:T(8,128)(2,1)S(1)}, u32[]{:S(2)}, u32[]{:S(2)}) async-start(bf16[16,48,128]{2,1,0:T(8,128)(2,1)} %get-tuple-element.45), calls=%async_computation.1 | async-start | bytes 393216 | tf_op jit(solution)/shard_map/all_to_all | solution.py:551
  30.7 1.9 %collective-permute-start.4 = (bf16[128,128]{1,0:T(8,128)(2,1)}, bf16[128,128]{1,0:T(8,128)(2,1)S(1)}, u32[]{:S(2)}, u32[]{:S(2)}) collective-permute-start(bf16[128,128]{1,0:T(8,128)(2,1)} %get-tuple-element.58), channel_id=1, source_target_pairs={{0,2},{2,0},{4,6},{6,4},{8,10},{10,8},{12,14},{14,12},{16,18},{18,... | collective-permute-start | bytes 98312 | tf_op jit(solution)/shard_map/ppermute | solution.py:552
  32.6 4.2 %collective-permute-start.5 = (bf16[128,128]{1,0:T(8,128)(2,1)}, bf16[128,128]{1,0:T(8,128)(2,1)S(1)}, u32[]{:S(2)}, u32[]{:S(2)}) collective-permute-start(bf16[128,128]{1,0:T(8,128)(2,1)} %get-tuple-element.43), channel_id=1, source_target_pairs={{0,30},{2,4},{4,2},{6,8},{8,6},{10,12},{12,10},{14,16},{16,14},{18... | collective-permute-start | bytes 98312 | tf_op jit(solution)/shard_map/ppermute | solution.py:540
  36.8 3.1 %begin.1 = (bf16[2,48,128]{2,1,0:T(8,128)(2,1)}, bf16[2,48,128]{2,1,0:T(8,128)(2,1)}, bf16[2,48,48]{2,1,0:T(8,128)(2,1)}, f32[48,128]{1,0:T(8,128)}, bf16[2,192,768]{2,1,0:T(8,128)(2,1)}) custom-call(bf16[1024,128]{1,0:T(8,128)(2,1)} %get-tuple-element.46.refs_0_.refs_4_, f32[1024,128]{1,0:T(8,128)} %get-tuple-element.47.refs_1_.refs_5_, ...), custom_call_target="tpu_custom_call" | custom-call | flops 67108864 | bytes 2204672 | tf_op jit(solution)/shard_map/begin/pallas_call | solution.py:457
  39.9 0.4 collective-permute-done.5.refs_9_.refs_12_.refs_10_
  40.3 2.8 %update.1 = (bf16[192,128]{1,0:T(8,128)(2,1)}, bf16[16,48,128]{2,1,0:T(8,128)(2,1)}) custom-call(bf16[16,48,128]{2,1,0:T(8,128)(2,1)S(1)} %all-to-all-done.1.refs_0_, bf16[2,192,768]{2,1,0:T(8,128)(2,1)} %get-tuple-element.51.refs_1_.refs_6_, f32[48,128]{1,0:T(8,128)} %get-tuple-element.52.refs_2_, bf16[2,48,48]{2,1,0:T(8,128)(2,1)} %get-tuple-element.53.refs_3_, ...), custom_call_target="tpu_custom_call" | custom-call | flops 16777216 | bytes 1311744 | tf_op jit(solution)/shard_map/update/pallas_call | solution.py:457
  43.2 5.6 %all-to-all-start.2 = ((bf16[16,48,128]{2,1,0:T(8,128)(2,1)}), bf16[16,48,128]{2,1,0:T(8,128)(2,1)S(1)}, u32[]{:S(2)}, u32[]{:S(2)}) async-start(bf16[16,48,128]{2,1,0:T(8,128)(2,1)} %get-tuple-element.59), calls=%async_computation.2 | async-start | bytes 393216 | tf_op jit(solution)/shard_map/all_to_all | solution.py:572
  48.7 7.5 %second_image.1 = (bf16[128,128]{1,0:T(8,128)(2,1)}, bf16[128,128]{1,0:T(8,128)(2,1)}, f32[2,512,128]{2,1,0:T(8,128)}, f32[2,512,128]{2,1,0:T(8,128)}) custom-call(bf16[2,512,1024]{2,1,0:T(8,128)(2,1)} %refs_0_.2, bf16[2,512,1024]{2,1,0:T(8,128)(2,1)S(1)} %collective-permute-done.2.refs_1_, bf16[2,512,1024]{2,1,0:T(8,128)(2,1)} %refs_2_.3, ...), custom_call_target="tpu_custom_call" | custom-call | flops 1073741824 | bytes 11585536 | tf_op jit(solution)/shard_map/second_image/pallas_call | solution.py:457
  56.2 0.1 collective-permute-start.6
  56.3 0.5 all-to-all-done.2.refs_0_
  56.8 2.2 %coarse.1 = bf16[16,48,128]{2,1,0:T(8,128)(2,1)} custom-call(bf16[16,48,128]{2,1,0:T(8,128)(2,1)S(1)} %all-to-all-done.2.refs_0_, bf16[2,96,768]{2,1,0:T(8,128)(2,1)} %get-tuple-element.64.refs_1_), custom_call_target="tpu_custom_call" | custom-call | flops 16777216 | bytes 688128 | tf_op jit(solution)/shard_map/coarse/pallas_call | solution.py:457
  59.0 6.5 %all-to-all-start.3 = ((bf16[16,48,128]{2,1,0:T(8,128)(2,1)}), bf16[16,48,128]{2,1,0:T(8,128)(2,1)S(1)}, u32[]{:S(2)}, u32[]{:S(2)}) async-start(bf16[16,48,128]{2,1,0:T(8,128)(2,1)} %coarse.1), calls=%async_computation.3 | async-start | bytes 393216 | tf_op jit(solution)/shard_map/all_to_all | solution.py:601
  65.5 1.9 %collective-permute-start.7 = (bf16[128,128]{1,0:T(8,128)(2,1)}, bf16[128,128]{1,0:T(8,128)(2,1)S(1)}, u32[]{:S(2)}, u32[]{:S(2)}) collective-permute-start(bf16[128,128]{1,0:T(8,128)(2,1)} %get-tuple-element.67), channel_id=1, source_target_pairs={{0,2},{2,0},{4,6},{6,4},{8,10},{10,8},{12,14},{14,12},{16,18},{18,... | collective-permute-start | bytes 98312 | tf_op jit(solution)/shard_map/ppermute | solution.py:602
  67.4 4.2 %collective-permute-start.8 = (bf16[128,128]{1,0:T(8,128)(2,1)}, bf16[128,128]{1,0:T(8,128)(2,1)S(1)}, u32[]{:S(2)}, u32[]{:S(2)}) collective-permute-start(bf16[128,128]{1,0:T(8,128)(2,1)} %get-tuple-element.62), channel_id=1, source_target_pairs={{0,30},{2,4},{4,2},{6,8},{8,6},{10,12},{12,10},{14,16},{16,14},{18... | collective-permute-start | bytes 98312 | tf_op jit(solution)/shard_map/ppermute | solution.py:591
  71.6 2.7 %base.1.refs_14_ = f32[2,2,512,128]{3,2,1,0:T(8,128)} custom-call(f32[2,512,128]{2,1,0:T(8,128)} %get-tuple-element.65.refs_0_, f32[2,512,128]{2,1,0:T(8,128)S(1)} %collective-permute-done.6.refs_1_), custom_call_target="tpu_custom_call" | custom-call | flops 16777216 | bytes 2097152 | tf_op jit(solution)/shard_map/base/pallas_call | solution.py:457
  74.3 1.6 %collective-permute-done.8.refs_4_ = bf16[128,128]{1,0:T(8,128)(2,1)S(1)} collective-permute-done((bf16[128,128]{1,0:T(8,128)(2,1)}, bf16[128,128]{1,0:T(8,128)(2,1)S(1)}, u32[]{:S(2)}, u32[]{:S(2)}) %collective-permute-start.8) | collective-permute-done | bytes 32800 | tf_op jit(solution)/shard_map/ppermute | solution.py:591
  75.9 0.5 collective-permute-start.10
  76.4 0.0 collective-permute-start.11
  76.4 1.0 %collective-permute-done.10.refs_3_ = bf16[128,128]{1,0:T(8,128)(2,1)S(1)} collective-permute-done((bf16[128,128]{1,0:T(8,128)(2,1)S(1)}, bf16[128,128]{1,0:T(8,128)(2,1)S(1)}, u32[]{:S(2)}, u32[]{:S(2)}) %collective-permute-start.10) | collective-permute-done | bytes 32800 | tf_op jit(solution)/shard_map/ppermute | solution.py:481
  77.4 0.2 collective-permute-done.11.refs_5_
  77.6 4.3 %last.1 = (f32[2,512,128]{2,1,0:T(8,128)}, f32[2,512,128]{2,1,0:T(8,128)}) custom-call(bf16[16,48,128]{2,1,0:T(8,128)(2,1)S(1)} %all-to-all-done.3.refs_0_, bf16[16,48,128]{2,1,0:T(8,128)(2,1)S(1)} %collective-permute-done.9.refs_1_, bf16[128,128]{1,0:T(8,128)(2,1)S(1)} %collective-permute-done.7.refs_2_, ...), custom_call_target="tpu_custom_call" | custom-call | flops 134217728 | bytes 3934208 | tf_op jit(solution)/shard_map/last/pallas_call | solution.py:457
  (9 shorter events, 0.0 us)
Async XLA Ops:
  0.6 2.0 %collective-permute-start.1 = (bf16[96,768]{1,0:T(8,128)(2,1)}, bf16[96,768]{1,0:T(8,128)(2,1)S(1)}, u32[]{:S(2)}, u32[]{:S(2)}) collective-permute-start(bf16[96,768]{1,0:T(8,128)(2,1)} %refs_0_.1), channel_id=1, source_target_pairs={{1,0},{0,1},{3,2},{2,3},{5,4},{4,5},{7,6},{6,7},{9,8},{8,9},{11,10... | collective-permute-start | bytes 442376 | tf_op jit(solution)/shard_map/ppermute | solution.py:481
  1.1 1.5 %collective-permute-start = (bf16[2,48,512]{2,1,0:T(8,128)(2,1)}, bf16[2,48,512]{2,1,0:T(8,128)(2,1)S(1)}, u32[]{:S(2)}, u32[]{:S(2)}) collective-permute-start(bf16[2,48,512]{2,1,0:T(8,128)(2,1)} %bitcast.1), channel_id=1, source_target_pairs={{1,0},{0,1},{3,2},{2,3},{5,4},{4,5},{7,6},{6,7},{9,8},{8,9},{11,10... | collective-permute-start | bytes 294920 | tf_op jit(solution)/shard_map/ppermute | solution.py:481
  2.7 10.9 %collective-permute-start.2 = (bf16[2,512,1024]{2,1,0:T(8,128)(2,1)}, bf16[2,512,1024]{2,1,0:T(8,128)(2,1)S(1)}, u32[]{:S(2)}, u32[]{:S(2)}) collective-permute-start(bf16[2,512,1024]{2,1,0:T(8,128)(2,1)} %refs_0_.2), channel_id=1, source_target_pairs={{1,0},{0,1},{3,2},{2,3},{5,4},{4,5},{7,6},{6,7},{9,8},{8,9},{11,10... | collective-permute-start | bytes 6291464 | tf_op jit(solution)/shard_map/ppermute | solution.py:481
  2.9 10.7 %collective-permute-start.3 = (bf16[2,512,1024]{2,1,0:T(8,128)(2,1)}, bf16[2,512,1024]{2,1,0:T(8,128)(2,1)}, u32[]{:S(2)}, u32[]{:S(2)}) collective-permute-start(bf16[2,512,1024]{2,1,0:T(8,128)(2,1)} %refs_2_.3), channel_id=1, source_target_pairs={{1,0},{0,1},{3,2},{2,3},{5,4},{4,5},{7,6},{6,7},{9,8},{8,9},{11,10... | collective-permute-start | bytes 6291464 | tf_op jit(solution)/shard_map/ppermute | solution.py:481
  5.5 18.4 %all-to-all-start = ((bf16[16,64,128]{2,1,0:T(8,128)(2,1)}), bf16[16,64,128]{2,1,0:T(8,128)(2,1)S(1)}, u32[]{:S(2)}, u32[]{:S(2)}) async-start(bf16[16,64,128]{2,1,0:T(8,128)(2,1)} %open.1), calls=%async_computation | async-start | bytes 524288 | tf_op jit(solution)/shard_map/all_to_all | solution.py:519
  27.1 13.2 %all-to-all-start.1 = ((bf16[16,48,128]{2,1,0:T(8,128)(2,1)}), bf16[16,48,128]{2,1,0:T(8,128)(2,1)S(1)}, u32[]{:S(2)}, u32[]{:S(2)}) async-start(bf16[16,48,128]{2,1,0:T(8,128)(2,1)} %get-tuple-element.45), calls=%async_computation.1 | async-start | bytes 393216 | tf_op jit(solution)/shard_map/all_to_all | solution.py:551
  30.7 9.2 %collective-permute-start.4 = (bf16[128,128]{1,0:T(8,128)(2,1)}, bf16[128,128]{1,0:T(8,128)(2,1)S(1)}, u32[]{:S(2)}, u32[]{:S(2)}) collective-permute-start(bf16[128,128]{1,0:T(8,128)(2,1)} %get-tuple-element.58), channel_id=1, source_target_pairs={{0,2},{2,0},{4,6},{6,4},{8,10},{10,8},{12,14},{14,12},{16,18},{18,... | collective-permute-start | bytes 98312 | tf_op jit(solution)/shard_map/ppermute | solution.py:552
  32.6 7.7 %collective-permute-start.5 = (bf16[128,128]{1,0:T(8,128)(2,1)}, bf16[128,128]{1,0:T(8,128)(2,1)S(1)}, u32[]{:S(2)}, u32[]{:S(2)}) collective-permute-start(bf16[128,128]{1,0:T(8,128)(2,1)} %get-tuple-element.43), channel_id=1, source_target_pairs={{0,30},{2,4},{4,2},{6,8},{8,6},{10,12},{12,10},{14,16},{16,14},{18... | collective-permute-start | bytes 98312 | tf_op jit(solution)/shard_map/ppermute | solution.py:540
  43.2 13.6 %all-to-all-start.2 = ((bf16[16,48,128]{2,1,0:T(8,128)(2,1)}), bf16[16,48,128]{2,1,0:T(8,128)(2,1)S(1)}, u32[]{:S(2)}, u32[]{:S(2)}) async-start(bf16[16,48,128]{2,1,0:T(8,128)(2,1)} %get-tuple-element.59), calls=%async_computation.2 | async-start | bytes 393216 | tf_op jit(solution)/shard_map/all_to_all | solution.py:572
  56.2 15.3 %collective-permute-start.6 = (f32[2,512,128]{2,1,0:T(8,128)}, f32[2,512,128]{2,1,0:T(8,128)S(1)}, u32[]{:S(2)}, u32[]{:S(2)}) collective-permute-start(f32[2,512,128]{2,1,0:T(8,128)} %get-tuple-element.66), channel_id=1, source_target_pairs={{0,1},{1,0},{2,3},{3,2},{4,5},{5,4},{6,7},{7,6},{8,9},{9,8},{10,11... | collective-permute-start | bytes 1572872 | tf_op jit(solution)/shard_map/ppermute | solution.py:605
  59.0 16.9 %all-to-all-start.3 = ((bf16[16,48,128]{2,1,0:T(8,128)(2,1)}), bf16[16,48,128]{2,1,0:T(8,128)(2,1)S(1)}, u32[]{:S(2)}, u32[]{:S(2)}) async-start(bf16[16,48,128]{2,1,0:T(8,128)(2,1)} %coarse.1), calls=%async_computation.3 | async-start | bytes 393216 | tf_op jit(solution)/shard_map/all_to_all | solution.py:601
  65.5 8.8 %collective-permute-start.7 = (bf16[128,128]{1,0:T(8,128)(2,1)}, bf16[128,128]{1,0:T(8,128)(2,1)S(1)}, u32[]{:S(2)}, u32[]{:S(2)}) collective-permute-start(bf16[128,128]{1,0:T(8,128)(2,1)} %get-tuple-element.67), channel_id=1, source_target_pairs={{0,2},{2,0},{4,6},{6,4},{8,10},{10,8},{12,14},{14,12},{16,18},{18,... | collective-permute-start | bytes 98312 | tf_op jit(solution)/shard_map/ppermute | solution.py:602
  67.4 8.5 %collective-permute-start.8 = (bf16[128,128]{1,0:T(8,128)(2,1)}, bf16[128,128]{1,0:T(8,128)(2,1)S(1)}, u32[]{:S(2)}, u32[]{:S(2)}) collective-permute-start(bf16[128,128]{1,0:T(8,128)(2,1)} %get-tuple-element.62), channel_id=1, source_target_pairs={{0,30},{2,4},{4,2},{6,8},{8,6},{10,12},{12,10},{14,16},{16,14},{18... | collective-permute-start | bytes 98312 | tf_op jit(solution)/shard_map/ppermute | solution.py:591
  75.9 1.7 %collective-permute-start.9 = (bf16[16,48,128]{2,1,0:T(8,128)(2,1)S(1)}, bf16[16,48,128]{2,1,0:T(8,128)(2,1)S(1)}, u32[]{:S(2)}, u32[]{:S(2)}) collective-permute-start(bf16[16,48,128]{2,1,0:T(8,128)(2,1)S(1)} %all-to-all-done.3.refs_0_), channel_id=1, source_target_pairs={{1,0},{0,1},{3,2},{2,3},{5,4},{4,5},{7,6},{6,7},{9,8},{8,9},{11,10... | collective-permute-start | bytes 589832 | tf_op jit(solution)/shard_map/ppermute | solution.py:481
  75.9 1.5 %collective-permute-start.10 = (bf16[128,128]{1,0:T(8,128)(2,1)S(1)}, bf16[128,128]{1,0:T(8,128)(2,1)S(1)}, u32[]{:S(2)}, u32[]{:S(2)}) collective-permute-start(bf16[128,128]{1,0:T(8,128)(2,1)S(1)} %collective-permute-done.7.refs_2_), channel_id=1, source_target_pairs={{1,0},{0,1},{3,2},{2,3},{5,4},{4,5},{7,6},{6,7},{9,8},{8,9},{11,10... | collective-permute-start | bytes 98312 | tf_op jit(solution)/shard_map/ppermute | solution.py:481
  76.4 1.2 %collective-permute-start.11 = (bf16[128,128]{1,0:T(8,128)(2,1)S(1)}, bf16[128,128]{1,0:T(8,128)(2,1)S(1)}, u32[]{:S(2)}, u32[]{:S(2)}) collective-permute-start(bf16[128,128]{1,0:T(8,128)(2,1)S(1)} %collective-permute-done.8.refs_4_), channel_id=1, source_target_pairs={{1,0},{0,1},{3,2},{2,3},{5,4},{4,5},{7,6},{6,7},{9,8},{8,9},{11,10... | collective-permute-start | bytes 98312 | tf_op jit(solution)/shard_map/ppermute | solution.py:481

commit v18 on v17

--- a/solution.py
+++ b/solution.py
@@ -133,6 +133,11 @@
     return jnp.concatenate(
         [pick_matrix(z, left_rows[s : s + 1, :]), pick_matrix(z, right_rows[s : s + 1, :])], axis=0
     )
+
+
+def halves(z, face):
+    part = z.face // 2
+    return (face[:part].astype(F32) + dot(face[part:], lane_matrix(z, 0, z.lanes // 2))).astype(BF16)
 
 
 def store_faces(z, before, after, first_pair, second_pair):
@@ -295,7 +300,10 @@
         faces = dot(own, lane_matrix(z, s * z.width, 0)).astype(BF16)
         new_before[s] = faces[: z.face]
         new_after[s] = faces[z.face :]
-    store_faces(z, new_before, new_after, first_pair, second_pair)
+    first = halves(z, new_before[0])
+    last = halves(z, new_after[z.subs - 1])
+    first_pair[...] = jnp.where(even(), last, first)
+    second_pair[...] = jnp.where(even(), first, last)
     inner = []
     for s in range(z.subs):
         move = lane_matrix(z, 0, s * z.width)
@@ -394,15 +402,17 @@
     start = piece_start(z, 0, z.own)
     m, half = z.modes, z.lanes // 2
     places = [lax.rem(lax.axis_index(GROUP) + k, z.group) * z.width for k in range(z.group)]
-    moves = [lane_matrix(z, 0, place) for place in places]
-
-    def all_cases(parts):
-        return sum(dot(part, move) for part, move in zip(parts, moves))
+
+    def all_cases(parts, source=0):
+        return sum(dot(part, lane_matrix(z, source, place)) for part, place in zip(parts, places))
+
+    def whole_face(parts):
+        return jnp.concatenate([all_cases(parts), all_cases(parts, half)], axis=0)
 
     modes = all_cases([picked_rows(z, piece, picks) for piece in arrived]).astype(BF16)
     swaps = list(zip(firsts, seconds))
-    outer_before = all_cases([jnp.where(even(), b[...], a[...]) for a, b in swaps])
-    outer_after = all_cases([jnp.where(even(), a[...], b[...]) for a, b in swaps])
+    outer_before = whole_face([jnp.where(even(), b[...], a[...]) for a, b in swaps])
+    outer_after = whole_face([jnp.where(even(), a[...], b[...]) for a, b in swaps])
     wait(3 * z.group + 7)
     totals = []
     for s in range(z.subs):
@@ -572,9 +582,10 @@
     restricted = spread(message)
 
     bases = [before, after, first_got, second_got]
+    half_face = shape((face // 2, lanes), BF16)
     first_pair, second_pair, *values = call(
         functools.partial(second_image_kernel, z),
-        [outer, outer, *[shape((2, z.own, lanes), F32)] * group],
+        [half_face, half_face, *[shape((2, z.own, lanes), F32)] * group],
         [
             *inverse_pieces, *stiffness_pieces, load_rows, image, tall, solved, chosen,
             *bases, left_rows, right_rows,

time: 82.6 us -> 82.1 us (level)
  no operation moved by 1% of the time
where the time goes in v18:
time: 82.1 us; the launch traced here: 81.5 us
  starting transfers between devices  37.6 us (46%)
  Pallas kernels  34.9 us (43%)
  waiting for transfers between devices  8.2 us (10%)
    pallas_call x9, Pallas kernels, call(): pl.pallas_call(whole, out_shape=[pltpu.HBM(o.shape, o.dtype) for o in out...  34.9 us
    all_to_all x2, starting transfers between devices, body(): restricted = spread(message)  13.6 us
    all_to_all x2, starting transfers between devices, body(): coarse = spread(message)  10.1 us
    ppermute x2, starting transfers between devices, body(): second_got = lax.ppermute(second_pair, 'sub', second_pairs)  8.32 us
    all_to_all x2, waiting for transfers between devices, body(): restricted = spread(message)  3.95 us
    ppermute x2, starting transfers between devices, body(): first_got = lax.ppermute(first_pair, 'sub', first_pairs)  3.86 us
    ppermute x7, waiting for transfers between devices, pieces_of(): lax.ppermute(block, GROUP, [((g + k) % group, g) for g in range(group)])  2.62 us
  transfers between devices with their start and end apart: 16, of which 7 were waited for; matrix products, arithmetic and copies ran while one was open for 0% of the time, Pallas kernels for 30%

profile of v18, /device:TPU:0, one launch (start us, length us, event | category | flops | bytes accessed | tf_op | source)
XLA Modules:
  0.0 81.5 jit_solution(13672165877468947962)
XLA Ops:
  0.6 0.5 collective-permute-start.1
  1.1 0.1 collective-permute-start
  1.2 1.4 %collective-permute-done.refs_1_.refs_5_ = bf16[2,48,512]{2,1,0:T(8,128)(2,1)S(1)} collective-permute-done((bf16[2,48,512]{2,1,0:T(8,128)(2,1)}, bf16[2,48,512]{2,1,0:T(8,128)(2,1)S(1)}, u32[]{:S(2)}, u32[]{:S(2)}) %collective-permute-start) | collective-permute-done | bytes 98336 | tf_op jit(solution)/shard_map/ppermute | solution.py:491
  2.7 0.0 collective-permute-done.1.refs_1_
  2.7 0.2 collective-permute-start.2
  2.9 0.3 collective-permute-start.3
  3.2 2.3 %open.1 = bf16[16,64,128]{2,1,0:T(8,128)(2,1)} custom-call(bf16[2,48,512]{2,1,0:T(8,128)(2,1)} %bitcast.2, bf16[2,48,512]{2,1,0:T(8,128)(2,1)S(1)} %collective-permute-done.refs_1_.refs_5_, bf16[2,1024,128]{2,1,0:T(8,128)(2,1)} %refs_6_.1, s32[2,48]{1,0:T(2,128)} %refs_3_.2), custom_call_target="tpu_custom_call" | custom-call | flops 67108864 | bytes 983424 | tf_op jit(solution)/shard_map/open/pallas_call | solution.py:467
  5.5 8.1 %all-to-all-start = ((bf16[16,64,128]{2,1,0:T(8,128)(2,1)}), bf16[16,64,128]{2,1,0:T(8,128)(2,1)S(1)}, u32[]{:S(2)}, u32[]{:S(2)}) async-start(bf16[16,64,128]{2,1,0:T(8,128)(2,1)} %open.1), calls=%async_computation | async-start | bytes 524288 | tf_op jit(solution)/shard_map/all_to_all | solution.py:529
  13.6 6.8 %first_image.1 = (bf16[1024,128]{1,0:T(8,128)(2,1)}, f32[1024,128]{1,0:T(8,128)}, f32[1024,128]{1,0:T(8,128)}, bf16[2,128,128]{2,1,0:T(8,128)(2,1)}, bf16[2,128,...) custom-call(bf16[2,512,1024]{2,1,0:T(8,128)(2,1)} %refs_0_.2, ...), custom_call_target="tpu_custom_call" | custom-call | flops 1073741824 | bytes 11339776 | tf_op jit(solution)/shard_map/first_image/pallas_call | solution.py:467
  20.4 3.5 %all-to-all-done.refs_2_ = bf16[16,64,128]{2,1,0:T(8,128)(2,1)S(1)} async-done(((bf16[16,64,128]{2,1,0:T(8,128)(2,1)}), bf16[16,64,128]{2,1,0:T(8,128)(2,1)S(1)}, u32[]{:S(2)}, u32[]{:S(2)}) %all-to-all-start) | async-done | bytes 262176 | tf_op jit(solution)/shard_map/all_to_all | solution.py:529
  23.9 3.2 %order.1 = (bf16[2,96,768]{2,1,0:T(8,128)(2,1)}, f32[2,16,128]{2,1,0:T(8,128)}, bf16[16,48,128]{2,1,0:T(8,128)(2,1)}) custom-call(bf16[96,768]{1,0:T(8,128)(2,1)} %refs_0_.1, bf16[96,768]{1,0:T(8,128)(2,1)S(1)} %collective-permute-done.1.refs_1_, bf16[16,64,128]{2,1,0:T(8,128)(2,1)S(1)} %all-to-all-done.refs_2_, bf16[128,768]{1,0:T(8,128)(2,1)} %constant.6.clone.refs_3_, ...), custom_call_target="tpu_custom_call" | custom-call | flops 452984832 | bytes 1310720 | tf_op jit(solution)/shard_map/order/pallas_call | solution.py:467
  27.1 3.6 %all-to-all-start.1 = ((bf16[16,48,128]{2,1,0:T(8,128)(2,1)}), bf16[16,48,128]{2,1,0:T(8,128)(2,1)S(1)}, u32[]{:S(2)}, u32[]{:S(2)}) async-start(bf16[16,48,128]{2,1,0:T(8,128)(2,1)} %get-tuple-element.45), calls=%async_computation.1 | async-start | bytes 393216 | tf_op jit(solution)/shard_map/all_to_all | solution.py:561
  30.7 1.9 %collective-permute-start.4 = (bf16[128,128]{1,0:T(8,128)(2,1)}, bf16[128,128]{1,0:T(8,128)(2,1)S(1)}, u32[]{:S(2)}, u32[]{:S(2)}) collective-permute-start(bf16[128,128]{1,0:T(8,128)(2,1)} %get-tuple-element.58), channel_id=1, source_target_pairs={{0,2},{2,0},{4,6},{6,4},{8,10},{10,8},{12,14},{14,12},{16,18},{18,... | collective-permute-start | bytes 98312 | tf_op jit(solution)/shard_map/ppermute | solution.py:562
  32.6 4.2 %collective-permute-start.5 = (bf16[128,128]{1,0:T(8,128)(2,1)}, bf16[128,128]{1,0:T(8,128)(2,1)S(1)}, u32[]{:S(2)}, u32[]{:S(2)}) collective-permute-start(bf16[128,128]{1,0:T(8,128)(2,1)} %get-tuple-element.43), channel_id=1, source_target_pairs={{0,30},{2,4},{4,2},{6,8},{8,6},{10,12},{12,10},{14,16},{16,14},{18... | collective-permute-start | bytes 98312 | tf_op jit(solution)/shard_map/ppermute | solution.py:550
  36.8 3.1 %begin.1 = (bf16[2,48,128]{2,1,0:T(8,128)(2,1)}, bf16[2,48,128]{2,1,0:T(8,128)(2,1)}, bf16[2,48,48]{2,1,0:T(8,128)(2,1)}, f32[48,128]{1,0:T(8,128)}, bf16[2,192,768]{2,1,0:T(8,128)(2,1)}) custom-call(bf16[1024,128]{1,0:T(8,128)(2,1)} %get-tuple-element.46.refs_0_.refs_4_, f32[1024,128]{1,0:T(8,128)} %get-tuple-element.47.refs_1_.refs_5_, ...), custom_call_target="tpu_custom_call" | custom-call | flops 67108864 | bytes 2204672 | tf_op jit(solution)/shard_map/begin/pallas_call | solution.py:467
  39.9 0.4 collective-permute-done.5.refs_9_.refs_12_.refs_10_
  40.3 2.8 %update.1 = (bf16[192,128]{1,0:T(8,128)(2,1)}, bf16[16,48,128]{2,1,0:T(8,128)(2,1)}) custom-call(bf16[16,48,128]{2,1,0:T(8,128)(2,1)S(1)} %all-to-all-done.1.refs_0_, bf16[2,192,768]{2,1,0:T(8,128)(2,1)} %get-tuple-element.51.refs_1_.refs_6_, f32[48,128]{1,0:T(8,128)} %get-tuple-element.52.refs_2_, bf16[2,48,48]{2,1,0:T(8,128)(2,1)} %get-tuple-element.53.refs_3_, ...), custom_call_target="tpu_custom_call" | custom-call | flops 16777216 | bytes 1311744 | tf_op jit(solution)/shard_map/update/pallas_call | solution.py:467
  43.2 5.6 %all-to-all-start.2 = ((bf16[16,48,128]{2,1,0:T(8,128)(2,1)}), bf16[16,48,128]{2,1,0:T(8,128)(2,1)S(1)}, u32[]{:S(2)}, u32[]{:S(2)}) async-start(bf16[16,48,128]{2,1,0:T(8,128)(2,1)} %get-tuple-element.59), calls=%async_computation.2 | async-start | bytes 393216 | tf_op jit(solution)/shard_map/all_to_all | solution.py:582
  48.7 7.5 %second_image.1 = (bf16[64,128]{1,0:T(8,128)(2,1)}, bf16[64,128]{1,0:T(8,128)(2,1)}, f32[2,512,128]{2,1,0:T(8,128)}, f32[2,512,128]{2,1,0:T(8,128)}) custom-call(bf16[2,512,1024]{2,1,0:T(8,128)(2,1)} %refs_0_.2, bf16[2,512,1024]{2,1,0:T(8,128)(2,1)S(1)} %collective-permute-done.2.refs_1_, bf16[2,512,1024]{2,1,0:T(8,128)(2,1)} %refs_2_.3, ...), custom_call_target="tpu_custom_call" | custom-call | flops 1073741824 | bytes 11552768 | tf_op jit(solution)/shard_map/second_image/pallas_call | solution.py:467
  56.3 0.1 collective-permute-start.6
  56.4 0.4 all-to-all-done.2.refs_0_
  56.8 2.2 %coarse.1 = bf16[16,48,128]{2,1,0:T(8,128)(2,1)} custom-call(bf16[16,48,128]{2,1,0:T(8,128)(2,1)S(1)} %all-to-all-done.2.refs_0_, bf16[2,96,768]{2,1,0:T(8,128)(2,1)} %get-tuple-element.64.refs_1_), custom_call_target="tpu_custom_call" | custom-call | flops 16777216 | bytes 688128 | tf_op jit(solution)/shard_map/coarse/pallas_call | solution.py:467
  59.0 6.5 %all-to-all-start.3 = ((bf16[16,48,128]{2,1,0:T(8,128)(2,1)}), bf16[16,48,128]{2,1,0:T(8,128)(2,1)S(1)}, u32[]{:S(2)}, u32[]{:S(2)}) async-start(bf16[16,48,128]{2,1,0:T(8,128)(2,1)} %coarse.1), calls=%async_computation.3 | async-start | bytes 393216 | tf_op jit(solution)/shard_map/all_to_all | solution.py:612
  65.5 1.9 %collective-permute-start.7 = (bf16[64,128]{1,0:T(8,128)(2,1)}, bf16[64,128]{1,0:T(8,128)(2,1)S(1)}, u32[]{:S(2)}, u32[]{:S(2)}) collective-permute-start(bf16[64,128]{1,0:T(8,128)(2,1)} %get-tuple-element.67), channel_id=1, source_target_pairs={{0,2},{2,0},{4,6},{6,4},{8,10},{10,8},{12,14},{14,12},{16,18},{18,... | collective-permute-start | bytes 49160 | tf_op jit(solution)/shard_map/ppermute | solution.py:613
  67.5 4.2 %collective-permute-start.8 = (bf16[64,128]{1,0:T(8,128)(2,1)}, bf16[64,128]{1,0:T(8,128)(2,1)S(1)}, u32[]{:S(2)}, u32[]{:S(2)}) collective-permute-start(bf16[64,128]{1,0:T(8,128)(2,1)} %get-tuple-element.62), channel_id=1, source_target_pairs={{0,30},{2,4},{4,2},{6,8},{8,6},{10,12},{12,10},{14,16},{16,14},{18... | collective-permute-start | bytes 49160 | tf_op jit(solution)/shard_map/ppermute | solution.py:602
  71.6 2.7 %base.1.refs_14_ = f32[2,2,512,128]{3,2,1,0:T(8,128)} custom-call(f32[2,512,128]{2,1,0:T(8,128)} %get-tuple-element.65.refs_0_, f32[2,512,128]{2,1,0:T(8,128)S(1)} %collective-permute-done.6.refs_1_), custom_call_target="tpu_custom_call" | custom-call | flops 16777216 | bytes 2097152 | tf_op jit(solution)/shard_map/base/pallas_call | solution.py:467
  74.3 1.2 %collective-permute-done.8.refs_4_ = bf16[64,128]{1,0:T(8,128)(2,1)S(1)} collective-permute-done((bf16[64,128]{1,0:T(8,128)(2,1)}, bf16[64,128]{1,0:T(8,128)(2,1)S(1)}, u32[]{:S(2)}, u32[]{:S(2)}) %collective-permute-start.8) | collective-permute-done | bytes 16416 | tf_op jit(solution)/shard_map/ppermute | solution.py:602
  75.5 0.5 collective-permute-start.10
  76.0 0.0 collective-permute-start.11
  76.0 1.0 %collective-permute-done.10.refs_3_ = bf16[64,128]{1,0:T(8,128)(2,1)S(1)} collective-permute-done((bf16[64,128]{1,0:T(8,128)(2,1)S(1)}, bf16[64,128]{1,0:T(8,128)(2,1)S(1)}, u32[]{:S(2)}, u32[]{:S(2)}) %collective-permute-start.10) | collective-permute-done | bytes 16416 | tf_op jit(solution)/shard_map/ppermute | solution.py:491
  77.0 0.2 collective-permute-done.11.refs_5_
  77.2 4.2 %last.1 = (f32[2,512,128]{2,1,0:T(8,128)}, f32[2,512,128]{2,1,0:T(8,128)}) custom-call(bf16[16,48,128]{2,1,0:T(8,128)(2,1)S(1)} %all-to-all-done.3.refs_0_, bf16[16,48,128]{2,1,0:T(8,128)(2,1)S(1)} %collective-permute-done.9.refs_1_, bf16[64,128]{1,0:T(8,128)(2,1)S(1)} %collective-permute-done.7.refs_2_, ...), custom_call_target="tpu_custom_call" | custom-call | flops 134217728 | bytes 3868672 | tf_op jit(solution)/shard_map/last/pallas_call | solution.py:467
  (9 shorter events, 0.0 us)
Async XLA Ops:
  0.6 2.0 %collective-permute-start.1 = (bf16[96,768]{1,0:T(8,128)(2,1)}, bf16[96,768]{1,0:T(8,128)(2,1)S(1)}, u32[]{:S(2)}, u32[]{:S(2)}) collective-permute-start(bf16[96,768]{1,0:T(8,128)(2,1)} %refs_0_.1), channel_id=1, source_target_pairs={{1,0},{0,1},{3,2},{2,3},{5,4},{4,5},{7,6},{6,7},{9,8},{8,9},{11,10... | collective-permute-start | bytes 442376 | tf_op jit(solution)/shard_map/ppermute | solution.py:491
  1.1 1.5 %collective-permute-start = (bf16[2,48,512]{2,1,0:T(8,128)(2,1)}, bf16[2,48,512]{2,1,0:T(8,128)(2,1)S(1)}, u32[]{:S(2)}, u32[]{:S(2)}) collective-permute-start(bf16[2,48,512]{2,1,0:T(8,128)(2,1)} %bitcast.1), channel_id=1, source_target_pairs={{1,0},{0,1},{3,2},{2,3},{5,4},{4,5},{7,6},{6,7},{9,8},{8,9},{11,10... | collective-permute-start | bytes 294920 | tf_op jit(solution)/shard_map/ppermute | solution.py:491
  2.7 10.9 %collective-permute-start.2 = (bf16[2,512,1024]{2,1,0:T(8,128)(2,1)}, bf16[2,512,1024]{2,1,0:T(8,128)(2,1)S(1)}, u32[]{:S(2)}, u32[]{:S(2)}) collective-permute-start(bf16[2,512,1024]{2,1,0:T(8,128)(2,1)} %refs_0_.2), channel_id=1, source_target_pairs={{1,0},{0,1},{3,2},{2,3},{5,4},{4,5},{7,6},{6,7},{9,8},{8,9},{11,10... | collective-permute-start | bytes 6291464 | tf_op jit(solution)/shard_map/ppermute | solution.py:491
  2.9 10.7 %collective-permute-start.3 = (bf16[2,512,1024]{2,1,0:T(8,128)(2,1)}, bf16[2,512,1024]{2,1,0:T(8,128)(2,1)}, u32[]{:S(2)}, u32[]{:S(2)}) collective-permute-start(bf16[2,512,1024]{2,1,0:T(8,128)(2,1)} %refs_2_.3), channel_id=1, source_target_pairs={{1,0},{0,1},{3,2},{2,3},{5,4},{4,5},{7,6},{6,7},{9,8},{8,9},{11,10... | collective-permute-start | bytes 6291464 | tf_op jit(solution)/shard_map/ppermute | solution.py:491
  5.5 18.4 %all-to-all-start = ((bf16[16,64,128]{2,1,0:T(8,128)(2,1)}), bf16[16,64,128]{2,1,0:T(8,128)(2,1)S(1)}, u32[]{:S(2)}, u32[]{:S(2)}) async-start(bf16[16,64,128]{2,1,0:T(8,128)(2,1)} %open.1), calls=%async_computation | async-start | bytes 524288 | tf_op jit(solution)/shard_map/all_to_all | solution.py:529
  27.1 13.2 %all-to-all-start.1 = ((bf16[16,48,128]{2,1,0:T(8,128)(2,1)}), bf16[16,48,128]{2,1,0:T(8,128)(2,1)S(1)}, u32[]{:S(2)}, u32[]{:S(2)}) async-start(bf16[16,48,128]{2,1,0:T(8,128)(2,1)} %get-tuple-element.45), calls=%async_computation.1 | async-start | bytes 393216 | tf_op jit(solution)/shard_map/all_to_all | solution.py:561
  30.7 9.2 %collective-permute-start.4 = (bf16[128,128]{1,0:T(8,128)(2,1)}, bf16[128,128]{1,0:T(8,128)(2,1)S(1)}, u32[]{:S(2)}, u32[]{:S(2)}) collective-permute-start(bf16[128,128]{1,0:T(8,128)(2,1)} %get-tuple-element.58), channel_id=1, source_target_pairs={{0,2},{2,0},{4,6},{6,4},{8,10},{10,8},{12,14},{14,12},{16,18},{18,... | collective-permute-start | bytes 98312 | tf_op jit(solution)/shard_map/ppermute | solution.py:562
  32.6 7.7 %collective-permute-start.5 = (bf16[128,128]{1,0:T(8,128)(2,1)}, bf16[128,128]{1,0:T(8,128)(2,1)S(1)}, u32[]{:S(2)}, u32[]{:S(2)}) collective-permute-start(bf16[128,128]{1,0:T(8,128)(2,1)} %get-tuple-element.43), channel_id=1, source_target_pairs={{0,30},{2,4},{4,2},{6,8},{8,6},{10,12},{12,10},{14,16},{16,14},{18... | collective-permute-start | bytes 98312 | tf_op jit(solution)/shard_map/ppermute | solution.py:550
  43.2 13.6 %all-to-all-start.2 = ((bf16[16,48,128]{2,1,0:T(8,128)(2,1)}), bf16[16,48,128]{2,1,0:T(8,128)(2,1)S(1)}, u32[]{:S(2)}, u32[]{:S(2)}) async-start(bf16[16,48,128]{2,1,0:T(8,128)(2,1)} %get-tuple-element.59), calls=%async_computation.2 | async-start | bytes 393216 | tf_op jit(solution)/shard_map/all_to_all | solution.py:582
  56.3 15.3 %collective-permute-start.6 = (f32[2,512,128]{2,1,0:T(8,128)}, f32[2,512,128]{2,1,0:T(8,128)S(1)}, u32[]{:S(2)}, u32[]{:S(2)}) collective-permute-start(f32[2,512,128]{2,1,0:T(8,128)} %get-tuple-element.66), channel_id=1, source_target_pairs={{0,1},{1,0},{2,3},{3,2},{4,5},{5,4},{6,7},{7,6},{8,9},{9,8},{10,11... | collective-permute-start | bytes 1572872 | tf_op jit(solution)/shard_map/ppermute | solution.py:616
  59.0 16.5 %all-to-all-start.3 = ((bf16[16,48,128]{2,1,0:T(8,128)(2,1)}), bf16[16,48,128]{2,1,0:T(8,128)(2,1)S(1)}, u32[]{:S(2)}, u32[]{:S(2)}) async-start(bf16[16,48,128]{2,1,0:T(8,128)(2,1)} %coarse.1), calls=%async_computation.3 | async-start | bytes 393216 | tf_op jit(solution)/shard_map/all_to_all | solution.py:612
  65.5 8.8 %collective-permute-start.7 = (bf16[64,128]{1,0:T(8,128)(2,1)}, bf16[64,128]{1,0:T(8,128)(2,1)S(1)}, u32[]{:S(2)}, u32[]{:S(2)}) collective-permute-start(bf16[64,128]{1,0:T(8,128)(2,1)} %get-tuple-element.67), channel_id=1, source_target_pairs={{0,2},{2,0},{4,6},{6,4},{8,10},{10,8},{12,14},{14,12},{16,18},{18,... | collective-permute-start | bytes 49160 | tf_op jit(solution)/shard_map/ppermute | solution.py:613
  67.5 8.1 %collective-permute-start.8 = (bf16[64,128]{1,0:T(8,128)(2,1)}, bf16[64,128]{1,0:T(8,128)(2,1)S(1)}, u32[]{:S(2)}, u32[]{:S(2)}) collective-permute-start(bf16[64,128]{1,0:T(8,128)(2,1)} %get-tuple-element.62), channel_id=1, source_target_pairs={{0,30},{2,4},{4,2},{6,8},{8,6},{10,12},{12,10},{14,16},{16,14},{18... | collective-permute-start | bytes 49160 | tf_op jit(solution)/shard_map/ppermute | solution.py:602
  75.5 1.7 %collective-permute-start.9 = (bf16[16,48,128]{2,1,0:T(8,128)(2,1)S(1)}, bf16[16,48,128]{2,1,0:T(8,128)(2,1)S(1)}, u32[]{:S(2)}, u32[]{:S(2)}) collective-permute-start(bf16[16,48,128]{2,1,0:T(8,128)(2,1)S(1)} %all-to-all-done.3.refs_0_), channel_id=1, source_target_pairs={{1,0},{0,1},{3,2},{2,3},{5,4},{4,5},{7,6},{6,7},{9,8},{8,9},{11,10... | collective-permute-start | bytes 589832 | tf_op jit(solution)/shard_map/ppermute | solution.py:491
  75.5 1.5 %collective-permute-start.10 = (bf16[64,128]{1,0:T(8,128)(2,1)S(1)}, bf16[64,128]{1,0:T(8,128)(2,1)S(1)}, u32[]{:S(2)}, u32[]{:S(2)}) collective-permute-start(bf16[64,128]{1,0:T(8,128)(2,1)S(1)} %collective-permute-done.7.refs_2_), channel_id=1, source_target_pairs={{1,0},{0,1},{3,2},{2,3},{5,4},{4,5},{7,6},{6,7},{9,8},{8,9},{11,10... | collective-permute-start | bytes 49160 | tf_op jit(solution)/shard_map/ppermute | solution.py:491
  76.0 1.2 %collective-permute-start.11 = (bf16[64,128]{1,0:T(8,128)(2,1)S(1)}, bf16[64,128]{1,0:T(8,128)(2,1)S(1)}, u32[]{:S(2)}, u32[]{:S(2)}) collective-permute-start(bf16[64,128]{1,0:T(8,128)(2,1)S(1)} %collective-permute-done.8.refs_4_), channel_id=1, source_target_pairs={{1,0},{0,1},{3,2},{2,3},{5,4},{4,5},{7,6},{6,7},{9,8},{8,9},{11,10... | collective-permute-start | bytes 49160 | tf_op jit(solution)/shard_map/ppermute | solution.py:491

commit v19 on v18

--- a/solution.py
+++ b/solution.py
@@ -395,7 +395,7 @@
             out[at, s] = total
 
 
-def last_kernel(z, wait, *refs):
+def last_kernel(z, wait, send, *refs):
     arrived, firsts, seconds = refs[: z.group], refs[z.group : 2 * z.group], refs[2 * z.group : 3 * z.group]
     picks, face_before, face_after, face_first, face_second, left_rows, right_rows = refs[3 * z.group : 3 * z.group + 7]
     tall, base, second_pass, final_residual = refs[3 * z.group + 7 :]
@@ -414,7 +414,6 @@
     outer_before = whole_face([jnp.where(even(), b[...], a[...]) for a, b in swaps])
     outer_after = whole_face([jnp.where(even(), a[...], b[...]) for a, b in swaps])
     wait(3 * z.group + 7)
-    totals = []
     for s in range(z.subs):
         faces = sides(z, face_before, face_after, face_first, face_second, s)
         both = []
@@ -430,16 +429,18 @@
         wide = jnp.concatenate([tall[s, pl.ds(start, z.own), :], scatter], axis=1)
         total = dot(wide, correction_side(z, modes, s, both[0].astype(BF16)))
         image = dot(scatter_matrix(z, right_rows[s : s + 1, :], start, z.own), both[1].astype(BF16))
-        totals.append((total[:, z.lanes :], total[:, : z.lanes] + image))
-    wait(3 * z.group + 8)
-    for s, (step, image) in enumerate(totals):
-        second_pass[s] = (base[0, s] + step)[:, : z.cases]
-        final_residual[s] = (base[1, s] - image)[:, : z.cases]
-
-
-def call(kernel, outs, operands, flops, scratch=(), late=(), loose=(), name=None):
+        if s == 0:
+            wait(3 * z.group + 8)
+        second_pass[s] = (base[0, s] + total[:, z.lanes :])[:, : z.cases]
+        send(0, s)
+        final_residual[s] = (base[1, s] - total[:, : z.lanes] - image)[:, : z.cases]
+        send(1, s)
+
+
+def call(kernel, outs, operands, flops, scratch=(), late=(), loose=(), early=False, name=None):
     moved = sum(int(np.prod(x.shape)) * x.dtype.itemsize for x in (*operands, *outs))
     n_in, n_out = len(operands), len(outs)
+    blocks = outs[0].shape[0] if early else 1
 
     def whole(*refs):
         hbm, refs = refs[: n_in + n_out], refs[n_in + n_out :]
@@ -452,10 +453,21 @@
             if i not in late:
                 copy.wait()
         extra = [lambda i: arriving[i].wait()] if late else []
-        kernel(*extra, *vmem, *rest)
-        leaving = [pltpu.make_async_copy(vmem[n_in + i], hbm[n_in + i], out_sems.at[i]) for i in range(n_out)]
-        for copy in leaving:
-            copy.start()
+        if early:
+            leaving = [
+                [
+                    pltpu.make_async_copy(vmem[n_in + i].at[at], hbm[n_in + i].at[at], out_sems.at[i * blocks + at])
+                    for at in range(blocks)
+                ]
+                for i in range(n_out)
+            ]
+            kernel(*extra, lambda i, at: leaving[i][at].start(), *vmem, *rest)
+            leaving = sum(leaving, [])
+        else:
+            leaving = [pltpu.make_async_copy(vmem[n_in + i], hbm[n_in + i], out_sems.at[i]) for i in range(n_out)]
+            kernel(*extra, *vmem, *rest)
+            for copy in leaving:
+                copy.start()
         for copy in leaving:
             copy.wait()
 
@@ -472,7 +484,7 @@
         scratch_shapes=[
             *[pltpu.VMEM(x.shape, x.dtype) for x in (*operands, *outs)],
             pltpu.SemaphoreType.DMA((n_in,)),
-            pltpu.SemaphoreType.DMA((n_out,)),
+            pltpu.SemaphoreType.DMA((n_out * blocks,)),
             *scratch,
         ],
         compiler_params=pltpu.CompilerParams(vmem_limit_bytes=VMEM_BYTES),
@@ -636,6 +648,7 @@
             work // 8,
             late=[3 * group + 7, 3 * group + 8],
             loose=[*range(3 * group), 3 * group + 3, 3 * group + 4],
+            early=True,
             name="last",
         )
     )

time: 82.1 us -> 82.1 us (level)
  no operation moved by 1% of the time
where the time goes in v19:
time: 82.1 us; the launch traced here: 81.5 us
  starting transfers between devices  37.6 us (46%)
  Pallas kernels  34.9 us (43%)
  waiting for transfers between devices  8.2 us (10%)
    pallas_call x9, Pallas kernels, call(): pl.pallas_call(whole, out_shape=[pltpu.HBM(o.shape, o.dtype) for o in out...  34.9 us
    all_to_all x2, starting transfers between devices, body(): restricted = spread(message)  13.6 us
    all_to_all x2, starting transfers between devices, body(): coarse = spread(message)  10.1 us
    ppermute x2, starting transfers between devices, body(): second_got = lax.ppermute(second_pair, 'sub', second_pairs)  8.32 us
    all_to_all x2, waiting for transfers between devices, body(): restricted = spread(message)  3.95 us
    ppermute x2, starting transfers between devices, body(): first_got = lax.ppermute(first_pair, 'sub', first_pairs)  3.86 us
    ppermute x7, waiting for transfers between devices, pieces_of(): lax.ppermute(block, GROUP, [((g + k) % group, g) for g in range(group)])  2.62 us
  transfers between devices with their start and end apart: 16, of which 7 were waited for; matrix products, arithmetic and copies ran while one was open for 0% of the time, Pallas kernels for 30%

profile of v19, /device:TPU:0, one launch (start us, length us, event | category | flops | bytes accessed | tf_op | source)
XLA Modules:
  0.0 81.5 jit_solution(16984983395280262822)
XLA Ops:
  0.6 0.5 collective-permute-start.1
  1.1 0.1 collective-permute-start
  1.2 1.4 %collective-permute-done.refs_1_.refs_5_ = bf16[2,48,512]{2,1,0:T(8,128)(2,1)S(1)} collective-permute-done((bf16[2,48,512]{2,1,0:T(8,128)(2,1)}, bf16[2,48,512]{2,1,0:T(8,128)(2,1)S(1)}, u32[]{:S(2)}, u32[]{:S(2)}) %collective-permute-start) | collective-permute-done | bytes 98336 | tf_op jit(solution)/shard_map/ppermute | solution.py:503
  2.7 0.2 collective-permute-start.2
  2.9 0.3 collective-permute-start.3
  3.2 2.3 %open.1 = bf16[16,64,128]{2,1,0:T(8,128)(2,1)} custom-call(bf16[2,48,512]{2,1,0:T(8,128)(2,1)} %bitcast.2, bf16[2,48,512]{2,1,0:T(8,128)(2,1)S(1)} %collective-permute-done.refs_1_.refs_5_, bf16[2,1024,128]{2,1,0:T(8,128)(2,1)} %refs_6_.1, s32[2,48]{1,0:T(2,128)} %refs_3_.2), custom_call_target="tpu_custom_call" | custom-call | flops 67108864 | bytes 983424 | tf_op jit(solution)/shard_map/open/pallas_call | solution.py:479
  5.5 8.1 %all-to-all-start = ((bf16[16,64,128]{2,1,0:T(8,128)(2,1)}), bf16[16,64,128]{2,1,0:T(8,128)(2,1)S(1)}, u32[]{:S(2)}, u32[]{:S(2)}) async-start(bf16[16,64,128]{2,1,0:T(8,128)(2,1)} %open.1), calls=%async_computation | async-start | bytes 524288 | tf_op jit(solution)/shard_map/all_to_all | solution.py:541
  13.5 0.0 collective-permute-done.2.refs_1_
  13.6 6.8 %first_image.1 = (bf16[1024,128]{1,0:T(8,128)(2,1)}, f32[1024,128]{1,0:T(8,128)}, f32[1024,128]{1,0:T(8,128)}, bf16[2,128,128]{2,1,0:T(8,128)(2,1)}, bf16[2,128,...) custom-call(bf16[2,512,1024]{2,1,0:T(8,128)(2,1)} %refs_0_.2, ...), custom_call_target="tpu_custom_call" | custom-call | flops 1073741824 | bytes 11339776 | tf_op jit(solution)/shard_map/first_image/pallas_call | solution.py:479
  20.4 3.5 %all-to-all-done.refs_2_ = bf16[16,64,128]{2,1,0:T(8,128)(2,1)S(1)} async-done(((bf16[16,64,128]{2,1,0:T(8,128)(2,1)}), bf16[16,64,128]{2,1,0:T(8,128)(2,1)S(1)}, u32[]{:S(2)}, u32[]{:S(2)}) %all-to-all-start) | async-done | bytes 262176 | tf_op jit(solution)/shard_map/all_to_all | solution.py:541
  23.9 3.2 %order.1 = (bf16[2,96,768]{2,1,0:T(8,128)(2,1)}, f32[2,16,128]{2,1,0:T(8,128)}, bf16[16,48,128]{2,1,0:T(8,128)(2,1)}) custom-call(bf16[96,768]{1,0:T(8,128)(2,1)} %refs_0_.1, bf16[96,768]{1,0:T(8,128)(2,1)S(1)} %collective-permute-done.1.refs_1_, bf16[16,64,128]{2,1,0:T(8,128)(2,1)S(1)} %all-to-all-done.refs_2_, bf16[128,768]{1,0:T(8,128)(2,1)} %constant.6.clone.refs_3_, ...), custom_call_target="tpu_custom_call" | custom-call | flops 452984832 | bytes 1310720 | tf_op jit(solution)/shard_map/order/pallas_call | solution.py:479
  27.1 3.6 %all-to-all-start.1 = ((bf16[16,48,128]{2,1,0:T(8,128)(2,1)}), bf16[16,48,128]{2,1,0:T(8,128)(2,1)S(1)}, u32[]{:S(2)}, u32[]{:S(2)}) async-start(bf16[16,48,128]{2,1,0:T(8,128)(2,1)} %get-tuple-element.45), calls=%async_computation.1 | async-start | bytes 393216 | tf_op jit(solution)/shard_map/all_to_all | solution.py:573
  30.7 1.9 %collective-permute-start.4 = (bf16[128,128]{1,0:T(8,128)(2,1)}, bf16[128,128]{1,0:T(8,128)(2,1)S(1)}, u32[]{:S(2)}, u32[]{:S(2)}) collective-permute-start(bf16[128,128]{1,0:T(8,128)(2,1)} %get-tuple-element.58), channel_id=1, source_target_pairs={{0,2},{2,0},{4,6},{6,4},{8,10},{10,8},{12,14},{14,12},{16,18},{18,... | collective-permute-start | bytes 98312 | tf_op jit(solution)/shard_map/ppermute | solution.py:574
  32.6 4.2 %collective-permute-start.5 = (bf16[128,128]{1,0:T(8,128)(2,1)}, bf16[128,128]{1,0:T(8,128)(2,1)S(1)}, u32[]{:S(2)}, u32[]{:S(2)}) collective-permute-start(bf16[128,128]{1,0:T(8,128)(2,1)} %get-tuple-element.43), channel_id=1, source_target_pairs={{0,30},{2,4},{4,2},{6,8},{8,6},{10,12},{12,10},{14,16},{16,14},{18... | collective-permute-start | bytes 98312 | tf_op jit(solution)/shard_map/ppermute | solution.py:562
  36.8 3.1 %begin.1 = (bf16[2,48,128]{2,1,0:T(8,128)(2,1)}, bf16[2,48,128]{2,1,0:T(8,128)(2,1)}, bf16[2,48,48]{2,1,0:T(8,128)(2,1)}, f32[48,128]{1,0:T(8,128)}, bf16[2,192,768]{2,1,0:T(8,128)(2,1)}) custom-call(bf16[1024,128]{1,0:T(8,128)(2,1)} %get-tuple-element.46.refs_0_.refs_4_, f32[1024,128]{1,0:T(8,128)} %get-tuple-element.47.refs_1_.refs_5_, ...), custom_call_target="tpu_custom_call" | custom-call | flops 67108864 | bytes 2204672 | tf_op jit(solution)/shard_map/begin/pallas_call | solution.py:479
  39.9 0.4 collective-permute-done.5.refs_9_.refs_12_.refs_10_
  40.3 2.8 %update.1 = (bf16[192,128]{1,0:T(8,128)(2,1)}, bf16[16,48,128]{2,1,0:T(8,128)(2,1)}) custom-call(bf16[16,48,128]{2,1,0:T(8,128)(2,1)S(1)} %all-to-all-done.1.refs_0_, bf16[2,192,768]{2,1,0:T(8,128)(2,1)} %get-tuple-element.51.refs_1_.refs_6_, f32[48,128]{1,0:T(8,128)} %get-tuple-element.52.refs_2_, bf16[2,48,48]{2,1,0:T(8,128)(2,1)} %get-tuple-element.53.refs_3_, ...), custom_call_target="tpu_custom_call" | custom-call | flops 16777216 | bytes 1311744 | tf_op jit(solution)/shard_map/update/pallas_call | solution.py:479
  43.2 5.6 %all-to-all-start.2 = ((bf16[16,48,128]{2,1,0:T(8,128)(2,1)}), bf16[16,48,128]{2,1,0:T(8,128)(2,1)S(1)}, u32[]{:S(2)}, u32[]{:S(2)}) async-start(bf16[16,48,128]{2,1,0:T(8,128)(2,1)} %get-tuple-element.59), calls=%async_computation.2 | async-start | bytes 393216 | tf_op jit(solution)/shard_map/all_to_all | solution.py:594
  48.7 7.5 %second_image.1 = (bf16[64,128]{1,0:T(8,128)(2,1)}, bf16[64,128]{1,0:T(8,128)(2,1)}, f32[2,512,128]{2,1,0:T(8,128)}, f32[2,512,128]{2,1,0:T(8,128)}) custom-call(bf16[2,512,1024]{2,1,0:T(8,128)(2,1)} %refs_0_.2, bf16[2,512,1024]{2,1,0:T(8,128)(2,1)S(1)} %collective-permute-done.2.refs_1_, bf16[2,512,1024]{2,1,0:T(8,128)(2,1)} %refs_2_.3, ...), custom_call_target="tpu_custom_call" | custom-call | flops 1073741824 | bytes 11552768 | tf_op jit(solution)/shard_map/second_image/pallas_call | solution.py:479
  56.3 0.1 collective-permute-start.6
  56.4 0.4 all-to-all-done.2.refs_0_
  56.8 2.2 %coarse.1 = bf16[16,48,128]{2,1,0:T(8,128)(2,1)} custom-call(bf16[16,48,128]{2,1,0:T(8,128)(2,1)S(1)} %all-to-all-done.2.refs_0_, bf16[2,96,768]{2,1,0:T(8,128)(2,1)} %get-tuple-element.64.refs_1_), custom_call_target="tpu_custom_call" | custom-call | flops 16777216 | bytes 688128 | tf_op jit(solution)/shard_map/coarse/pallas_call | solution.py:479
  59.0 6.5 %all-to-all-start.3 = ((bf16[16,48,128]{2,1,0:T(8,128)(2,1)}), bf16[16,48,128]{2,1,0:T(8,128)(2,1)S(1)}, u32[]{:S(2)}, u32[]{:S(2)}) async-start(bf16[16,48,128]{2,1,0:T(8,128)(2,1)} %coarse.1), calls=%async_computation.3 | async-start | bytes 393216 | tf_op jit(solution)/shard_map/all_to_all | solution.py:624
  65.5 1.9 %collective-permute-start.7 = (bf16[64,128]{1,0:T(8,128)(2,1)}, bf16[64,128]{1,0:T(8,128)(2,1)S(1)}, u32[]{:S(2)}, u32[]{:S(2)}) collective-permute-start(bf16[64,128]{1,0:T(8,128)(2,1)} %get-tuple-element.67), channel_id=1, source_target_pairs={{0,2},{2,0},{4,6},{6,4},{8,10},{10,8},{12,14},{14,12},{16,18},{18,... | collective-permute-start | bytes 49160 | tf_op jit(solution)/shard_map/ppermute | solution.py:625
  67.5 4.2 %collective-permute-start.8 = (bf16[64,128]{1,0:T(8,128)(2,1)}, bf16[64,128]{1,0:T(8,128)(2,1)S(1)}, u32[]{:S(2)}, u32[]{:S(2)}) collective-permute-start(bf16[64,128]{1,0:T(8,128)(2,1)} %get-tuple-element.62), channel_id=1, source_target_pairs={{0,30},{2,4},{4,2},{6,8},{8,6},{10,12},{12,10},{14,16},{16,14},{18... | collective-permute-start | bytes 49160 | tf_op jit(solution)/shard_map/ppermute | solution.py:614
  71.6 2.7 %base.1.refs_14_ = f32[2,2,512,128]{3,2,1,0:T(8,128)} custom-call(f32[2,512,128]{2,1,0:T(8,128)} %get-tuple-element.65.refs_0_, f32[2,512,128]{2,1,0:T(8,128)S(1)} %collective-permute-done.6.refs_1_), custom_call_target="tpu_custom_call" | custom-call | flops 16777216 | bytes 2097152 | tf_op jit(solution)/shard_map/base/pallas_call | solution.py:479
  74.3 1.2 %collective-permute-done.8.refs_4_ = bf16[64,128]{1,0:T(8,128)(2,1)S(1)} collective-permute-done((bf16[64,128]{1,0:T(8,128)(2,1)}, bf16[64,128]{1,0:T(8,128)(2,1)S(1)}, u32[]{:S(2)}, u32[]{:S(2)}) %collective-permute-start.8) | collective-permute-done | bytes 16416 | tf_op jit(solution)/shard_map/ppermute | solution.py:614
  75.5 0.5 collective-permute-start.10
  76.0 0.0 collective-permute-start.11
  76.0 1.0 %collective-permute-done.10.refs_3_ = bf16[64,128]{1,0:T(8,128)(2,1)S(1)} collective-permute-done((bf16[64,128]{1,0:T(8,128)(2,1)S(1)}, bf16[64,128]{1,0:T(8,128)(2,1)S(1)}, u32[]{:S(2)}, u32[]{:S(2)}) %collective-permute-start.10) | collective-permute-done | bytes 16416 | tf_op jit(solution)/shard_map/ppermute | solution.py:503
  77.0 0.2 collective-permute-done.11.refs_5_
  77.2 4.2 %last.1 = (f32[2,512,128]{2,1,0:T(8,128)}, f32[2,512,128]{2,1,0:T(8,128)}) custom-call(bf16[16,48,128]{2,1,0:T(8,128)(2,1)S(1)} %all-to-all-done.3.refs_0_, bf16[16,48,128]{2,1,0:T(8,128)(2,1)S(1)} %collective-permute-done.9.refs_1_, bf16[64,128]{1,0:T(8,128)(2,1)S(1)} %collective-permute-done.7.refs_2_, ...), custom_call_target="tpu_custom_call" | custom-call | flops 134217728 | bytes 3868672 | tf_op jit(solution)/shard_map/last/pallas_call | solution.py:479
  (9 shorter events, 0.0 us)
Async XLA Ops:
  0.6 2.0 %collective-permute-start.1 = (bf16[96,768]{1,0:T(8,128)(2,1)}, bf16[96,768]{1,0:T(8,128)(2,1)S(1)}, u32[]{:S(2)}, u32[]{:S(2)}) collective-permute-start(bf16[96,768]{1,0:T(8,128)(2,1)} %refs_0_.1), channel_id=1, source_target_pairs={{1,0},{0,1},{3,2},{2,3},{5,4},{4,5},{7,6},{6,7},{9,8},{8,9},{11,10... | collective-permute-start | bytes 442376 | tf_op jit(solution)/shard_map/ppermute | solution.py:503
  1.1 1.5 %collective-permute-start = (bf16[2,48,512]{2,1,0:T(8,128)(2,1)}, bf16[2,48,512]{2,1,0:T(8,128)(2,1)S(1)}, u32[]{:S(2)}, u32[]{:S(2)}) collective-permute-start(bf16[2,48,512]{2,1,0:T(8,128)(2,1)} %bitcast.1), channel_id=1, source_target_pairs={{1,0},{0,1},{3,2},{2,3},{5,4},{4,5},{7,6},{6,7},{9,8},{8,9},{11,10... | collective-permute-start | bytes 294920 | tf_op jit(solution)/shard_map/ppermute | solution.py:503
  2.7 10.9 %collective-permute-start.2 = (bf16[2,512,1024]{2,1,0:T(8,128)(2,1)}, bf16[2,512,1024]{2,1,0:T(8,128)(2,1)S(1)}, u32[]{:S(2)}, u32[]{:S(2)}) collective-permute-start(bf16[2,512,1024]{2,1,0:T(8,128)(2,1)} %refs_0_.2), channel_id=1, source_target_pairs={{1,0},{0,1},{3,2},{2,3},{5,4},{4,5},{7,6},{6,7},{9,8},{8,9},{11,10... | collective-permute-start | bytes 6291464 | tf_op jit(solution)/shard_map/ppermute | solution.py:503
  2.9 10.7 %collective-permute-start.3 = (bf16[2,512,1024]{2,1,0:T(8,128)(2,1)}, bf16[2,512,1024]{2,1,0:T(8,128)(2,1)}, u32[]{:S(2)}, u32[]{:S(2)}) collective-permute-start(bf16[2,512,1024]{2,1,0:T(8,128)(2,1)} %refs_2_.3), channel_id=1, source_target_pairs={{1,0},{0,1},{3,2},{2,3},{5,4},{4,5},{7,6},{6,7},{9,8},{8,9},{11,10... | collective-permute-start | bytes 6291464 | tf_op jit(solution)/shard_map/ppermute | solution.py:503
  5.5 18.4 %all-to-all-start = ((bf16[16,64,128]{2,1,0:T(8,128)(2,1)}), bf16[16,64,128]{2,1,0:T(8,128)(2,1)S(1)}, u32[]{:S(2)}, u32[]{:S(2)}) async-start(bf16[16,64,128]{2,1,0:T(8,128)(2,1)} %open.1), calls=%async_computation | async-start | bytes 524288 | tf_op jit(solution)/shard_map/all_to_all | solution.py:541
  27.1 13.2 %all-to-all-start.1 = ((bf16[16,48,128]{2,1,0:T(8,128)(2,1)}), bf16[16,48,128]{2,1,0:T(8,128)(2,1)S(1)}, u32[]{:S(2)}, u32[]{:S(2)}) async-start(bf16[16,48,128]{2,1,0:T(8,128)(2,1)} %get-tuple-element.45), calls=%async_computation.1 | async-start | bytes 393216 | tf_op jit(solution)/shard_map/all_to_all | solution.py:573
  30.7 9.2 %collective-permute-start.4 = (bf16[128,128]{1,0:T(8,128)(2,1)}, bf16[128,128]{1,0:T(8,128)(2,1)S(1)}, u32[]{:S(2)}, u32[]{:S(2)}) collective-permute-start(bf16[128,128]{1,0:T(8,128)(2,1)} %get-tuple-element.58), channel_id=1, source_target_pairs={{0,2},{2,0},{4,6},{6,4},{8,10},{10,8},{12,14},{14,12},{16,18},{18,... | collective-permute-start | bytes 98312 | tf_op jit(solution)/shard_map/ppermute | solution.py:574
  32.6 7.7 %collective-permute-start.5 = (bf16[128,128]{1,0:T(8,128)(2,1)}, bf16[128,128]{1,0:T(8,128)(2,1)S(1)}, u32[]{:S(2)}, u32[]{:S(2)}) collective-permute-start(bf16[128,128]{1,0:T(8,128)(2,1)} %get-tuple-element.43), channel_id=1, source_target_pairs={{0,30},{2,4},{4,2},{6,8},{8,6},{10,12},{12,10},{14,16},{16,14},{18... | collective-permute-start | bytes 98312 | tf_op jit(solution)/shard_map/ppermute | solution.py:562
  43.2 13.6 %all-to-all-start.2 = ((bf16[16,48,128]{2,1,0:T(8,128)(2,1)}), bf16[16,48,128]{2,1,0:T(8,128)(2,1)S(1)}, u32[]{:S(2)}, u32[]{:S(2)}) async-start(bf16[16,48,128]{2,1,0:T(8,128)(2,1)} %get-tuple-element.59), calls=%async_computation.2 | async-start | bytes 393216 | tf_op jit(solution)/shard_map/all_to_all | solution.py:594
  56.3 15.3 %collective-permute-start.6 = (f32[2,512,128]{2,1,0:T(8,128)}, f32[2,512,128]{2,1,0:T(8,128)S(1)}, u32[]{:S(2)}, u32[]{:S(2)}) collective-permute-start(f32[2,512,128]{2,1,0:T(8,128)} %get-tuple-element.66), channel_id=1, source_target_pairs={{0,1},{1,0},{2,3},{3,2},{4,5},{5,4},{6,7},{7,6},{8,9},{9,8},{10,11... | collective-permute-start | bytes 1572872 | tf_op jit(solution)/shard_map/ppermute | solution.py:628
  59.0 16.5 %all-to-all-start.3 = ((bf16[16,48,128]{2,1,0:T(8,128)(2,1)}), bf16[16,48,128]{2,1,0:T(8,128)(2,1)S(1)}, u32[]{:S(2)}, u32[]{:S(2)}) async-start(bf16[16,48,128]{2,1,0:T(8,128)(2,1)} %coarse.1), calls=%async_computation.3 | async-start | bytes 393216 | tf_op jit(solution)/shard_map/all_to_all | solution.py:624
  65.5 8.8 %collective-permute-start.7 = (bf16[64,128]{1,0:T(8,128)(2,1)}, bf16[64,128]{1,0:T(8,128)(2,1)S(1)}, u32[]{:S(2)}, u32[]{:S(2)}) collective-permute-start(bf16[64,128]{1,0:T(8,128)(2,1)} %get-tuple-element.67), channel_id=1, source_target_pairs={{0,2},{2,0},{4,6},{6,4},{8,10},{10,8},{12,14},{14,12},{16,18},{18,... | collective-permute-start | bytes 49160 | tf_op jit(solution)/shard_map/ppermute | solution.py:625
  67.5 8.1 %collective-permute-start.8 = (bf16[64,128]{1,0:T(8,128)(2,1)}, bf16[64,128]{1,0:T(8,128)(2,1)S(1)}, u32[]{:S(2)}, u32[]{:S(2)}) collective-permute-start(bf16[64,128]{1,0:T(8,128)(2,1)} %get-tuple-element.62), channel_id=1, source_target_pairs={{0,30},{2,4},{4,2},{6,8},{8,6},{10,12},{12,10},{14,16},{16,14},{18... | collective-permute-start | bytes 49160 | tf_op jit(solution)/shard_map/ppermute | solution.py:614
  75.5 1.7 %collective-permute-start.9 = (bf16[16,48,128]{2,1,0:T(8,128)(2,1)S(1)}, bf16[16,48,128]{2,1,0:T(8,128)(2,1)S(1)}, u32[]{:S(2)}, u32[]{:S(2)}) collective-permute-start(bf16[16,48,128]{2,1,0:T(8,128)(2,1)S(1)} %all-to-all-done.3.refs_0_), channel_id=1, source_target_pairs={{1,0},{0,1},{3,2},{2,3},{5,4},{4,5},{7,6},{6,7},{9,8},{8,9},{11,10... | collective-permute-start | bytes 589832 | tf_op jit(solution)/shard_map/ppermute | solution.py:503
  75.5 1.5 %collective-permute-start.10 = (bf16[64,128]{1,0:T(8,128)(2,1)S(1)}, bf16[64,128]{1,0:T(8,128)(2,1)S(1)}, u32[]{:S(2)}, u32[]{:S(2)}) collective-permute-start(bf16[64,128]{1,0:T(8,128)(2,1)S(1)} %collective-permute-done.7.refs_2_), channel_id=1, source_target_pairs={{1,0},{0,1},{3,2},{2,3},{5,4},{4,5},{7,6},{6,7},{9,8},{8,9},{11,10... | collective-permute-start | bytes 49160 | tf_op jit(solution)/shard_map/ppermute | solution.py:503
  76.0 1.2 %collective-permute-start.11 = (bf16[64,128]{1,0:T(8,128)(2,1)S(1)}, bf16[64,128]{1,0:T(8,128)(2,1)S(1)}, u32[]{:S(2)}, u32[]{:S(2)}) collective-permute-start(bf16[64,128]{1,0:T(8,128)(2,1)S(1)} %collective-permute-done.8.refs_4_), channel_id=1, source_target_pairs={{1,0},{0,1},{3,2},{2,3},{5,4},{4,5},{7,6},{6,7},{9,8},{8,9},{11,10... | collective-permute-start | bytes 49160 | tf_op jit(solution)/shard_map/ppermute | solution.py:503

commit v20 on v18

--- a/solution.py
+++ b/solution.py
@@ -496,10 +496,10 @@
     z = Sizes(loads, stiffness, coarse_basis, coarse_inverse, left_rows)
     n, group, subs, rows, lanes, modes, face = z.n, z.group, z.subs, z.rows, z.lanes, z.modes, z.face
     basis_pieces = pieces_of(jnp.swapaxes(coarse_basis, 1, 2), group)
+    basis_pieces, coarse_inverse, local_inverse, stiffness = lax.optimization_barrier(
+        (basis_pieces, coarse_inverse, local_inverse, stiffness)
+    )
     inverse_columns = pieces_of(coarse_inverse, group)
-    basis_pieces, inverse_columns, local_inverse, stiffness = lax.optimization_barrier(
-        (basis_pieces, inverse_columns, local_inverse, stiffness)
-    )
     column = np.arange(z.columns)
     repeat = jnp.asarray(np.arange(lanes)[:, None] == column[None, :] % modes, BF16)
     own_row = jnp.asarray(np.arange(n)[:, None] == column[None, :] // modes, F32)
@@ -547,8 +547,8 @@
         loose=[*arrivals, *range(2 * group + 1, 3 * group)],
         name="first_image",
     )
-    second_got = lax.ppermute(second_pair, "sub", second_pairs)
-    restricted, second_pair = lax.optimization_barrier((restricted, second_pair))
+    first_got = lax.ppermute(first_pair, "sub", first_pairs)
+    restricted, first_pair = lax.optimization_barrier((restricted, first_pair))
     near = (subs + 2) * modes
     ordered_inverse, index, message = call(
         functools.partial(order_kernel, z),
@@ -559,7 +559,7 @@
         name="order",
     )
     coarse = spread(message)
-    first_got = lax.ppermute(first_pair, "sub", first_pairs)
+    second_got = lax.ppermute(second_pair, "sub", second_pairs)
     side = shape((subs, modes, face), BF16)
     left_t, right_t, inner, start_modes, picks = call(
         functools.partial(begin_kernel, z),
@@ -599,8 +599,8 @@
         loose=[*arrivals, 2 * group + 7, 2 * group + 8],
         name="second_image",
     )
-    second_got = lax.ppermute(second_pair, "sub", second_pairs)
-    restricted, second_pair = lax.optimization_barrier((restricted, second_pair))
+    first_got = lax.ppermute(first_pair, "sub", first_pairs)
+    restricted, first_pair = lax.optimization_barrier((restricted, first_pair))
     (message,) = call(
         functools.partial(coarse_kernel, z),
         [copies],
@@ -610,7 +610,7 @@
         name="coarse",
     )
     coarse = spread(message)
-    first_got = lax.ppermute(first_pair, "sub", first_pairs)
+    second_got = lax.ppermute(second_pair, "sub", second_pairs)
     swapped = [values[0]]
     for k in range(1, group):
         swapped.append(lax.ppermute(values[k], GROUP, [(g, (g + k) % group) for g in range(group)]))

time: 82.1 us -> 81.3 us (level)
  starting transfers between devices: 37.6 us -> 35.5 us
  waiting for transfers between devices: 8.2 us -> 9.48 us
    ppermute x2, starting transfers between devices: 3.86 us -> 0.01 us  [body(): first_got = lax.ppermute(first_pair, 'sub', first_pairs)]
    ppermute x2, starting transfers between devices: 8.32 us -> 11.1 us  [body(): second_got = lax.ppermute(second_pair, 'sub', second_pairs)]
    ppermute x2, waiting for transfers between devices: 1.62 us -> 3.47 us  [body(): second_got = lax.ppermute(second_pair, 'sub', second_pairs)]
    all_to_all x2, starting transfers between devices: 13.6 us -> 12.5 us  [body(): restricted = spread(message)]
  transfers between devices with their start and end apart: 16 -> 16, of which waited for: 7 -> 7; matrix products, arithmetic and copies ran while one was open for 0% -> 0% of each run, Pallas kernels for 30% -> 31%
where the time goes in v20:
time: 81.3 us; the launch traced here: 80.6 us
  starting transfers between devices  35.5 us (44%)
  Pallas kernels  34.9 us (43%)
  waiting for transfers between devices  9.48 us (12%)
    pallas_call x9, Pallas kernels, call(): pl.pallas_call(whole, out_shape=[pltpu.HBM(o.shape, o.dtype) for o in out...  34.9 us
    all_to_all x2, starting transfers between devices, body(): restricted = spread(message)  12.5 us
    ppermute x2, starting transfers between devices, body(): second_got = lax.ppermute(second_pair, 'sub', second_pairs)  11.1 us
    all_to_all x2, starting transfers between devices, body(): coarse = spread(message)  10.1 us
    all_to_all x2, waiting for transfers between devices, body(): restricted = spread(message)  3.72 us
    ppermute x2, waiting for transfers between devices, body(): second_got = lax.ppermute(second_pair, 'sub', second_pairs)  3.47 us
    ppermute x7, waiting for transfers between devices, pieces_of(): lax.ppermute(block, GROUP, [((g + k) % group, g) for g in range(group)])  2.28 us
    ppermute x7, starting transfers between devices, pieces_of(): lax.ppermute(block, GROUP, [((g + k) % group, g) for g in range(group)])  1.68 us
  transfers between devices with their start and end apart: 16, of which 7 were waited for; matrix products, arithmetic and copies ran while one was open for 0% of the time, Pallas kernels for 31%

profile of v20, /device:TPU:0, one launch (start us, length us, event | category | flops | bytes accessed | tf_op | source)
XLA Modules:
  0.0 80.6 jit_solution(653456670598983360)
XLA Ops:
  0.6 0.5 collective-permute-start
  1.1 1.2 %collective-permute-done.refs_1_.refs_5_ = bf16[2,48,512]{2,1,0:T(8,128)(2,1)S(1)} collective-permute-done((bf16[2,48,512]{2,1,0:T(8,128)(2,1)}, bf16[2,48,512]{2,1,0:T(8,128)(2,1)S(1)}, u32[]{:S(2)}, u32[]{:S(2)}) %collective-permute-start) | collective-permute-done | bytes 98336 | tf_op jit(solution)/shard_map/ppermute | solution.py:491
  2.3 0.4 collective-permute-start.2
  2.7 0.2 collective-permute-start.3
  2.8 2.3 %open.1 = bf16[16,64,128]{2,1,0:T(8,128)(2,1)} custom-call(bf16[2,48,512]{2,1,0:T(8,128)(2,1)} %bitcast.2, bf16[2,48,512]{2,1,0:T(8,128)(2,1)S(1)} %collective-permute-done.refs_1_.refs_5_, bf16[2,1024,128]{2,1,0:T(8,128)(2,1)} %refs_6_.1, s32[2,48]{1,0:T(2,128)} %refs_3_.2), custom_call_target="tpu_custom_call" | custom-call | flops 67108864 | bytes 983424 | tf_op jit(solution)/shard_map/open/pallas_call | solution.py:467
  5.1 8.2 %all-to-all-start = ((bf16[16,64,128]{2,1,0:T(8,128)(2,1)}), bf16[16,64,128]{2,1,0:T(8,128)(2,1)S(1)}, u32[]{:S(2)}, u32[]{:S(2)}) async-start(bf16[16,64,128]{2,1,0:T(8,128)(2,1)} %open.1), calls=%async_computation | async-start | bytes 524288 | tf_op jit(solution)/shard_map/all_to_all | solution.py:529
  13.3 0.1 collective-permute-start.1
  13.4 0.0 collective-permute-done.2.refs_1_
  13.4 0.0 collective-permute-done.3.refs_3_
  13.4 6.8 %first_image.1 = (bf16[1024,128]{1,0:T(8,128)(2,1)}, f32[1024,128]{1,0:T(8,128)}, f32[1024,128]{1,0:T(8,128)}, bf16[2,128,128]{2,1,0:T(8,128)(2,1)}, bf16[2,128,...) custom-call(bf16[2,512,1024]{2,1,0:T(8,128)(2,1)} %refs_0_.2, ...), custom_call_target="tpu_custom_call" | custom-call | flops 1073741824 | bytes 11339776 | tf_op jit(solution)/shard_map/first_image/pallas_call | solution.py:467
  20.2 3.3 %all-to-all-done.refs_2_ = bf16[16,64,128]{2,1,0:T(8,128)(2,1)S(1)} async-done(((bf16[16,64,128]{2,1,0:T(8,128)(2,1)}), bf16[16,64,128]{2,1,0:T(8,128)(2,1)S(1)}, u32[]{:S(2)}, u32[]{:S(2)}) %all-to-all-start) | async-done | bytes 262176 | tf_op jit(solution)/shard_map/all_to_all | solution.py:529
  23.5 3.2 %order.1 = (bf16[2,96,768]{2,1,0:T(8,128)(2,1)}, f32[2,16,128]{2,1,0:T(8,128)}, bf16[16,48,128]{2,1,0:T(8,128)(2,1)}) custom-call(bf16[96,768]{1,0:T(8,128)(2,1)} %refs_0_.1, bf16[96,768]{1,0:T(8,128)(2,1)S(1)} %collective-permute-done.1.refs_1_, bf16[16,64,128]{2,1,0:T(8,128)(2,1)S(1)} %all-to-all-done.refs_2_, bf16[128,768]{1,0:T(8,128)(2,1)} %constant.6.clone.refs_3_, ...), custom_call_target="tpu_custom_call" | custom-call | flops 452984832 | bytes 1310720 | tf_op jit(solution)/shard_map/order/pallas_call | solution.py:467
  26.8 3.6 %all-to-all-start.1 = ((bf16[16,48,128]{2,1,0:T(8,128)(2,1)}), bf16[16,48,128]{2,1,0:T(8,128)(2,1)S(1)}, u32[]{:S(2)}, u32[]{:S(2)}) async-start(bf16[16,48,128]{2,1,0:T(8,128)(2,1)} %get-tuple-element.43), calls=%async_computation.1 | async-start | bytes 393216 | tf_op jit(solution)/shard_map/all_to_all | solution.py:561
  30.4 5.5 %collective-permute-start.5 = (bf16[128,128]{1,0:T(8,128)(2,1)}, bf16[128,128]{1,0:T(8,128)(2,1)S(1)}, u32[]{:S(2)}, u32[]{:S(2)}) collective-permute-start(bf16[128,128]{1,0:T(8,128)(2,1)} %get-tuple-element.56), channel_id=1, source_target_pairs={{0,30},{2,4},{4,2},{6,8},{8,6},{10,12},{12,10},{14,16},{16,14},{18... | collective-permute-start | bytes 98312 | tf_op jit(solution)/shard_map/ppermute | solution.py:562
  35.9 3.1 %begin.1 = (bf16[2,48,128]{2,1,0:T(8,128)(2,1)}, bf16[2,48,128]{2,1,0:T(8,128)(2,1)}, bf16[2,48,48]{2,1,0:T(8,128)(2,1)}, f32[48,128]{1,0:T(8,128)}, bf16[2,192,768]{2,1,0:T(8,128)(2,1)}) custom-call(bf16[1024,128]{1,0:T(8,128)(2,1)} %get-tuple-element.44.refs_0_.refs_4_, f32[1024,128]{1,0:T(8,128)} %get-tuple-element.45.refs_1_.refs_5_, ...), custom_call_target="tpu_custom_call" | custom-call | flops 67108864 | bytes 2204672 | tf_op jit(solution)/shard_map/begin/pallas_call | solution.py:467
  39.1 1.7 %collective-permute-done.5.refs_9_.refs_12_.refs_10_ = bf16[128,128]{1,0:T(8,128)(2,1)S(1)} collective-permute-done((bf16[128,128]{1,0:T(8,128)(2,1)}, bf16[128,128]{1,0:T(8,128)(2,1)S(1)}, u32[]{:S(2)}, u32[]{:S(2)}) %collective-permute-start.5) | collective-permute-done | bytes 32800 | tf_op jit(solution)/shard_map/ppermute | solution.py:562
  40.8 2.8 %update.1 = (bf16[192,128]{1,0:T(8,128)(2,1)}, bf16[16,48,128]{2,1,0:T(8,128)(2,1)}) custom-call(bf16[16,48,128]{2,1,0:T(8,128)(2,1)S(1)} %all-to-all-done.1.refs_0_, bf16[2,192,768]{2,1,0:T(8,128)(2,1)} %get-tuple-element.49.refs_1_.refs_6_, f32[48,128]{1,0:T(8,128)} %get-tuple-element.50.refs_2_, bf16[2,48,48]{2,1,0:T(8,128)(2,1)} %get-tuple-element.51.refs_3_, ...), custom_call_target="tpu_custom_call" | custom-call | flops 16777216 | bytes 1311744 | tf_op jit(solution)/shard_map/update/pallas_call | solution.py:467
  43.6 4.3 %all-to-all-start.2 = ((bf16[16,48,128]{2,1,0:T(8,128)(2,1)}), bf16[16,48,128]{2,1,0:T(8,128)(2,1)S(1)}, u32[]{:S(2)}, u32[]{:S(2)}) async-start(bf16[16,48,128]{2,1,0:T(8,128)(2,1)} %get-tuple-element.57), calls=%async_computation.2 | async-start | bytes 393216 | tf_op jit(solution)/shard_map/all_to_all | solution.py:582
  47.9 7.5 %second_image.1 = (bf16[64,128]{1,0:T(8,128)(2,1)}, bf16[64,128]{1,0:T(8,128)(2,1)}, f32[2,512,128]{2,1,0:T(8,128)}, f32[2,512,128]{2,1,0:T(8,128)}) custom-call(bf16[2,512,1024]{2,1,0:T(8,128)(2,1)} %refs_0_.2, bf16[2,512,1024]{2,1,0:T(8,128)(2,1)S(1)} %collective-permute-done.2.refs_1_, bf16[2,512,1024]{2,1,0:T(8,128)(2,1)} %refs_2_.3, ...), custom_call_target="tpu_custom_call" | custom-call | flops 1073741824 | bytes 11552768 | tf_op jit(solution)/shard_map/second_image/pallas_call | solution.py:467
  55.5 0.1 collective-permute-start.6
  55.6 0.4 all-to-all-done.2.refs_0_
  56.0 2.2 %coarse.1 = bf16[16,48,128]{2,1,0:T(8,128)(2,1)} custom-call(bf16[16,48,128]{2,1,0:T(8,128)(2,1)S(1)} %all-to-all-done.2.refs_0_, bf16[2,96,768]{2,1,0:T(8,128)(2,1)} %get-tuple-element.62.refs_1_), custom_call_target="tpu_custom_call" | custom-call | flops 16777216 | bytes 688128 | tf_op jit(solution)/shard_map/coarse/pallas_call | solution.py:467
  58.2 6.5 %all-to-all-start.3 = ((bf16[16,48,128]{2,1,0:T(8,128)(2,1)}), bf16[16,48,128]{2,1,0:T(8,128)(2,1)S(1)}, u32[]{:S(2)}, u32[]{:S(2)}) async-start(bf16[16,48,128]{2,1,0:T(8,128)(2,1)} %coarse.1), calls=%async_computation.3 | async-start | bytes 393216 | tf_op jit(solution)/shard_map/all_to_all | solution.py:612
  64.7 5.5 %collective-permute-start.8 = (bf16[64,128]{1,0:T(8,128)(2,1)}, bf16[64,128]{1,0:T(8,128)(2,1)S(1)}, u32[]{:S(2)}, u32[]{:S(2)}) collective-permute-start(bf16[64,128]{1,0:T(8,128)(2,1)} %get-tuple-element.65), channel_id=1, source_target_pairs={{0,30},{2,4},{4,2},{6,8},{8,6},{10,12},{12,10},{14,16},{16,14},{18... | collective-permute-start | bytes 49160 | tf_op jit(solution)/shard_map/ppermute | solution.py:613
  70.2 0.0 collective-permute-start.7
  70.2 2.7 %base.1.refs_14_ = f32[2,2,512,128]{3,2,1,0:T(8,128)} custom-call(f32[2,512,128]{2,1,0:T(8,128)} %get-tuple-element.63.refs_0_, f32[2,512,128]{2,1,0:T(8,128)S(1)} %collective-permute-done.6.refs_1_), custom_call_target="tpu_custom_call" | custom-call | flops 16777216 | bytes 2097152 | tf_op jit(solution)/shard_map/base/pallas_call | solution.py:467
  72.9 1.8 %collective-permute-done.8.refs_4_ = bf16[64,128]{1,0:T(8,128)(2,1)S(1)} collective-permute-done((bf16[64,128]{1,0:T(8,128)(2,1)}, bf16[64,128]{1,0:T(8,128)(2,1)S(1)}, u32[]{:S(2)}, u32[]{:S(2)}) %collective-permute-start.8) | collective-permute-done | bytes 16416 | tf_op jit(solution)/shard_map/ppermute | solution.py:613
  74.7 0.5 collective-permute-start.10
  75.2 0.1 collective-permute-start.11
  75.3 0.9 %collective-permute-done.10.refs_3_ = bf16[64,128]{1,0:T(8,128)(2,1)S(1)} collective-permute-done((bf16[64,128]{1,0:T(8,128)(2,1)S(1)}, bf16[64,128]{1,0:T(8,128)(2,1)S(1)}, u32[]{:S(2)}, u32[]{:S(2)}) %collective-permute-start.10) | collective-permute-done | bytes 16416 | tf_op jit(solution)/shard_map/ppermute | solution.py:491
  76.2 0.2 collective-permute-done.11.refs_5_
  76.4 4.2 %last.1 = (f32[2,512,128]{2,1,0:T(8,128)}, f32[2,512,128]{2,1,0:T(8,128)}) custom-call(bf16[16,48,128]{2,1,0:T(8,128)(2,1)S(1)} %all-to-all-done.3.refs_0_, bf16[16,48,128]{2,1,0:T(8,128)(2,1)S(1)} %collective-permute-done.9.refs_1_, bf16[64,128]{1,0:T(8,128)(2,1)S(1)} %collective-permute-done.7.refs_2_, ...), custom_call_target="tpu_custom_call" | custom-call | flops 134217728 | bytes 3868672 | tf_op jit(solution)/shard_map/last/pallas_call | solution.py:467
  (9 shorter events, 0.0 us)
Async XLA Ops:
  0.6 1.7 %collective-permute-start = (bf16[2,48,512]{2,1,0:T(8,128)(2,1)}, bf16[2,48,512]{2,1,0:T(8,128)(2,1)S(1)}, u32[]{:S(2)}, u32[]{:S(2)}) collective-permute-start(bf16[2,48,512]{2,1,0:T(8,128)(2,1)} %bitcast.1), channel_id=1, source_target_pairs={{1,0},{0,1},{3,2},{2,3},{5,4},{4,5},{7,6},{6,7},{9,8},{8,9},{11,10... | collective-permute-start | bytes 294920 | tf_op jit(solution)/shard_map/ppermute | solution.py:491
  2.3 11.1 %collective-permute-start.2 = (bf16[2,512,1024]{2,1,0:T(8,128)(2,1)}, bf16[2,512,1024]{2,1,0:T(8,128)(2,1)S(1)}, u32[]{:S(2)}, u32[]{:S(2)}) collective-permute-start(bf16[2,512,1024]{2,1,0:T(8,128)(2,1)} %refs_0_.2), channel_id=1, source_target_pairs={{1,0},{0,1},{3,2},{2,3},{5,4},{4,5},{7,6},{6,7},{9,8},{8,9},{11,10... | collective-permute-start | bytes 6291464 | tf_op jit(solution)/shard_map/ppermute | solution.py:491
  2.7 10.8 %collective-permute-start.3 = (bf16[2,512,1024]{2,1,0:T(8,128)(2,1)}, bf16[2,512,1024]{2,1,0:T(8,128)(2,1)}, u32[]{:S(2)}, u32[]{:S(2)}) collective-permute-start(bf16[2,512,1024]{2,1,0:T(8,128)(2,1)} %refs_2_.3), channel_id=1, source_target_pairs={{1,0},{0,1},{3,2},{2,3},{5,4},{4,5},{7,6},{6,7},{9,8},{8,9},{11,10... | collective-permute-start | bytes 6291464 | tf_op jit(solution)/shard_map/ppermute | solution.py:491
  5.1 18.4 %all-to-all-start = ((bf16[16,64,128]{2,1,0:T(8,128)(2,1)}), bf16[16,64,128]{2,1,0:T(8,128)(2,1)S(1)}, u32[]{:S(2)}, u32[]{:S(2)}) async-start(bf16[16,64,128]{2,1,0:T(8,128)(2,1)} %open.1), calls=%async_computation | async-start | bytes 524288 | tf_op jit(solution)/shard_map/all_to_all | solution.py:529
  13.3 10.2 %collective-permute-start.1 = (bf16[96,768]{1,0:T(8,128)(2,1)}, bf16[96,768]{1,0:T(8,128)(2,1)S(1)}, u32[]{:S(2)}, u32[]{:S(2)}) collective-permute-start(bf16[96,768]{1,0:T(8,128)(2,1)} %refs_0_.1), channel_id=1, source_target_pairs={{1,0},{0,1},{3,2},{2,3},{5,4},{4,5},{7,6},{6,7},{9,8},{8,9},{11,10... | collective-permute-start | bytes 442376 | tf_op jit(solution)/shard_map/ppermute | solution.py:491
  26.8 14.0 %all-to-all-start.1 = ((bf16[16,48,128]{2,1,0:T(8,128)(2,1)}), bf16[16,48,128]{2,1,0:T(8,128)(2,1)S(1)}, u32[]{:S(2)}, u32[]{:S(2)}) async-start(bf16[16,48,128]{2,1,0:T(8,128)(2,1)} %get-tuple-element.43), calls=%async_computation.1 | async-start | bytes 393216 | tf_op jit(solution)/shard_map/all_to_all | solution.py:561
  30.4 10.4 %collective-permute-start.5 = (bf16[128,128]{1,0:T(8,128)(2,1)}, bf16[128,128]{1,0:T(8,128)(2,1)S(1)}, u32[]{:S(2)}, u32[]{:S(2)}) collective-permute-start(bf16[128,128]{1,0:T(8,128)(2,1)} %get-tuple-element.56), channel_id=1, source_target_pairs={{0,30},{2,4},{4,2},{6,8},{8,6},{10,12},{12,10},{14,16},{16,14},{18... | collective-permute-start | bytes 98312 | tf_op jit(solution)/shard_map/ppermute | solution.py:562
  35.9 4.8 %collective-permute-start.4 = (bf16[128,128]{1,0:T(8,128)(2,1)}, bf16[128,128]{1,0:T(8,128)(2,1)S(1)}, u32[]{:S(2)}, u32[]{:S(2)}) collective-permute-start(bf16[128,128]{1,0:T(8,128)(2,1)} %get-tuple-element.41), channel_id=1, source_target_pairs={{0,2},{2,0},{4,6},{6,4},{8,10},{10,8},{12,14},{14,12},{16,18},{18,... | collective-permute-start | bytes 98312 | tf_op jit(solution)/shard_map/ppermute | solution.py:550
  43.6 12.4 %all-to-all-start.2 = ((bf16[16,48,128]{2,1,0:T(8,128)(2,1)}), bf16[16,48,128]{2,1,0:T(8,128)(2,1)S(1)}, u32[]{:S(2)}, u32[]{:S(2)}) async-start(bf16[16,48,128]{2,1,0:T(8,128)(2,1)} %get-tuple-element.57), calls=%async_computation.2 | async-start | bytes 393216 | tf_op jit(solution)/shard_map/all_to_all | solution.py:582
  55.5 14.8 %collective-permute-start.6 = (f32[2,512,128]{2,1,0:T(8,128)}, f32[2,512,128]{2,1,0:T(8,128)S(1)}, u32[]{:S(2)}, u32[]{:S(2)}) collective-permute-start(f32[2,512,128]{2,1,0:T(8,128)} %get-tuple-element.64), channel_id=1, source_target_pairs={{0,1},{1,0},{2,3},{3,2},{4,5},{5,4},{6,7},{7,6},{8,9},{9,8},{10,11... | collective-permute-start | bytes 1572872 | tf_op jit(solution)/shard_map/ppermute | solution.py:616
  58.2 16.5 %all-to-all-start.3 = ((bf16[16,48,128]{2,1,0:T(8,128)(2,1)}), bf16[16,48,128]{2,1,0:T(8,128)(2,1)S(1)}, u32[]{:S(2)}, u32[]{:S(2)}) async-start(bf16[16,48,128]{2,1,0:T(8,128)(2,1)} %coarse.1), calls=%async_computation.3 | async-start | bytes 393216 | tf_op jit(solution)/shard_map/all_to_all | solution.py:612
  64.7 10.0 %collective-permute-start.8 = (bf16[64,128]{1,0:T(8,128)(2,1)}, bf16[64,128]{1,0:T(8,128)(2,1)S(1)}, u32[]{:S(2)}, u32[]{:S(2)}) collective-permute-start(bf16[64,128]{1,0:T(8,128)(2,1)} %get-tuple-element.65), channel_id=1, source_target_pairs={{0,30},{2,4},{4,2},{6,8},{8,6},{10,12},{12,10},{14,16},{16,14},{18... | collective-permute-start | bytes 49160 | tf_op jit(solution)/shard_map/ppermute | solution.py:613
  70.2 4.5 %collective-permute-start.7 = (bf16[64,128]{1,0:T(8,128)(2,1)}, bf16[64,128]{1,0:T(8,128)(2,1)S(1)}, u32[]{:S(2)}, u32[]{:S(2)}) collective-permute-start(bf16[64,128]{1,0:T(8,128)(2,1)} %get-tuple-element.60), channel_id=1, source_target_pairs={{0,2},{2,0},{4,6},{6,4},{8,10},{10,8},{12,14},{14,12},{16,18},{18,... | collective-permute-start | bytes 49160 | tf_op jit(solution)/shard_map/ppermute | solution.py:602
  74.7 1.7 %collective-permute-start.9 = (bf16[16,48,128]{2,1,0:T(8,128)(2,1)S(1)}, bf16[16,48,128]{2,1,0:T(8,128)(2,1)S(1)}, u32[]{:S(2)}, u32[]{:S(2)}) collective-permute-start(bf16[16,48,128]{2,1,0:T(8,128)(2,1)S(1)} %all-to-all-done.3.refs_0_), channel_id=1, source_target_pairs={{1,0},{0,1},{3,2},{2,3},{5,4},{4,5},{7,6},{6,7},{9,8},{8,9},{11,10... | collective-permute-start | bytes 589832 | tf_op jit(solution)/shard_map/ppermute | solution.py:491
  74.7 1.5 %collective-permute-start.10 = (bf16[64,128]{1,0:T(8,128)(2,1)S(1)}, bf16[64,128]{1,0:T(8,128)(2,1)S(1)}, u32[]{:S(2)}, u32[]{:S(2)}) collective-permute-start(bf16[64,128]{1,0:T(8,128)(2,1)S(1)} %collective-permute-done.7.refs_2_), channel_id=1, source_target_pairs={{1,0},{0,1},{3,2},{2,3},{5,4},{4,5},{7,6},{6,7},{9,8},{8,9},{11,10... | collective-permute-start | bytes 49160 | tf_op jit(solution)/shard_map/ppermute | solution.py:491
  75.2 1.2 %collective-permute-start.11 = (bf16[64,128]{1,0:T(8,128)(2,1)S(1)}, bf16[64,128]{1,0:T(8,128)(2,1)S(1)}, u32[]{:S(2)}, u32[]{:S(2)}) collective-permute-start(bf16[64,128]{1,0:T(8,128)(2,1)S(1)} %collective-permute-done.8.refs_4_), channel_id=1, source_target_pairs={{1,0},{0,1},{3,2},{2,3},{5,4},{4,5},{7,6},{6,7},{9,8},{8,9},{11,10... | collective-permute-start | bytes 49160 | tf_op jit(solution)/shard_map/ppermute | solution.py:491

commit v21 on v20

--- a/solution.py
+++ b/solution.py
@@ -623,7 +623,7 @@
         loose=range(1, group),
         name="base",
     )
-    coarse, base, first_got, second_got = lax.optimization_barrier((coarse, base, first_got, second_got))
+    base, first_got, second_got = lax.optimization_barrier((base, first_got, second_got))
     out = shape((subs, z.own, z.cases), F32)
     return tuple(
         call(

time: 81.3 us -> 86.5 us (1.064)
  waiting for transfers between devices: 9.48 us -> 18.1 us
  starting transfers between devices: 35.5 us -> 32 us
    all_to_all x2, waiting for transfers between devices: 0.01 us -> 8.01 us  [body(): coarse = spread(message)]
    ppermute x2, starting transfers between devices: 11.1 us -> 7.27 us  [body(): second_got = lax.ppermute(second_pair, 'sub', second_pairs)]
  transfers between devices with their start and end apart: 16 -> 16, of which waited for: 7 -> 8; matrix products, arithmetic and copies ran while one was open for 0% -> 0% of each run, Pallas kernels for 31% -> 26%
where the time goes in v21:
time: 86.5 us; the launch traced here: 85.8 us
  Pallas kernels  34.9 us (40%)
  starting transfers between devices  32 us (37%)
  waiting for transfers between devices  18.1 us (21%)
    pallas_call x9, Pallas kernels, call(): pl.pallas_call(whole, out_shape=[pltpu.HBM(o.shape, o.dtype) for o in out...  34.9 us
    all_to_all x2, starting transfers between devices, body(): restricted = spread(message)  12.5 us
    all_to_all x2, starting transfers between devices, body(): coarse = spread(message)  10 us
    all_to_all x2, waiting for transfers between devices, body(): coarse = spread(message)  8.01 us
    ppermute x2, starting transfers between devices, body(): second_got = lax.ppermute(second_pair, 'sub', second_pairs)  7.27 us
    ppermute x2, waiting for transfers between devices, body(): second_got = lax.ppermute(second_pair, 'sub', second_pairs)  4.28 us
    all_to_all x2, waiting for transfers between devices, body(): restricted = spread(message)  3.8 us
    ppermute x7, waiting for transfers between devices, pieces_of(): lax.ppermute(block, GROUP, [((g + k) % group, g) for g in range(group)])  2 us
  transfers between devices with their start and end apart: 16, of which 8 were waited for; matrix products, arithmetic and copies ran while one was open for 0% of the time, Pallas kernels for 26%

profile of v21, /device:TPU:0, one launch (start us, length us, event | category | flops | bytes accessed | tf_op | source)
XLA Modules:
  0.0 85.8 jit_solution(3804152706811226221)
XLA Ops:
  0.6 0.5 collective-permute-start
  1.1 1.2 %collective-permute-done.refs_1_.refs_5_ = bf16[2,48,512]{2,1,0:T(8,128)(2,1)S(1)} collective-permute-done((bf16[2,48,512]{2,1,0:T(8,128)(2,1)}, bf16[2,48,512]{2,1,0:T(8,128)(2,1)S(1)}, u32[]{:S(2)}, u32[]{:S(2)}) %collective-permute-start) | collective-permute-done | bytes 98336 | tf_op jit(solution)/shard_map/ppermute | solution.py:491
  2.3 0.4 collective-permute-start.2
  2.7 0.2 collective-permute-start.3
  2.8 2.3 %open.1 = bf16[16,64,128]{2,1,0:T(8,128)(2,1)} custom-call(bf16[2,48,512]{2,1,0:T(8,128)(2,1)} %bitcast.2, bf16[2,48,512]{2,1,0:T(8,128)(2,1)S(1)} %collective-permute-done.refs_1_.refs_5_, bf16[2,1024,128]{2,1,0:T(8,128)(2,1)} %refs_6_.1, s32[2,48]{1,0:T(2,128)} %refs_3_.2), custom_call_target="tpu_custom_call" | custom-call | flops 67108864 | bytes 983424 | tf_op jit(solution)/shard_map/open/pallas_call | solution.py:467
  5.1 8.2 %all-to-all-start = ((bf16[16,64,128]{2,1,0:T(8,128)(2,1)}), bf16[16,64,128]{2,1,0:T(8,128)(2,1)S(1)}, u32[]{:S(2)}, u32[]{:S(2)}) async-start(bf16[16,64,128]{2,1,0:T(8,128)(2,1)} %open.1), calls=%async_computation | async-start | bytes 524288 | tf_op jit(solution)/shard_map/all_to_all | solution.py:529
  13.3 0.1 collective-permute-start.1
  13.4 0.0 collective-permute-done.2.refs_1_
  13.4 6.8 %first_image.1 = (bf16[1024,128]{1,0:T(8,128)(2,1)}, f32[1024,128]{1,0:T(8,128)}, f32[1024,128]{1,0:T(8,128)}, bf16[2,128,128]{2,1,0:T(8,128)(2,1)}, bf16[2,128,...) custom-call(bf16[2,512,1024]{2,1,0:T(8,128)(2,1)} %refs_0_.2, ...), custom_call_target="tpu_custom_call" | custom-call | flops 1073741824 | bytes 11339776 | tf_op jit(solution)/shard_map/first_image/pallas_call | solution.py:467
  20.2 3.3 %all-to-all-done.refs_2_ = bf16[16,64,128]{2,1,0:T(8,128)(2,1)S(1)} async-done(((bf16[16,64,128]{2,1,0:T(8,128)(2,1)}), bf16[16,64,128]{2,1,0:T(8,128)(2,1)S(1)}, u32[]{:S(2)}, u32[]{:S(2)}) %all-to-all-start) | async-done | bytes 262176 | tf_op jit(solution)/shard_map/all_to_all | solution.py:529
  23.5 3.2 %order.1 = (bf16[2,96,768]{2,1,0:T(8,128)(2,1)}, f32[2,16,128]{2,1,0:T(8,128)}, bf16[16,48,128]{2,1,0:T(8,128)(2,1)}) custom-call(bf16[96,768]{1,0:T(8,128)(2,1)} %refs_0_.1, bf16[96,768]{1,0:T(8,128)(2,1)S(1)} %collective-permute-done.1.refs_1_, bf16[16,64,128]{2,1,0:T(8,128)(2,1)S(1)} %all-to-all-done.refs_2_, bf16[128,768]{1,0:T(8,128)(2,1)} %constant.6.clone.refs_3_, ...), custom_call_target="tpu_custom_call" | custom-call | flops 452984832 | bytes 1310720 | tf_op jit(solution)/shard_map/order/pallas_call | solution.py:467
  26.8 3.6 %all-to-all-start.1 = ((bf16[16,48,128]{2,1,0:T(8,128)(2,1)}), bf16[16,48,128]{2,1,0:T(8,128)(2,1)S(1)}, u32[]{:S(2)}, u32[]{:S(2)}) async-start(bf16[16,48,128]{2,1,0:T(8,128)(2,1)} %get-tuple-element.42), calls=%async_computation.1 | async-start | bytes 393216 | tf_op jit(solution)/shard_map/all_to_all | solution.py:561
  30.4 5.5 %collective-permute-start.5 = (bf16[128,128]{1,0:T(8,128)(2,1)}, bf16[128,128]{1,0:T(8,128)(2,1)S(1)}, u32[]{:S(2)}, u32[]{:S(2)}) collective-permute-start(bf16[128,128]{1,0:T(8,128)(2,1)} %get-tuple-element.55), channel_id=1, source_target_pairs={{0,30},{2,4},{4,2},{6,8},{8,6},{10,12},{12,10},{14,16},{16,14},{18... | collective-permute-start | bytes 98312 | tf_op jit(solution)/shard_map/ppermute | solution.py:562
  35.9 3.1 %begin.1 = (bf16[2,48,128]{2,1,0:T(8,128)(2,1)}, bf16[2,48,128]{2,1,0:T(8,128)(2,1)}, bf16[2,48,48]{2,1,0:T(8,128)(2,1)}, f32[48,128]{1,0:T(8,128)}, bf16[2,192,768]{2,1,0:T(8,128)(2,1)}) custom-call(bf16[1024,128]{1,0:T(8,128)(2,1)} %get-tuple-element.43.refs_0_.refs_4_, f32[1024,128]{1,0:T(8,128)} %get-tuple-element.44.refs_1_.refs_5_, ...), custom_call_target="tpu_custom_call" | custom-call | flops 67108864 | bytes 2204672 | tf_op jit(solution)/shard_map/begin/pallas_call | solution.py:467
  39.1 1.7 %collective-permute-done.5.refs_9_.refs_12_.refs_10_ = bf16[128,128]{1,0:T(8,128)(2,1)S(1)} collective-permute-done((bf16[128,128]{1,0:T(8,128)(2,1)}, bf16[128,128]{1,0:T(8,128)(2,1)S(1)}, u32[]{:S(2)}, u32[]{:S(2)}) %collective-permute-start.5) | collective-permute-done | bytes 32800 | tf_op jit(solution)/shard_map/ppermute | solution.py:562
  40.8 0.0 collective-permute-done.4.refs_8_.refs_11_.refs_9_
  40.8 2.8 %update.1 = (bf16[192,128]{1,0:T(8,128)(2,1)}, bf16[16,48,128]{2,1,0:T(8,128)(2,1)}) custom-call(bf16[16,48,128]{2,1,0:T(8,128)(2,1)S(1)} %all-to-all-done.1.refs_0_, bf16[2,192,768]{2,1,0:T(8,128)(2,1)} %get-tuple-element.48.refs_1_.refs_6_, f32[48,128]{1,0:T(8,128)} %get-tuple-element.49.refs_2_, bf16[2,48,48]{2,1,0:T(8,128)(2,1)} %get-tuple-element.50.refs_3_, ...), custom_call_target="tpu_custom_call" | custom-call | flops 16777216 | bytes 1311744 | tf_op jit(solution)/shard_map/update/pallas_call | solution.py:467
  43.6 4.3 %all-to-all-start.2 = ((bf16[16,48,128]{2,1,0:T(8,128)(2,1)}), bf16[16,48,128]{2,1,0:T(8,128)(2,1)S(1)}, u32[]{:S(2)}, u32[]{:S(2)}) async-start(bf16[16,48,128]{2,1,0:T(8,128)(2,1)} %get-tuple-element.56), calls=%async_computation.2 | async-start | bytes 393216 | tf_op jit(solution)/shard_map/all_to_all | solution.py:582
  47.9 7.5 %second_image.1 = (bf16[64,128]{1,0:T(8,128)(2,1)}, bf16[64,128]{1,0:T(8,128)(2,1)}, f32[2,512,128]{2,1,0:T(8,128)}, f32[2,512,128]{2,1,0:T(8,128)}) custom-call(bf16[2,512,1024]{2,1,0:T(8,128)(2,1)} %refs_0_.2, bf16[2,512,1024]{2,1,0:T(8,128)(2,1)S(1)} %collective-permute-done.2.refs_1_, bf16[2,512,1024]{2,1,0:T(8,128)(2,1)} %refs_2_.3, ...), custom_call_target="tpu_custom_call" | custom-call | flops 1073741824 | bytes 11552768 | tf_op jit(solution)/shard_map/second_image/pallas_call | solution.py:467
  55.5 0.5 all-to-all-done.2.refs_0_
  56.0 2.2 %coarse.1 = bf16[16,48,128]{2,1,0:T(8,128)(2,1)} custom-call(bf16[16,48,128]{2,1,0:T(8,128)(2,1)S(1)} %all-to-all-done.2.refs_0_, bf16[2,96,768]{2,1,0:T(8,128)(2,1)} %get-tuple-element.61.refs_1_), custom_call_target="tpu_custom_call" | custom-call | flops 16777216 | bytes 688128 | tf_op jit(solution)/shard_map/coarse/pallas_call | solution.py:467
  58.2 6.4 %all-to-all-start.3 = ((bf16[16,48,128]{2,1,0:T(8,128)(2,1)}), bf16[16,48,128]{2,1,0:T(8,128)(2,1)S(1)}, u32[]{:S(2)}, u32[]{:S(2)}) async-start(bf16[16,48,128]{2,1,0:T(8,128)(2,1)} %coarse.1), calls=%async_computation.3 | async-start | bytes 393216 | tf_op jit(solution)/shard_map/all_to_all | solution.py:612
  64.6 0.1 collective-permute-start.7
  64.7 8.0 %all-to-all-done.3.refs_0_ = bf16[16,48,128]{2,1,0:T(8,128)(2,1)S(1)} async-done(((bf16[16,48,128]{2,1,0:T(8,128)(2,1)}), bf16[16,48,128]{2,1,0:T(8,128)(2,1)S(1)}, u32[]{:S(2)}, u32[]{:S(2)}) %all-to-all-start.3) | async-done | bytes 196640 | tf_op jit(solution)/shard_map/all_to_all | solution.py:612
  72.7 1.7 %collective-permute-start.9 = (bf16[64,128]{1,0:T(8,128)(2,1)}, bf16[64,128]{1,0:T(8,128)(2,1)S(1)}, u32[]{:S(2)}, u32[]{:S(2)}) collective-permute-start(bf16[64,128]{1,0:T(8,128)(2,1)} %get-tuple-element.64), channel_id=1, source_target_pairs={{0,30},{2,4},{4,2},{6,8},{8,6},{10,12},{12,10},{14,16},{16,14},{18... | collective-permute-start | bytes 49160 | tf_op jit(solution)/shard_map/ppermute | solution.py:613
  74.4 0.5 collective-permute-start.8
  75.0 2.7 %base.1.refs_14_ = f32[2,2,512,128]{3,2,1,0:T(8,128)} custom-call(f32[2,512,128]{2,1,0:T(8,128)} %get-tuple-element.62.refs_0_, f32[2,512,128]{2,1,0:T(8,128)S(1)} %collective-permute-done.7.refs_1_), custom_call_target="tpu_custom_call" | custom-call | flops 16777216 | bytes 2097152 | tf_op jit(solution)/shard_map/base/pallas_call | solution.py:467
  77.7 2.6 %collective-permute-done.9.refs_4_ = bf16[64,128]{1,0:T(8,128)(2,1)S(1)} collective-permute-done((bf16[64,128]{1,0:T(8,128)(2,1)}, bf16[64,128]{1,0:T(8,128)(2,1)S(1)}, u32[]{:S(2)}, u32[]{:S(2)}) %collective-permute-start.9) | collective-permute-done | bytes 16416 | tf_op jit(solution)/shard_map/ppermute | solution.py:613
  80.3 0.5 collective-permute-start.11
  80.8 0.7 collective-permute-done.10.refs_3_
  81.5 0.2 collective-permute-done.11.refs_5_
  81.6 4.2 %last.1 = (f32[2,512,128]{2,1,0:T(8,128)}, f32[2,512,128]{2,1,0:T(8,128)}) custom-call(bf16[16,48,128]{2,1,0:T(8,128)(2,1)S(1)} %all-to-all-done.3.refs_0_, bf16[16,48,128]{2,1,0:T(8,128)(2,1)S(1)} %collective-permute-done.6.refs_1_, bf16[64,128]{1,0:T(8,128)(2,1)S(1)} %collective-permute-done.8.refs_2_, ...), custom_call_target="tpu_custom_call" | custom-call | flops 134217728 | bytes 3868672 | tf_op jit(solution)/shard_map/last/pallas_call | solution.py:467
  (9 shorter events, 0.0 us)
Async XLA Ops:
  0.6 1.7 %collective-permute-start = (bf16[2,48,512]{2,1,0:T(8,128)(2,1)}, bf16[2,48,512]{2,1,0:T(8,128)(2,1)S(1)}, u32[]{:S(2)}, u32[]{:S(2)}) collective-permute-start(bf16[2,48,512]{2,1,0:T(8,128)(2,1)} %bitcast.1), channel_id=1, source_target_pairs={{1,0},{0,1},{3,2},{2,3},{5,4},{4,5},{7,6},{6,7},{9,8},{8,9},{11,10... | collective-permute-start | bytes 294920 | tf_op jit(solution)/shard_map/ppermute | solution.py:491
  2.3 11.1 %collective-permute-start.2 = (bf16[2,512,1024]{2,1,0:T(8,128)(2,1)}, bf16[2,512,1024]{2,1,0:T(8,128)(2,1)S(1)}, u32[]{:S(2)}, u32[]{:S(2)}) collective-permute-start(bf16[2,512,1024]{2,1,0:T(8,128)(2,1)} %refs_0_.2), channel_id=1, source_target_pairs={{1,0},{0,1},{3,2},{2,3},{5,4},{4,5},{7,6},{6,7},{9,8},{8,9},{11,10... | collective-permute-start | bytes 6291464 | tf_op jit(solution)/shard_map/ppermute | solution.py:491
  2.7 10.8 %collective-permute-start.3 = (bf16[2,512,1024]{2,1,0:T(8,128)(2,1)}, bf16[2,512,1024]{2,1,0:T(8,128)(2,1)}, u32[]{:S(2)}, u32[]{:S(2)}) collective-permute-start(bf16[2,512,1024]{2,1,0:T(8,128)(2,1)} %refs_2_.3), channel_id=1, source_target_pairs={{1,0},{0,1},{3,2},{2,3},{5,4},{4,5},{7,6},{6,7},{9,8},{8,9},{11,10... | collective-permute-start | bytes 6291464 | tf_op jit(solution)/shard_map/ppermute | solution.py:491
  5.1 18.4 %all-to-all-start = ((bf16[16,64,128]{2,1,0:T(8,128)(2,1)}), bf16[16,64,128]{2,1,0:T(8,128)(2,1)S(1)}, u32[]{:S(2)}, u32[]{:S(2)}) async-start(bf16[16,64,128]{2,1,0:T(8,128)(2,1)} %open.1), calls=%async_computation | async-start | bytes 524288 | tf_op jit(solution)/shard_map/all_to_all | solution.py:529
  13.3 10.2 %collective-permute-start.1 = (bf16[96,768]{1,0:T(8,128)(2,1)}, bf16[96,768]{1,0:T(8,128)(2,1)S(1)}, u32[]{:S(2)}, u32[]{:S(2)}) collective-permute-start(bf16[96,768]{1,0:T(8,128)(2,1)} %refs_0_.1), channel_id=1, source_target_pairs={{1,0},{0,1},{3,2},{2,3},{5,4},{4,5},{7,6},{6,7},{9,8},{8,9},{11,10... | collective-permute-start | bytes 442376 | tf_op jit(solution)/shard_map/ppermute | solution.py:491
  26.8 14.0 %all-to-all-start.1 = ((bf16[16,48,128]{2,1,0:T(8,128)(2,1)}), bf16[16,48,128]{2,1,0:T(8,128)(2,1)S(1)}, u32[]{:S(2)}, u32[]{:S(2)}) async-start(bf16[16,48,128]{2,1,0:T(8,128)(2,1)} %get-tuple-element.42), calls=%async_computation.1 | async-start | bytes 393216 | tf_op jit(solution)/shard_map/all_to_all | solution.py:561
  30.4 10.4 %collective-permute-start.5 = (bf16[128,128]{1,0:T(8,128)(2,1)}, bf16[128,128]{1,0:T(8,128)(2,1)S(1)}, u32[]{:S(2)}, u32[]{:S(2)}) collective-permute-start(bf16[128,128]{1,0:T(8,128)(2,1)} %get-tuple-element.55), channel_id=1, source_target_pairs={{0,30},{2,4},{4,2},{6,8},{8,6},{10,12},{12,10},{14,16},{16,14},{18... | collective-permute-start | bytes 98312 | tf_op jit(solution)/shard_map/ppermute | solution.py:562
  35.9 4.8 %collective-permute-start.4 = (bf16[128,128]{1,0:T(8,128)(2,1)}, bf16[128,128]{1,0:T(8,128)(2,1)S(1)}, u32[]{:S(2)}, u32[]{:S(2)}) collective-permute-start(bf16[128,128]{1,0:T(8,128)(2,1)} %get-tuple-element.40), channel_id=1, source_target_pairs={{0,2},{2,0},{4,6},{6,4},{8,10},{10,8},{12,14},{14,12},{16,18},{18,... | collective-permute-start | bytes 98312 | tf_op jit(solution)/shard_map/ppermute | solution.py:550
  43.6 12.4 %all-to-all-start.2 = ((bf16[16,48,128]{2,1,0:T(8,128)(2,1)}), bf16[16,48,128]{2,1,0:T(8,128)(2,1)S(1)}, u32[]{:S(2)}, u32[]{:S(2)}) async-start(bf16[16,48,128]{2,1,0:T(8,128)(2,1)} %get-tuple-element.56), calls=%async_computation.2 | async-start | bytes 393216 | tf_op jit(solution)/shard_map/all_to_all | solution.py:582
  58.2 14.5 %all-to-all-start.3 = ((bf16[16,48,128]{2,1,0:T(8,128)(2,1)}), bf16[16,48,128]{2,1,0:T(8,128)(2,1)S(1)}, u32[]{:S(2)}, u32[]{:S(2)}) async-start(bf16[16,48,128]{2,1,0:T(8,128)(2,1)} %coarse.1), calls=%async_computation.3 | async-start | bytes 393216 | tf_op jit(solution)/shard_map/all_to_all | solution.py:612
  64.6 10.4 %collective-permute-start.7 = (f32[2,512,128]{2,1,0:T(8,128)}, f32[2,512,128]{2,1,0:T(8,128)S(1)}, u32[]{:S(2)}, u32[]{:S(2)}) collective-permute-start(f32[2,512,128]{2,1,0:T(8,128)} %get-tuple-element.63), channel_id=1, source_target_pairs={{0,1},{1,0},{2,3},{3,2},{4,5},{5,4},{6,7},{7,6},{8,9},{9,8},{10,11... | collective-permute-start | bytes 1572872 | tf_op jit(solution)/shard_map/ppermute | solution.py:616
  72.7 8.9 %collective-permute-start.6 = (bf16[16,48,128]{2,1,0:T(8,128)(2,1)S(1)}, bf16[16,48,128]{2,1,0:T(8,128)(2,1)S(1)}, u32[]{:S(2)}, u32[]{:S(2)}) collective-permute-start(bf16[16,48,128]{2,1,0:T(8,128)(2,1)S(1)} %all-to-all-done.3.refs_0_), channel_id=1, source_target_pairs={{1,0},{0,1},{3,2},{2,3},{5,4},{4,5},{7,6},{6,7},{9,8},{8,9},{11,10... | collective-permute-start | bytes 589832 | tf_op jit(solution)/shard_map/ppermute | solution.py:491
  72.7 7.5 %collective-permute-start.9 = (bf16[64,128]{1,0:T(8,128)(2,1)}, bf16[64,128]{1,0:T(8,128)(2,1)S(1)}, u32[]{:S(2)}, u32[]{:S(2)}) collective-permute-start(bf16[64,128]{1,0:T(8,128)(2,1)} %get-tuple-element.64), channel_id=1, source_target_pairs={{0,30},{2,4},{4,2},{6,8},{8,6},{10,12},{12,10},{14,16},{16,14},{18... | collective-permute-start | bytes 49160 | tf_op jit(solution)/shard_map/ppermute | solution.py:613
  74.4 5.8 %collective-permute-start.8 = (bf16[64,128]{1,0:T(8,128)(2,1)}, bf16[64,128]{1,0:T(8,128)(2,1)S(1)}, u32[]{:S(2)}, u32[]{:S(2)}) collective-permute-start(bf16[64,128]{1,0:T(8,128)(2,1)} %get-tuple-element.59), channel_id=1, source_target_pairs={{0,2},{2,0},{4,6},{6,4},{8,10},{10,8},{12,14},{14,12},{16,18},{18,... | collective-permute-start | bytes 49160 | tf_op jit(solution)/shard_map/ppermute | solution.py:602
  80.3 1.2 %collective-permute-start.10 = (bf16[64,128]{1,0:T(8,128)(2,1)S(1)}, bf16[64,128]{1,0:T(8,128)(2,1)S(1)}, u32[]{:S(2)}, u32[]{:S(2)}) collective-permute-start(bf16[64,128]{1,0:T(8,128)(2,1)S(1)} %collective-permute-done.8.refs_2_), channel_id=1, source_target_pairs={{1,0},{0,1},{3,2},{2,3},{5,4},{4,5},{7,6},{6,7},{9,8},{8,9},{11,10... | collective-permute-start | bytes 49160 | tf_op jit(solution)/shard_map/ppermute | solution.py:491
  80.3 1.3 %collective-permute-start.11 = (bf16[64,128]{1,0:T(8,128)(2,1)S(1)}, bf16[64,128]{1,0:T(8,128)(2,1)S(1)}, u32[]{:S(2)}, u32[]{:S(2)}) collective-permute-start(bf16[64,128]{1,0:T(8,128)(2,1)S(1)} %collective-permute-done.9.refs_4_), channel_id=1, source_target_pairs={{1,0},{0,1},{3,2},{2,3},{5,4},{4,5},{7,6},{6,7},{9,8},{8,9},{11,10... | collective-permute-start | bytes 49160 | tf_op jit(solution)/shard_map/ppermute | solution.py:491

commit v22 on v20

--- a/solution.py
+++ b/solution.py
@@ -326,7 +326,8 @@
 
 def coarse_rows(z, ordered_inverse, arrived, message):
     flat = arrived[:, : z.modes, :].reshape(z.columns, z.lanes)
-    rows = fold(z, select(z, [dot(ordered_inverse[s], flat) for s in range(z.subs)]))
+    product = dot(ordered_inverse[...].reshape(z.subs * z.owned, z.columns), flat)
+    rows = fold(z, select(z, [product[s * z.owned : (s + 1) * z.owned] for s in range(z.subs)]))
     packed = select(z, [rows[s * z.modes : (s + 1) * z.modes, :] for s in range(z.subs)]).astype(BF16)
     for k in range(z.n):
         message[k] = packed
@@ -336,11 +337,16 @@
     blocks = refs[: z.group]
     arrived, repeat, own_row, ordered_inverse, index, message = refs[z.group :]
     digits = arrived[:, z.modes :, :].astype(F32)
+    pairs = []
     for s in range(z.subs):
         high = jnp.sum(jnp.where(digit_row(digits.shape, 2 * s), digits, 0.0), axis=1)
         low = jnp.sum(jnp.where(digit_row(digits.shape, 2 * s + 1), digits, 0.0), axis=1)
         index[s] = high * DIGIT + low
-        spread = dot(high.astype(BF16), repeat[...]) * DIGIT + dot(low.astype(BF16), repeat[...])
+        pairs += [high.astype(BF16), low.astype(BF16)]
+    spreads = dot(jnp.concatenate(pairs, axis=0), repeat[...])
+    for s in range(z.subs):
+        at_high, at_low = 2 * s * z.n, (2 * s + 1) * z.n
+        spread = spreads[at_high : at_high + z.n] * DIGIT + spreads[at_low : at_low + z.n]
         places = jnp.sum(spread * own_row[...], axis=0, keepdims=True).astype(jnp.int32)
         for at in range(0, z.columns, 768):
             wide = min(768, z.columns - at)
@@ -362,7 +368,9 @@
 
 def picked_rows(z, arrived, picks):
     flat = arrived[...].reshape(z.columns, z.lanes)
-    return fold(z, select(z, [dot(picks[h], flat) for h in range(z.subs)])).astype(BF16)
+    near = picks.shape[1]
+    product = dot(picks[...].reshape(z.subs * near, z.columns), flat)
+    return fold(z, select(z, [product[h * near : (h + 1) * near] for h in range(z.subs)])).astype(BF16)
 
 
 def update_kernel(z, *refs):

time: 81.3 us -> 81.4 us (level)
  no operation moved by 1% of the time
where the time goes in v22:
time: 81.4 us; the launch traced here: 80.7 us
  starting transfers between devices  35.5 us (44%)
  Pallas kernels  35 us (43%)
  waiting for transfers between devices  9.48 us (12%)
    pallas_call x9, Pallas kernels, call(): pl.pallas_call(whole, out_shape=[pltpu.HBM(o.shape, o.dtype) for o in out...  35 us
    all_to_all x2, starting transfers between devices, body(): restricted = spread(message)  12.5 us
    ppermute x2, starting transfers between devices, body(): second_got = lax.ppermute(second_pair, 'sub', second_pairs)  11.1 us
    all_to_all x2, starting transfers between devices, body(): coarse = spread(message)  10.1 us
    all_to_all x2, waiting for transfers between devices, body(): restricted = spread(message)  3.72 us
    ppermute x2, waiting for transfers between devices, body(): second_got = lax.ppermute(second_pair, 'sub', second_pairs)  3.47 us
    ppermute x7, waiting for transfers between devices, pieces_of(): lax.ppermute(block, GROUP, [((g + k) % group, g) for g in range(group)])  2.28 us
    ppermute x7, starting transfers between devices, pieces_of(): lax.ppermute(block, GROUP, [((g + k) % group, g) for g in range(group)])  1.68 us
  transfers between devices with their start and end apart: 16, of which 7 were waited for; matrix products, arithmetic and copies ran while one was open for 0% of the time, Pallas kernels for 31%

profile of v22, /device:TPU:0, one launch (start us, length us, event | category | flops | bytes accessed | tf_op | source)
XLA Modules:
  0.0 80.7 jit_solution(15833354556888593981)
XLA Ops:
  0.6 0.5 collective-permute-start
  1.1 1.2 %collective-permute-done.refs_1_.refs_5_ = bf16[2,48,512]{2,1,0:T(8,128)(2,1)S(1)} collective-permute-done((bf16[2,48,512]{2,1,0:T(8,128)(2,1)}, bf16[2,48,512]{2,1,0:T(8,128)(2,1)S(1)}, u32[]{:S(2)}, u32[]{:S(2)}) %collective-permute-start) | collective-permute-done | bytes 98336 | tf_op jit(solution)/shard_map/ppermute | solution.py:499
  2.3 0.4 collective-permute-start.2
  2.7 0.2 collective-permute-start.3
  2.8 2.3 %open.1 = bf16[16,64,128]{2,1,0:T(8,128)(2,1)} custom-call(bf16[2,48,512]{2,1,0:T(8,128)(2,1)} %bitcast.2, bf16[2,48,512]{2,1,0:T(8,128)(2,1)S(1)} %collective-permute-done.refs_1_.refs_5_, bf16[2,1024,128]{2,1,0:T(8,128)(2,1)} %refs_6_.1, s32[2,48]{1,0:T(2,128)} %refs_3_.2), custom_call_target="tpu_custom_call" | custom-call | flops 67108864 | bytes 983424 | tf_op jit(solution)/shard_map/open/pallas_call | solution.py:475
  5.1 8.2 %all-to-all-start = ((bf16[16,64,128]{2,1,0:T(8,128)(2,1)}), bf16[16,64,128]{2,1,0:T(8,128)(2,1)S(1)}, u32[]{:S(2)}, u32[]{:S(2)}) async-start(bf16[16,64,128]{2,1,0:T(8,128)(2,1)} %open.1), calls=%async_computation | async-start | bytes 524288 | tf_op jit(solution)/shard_map/all_to_all | solution.py:537
  13.3 0.1 collective-permute-start.1
  13.4 0.0 collective-permute-done.2.refs_1_
  13.4 6.8 %first_image.1 = (bf16[1024,128]{1,0:T(8,128)(2,1)}, f32[1024,128]{1,0:T(8,128)}, f32[1024,128]{1,0:T(8,128)}, bf16[2,128,128]{2,1,0:T(8,128)(2,1)}, bf16[2,128,...) custom-call(bf16[2,512,1024]{2,1,0:T(8,128)(2,1)} %refs_0_.2, ...), custom_call_target="tpu_custom_call" | custom-call | flops 1073741824 | bytes 11339776 | tf_op jit(solution)/shard_map/first_image/pallas_call | solution.py:475
  20.2 3.3 %all-to-all-done.refs_2_ = bf16[16,64,128]{2,1,0:T(8,128)(2,1)S(1)} async-done(((bf16[16,64,128]{2,1,0:T(8,128)(2,1)}), bf16[16,64,128]{2,1,0:T(8,128)(2,1)S(1)}, u32[]{:S(2)}, u32[]{:S(2)}) %all-to-all-start) | async-done | bytes 262176 | tf_op jit(solution)/shard_map/all_to_all | solution.py:537
  23.5 3.1 %order.1 = (bf16[2,96,768]{2,1,0:T(8,128)(2,1)}, f32[2,16,128]{2,1,0:T(8,128)}, bf16[16,48,128]{2,1,0:T(8,128)(2,1)}) custom-call(bf16[96,768]{1,0:T(8,128)(2,1)} %refs_0_.1, bf16[96,768]{1,0:T(8,128)(2,1)S(1)} %collective-permute-done.1.refs_1_, bf16[16,64,128]{2,1,0:T(8,128)(2,1)S(1)} %all-to-all-done.refs_2_, bf16[128,768]{1,0:T(8,128)(2,1)} %constant.6.clone.refs_3_, ...), custom_call_target="tpu_custom_call" | custom-call | flops 452984832 | bytes 1310720 | tf_op jit(solution)/shard_map/order/pallas_call | solution.py:475
  26.6 3.6 %all-to-all-start.1 = ((bf16[16,48,128]{2,1,0:T(8,128)(2,1)}), bf16[16,48,128]{2,1,0:T(8,128)(2,1)S(1)}, u32[]{:S(2)}, u32[]{:S(2)}) async-start(bf16[16,48,128]{2,1,0:T(8,128)(2,1)} %get-tuple-element.43), calls=%async_computation.1 | async-start | bytes 393216 | tf_op jit(solution)/shard_map/all_to_all | solution.py:569
  30.2 5.5 %collective-permute-start.5 = (bf16[128,128]{1,0:T(8,128)(2,1)}, bf16[128,128]{1,0:T(8,128)(2,1)S(1)}, u32[]{:S(2)}, u32[]{:S(2)}) collective-permute-start(bf16[128,128]{1,0:T(8,128)(2,1)} %get-tuple-element.56), channel_id=1, source_target_pairs={{0,30},{2,4},{4,2},{6,8},{8,6},{10,12},{12,10},{14,16},{16,14},{18... | collective-permute-start | bytes 98312 | tf_op jit(solution)/shard_map/ppermute | solution.py:570
  35.8 3.1 %begin.1 = (bf16[2,48,128]{2,1,0:T(8,128)(2,1)}, bf16[2,48,128]{2,1,0:T(8,128)(2,1)}, bf16[2,48,48]{2,1,0:T(8,128)(2,1)}, f32[48,128]{1,0:T(8,128)}, bf16[2,192,768]{2,1,0:T(8,128)(2,1)}) custom-call(bf16[1024,128]{1,0:T(8,128)(2,1)} %get-tuple-element.44.refs_0_.refs_4_, f32[1024,128]{1,0:T(8,128)} %get-tuple-element.45.refs_1_.refs_5_, ...), custom_call_target="tpu_custom_call" | custom-call | flops 67108864 | bytes 2204672 | tf_op jit(solution)/shard_map/begin/pallas_call | solution.py:475
  38.9 1.7 %collective-permute-done.5.refs_9_.refs_12_.refs_10_ = bf16[128,128]{1,0:T(8,128)(2,1)S(1)} collective-permute-done((bf16[128,128]{1,0:T(8,128)(2,1)}, bf16[128,128]{1,0:T(8,128)(2,1)S(1)}, u32[]{:S(2)}, u32[]{:S(2)}) %collective-permute-start.5) | collective-permute-done | bytes 32800 | tf_op jit(solution)/shard_map/ppermute | solution.py:570
  40.6 0.0 collective-permute-done.4.refs_8_.refs_11_.refs_9_
  40.6 3.1 %update.1 = (bf16[192,128]{1,0:T(8,128)(2,1)}, bf16[16,48,128]{2,1,0:T(8,128)(2,1)}) custom-call(bf16[16,48,128]{2,1,0:T(8,128)(2,1)S(1)} %all-to-all-done.1.refs_0_, bf16[2,192,768]{2,1,0:T(8,128)(2,1)} %get-tuple-element.49.refs_1_.refs_6_, f32[48,128]{1,0:T(8,128)} %get-tuple-element.50.refs_2_, bf16[2,48,48]{2,1,0:T(8,128)(2,1)} %get-tuple-element.51.refs_3_, ...), custom_call_target="tpu_custom_call" | custom-call | flops 16777216 | bytes 1311744 | tf_op jit(solution)/shard_map/update/pallas_call | solution.py:475
  43.7 4.3 %all-to-all-start.2 = ((bf16[16,48,128]{2,1,0:T(8,128)(2,1)}), bf16[16,48,128]{2,1,0:T(8,128)(2,1)S(1)}, u32[]{:S(2)}, u32[]{:S(2)}) async-start(bf16[16,48,128]{2,1,0:T(8,128)(2,1)} %get-tuple-element.57), calls=%async_computation.2 | async-start | bytes 393216 | tf_op jit(solution)/shard_map/all_to_all | solution.py:590
  48.0 7.5 %second_image.1 = (bf16[64,128]{1,0:T(8,128)(2,1)}, bf16[64,128]{1,0:T(8,128)(2,1)}, f32[2,512,128]{2,1,0:T(8,128)}, f32[2,512,128]{2,1,0:T(8,128)}) custom-call(bf16[2,512,1024]{2,1,0:T(8,128)(2,1)} %refs_0_.2, bf16[2,512,1024]{2,1,0:T(8,128)(2,1)S(1)} %collective-permute-done.2.refs_1_, bf16[2,512,1024]{2,1,0:T(8,128)(2,1)} %refs_2_.3, ...), custom_call_target="tpu_custom_call" | custom-call | flops 1073741824 | bytes 11552768 | tf_op jit(solution)/shard_map/second_image/pallas_call | solution.py:475
  55.5 0.1 collective-permute-start.6
  55.6 0.4 all-to-all-done.2.refs_0_
  56.0 2.2 %coarse.1 = bf16[16,48,128]{2,1,0:T(8,128)(2,1)} custom-call(bf16[16,48,128]{2,1,0:T(8,128)(2,1)S(1)} %all-to-all-done.2.refs_0_, bf16[2,96,768]{2,1,0:T(8,128)(2,1)} %get-tuple-element.62.refs_1_), custom_call_target="tpu_custom_call" | custom-call | flops 16777216 | bytes 688128 | tf_op jit(solution)/shard_map/coarse/pallas_call | solution.py:475
  58.2 6.5 %all-to-all-start.3 = ((bf16[16,48,128]{2,1,0:T(8,128)(2,1)}), bf16[16,48,128]{2,1,0:T(8,128)(2,1)S(1)}, u32[]{:S(2)}, u32[]{:S(2)}) async-start(bf16[16,48,128]{2,1,0:T(8,128)(2,1)} %coarse.1), calls=%async_computation.3 | async-start | bytes 393216 | tf_op jit(solution)/shard_map/all_to_all | solution.py:620
  64.7 5.5 %collective-permute-start.8 = (bf16[64,128]{1,0:T(8,128)(2,1)}, bf16[64,128]{1,0:T(8,128)(2,1)S(1)}, u32[]{:S(2)}, u32[]{:S(2)}) collective-permute-start(bf16[64,128]{1,0:T(8,128)(2,1)} %get-tuple-element.65), channel_id=1, source_target_pairs={{0,30},{2,4},{4,2},{6,8},{8,6},{10,12},{12,10},{14,16},{16,14},{18... | collective-permute-start | bytes 49160 | tf_op jit(solution)/shard_map/ppermute | solution.py:621
  70.3 0.0 collective-permute-start.7
  70.3 2.7 %base.1.refs_14_ = f32[2,2,512,128]{3,2,1,0:T(8,128)} custom-call(f32[2,512,128]{2,1,0:T(8,128)} %get-tuple-element.63.refs_0_, f32[2,512,128]{2,1,0:T(8,128)S(1)} %collective-permute-done.6.refs_1_), custom_call_target="tpu_custom_call" | custom-call | flops 16777216 | bytes 2097152 | tf_op jit(solution)/shard_map/base/pallas_call | solution.py:475
  73.0 1.8 %collective-permute-done.8.refs_4_ = bf16[64,128]{1,0:T(8,128)(2,1)S(1)} collective-permute-done((bf16[64,128]{1,0:T(8,128)(2,1)}, bf16[64,128]{1,0:T(8,128)(2,1)S(1)}, u32[]{:S(2)}, u32[]{:S(2)}) %collective-permute-start.8) | collective-permute-done | bytes 16416 | tf_op jit(solution)/shard_map/ppermute | solution.py:621
  74.8 0.5 collective-permute-start.10
  75.3 0.1 collective-permute-start.11
  75.3 0.9 %collective-permute-done.10.refs_3_ = bf16[64,128]{1,0:T(8,128)(2,1)S(1)} collective-permute-done((bf16[64,128]{1,0:T(8,128)(2,1)S(1)}, bf16[64,128]{1,0:T(8,128)(2,1)S(1)}, u32[]{:S(2)}, u32[]{:S(2)}) %collective-permute-start.10) | collective-permute-done | bytes 16416 | tf_op jit(solution)/shard_map/ppermute | solution.py:499
  76.2 0.2 collective-permute-done.11.refs_5_
  76.5 4.2 %last.1 = (f32[2,512,128]{2,1,0:T(8,128)}, f32[2,512,128]{2,1,0:T(8,128)}) custom-call(bf16[16,48,128]{2,1,0:T(8,128)(2,1)S(1)} %all-to-all-done.3.refs_0_, bf16[16,48,128]{2,1,0:T(8,128)(2,1)S(1)} %collective-permute-done.9.refs_1_, bf16[64,128]{1,0:T(8,128)(2,1)S(1)} %collective-permute-done.7.refs_2_, ...), custom_call_target="tpu_custom_call" | custom-call | flops 134217728 | bytes 3868672 | tf_op jit(solution)/shard_map/last/pallas_call | solution.py:475
  (9 shorter events, 0.0 us)
Async XLA Ops:
  0.6 1.7 %collective-permute-start = (bf16[2,48,512]{2,1,0:T(8,128)(2,1)}, bf16[2,48,512]{2,1,0:T(8,128)(2,1)S(1)}, u32[]{:S(2)}, u32[]{:S(2)}) collective-permute-start(bf16[2,48,512]{2,1,0:T(8,128)(2,1)} %bitcast.1), channel_id=1, source_target_pairs={{1,0},{0,1},{3,2},{2,3},{5,4},{4,5},{7,6},{6,7},{9,8},{8,9},{11,10... | collective-permute-start | bytes 294920 | tf_op jit(solution)/shard_map/ppermute | solution.py:499
  2.3 11.1 %collective-permute-start.2 = (bf16[2,512,1024]{2,1,0:T(8,128)(2,1)}, bf16[2,512,1024]{2,1,0:T(8,128)(2,1)S(1)}, u32[]{:S(2)}, u32[]{:S(2)}) collective-permute-start(bf16[2,512,1024]{2,1,0:T(8,128)(2,1)} %refs_0_.2), channel_id=1, source_target_pairs={{1,0},{0,1},{3,2},{2,3},{5,4},{4,5},{7,6},{6,7},{9,8},{8,9},{11,10... | collective-permute-start | bytes 6291464 | tf_op jit(solution)/shard_map/ppermute | solution.py:499
  2.7 10.8 %collective-permute-start.3 = (bf16[2,512,1024]{2,1,0:T(8,128)(2,1)}, bf16[2,512,1024]{2,1,0:T(8,128)(2,1)}, u32[]{:S(2)}, u32[]{:S(2)}) collective-permute-start(bf16[2,512,1024]{2,1,0:T(8,128)(2,1)} %refs_2_.3), channel_id=1, source_target_pairs={{1,0},{0,1},{3,2},{2,3},{5,4},{4,5},{7,6},{6,7},{9,8},{8,9},{11,10... | collective-permute-start | bytes 6291464 | tf_op jit(solution)/shard_map/ppermute | solution.py:499
  5.1 18.4 %all-to-all-start = ((bf16[16,64,128]{2,1,0:T(8,128)(2,1)}), bf16[16,64,128]{2,1,0:T(8,128)(2,1)S(1)}, u32[]{:S(2)}, u32[]{:S(2)}) async-start(bf16[16,64,128]{2,1,0:T(8,128)(2,1)} %open.1), calls=%async_computation | async-start | bytes 524288 | tf_op jit(solution)/shard_map/all_to_all | solution.py:537
  13.3 10.2 %collective-permute-start.1 = (bf16[96,768]{1,0:T(8,128)(2,1)}, bf16[96,768]{1,0:T(8,128)(2,1)S(1)}, u32[]{:S(2)}, u32[]{:S(2)}) collective-permute-start(bf16[96,768]{1,0:T(8,128)(2,1)} %refs_0_.1), channel_id=1, source_target_pairs={{1,0},{0,1},{3,2},{2,3},{5,4},{4,5},{7,6},{6,7},{9,8},{8,9},{11,10... | collective-permute-start | bytes 442376 | tf_op jit(solution)/shard_map/ppermute | solution.py:499
  26.6 14.0 %all-to-all-start.1 = ((bf16[16,48,128]{2,1,0:T(8,128)(2,1)}), bf16[16,48,128]{2,1,0:T(8,128)(2,1)S(1)}, u32[]{:S(2)}, u32[]{:S(2)}) async-start(bf16[16,48,128]{2,1,0:T(8,128)(2,1)} %get-tuple-element.43), calls=%async_computation.1 | async-start | bytes 393216 | tf_op jit(solution)/shard_map/all_to_all | solution.py:569
  30.2 10.4 %collective-permute-start.5 = (bf16[128,128]{1,0:T(8,128)(2,1)}, bf16[128,128]{1,0:T(8,128)(2,1)S(1)}, u32[]{:S(2)}, u32[]{:S(2)}) collective-permute-start(bf16[128,128]{1,0:T(8,128)(2,1)} %get-tuple-element.56), channel_id=1, source_target_pairs={{0,30},{2,4},{4,2},{6,8},{8,6},{10,12},{12,10},{14,16},{16,14},{18... | collective-permute-start | bytes 98312 | tf_op jit(solution)/shard_map/ppermute | solution.py:570
  35.8 4.8 %collective-permute-start.4 = (bf16[128,128]{1,0:T(8,128)(2,1)}, bf16[128,128]{1,0:T(8,128)(2,1)S(1)}, u32[]{:S(2)}, u32[]{:S(2)}) collective-permute-start(bf16[128,128]{1,0:T(8,128)(2,1)} %get-tuple-element.41), channel_id=1, source_target_pairs={{0,2},{2,0},{4,6},{6,4},{8,10},{10,8},{12,14},{14,12},{16,18},{18,... | collective-permute-start | bytes 98312 | tf_op jit(solution)/shard_map/ppermute | solution.py:558
  43.7 12.4 %all-to-all-start.2 = ((bf16[16,48,128]{2,1,0:T(8,128)(2,1)}), bf16[16,48,128]{2,1,0:T(8,128)(2,1)S(1)}, u32[]{:S(2)}, u32[]{:S(2)}) async-start(bf16[16,48,128]{2,1,0:T(8,128)(2,1)} %get-tuple-element.57), calls=%async_computation.2 | async-start | bytes 393216 | tf_op jit(solution)/shard_map/all_to_all | solution.py:590
  55.5 14.8 %collective-permute-start.6 = (f32[2,512,128]{2,1,0:T(8,128)}, f32[2,512,128]{2,1,0:T(8,128)S(1)}, u32[]{:S(2)}, u32[]{:S(2)}) collective-permute-start(f32[2,512,128]{2,1,0:T(8,128)} %get-tuple-element.64), channel_id=1, source_target_pairs={{0,1},{1,0},{2,3},{3,2},{4,5},{5,4},{6,7},{7,6},{8,9},{9,8},{10,11... | collective-permute-start | bytes 1572872 | tf_op jit(solution)/shard_map/ppermute | solution.py:624
  58.2 16.5 %all-to-all-start.3 = ((bf16[16,48,128]{2,1,0:T(8,128)(2,1)}), bf16[16,48,128]{2,1,0:T(8,128)(2,1)S(1)}, u32[]{:S(2)}, u32[]{:S(2)}) async-start(bf16[16,48,128]{2,1,0:T(8,128)(2,1)} %coarse.1), calls=%async_computation.3 | async-start | bytes 393216 | tf_op jit(solution)/shard_map/all_to_all | solution.py:620
  64.7 10.0 %collective-permute-start.8 = (bf16[64,128]{1,0:T(8,128)(2,1)}, bf16[64,128]{1,0:T(8,128)(2,1)S(1)}, u32[]{:S(2)}, u32[]{:S(2)}) collective-permute-start(bf16[64,128]{1,0:T(8,128)(2,1)} %get-tuple-element.65), channel_id=1, source_target_pairs={{0,30},{2,4},{4,2},{6,8},{8,6},{10,12},{12,10},{14,16},{16,14},{18... | collective-permute-start | bytes 49160 | tf_op jit(solution)/shard_map/ppermute | solution.py:621
  70.3 4.5 %collective-permute-start.7 = (bf16[64,128]{1,0:T(8,128)(2,1)}, bf16[64,128]{1,0:T(8,128)(2,1)S(1)}, u32[]{:S(2)}, u32[]{:S(2)}) collective-permute-start(bf16[64,128]{1,0:T(8,128)(2,1)} %get-tuple-element.60), channel_id=1, source_target_pairs={{0,2},{2,0},{4,6},{6,4},{8,10},{10,8},{12,14},{14,12},{16,18},{18,... | collective-permute-start | bytes 49160 | tf_op jit(solution)/shard_map/ppermute | solution.py:610
  74.8 1.7 %collective-permute-start.9 = (bf16[16,48,128]{2,1,0:T(8,128)(2,1)S(1)}, bf16[16,48,128]{2,1,0:T(8,128)(2,1)S(1)}, u32[]{:S(2)}, u32[]{:S(2)}) collective-permute-start(bf16[16,48,128]{2,1,0:T(8,128)(2,1)S(1)} %all-to-all-done.3.refs_0_), channel_id=1, source_target_pairs={{1,0},{0,1},{3,2},{2,3},{5,4},{4,5},{7,6},{6,7},{9,8},{8,9},{11,10... | collective-permute-start | bytes 589832 | tf_op jit(solution)/shard_map/ppermute | solution.py:499
  74.8 1.5 %collective-permute-start.10 = (bf16[64,128]{1,0:T(8,128)(2,1)S(1)}, bf16[64,128]{1,0:T(8,128)(2,1)S(1)}, u32[]{:S(2)}, u32[]{:S(2)}) collective-permute-start(bf16[64,128]{1,0:T(8,128)(2,1)S(1)} %collective-permute-done.7.refs_2_), channel_id=1, source_target_pairs={{1,0},{0,1},{3,2},{2,3},{5,4},{4,5},{7,6},{6,7},{9,8},{8,9},{11,10... | collective-permute-start | bytes 49160 | tf_op jit(solution)/shard_map/ppermute | solution.py:499
  75.3 1.2 %collective-permute-start.11 = (bf16[64,128]{1,0:T(8,128)(2,1)S(1)}, bf16[64,128]{1,0:T(8,128)(2,1)S(1)}, u32[]{:S(2)}, u32[]{:S(2)}) collective-permute-start(bf16[64,128]{1,0:T(8,128)(2,1)S(1)} %collective-permute-done.8.refs_4_), channel_id=1, source_target_pairs={{1,0},{0,1},{3,2},{2,3},{5,4},{4,5},{7,6},{6,7},{9,8},{8,9},{11,10... | collective-permute-start | bytes 49160 | tf_op jit(solution)/shard_map/ppermute | solution.py:499

commit v23 on v22

--- a/solution.py
+++ b/solution.py
@@ -368,9 +368,7 @@
 
 def picked_rows(z, arrived, picks):
     flat = arrived[...].reshape(z.columns, z.lanes)
-    near = picks.shape[1]
-    product = dot(picks[...].reshape(z.subs * near, z.columns), flat)
-    return fold(z, select(z, [product[h * near : (h + 1) * near] for h in range(z.subs)])).astype(BF16)
+    return fold(z, select(z, [dot(picks[h], flat) for h in range(z.subs)])).astype(BF16)
 
 
 def update_kernel(z, *refs):

time: 81.4 us -> 81.1 us (level)
  no operation moved by 1% of the time
where the time goes in v23:
time: 81.1 us; the launch traced here: 80.5 us
  starting transfers between devices  35.5 us (44%)
  Pallas kernels  34.8 us (43%)
  waiting for transfers between devices  9.48 us (12%)
    pallas_call x9, Pallas kernels, call(): pl.pallas_call(whole, out_shape=[pltpu.HBM(o.shape, o.dtype) for o in out...  34.8 us
    all_to_all x2, starting transfers between devices, body(): restricted = spread(message)  12.5 us
    ppermute x2, starting transfers between devices, body(): second_got = lax.ppermute(second_pair, 'sub', second_pairs)  11.1 us
    all_to_all x2, starting transfers between devices, body(): coarse = spread(message)  10.1 us
    all_to_all x2, waiting for transfers between devices, body(): restricted = spread(message)  3.72 us
    ppermute x2, waiting for transfers between devices, body(): second_got = lax.ppermute(second_pair, 'sub', second_pairs)  3.47 us
    ppermute x7, waiting for transfers between devices, pieces_of(): lax.ppermute(block, GROUP, [((g + k) % group, g) for g in range(group)])  2.28 us
    ppermute x7, starting transfers between devices, pieces_of(): lax.ppermute(block, GROUP, [((g + k) % group, g) for g in range(group)])  1.68 us
  transfers between devices with their start and end apart: 16, of which 7 were waited for; matrix products, arithmetic and copies ran while one was open for 0% of the time, Pallas kernels for 31%

profile of v23, /device:TPU:0, one launch (start us, length us, event | category | flops | bytes accessed | tf_op | source)
XLA Modules:
  0.0 80.5 jit_solution(12604794551452740355)
XLA Ops:
  0.6 0.5 collective-permute-start
  1.1 1.2 %collective-permute-done.refs_1_.refs_5_ = bf16[2,48,512]{2,1,0:T(8,128)(2,1)S(1)} collective-permute-done((bf16[2,48,512]{2,1,0:T(8,128)(2,1)}, bf16[2,48,512]{2,1,0:T(8,128)(2,1)S(1)}, u32[]{:S(2)}, u32[]{:S(2)}) %collective-permute-start) | collective-permute-done | bytes 98336 | tf_op jit(solution)/shard_map/ppermute | solution.py:497
  2.3 0.4 collective-permute-start.2
  2.7 0.2 collective-permute-start.3
  2.8 2.3 %open.1 = bf16[16,64,128]{2,1,0:T(8,128)(2,1)} custom-call(bf16[2,48,512]{2,1,0:T(8,128)(2,1)} %bitcast.2, bf16[2,48,512]{2,1,0:T(8,128)(2,1)S(1)} %collective-permute-done.refs_1_.refs_5_, bf16[2,1024,128]{2,1,0:T(8,128)(2,1)} %refs_6_.1, s32[2,48]{1,0:T(2,128)} %refs_3_.2), custom_call_target="tpu_custom_call" | custom-call | flops 67108864 | bytes 983424 | tf_op jit(solution)/shard_map/open/pallas_call | solution.py:473
  5.1 8.2 %all-to-all-start = ((bf16[16,64,128]{2,1,0:T(8,128)(2,1)}), bf16[16,64,128]{2,1,0:T(8,128)(2,1)S(1)}, u32[]{:S(2)}, u32[]{:S(2)}) async-start(bf16[16,64,128]{2,1,0:T(8,128)(2,1)} %open.1), calls=%async_computation | async-start | bytes 524288 | tf_op jit(solution)/shard_map/all_to_all | solution.py:535
  13.3 0.1 collective-permute-start.1
  13.4 0.0 collective-permute-done.2.refs_1_
  13.4 6.8 %first_image.1 = (bf16[1024,128]{1,0:T(8,128)(2,1)}, f32[1024,128]{1,0:T(8,128)}, f32[1024,128]{1,0:T(8,128)}, bf16[2,128,128]{2,1,0:T(8,128)(2,1)}, bf16[2,128,...) custom-call(bf16[2,512,1024]{2,1,0:T(8,128)(2,1)} %refs_0_.2, ...), custom_call_target="tpu_custom_call" | custom-call | flops 1073741824 | bytes 11339776 | tf_op jit(solution)/shard_map/first_image/pallas_call | solution.py:473
  20.2 3.3 %all-to-all-done.refs_2_ = bf16[16,64,128]{2,1,0:T(8,128)(2,1)S(1)} async-done(((bf16[16,64,128]{2,1,0:T(8,128)(2,1)}), bf16[16,64,128]{2,1,0:T(8,128)(2,1)S(1)}, u32[]{:S(2)}, u32[]{:S(2)}) %all-to-all-start) | async-done | bytes 262176 | tf_op jit(solution)/shard_map/all_to_all | solution.py:535
  23.5 3.1 %order.1 = (bf16[2,96,768]{2,1,0:T(8,128)(2,1)}, f32[2,16,128]{2,1,0:T(8,128)}, bf16[16,48,128]{2,1,0:T(8,128)(2,1)}) custom-call(bf16[96,768]{1,0:T(8,128)(2,1)} %refs_0_.1, bf16[96,768]{1,0:T(8,128)(2,1)S(1)} %collective-permute-done.1.refs_1_, bf16[16,64,128]{2,1,0:T(8,128)(2,1)S(1)} %all-to-all-done.refs_2_, bf16[128,768]{1,0:T(8,128)(2,1)} %constant.6.clone.refs_3_, ...), custom_call_target="tpu_custom_call" | custom-call | flops 452984832 | bytes 1310720 | tf_op jit(solution)/shard_map/order/pallas_call | solution.py:473
  26.6 3.6 %all-to-all-start.1 = ((bf16[16,48,128]{2,1,0:T(8,128)(2,1)}), bf16[16,48,128]{2,1,0:T(8,128)(2,1)S(1)}, u32[]{:S(2)}, u32[]{:S(2)}) async-start(bf16[16,48,128]{2,1,0:T(8,128)(2,1)} %get-tuple-element.43), calls=%async_computation.1 | async-start | bytes 393216 | tf_op jit(solution)/shard_map/all_to_all | solution.py:567
  30.2 5.5 %collective-permute-start.5 = (bf16[128,128]{1,0:T(8,128)(2,1)}, bf16[128,128]{1,0:T(8,128)(2,1)S(1)}, u32[]{:S(2)}, u32[]{:S(2)}) collective-permute-start(bf16[128,128]{1,0:T(8,128)(2,1)} %get-tuple-element.56), channel_id=1, source_target_pairs={{0,30},{2,4},{4,2},{6,8},{8,6},{10,12},{12,10},{14,16},{16,14},{18... | collective-permute-start | bytes 98312 | tf_op jit(solution)/shard_map/ppermute | solution.py:568
  35.8 3.1 %begin.1 = (bf16[2,48,128]{2,1,0:T(8,128)(2,1)}, bf16[2,48,128]{2,1,0:T(8,128)(2,1)}, bf16[2,48,48]{2,1,0:T(8,128)(2,1)}, f32[48,128]{1,0:T(8,128)}, bf16[2,192,768]{2,1,0:T(8,128)(2,1)}) custom-call(bf16[1024,128]{1,0:T(8,128)(2,1)} %get-tuple-element.44.refs_0_.refs_4_, f32[1024,128]{1,0:T(8,128)} %get-tuple-element.45.refs_1_.refs_5_, ...), custom_call_target="tpu_custom_call" | custom-call | flops 67108864 | bytes 2204672 | tf_op jit(solution)/shard_map/begin/pallas_call | solution.py:473
  38.9 1.7 %collective-permute-done.5.refs_9_.refs_12_.refs_10_ = bf16[128,128]{1,0:T(8,128)(2,1)S(1)} collective-permute-done((bf16[128,128]{1,0:T(8,128)(2,1)}, bf16[128,128]{1,0:T(8,128)(2,1)S(1)}, u32[]{:S(2)}, u32[]{:S(2)}) %collective-permute-start.5) | collective-permute-done | bytes 32800 | tf_op jit(solution)/shard_map/ppermute | solution.py:568
  40.6 0.0 collective-permute-done.4.refs_8_.refs_11_.refs_9_
  40.6 0.0 all-to-all-done.1.refs_0_
  40.6 2.8 %update.1 = (bf16[192,128]{1,0:T(8,128)(2,1)}, bf16[16,48,128]{2,1,0:T(8,128)(2,1)}) custom-call(bf16[16,48,128]{2,1,0:T(8,128)(2,1)S(1)} %all-to-all-done.1.refs_0_, bf16[2,192,768]{2,1,0:T(8,128)(2,1)} %get-tuple-element.49.refs_1_.refs_6_, f32[48,128]{1,0:T(8,128)} %get-tuple-element.50.refs_2_, bf16[2,48,48]{2,1,0:T(8,128)(2,1)} %get-tuple-element.51.refs_3_, ...), custom_call_target="tpu_custom_call" | custom-call | flops 16777216 | bytes 1311744 | tf_op jit(solution)/shard_map/update/pallas_call | solution.py:473
  43.5 4.3 %all-to-all-start.2 = ((bf16[16,48,128]{2,1,0:T(8,128)(2,1)}), bf16[16,48,128]{2,1,0:T(8,128)(2,1)S(1)}, u32[]{:S(2)}, u32[]{:S(2)}) async-start(bf16[16,48,128]{2,1,0:T(8,128)(2,1)} %get-tuple-element.57), calls=%async_computation.2 | async-start | bytes 393216 | tf_op jit(solution)/shard_map/all_to_all | solution.py:588
  47.7 7.6 %second_image.1 = (bf16[64,128]{1,0:T(8,128)(2,1)}, bf16[64,128]{1,0:T(8,128)(2,1)}, f32[2,512,128]{2,1,0:T(8,128)}, f32[2,512,128]{2,1,0:T(8,128)}) custom-call(bf16[2,512,1024]{2,1,0:T(8,128)(2,1)} %refs_0_.2, bf16[2,512,1024]{2,1,0:T(8,128)(2,1)S(1)} %collective-permute-done.2.refs_1_, bf16[2,512,1024]{2,1,0:T(8,128)(2,1)} %refs_2_.3, ...), custom_call_target="tpu_custom_call" | custom-call | flops 1073741824 | bytes 11552768 | tf_op jit(solution)/shard_map/second_image/pallas_call | solution.py:473
  55.3 0.1 collective-permute-start.6
  55.4 0.4 all-to-all-done.2.refs_0_
  55.8 2.2 %coarse.1 = bf16[16,48,128]{2,1,0:T(8,128)(2,1)} custom-call(bf16[16,48,128]{2,1,0:T(8,128)(2,1)S(1)} %all-to-all-done.2.refs_0_, bf16[2,96,768]{2,1,0:T(8,128)(2,1)} %get-tuple-element.62.refs_1_), custom_call_target="tpu_custom_call" | custom-call | flops 16777216 | bytes 688128 | tf_op jit(solution)/shard_map/coarse/pallas_call | solution.py:473
  58.0 6.5 %all-to-all-start.3 = ((bf16[16,48,128]{2,1,0:T(8,128)(2,1)}), bf16[16,48,128]{2,1,0:T(8,128)(2,1)S(1)}, u32[]{:S(2)}, u32[]{:S(2)}) async-start(bf16[16,48,128]{2,1,0:T(8,128)(2,1)} %coarse.1), calls=%async_computation.3 | async-start | bytes 393216 | tf_op jit(solution)/shard_map/all_to_all | solution.py:618
  64.5 5.5 %collective-permute-start.8 = (bf16[64,128]{1,0:T(8,128)(2,1)}, bf16[64,128]{1,0:T(8,128)(2,1)S(1)}, u32[]{:S(2)}, u32[]{:S(2)}) collective-permute-start(bf16[64,128]{1,0:T(8,128)(2,1)} %get-tuple-element.65), channel_id=1, source_target_pairs={{0,30},{2,4},{4,2},{6,8},{8,6},{10,12},{12,10},{14,16},{16,14},{18... | collective-permute-start | bytes 49160 | tf_op jit(solution)/shard_map/ppermute | solution.py:619
  70.1 2.7 %base.1.refs_14_ = f32[2,2,512,128]{3,2,1,0:T(8,128)} custom-call(f32[2,512,128]{2,1,0:T(8,128)} %get-tuple-element.63.refs_0_, f32[2,512,128]{2,1,0:T(8,128)S(1)} %collective-permute-done.6.refs_1_), custom_call_target="tpu_custom_call" | custom-call | flops 16777216 | bytes 2097152 | tf_op jit(solution)/shard_map/base/pallas_call | solution.py:473
  72.8 1.8 %collective-permute-done.8.refs_4_ = bf16[64,128]{1,0:T(8,128)(2,1)S(1)} collective-permute-done((bf16[64,128]{1,0:T(8,128)(2,1)}, bf16[64,128]{1,0:T(8,128)(2,1)S(1)}, u32[]{:S(2)}, u32[]{:S(2)}) %collective-permute-start.8) | collective-permute-done | bytes 16416 | tf_op jit(solution)/shard_map/ppermute | solution.py:619
  74.6 0.5 collective-permute-start.10
  75.1 0.1 collective-permute-start.11
  75.1 0.9 %collective-permute-done.10.refs_3_ = bf16[64,128]{1,0:T(8,128)(2,1)S(1)} collective-permute-done((bf16[64,128]{1,0:T(8,128)(2,1)S(1)}, bf16[64,128]{1,0:T(8,128)(2,1)S(1)}, u32[]{:S(2)}, u32[]{:S(2)}) %collective-permute-start.10) | collective-permute-done | bytes 16416 | tf_op jit(solution)/shard_map/ppermute | solution.py:497
  76.0 0.2 collective-permute-done.11.refs_5_
  76.2 4.2 %last.1 = (f32[2,512,128]{2,1,0:T(8,128)}, f32[2,512,128]{2,1,0:T(8,128)}) custom-call(bf16[16,48,128]{2,1,0:T(8,128)(2,1)S(1)} %all-to-all-done.3.refs_0_, bf16[16,48,128]{2,1,0:T(8,128)(2,1)S(1)} %collective-permute-done.9.refs_1_, bf16[64,128]{1,0:T(8,128)(2,1)S(1)} %collective-permute-done.7.refs_2_, ...), custom_call_target="tpu_custom_call" | custom-call | flops 134217728 | bytes 3868672 | tf_op jit(solution)/shard_map/last/pallas_call | solution.py:473
  (9 shorter events, 0.0 us)
Async XLA Ops:
  0.6 1.7 %collective-permute-start = (bf16[2,48,512]{2,1,0:T(8,128)(2,1)}, bf16[2,48,512]{2,1,0:T(8,128)(2,1)S(1)}, u32[]{:S(2)}, u32[]{:S(2)}) collective-permute-start(bf16[2,48,512]{2,1,0:T(8,128)(2,1)} %bitcast.1), channel_id=1, source_target_pairs={{1,0},{0,1},{3,2},{2,3},{5,4},{4,5},{7,6},{6,7},{9,8},{8,9},{11,10... | collective-permute-start | bytes 294920 | tf_op jit(solution)/shard_map/ppermute | solution.py:497
  2.3 11.1 %collective-permute-start.2 = (bf16[2,512,1024]{2,1,0:T(8,128)(2,1)}, bf16[2,512,1024]{2,1,0:T(8,128)(2,1)S(1)}, u32[]{:S(2)}, u32[]{:S(2)}) collective-permute-start(bf16[2,512,1024]{2,1,0:T(8,128)(2,1)} %refs_0_.2), channel_id=1, source_target_pairs={{1,0},{0,1},{3,2},{2,3},{5,4},{4,5},{7,6},{6,7},{9,8},{8,9},{11,10... | collective-permute-start | bytes 6291464 | tf_op jit(solution)/shard_map/ppermute | solution.py:497
  2.7 10.8 %collective-permute-start.3 = (bf16[2,512,1024]{2,1,0:T(8,128)(2,1)}, bf16[2,512,1024]{2,1,0:T(8,128)(2,1)}, u32[]{:S(2)}, u32[]{:S(2)}) collective-permute-start(bf16[2,512,1024]{2,1,0:T(8,128)(2,1)} %refs_2_.3), channel_id=1, source_target_pairs={{1,0},{0,1},{3,2},{2,3},{5,4},{4,5},{7,6},{6,7},{9,8},{8,9},{11,10... | collective-permute-start | bytes 6291464 | tf_op jit(solution)/shard_map/ppermute | solution.py:497
  5.1 18.4 %all-to-all-start = ((bf16[16,64,128]{2,1,0:T(8,128)(2,1)}), bf16[16,64,128]{2,1,0:T(8,128)(2,1)S(1)}, u32[]{:S(2)}, u32[]{:S(2)}) async-start(bf16[16,64,128]{2,1,0:T(8,128)(2,1)} %open.1), calls=%async_computation | async-start | bytes 524288 | tf_op jit(solution)/shard_map/all_to_all | solution.py:535
  13.3 10.2 %collective-permute-start.1 = (bf16[96,768]{1,0:T(8,128)(2,1)}, bf16[96,768]{1,0:T(8,128)(2,1)S(1)}, u32[]{:S(2)}, u32[]{:S(2)}) collective-permute-start(bf16[96,768]{1,0:T(8,128)(2,1)} %refs_0_.1), channel_id=1, source_target_pairs={{1,0},{0,1},{3,2},{2,3},{5,4},{4,5},{7,6},{6,7},{9,8},{8,9},{11,10... | collective-permute-start | bytes 442376 | tf_op jit(solution)/shard_map/ppermute | solution.py:497
  26.6 14.0 %all-to-all-start.1 = ((bf16[16,48,128]{2,1,0:T(8,128)(2,1)}), bf16[16,48,128]{2,1,0:T(8,128)(2,1)S(1)}, u32[]{:S(2)}, u32[]{:S(2)}) async-start(bf16[16,48,128]{2,1,0:T(8,128)(2,1)} %get-tuple-element.43), calls=%async_computation.1 | async-start | bytes 393216 | tf_op jit(solution)/shard_map/all_to_all | solution.py:567
  30.2 10.4 %collective-permute-start.5 = (bf16[128,128]{1,0:T(8,128)(2,1)}, bf16[128,128]{1,0:T(8,128)(2,1)S(1)}, u32[]{:S(2)}, u32[]{:S(2)}) collective-permute-start(bf16[128,128]{1,0:T(8,128)(2,1)} %get-tuple-element.56), channel_id=1, source_target_pairs={{0,30},{2,4},{4,2},{6,8},{8,6},{10,12},{12,10},{14,16},{16,14},{18... | collective-permute-start | bytes 98312 | tf_op jit(solution)/shard_map/ppermute | solution.py:568
  35.8 4.8 %collective-permute-start.4 = (bf16[128,128]{1,0:T(8,128)(2,1)}, bf16[128,128]{1,0:T(8,128)(2,1)S(1)}, u32[]{:S(2)}, u32[]{:S(2)}) collective-permute-start(bf16[128,128]{1,0:T(8,128)(2,1)} %get-tuple-element.41), channel_id=1, source_target_pairs={{0,2},{2,0},{4,6},{6,4},{8,10},{10,8},{12,14},{14,12},{16,18},{18,... | collective-permute-start | bytes 98312 | tf_op jit(solution)/shard_map/ppermute | solution.py:556
  43.5 12.4 %all-to-all-start.2 = ((bf16[16,48,128]{2,1,0:T(8,128)(2,1)}), bf16[16,48,128]{2,1,0:T(8,128)(2,1)S(1)}, u32[]{:S(2)}, u32[]{:S(2)}) async-start(bf16[16,48,128]{2,1,0:T(8,128)(2,1)} %get-tuple-element.57), calls=%async_computation.2 | async-start | bytes 393216 | tf_op jit(solution)/shard_map/all_to_all | solution.py:588
  55.3 14.8 %collective-permute-start.6 = (f32[2,512,128]{2,1,0:T(8,128)}, f32[2,512,128]{2,1,0:T(8,128)S(1)}, u32[]{:S(2)}, u32[]{:S(2)}) collective-permute-start(f32[2,512,128]{2,1,0:T(8,128)} %get-tuple-element.64), channel_id=1, source_target_pairs={{0,1},{1,0},{2,3},{3,2},{4,5},{5,4},{6,7},{7,6},{8,9},{9,8},{10,11... | collective-permute-start | bytes 1572872 | tf_op jit(solution)/shard_map/ppermute | solution.py:622
  58.0 16.5 %all-to-all-start.3 = ((bf16[16,48,128]{2,1,0:T(8,128)(2,1)}), bf16[16,48,128]{2,1,0:T(8,128)(2,1)S(1)}, u32[]{:S(2)}, u32[]{:S(2)}) async-start(bf16[16,48,128]{2,1,0:T(8,128)(2,1)} %coarse.1), calls=%async_computation.3 | async-start | bytes 393216 | tf_op jit(solution)/shard_map/all_to_all | solution.py:618
  64.5 10.0 %collective-permute-start.8 = (bf16[64,128]{1,0:T(8,128)(2,1)}, bf16[64,128]{1,0:T(8,128)(2,1)S(1)}, u32[]{:S(2)}, u32[]{:S(2)}) collective-permute-start(bf16[64,128]{1,0:T(8,128)(2,1)} %get-tuple-element.65), channel_id=1, source_target_pairs={{0,30},{2,4},{4,2},{6,8},{8,6},{10,12},{12,10},{14,16},{16,14},{18... | collective-permute-start | bytes 49160 | tf_op jit(solution)/shard_map/ppermute | solution.py:619
  70.1 4.5 %collective-permute-start.7 = (bf16[64,128]{1,0:T(8,128)(2,1)}, bf16[64,128]{1,0:T(8,128)(2,1)S(1)}, u32[]{:S(2)}, u32[]{:S(2)}) collective-permute-start(bf16[64,128]{1,0:T(8,128)(2,1)} %get-tuple-element.60), channel_id=1, source_target_pairs={{0,2},{2,0},{4,6},{6,4},{8,10},{10,8},{12,14},{14,12},{16,18},{18,... | collective-permute-start | bytes 49160 | tf_op jit(solution)/shard_map/ppermute | solution.py:608
  74.5 1.7 %collective-permute-start.9 = (bf16[16,48,128]{2,1,0:T(8,128)(2,1)S(1)}, bf16[16,48,128]{2,1,0:T(8,128)(2,1)S(1)}, u32[]{:S(2)}, u32[]{:S(2)}) collective-permute-start(bf16[16,48,128]{2,1,0:T(8,128)(2,1)S(1)} %all-to-all-done.3.refs_0_), channel_id=1, source_target_pairs={{1,0},{0,1},{3,2},{2,3},{5,4},{4,5},{7,6},{6,7},{9,8},{8,9},{11,10... | collective-permute-start | bytes 589832 | tf_op jit(solution)/shard_map/ppermute | solution.py:497
  74.6 1.5 %collective-permute-start.10 = (bf16[64,128]{1,0:T(8,128)(2,1)S(1)}, bf16[64,128]{1,0:T(8,128)(2,1)S(1)}, u32[]{:S(2)}, u32[]{:S(2)}) collective-permute-start(bf16[64,128]{1,0:T(8,128)(2,1)S(1)} %collective-permute-done.7.refs_2_), channel_id=1, source_target_pairs={{1,0},{0,1},{3,2},{2,3},{5,4},{4,5},{7,6},{6,7},{9,8},{8,9},{11,10... | collective-permute-start | bytes 49160 | tf_op jit(solution)/shard_map/ppermute | solution.py:497
  75.1 1.2 %collective-permute-start.11 = (bf16[64,128]{1,0:T(8,128)(2,1)S(1)}, bf16[64,128]{1,0:T(8,128)(2,1)S(1)}, u32[]{:S(2)}, u32[]{:S(2)}) collective-permute-start(bf16[64,128]{1,0:T(8,128)(2,1)S(1)} %collective-permute-done.8.refs_4_), channel_id=1, source_target_pairs={{1,0},{0,1},{3,2},{2,3},{5,4},{4,5},{7,6},{6,7},{9,8},{8,9},{11,10... | collective-permute-start | bytes 49160 | tf_op jit(solution)/shard_map/ppermute | solution.py:497
